TPU v7x, 32 devices: a whole 2x2x4 slice. The times are simulated.
32 devices in a mesh: ctx: 32 (over z, y, x, core), dp: 1.
Axes of the slice: x: 2, y: 2, z: 4, core: 2. Of those that a mesh axis runs over, the one named last changes fastest.
Arguments:
- tokens: bfloat16 [1, 8192, 768], P('dp', 'ctx'), may hold values from -40 to 40
- cotangent: bfloat16 [1, 8192, 768], P('dp', 'ctx'), may hold values from -200 to 200
- norm_gain: float32 [768], replicated, may hold values from 0.1 to 1.9
- conv_weight: bfloat16 [3, 768, 768], P(None, 'ctx'), may hold values from -0.125 to 0.125
- up_weight: bfloat16 [768, 1152], P('ctx'), may hold values from -0.21875 to 0.21875
- down_weight: bfloat16 [1152, 768], P('ctx'), may hold values from -0.1875 to 0.1875
- contig_first_bins: int32 [4], replicated, may hold values from 0 to 6655, as said below
Outputs:
- output: bfloat16 [1, 8192, 768], P('dp', 'ctx')
- input_grad: bfloat16 [1, 8192, 768], P('dp', 'ctx')
- down_grad: float32 [1152, 768], P('ctx', 'dp')
- gain_grad: float32 [768], P('dp')
Inputs may be any that keep to these rules, and one draw needn't show every extreme that they name: contig_first_bins[0] = 0; the starts increase strictly, consecutive ones at least 1024 bins apart; the last contig starts at 6655.
All inputs are finite; a program needn't handle non-finite values.
Results may differ from a plain program's by a relative error of at most 0.0054.
Values may be sent and summed in bfloat16 or wider, within the bound.
No kernel may reach another device: no remote copies, remote signals or barrier semaphores. Data moves between devices by JAX's collectives and lax.ppermute only.
A program may use at most 64 MiB of HBM per device.

v0:
```python
import jax
import jax.numpy as jnp
from jax import lax
from jax.sharding import PartitionSpec as P

DILATION_BINS = 64


root_half = 0.7071067811865476
inv_root_two_pi = 0.3989422804014327


def with_halo(value, sides, width):
    for axis, dim in sides:
        devices, length = (lax.axis_size(axis), value.shape[dim])
        up = [(i, (i + 1) % devices) for i in range(devices - 1)]
        down = [(j, i) for i, j in up]
        last = lax.slice_in_dim(value, length - width, length, axis=dim)
        leading = lax.slice_in_dim(value, 0, width, axis=dim)
        before = lax.ppermute(last, axis, up)
        after = lax.ppermute(leading, axis, down)
        value = jnp.concatenate([before, value, after], axis=dim)
    return value


def segment_lookup(bin_position, contig_first_bins):
    return jnp.sum((contig_first_bins[None, :] <= bin_position[:, None]).astype(jnp.int32), axis=1)


def tap_masks(bin_position, contig_first_bins, overall_bin_count):
    current_segment = segment_lookup(bin_position, contig_first_bins)
    preceding_segment = segment_lookup(bin_position - DILATION_BINS, contig_first_bins)
    following_segment = segment_lookup(bin_position + DILATION_BINS, contig_first_bins)
    left_valid_mask = jnp.logical_and(
        bin_position >= DILATION_BINS, preceding_segment == current_segment
    )
    right_valid_mask = jnp.logical_and(
        bin_position + DILATION_BINS < overall_bin_count, following_segment == current_segment
    )
    return (
        left_valid_mask.astype(jnp.bfloat16)[:, None],
        right_valid_mask.astype(jnp.bfloat16)[:, None],
    )


def gelu_value(pre_value):
    return 0.5 * pre_value * (1.0 + lax.erf(pre_value * root_half))


def gelu_slope(pre_value):
    return (
        0.5 * (1.0 + lax.erf(pre_value * root_half))
        + pre_value * jnp.exp(-0.5 * pre_value * pre_value) * inv_root_two_pi
    )


def body(tokens, cotangent, norm_gain, conv_weight, up_weight, down_weight, contig_first_bins):
    seq_count, bin_count, feat_width = tokens.shape
    ctx_count = lax.axis_size("ctx")
    data_count = lax.axis_size("dp")
    conv_full, up_full, down_full = (
        lax.all_gather(conv_weight, "ctx", axis=1, tiled=True),
        lax.all_gather(up_weight, "ctx", axis=0, tiled=True),
        lax.all_gather(down_weight, "ctx", axis=0, tiled=True),
    )
    bin_position = lax.axis_index("ctx") * bin_count + jnp.arange(bin_count, dtype=jnp.int32)
    left_valid_mask, right_valid_mask = tap_masks(
        bin_position, contig_first_bins, ctx_count * bin_count
    )
    tok_float = tokens.astype(jnp.float32)
    inverse = lax.rsqrt(jnp.mean(tok_float * tok_float, axis=2, keepdims=True) + 1e-05)
    scaled = tok_float * inverse
    normalized_input = (scaled * norm_gain).astype(jnp.bfloat16)
    padded_input = with_halo(normalized_input, (("ctx", 1),), DILATION_BINS)
    preceding_value = padded_input[:, :bin_count] * left_valid_mask
    following_tap = padded_input[:, 2 * DILATION_BINS :] * right_valid_mask
    stacked = jnp.concatenate([preceding_value, normalized_input, following_tap], axis=2).reshape(
        seq_count * bin_count, 3 * feat_width
    )
    conv_out = jnp.dot(
        stacked, conv_full.reshape(3 * feat_width, feat_width), preferred_element_type=jnp.float32
    )
    mixed_sum = tok_float.reshape(-1, feat_width) + conv_out
    pre_act = jnp.dot(mixed_sum.astype(jnp.bfloat16), up_full, preferred_element_type=jnp.float32)
    hidden = gelu_value(pre_act).astype(jnp.bfloat16)
    output = (mixed_sum + jnp.dot(hidden, down_full, preferred_element_type=jnp.float32)).astype(
        jnp.bfloat16
    )
    grad_flat = cotangent.reshape(-1, feat_width)
    hidden_grad = lax.dot_general(
        grad_flat, down_full, (((1,), (1,)), ((), ())), preferred_element_type=jnp.float32
    )
    pre_grad = (hidden_grad * gelu_slope(pre_act)).astype(jnp.bfloat16)
    mixed_grad = grad_flat.astype(jnp.float32) + lax.dot_general(
        pre_grad, up_full, (((1,), (1,)), ((), ())), preferred_element_type=jnp.float32
    )
    convolution_gradient = mixed_grad.astype(jnp.bfloat16).reshape(seq_count, bin_count, feat_width)
    padded_gradient = with_halo(convolution_gradient, (("ctx", 1),), DILATION_BINS)
    preceding_gradient = padded_gradient[:, :bin_count] * left_valid_mask
    following_gradient = padded_gradient[:, 2 * DILATION_BINS :] * right_valid_mask
    back_stack = jnp.stack(
        [following_gradient, convolution_gradient, preceding_gradient], axis=2
    ).reshape(seq_count * bin_count, 3, feat_width)
    normed_grad = lax.dot_general(
        back_stack, conv_full, (((1, 2), (0, 2)), ((), ())), preferred_element_type=jnp.float32
    )
    scaled_flat = scaled.reshape(-1, feat_width)
    scaled_grad = normed_grad * norm_gain
    inner_mean = jnp.mean(scaled_grad * scaled_flat, axis=1, keepdims=True)
    input_grad = (
        mixed_grad + inverse.reshape(-1, 1) * (scaled_grad - scaled_flat * inner_mean)
    ).astype(jnp.bfloat16)
    gain_term = jnp.sum(normed_grad * scaled_flat, axis=0)
    factor = float(ctx_count * data_count * bin_count * seq_count) ** (-0.5)
    ff_count = hidden.shape[1]
    ff_part = ff_count // ctx_count
    width_part = feat_width // data_count
    blocks = jnp.einsum(
        "rcf,rdw->cdfw",
        hidden.reshape(-1, ctx_count, ff_part),
        grad_flat.reshape(-1, data_count, width_part),
        preferred_element_type=jnp.float32,
    ).reshape(-1, width_part)
    down_part = lax.psum_scatter(blocks, ("ctx", "dp"), scatter_dimension=0, tiled=True)
    gain_all = lax.psum(gain_term, ("ctx", "dp"))
    gain_part = lax.dynamic_slice_in_dim(gain_all, lax.axis_index("dp") * width_part, width_part)
    return (
        output.reshape(tokens.shape),
        input_grad.reshape(tokens.shape),
        down_part * factor,
        gain_part * factor,
    )


def solution(mesh):
    placed = (
        P("dp", "ctx", None),
        P("dp", "ctx", None),
        P(),
        P(None, "ctx", None),
        P("ctx", None),
        P("ctx", None),
        P(),
    )
    return jax.shard_map(
        body,
        mesh=mesh,
        in_specs=placed,
        out_specs=(P("dp", "ctx", None), P("dp", "ctx", None), P("ctx", "dp"), P("dp")),
        check_vma=False,
    )
```

profile of v0, /device:TPU:0, one launch (start us, length us, event | category | flops | bytes accessed | tf_op | source)
XLA Modules:
  0.0 355.7 jit_solution(17080828096846556338)
XLA Ops:
  7.2 0.0 all-gather.9.cloned.1.call-start
  7.2 0.7 all-gather.9.cloned.1.call-update
  7.9 0.0 all-gather.5.cloned.1.call-start
  8.0 0.7 all-gather.5.cloned.1.call-update
  8.7 0.0 all-gather.7.cloned.1.call-start
  8.7 0.7 all-gather.7.cloned.1.call-update
  9.4 1.2 fusion.28
  10.6 1.2 fusion.27
  11.7 2.4 collective-permute-start
  14.1 1.3 collective-permute-start.1
  15.5 0.1 convert_reduce_fusion.2
  15.6 0.0 collective-permute-done
  15.6 3.8 %collective-permute-done.1 = bf16[1,64,768]{2,1,0:T(8,128)(2,1)S(1)} collective-permute-done((bf16[1,64,768]{2,1,0:T(8,128)(2,1)S(1)}, bf16[1,64,768]{2,1,0:T(8,128)(2,1)S(1)}, u32[]{:S(2)}, u32[]{:S(2)}) %collective-permute-start.1) | collective-permute-done | bytes 98336 | tf_op jit(solution)/shard_map/ppermute | solution.py:21
  19.4 1.1 fusion.38
  20.5 49.3 %all-gather.9.cloned.1.call-done = bf16[32,36,768]{2,1,0:T(8,128)(2,1)} async-done(((bf16[1,36,768]{2,1,0:T(8,128)(2,1)}), bf16[32,36,768]{2,1,0:T(8,128)(2,1)}) %all-gather.9.cloned.1.call-update) | async-done | bytes 1769488 | tf_op jit(solution)/shard_map/all_gather | solution.py:64
  69.8 2.5 reshape.122
  72.2 59.5 %all-gather.5.cloned.1.call-done = bf16[3,768,768]{2,1,0:T(8,128)(2,1)} async-done(((bf16[3,24,768]{2,1,0:T(8,128)(2,1)}), bf16[3,768,768]{2,1,0:T(8,128)(2,1)}) %all-gather.5.cloned.1.call-update) | async-done | bytes 3538960 | tf_op jit(solution)/shard_map/all_gather | solution.py:62
  131.7 3.3 convolution_add_fusion.2
  135.1 53.9 %all-gather.7.cloned.1.call-done = bf16[768,1152]{1,0:T(8,128)(2,1)} async-done(((bf16[24,1152]{1,0:T(8,128)(2,1)}), bf16[768,1152]{1,0:T(8,128)(2,1)}) %all-gather.7.cloned.1.call-update) | async-done | bytes 1769488 | tf_op jit(solution)/shard_map/all_gather | solution.py:63
  189.0 3.2 multiply_convert_fusion
  192.2 1.1 copy.14
  193.3 1.2 reshape.119
  194.6 3.4 convolution_add_fusion
  197.9 0.0 copy-start.10
  198.0 0.8 convert_bitcast_fusion.1
  198.8 0.7 copy-done.7
  199.5 0.7 fusion.51
  200.2 1.3 collective-permute-start.2
  201.5 3.7 %collective-permute-start.3 = (bf16[1,64,768]{2,1,0:T(8,128)(2,1)}, bf16[1,64,768]{2,1,0:T(8,128)(2,1)}, u32[]{:S(2)}, u32[]{:S(2)}) collective-permute-start(bf16[1,64,768]{2,1,0:T(8,128)(2,1)} %get-tuple-element.14), channel_id=1, source_target_pairs={{0,1},{1,2},{2,3},{3,4},{4,5},{5,6},{6,7},{7,8},{8,9},{9,10},{10,1... | collective-permute-start | bytes 294920 | tf_op jit(solution)/shard_map/ppermute | solution.py:20
  205.2 2.5 convolution_bitcast_fusion
  207.7 2.9 reshape.120
  210.7 83.0 %fusion = f32[40,768]{1,0:T(8,128)} fusion(f32[1152,768]{1,0:T(8,128)S(1)} %reshape.120), kind=kCustom, calls=%all-reduce-scatter | all-reduce-scatter fusion | flops 983041 | bytes 3661824
  293.6 3.4 fusion.3
  297.1 1.4 collective-permute-start.6
  298.5 1.3 collective-permute-start.5
  299.8 1.3 collective-permute-start.4
  301.1 0.0 collective-permute-done.2
  301.1 1.3 collective-permute-start.7
  302.4 0.0 collective-permute-done.3
  302.4 1.1 fusion.36
  303.6 1.2 fusion.26
  304.9 41.3 %psum.7 = f32[768]{0:T(1024)S(1)} all-reduce(f32[768]{0:T(1024)S(1)} %get-tuple-element.4), channel_id=1, replica_groups=mesh['ctx'=32,'dp'=1] {'ctx','dp'}, use_global_device_ids=true, to_apply=%region_7.0 | all-reduce | flops 768 | bytes 6144 | tf_op jit(solution)/shard_map/psum | solution.py:125
  346.2 1.0 fusion.32
  347.2 0.6 broadcast_multiply_fusion
  347.8 0.0 collective-permute-done.7
  347.8 0.0 collective-permute-done.6
  347.8 0.6 concatenate.22
  348.5 0.7 dynamic-slice_multiply_fusion
  (37 shorter events, 0.1 us)
Async XLA Ops:
  7.2 8.3 %copy-start.13 = (s32[4]{0:T(128)S(1)}, s32[4]{0:T(128)}, u32[]{:S(2)}) copy-start(s32[4]{0:T(128)} %param.13) | copy-start | bytes 52
  7.2 62.6 %all-gather.9.cloned.1.call-start = ((), (), s32[]{:S(2)}) async-start(), calls=%async_computation.2 | async-start | bytes 2027520 | tf_op jit(solution)/shard_map/all_gather | solution.py:64
  7.9 123.8 %all-gather.5.cloned.1.call-start = ((), (), s32[]{:S(2)}) async-start(), calls=%async_computation | async-start | bytes 3649536 | tf_op jit(solution)/shard_map/all_gather | solution.py:62
  8.7 180.4 %all-gather.7.cloned.1.call-start = ((), (), s32[]{:S(2)}) async-start(), calls=%async_computation.1 | async-start | bytes 1824768 | tf_op jit(solution)/shard_map/all_gather | solution.py:63
  11.7 3.8 %collective-permute-start = (bf16[1,64,768]{2,1,0:T(8,128)(2,1)S(1)}, bf16[1,64,768]{2,1,0:T(8,128)(2,1)S(1)}, u32[]{:S(2)}, u32[]{:S(2)}) collective-permute-start(bf16[1,64,768]{2,1,0:T(8,128)(2,1)S(1)} %get-tuple-element.17), channel_id=1, source_target_pairs={{0,1},{1,2},{2,3},{3,4},{4,5},{5,6},{6,7},{7,8},{8,9},{9,10},{10,1... | collective-permute-start | bytes 294920 | tf_op jit(solution)/shard_map/ppermute | solution.py:20
  14.1 5.3 %collective-permute-start.1 = (bf16[1,64,768]{2,1,0:T(8,128)(2,1)S(1)}, bf16[1,64,768]{2,1,0:T(8,128)(2,1)S(1)}, u32[]{:S(2)}, u32[]{:S(2)}) collective-permute-start(bf16[1,64,768]{2,1,0:T(8,128)(2,1)S(1)} %get-tuple-element.18), channel_id=1, source_target_pairs={{1,0},{2,1},{3,2},{4,3},{5,4},{6,5},{7,6},{8,7},{9,8},{10,9},{11,1... | collective-permute-start | bytes 294920 | tf_op jit(solution)/shard_map/ppermute | solution.py:21
  20.5 111.2 %copy-start.2 = (bf16[1,256,768]{2,1,0:T(8,128)(2,1)S(1)}, bf16[1,256,768]{2,1,0:T(8,128)(2,1)}, u32[]{:S(2)}) copy-start(bf16[1,256,768]{2,1,0:T(8,128)(2,1)} %param.7) | copy-start | bytes 1179652
  72.2 122.3 %copy-start = (bf16[1152,768]{1,0:T(8,128)(2,1)}, bf16[1152,768]{1,0:T(8,128)(2,1)S(1)}, u32[]{:S(2)}) copy-start(bf16[1152,768]{1,0:T(8,128)(2,1)S(1)} %reshape.122) | copy-start | bytes 5308420
  135.1 57.2 %copy-start.6 = (f32[256,768]{1,0:T(8,128)}, f32[256,768]{1,0:T(8,128)S(1)}, u32[]{:S(2)}) copy-start(f32[256,768]{1,0:T(8,128)S(1)} %convolution_add_fusion.2) | copy-start | bytes 2359300
  192.2 2.3 copy-start.1
  197.9 7.2 %copy-start.4 = (f32[256,768]{1,0:T(8,128)}, f32[256,768]{1,0:T(8,128)S(1)}, u32[]{:S(2)}) copy-start(f32[256,768]{1,0:T(8,128)S(1)} %convolution_add_fusion) | copy-start | bytes 2359300
  197.9 7.2 %copy-start.10 = (bf16[1,256,768]{2,1,0:T(8,128)(2,1)S(1)}, bf16[1,256,768]{2,1,0:T(8,128)(2,1)}, u32[]{:S(2)}) copy-start(bf16[1,256,768]{2,1,0:T(8,128)(2,1)} %param.8) | copy-start | bytes 1179652
  198.8 0.7 copy-start.7
  200.2 100.9 %collective-permute-start.2 = (bf16[1,64,768]{2,1,0:T(8,128)(2,1)}, bf16[1,64,768]{2,1,0:T(8,128)(2,1)}, u32[]{:S(2)}, u32[]{:S(2)}) collective-permute-start(bf16[1,64,768]{2,1,0:T(8,128)(2,1)} %get-tuple-element.13), channel_id=1, source_target_pairs={{1,0},{2,1},{3,2},{4,3},{5,4},{6,5},{7,6},{8,7},{9,8},{10,9},{11,1... | collective-permute-start | bytes 294920 | tf_op jit(solution)/shard_map/ppermute | solution.py:21
  201.5 100.9 %collective-permute-start.3 = (bf16[1,64,768]{2,1,0:T(8,128)(2,1)}, bf16[1,64,768]{2,1,0:T(8,128)(2,1)}, u32[]{:S(2)}, u32[]{:S(2)}) collective-permute-start(bf16[1,64,768]{2,1,0:T(8,128)(2,1)} %get-tuple-element.14), channel_id=1, source_target_pairs={{0,1},{1,2},{2,3},{3,4},{4,5},{5,6},{6,7},{7,8},{8,9},{9,10},{10,1... | collective-permute-start | bytes 294920 | tf_op jit(solution)/shard_map/ppermute | solution.py:20
  293.6 3.4 copy-start.9
  293.6 8.8 %copy-start.8 = (bf16[1,256,768]{2,1,0:T(8,128)(2,1)S(1)}, bf16[1,256,768]{2,1,0:T(8,128)(2,1)}, u32[]{:S(2)}) copy-start(bf16[1,256,768]{2,1,0:T(8,128)(2,1)} %copy-done.7) | copy-start | bytes 1179652
  293.6 10.0 %copy-start.14 = (bf16[3,768,768]{2,1,0:T(8,128)(2,1)S(1)}, bf16[3,768,768]{2,1,0:T(8,128)(2,1)}, u32[]{:S(2)}) copy-start(bf16[3,768,768]{2,1,0:T(8,128)(2,1)} %all-gather.5.cloned.1.call-done) | copy-start | bytes 10616836
  297.0 6.6 %copy-start.3 = (bf16[1,256,768]{2,1,0:T(8,128)(2,1)S(1)}, bf16[1,256,768]{2,1,0:T(8,128)(2,1)}, u32[]{:S(2)}) copy-start(bf16[1,256,768]{2,1,0:T(8,128)(2,1)} %param.7) | copy-start | bytes 1179652
  297.0 6.6 %copy-start.11 = (bf16[1,256,1,768]{3,1,2,0:T(8,128)(2,1)S(1)}, bf16[1,256,1,768]{3,1,2,0:T(8,128)(2,1)}, u32[]{:S(2)}) copy-start(bf16[1,256,1,768]{3,1,2,0:T(8,128)(2,1)} %get-tuple-element.9) | copy-start | bytes 1179652
  297.0 6.6 %copy-start.12 = (f32[768]{0:T(1024)S(1)}, f32[768]{0:T(1024)}, u32[]{:S(2)}) copy-start(f32[768]{0:T(1024)} %param.9) | copy-start | bytes 9220
  297.1 50.7 %collective-permute-start.6 = (f32[40,768]{1,0:T(8,128)S(1)}, f32[40,768]{1,0:T(8,128)S(1)}, u32[]{:S(2)}, u32[]{:S(2)}) collective-permute-start(f32[40,768]{1,0:T(8,128)S(1)} %copy-done.9), channel_id=1, source_target_pairs={{0,3},{1,4},{2,5},{3,6},{4,7},{5,8},{6,9},{7,10},{8,11},{9,12},{10... | collective-permute-start | bytes 368648
  298.5 49.3 %collective-permute-start.5 = (f32[40,768]{1,0:T(8,128)S(1)}, f32[40,768]{1,0:T(8,128)S(1)}, u32[]{:S(2)}, u32[]{:S(2)}) collective-permute-start(f32[40,768]{1,0:T(8,128)S(1)} %copy-done.9), channel_id=1, source_target_pairs={{0,2},{1,3},{2,4},{3,5},{4,6},{5,7},{6,8},{7,9},{8,10},{9,11},{10,... | collective-permute-start | bytes 368648
  299.8 48.0 %collective-permute-start.4 = (f32[40,768]{1,0:T(8,128)S(1)}, f32[40,768]{1,0:T(8,128)S(1)}, u32[]{:S(2)}, u32[]{:S(2)}) collective-permute-start(f32[40,768]{1,0:T(8,128)S(1)} %copy-done.9), channel_id=1, source_target_pairs={{0,1},{1,2},{2,3},{3,4},{4,5},{5,6},{6,7},{7,8},{8,9},{9,10},{10,1... | collective-permute-start | bytes 368648
  301.1 46.7 %collective-permute-start.7 = (f32[4,768]{1,0:T(4,128)S(1)}, f32[4,768]{1,0:T(4,128)S(1)}, u32[]{:S(2)}, u32[]{:S(2)}) collective-permute-start(f32[4,768]{1,0:T(4,128)S(1)} %slice.40), channel_id=1, source_target_pairs={{0,4},{1,5},{2,6},{3,7},{4,8},{5,9},{6,10},{7,11},{8,12},{9,13},{1... | collective-permute-start | bytes 36872
  303.6 42.6 %copy-start.5 = (f32[256,768]{1,0:T(8,128)S(1)}, f32[256,768]{1,0:T(8,128)}, u32[]{:S(2)}) copy-start(f32[256,768]{1,0:T(8,128)} %copy-done.4) | copy-start | bytes 2359300
Sparse Core Ops, SparseCore 0:
  10.9 58.7 all-gather.8
  72.7 58.9 all-gather.4
  134.5 54.4 all-gather.6
where the time goes:
time: 356 us
  waiting for transfers between devices  169 us (47%)
  blocking collectives  124 us (35%)
  matrix products  17.1 us (5%)
  between operations  14.1 us (4%)
  starting transfers between devices  14 us (4%)
  local copies, waits for them, and re-layouts  9.84 us (3%)
  other arithmetic  7.71 us (2%)
    unnamed x1, blocking collectives  83 us
    all_gather x1, waiting for transfers between devices, body(): lax.all_gather(conv_weight, 'ctx', axis=1, tiled=True)  59.5 us
    all_gather x1, waiting for transfers between devices, body(): lax.all_gather(up_weight, 'ctx', axis=0, tiled=True)  53.9 us
    all_gather x1, waiting for transfers between devices, body(): lax.all_gather(down_weight, 'ctx', axis=0, tiled=True)  49.3 us
    psum x1, blocking collectives, body(): gain_all = lax.psum(gain_term, ('ctx', 'dp'))  41.3 us
  transfers between devices with their start and end apart: 11, of which 4 were waited for; matrix products, arithmetic and copies ran while one was open for 30% of the time, Pallas kernels for 0%

commit v1 on v0

--- a/solution.py
+++ b/solution.py
@@ -1,6 +1,8 @@
 import jax
 import jax.numpy as jnp
 from jax import lax
+from jax.experimental import pallas as pl
+from jax.experimental.pallas import tpu as pltpu
 from jax.sharding import PartitionSpec as P
 
 DILATION_BINS = 64
@@ -54,15 +56,206 @@
     )
 
 
+def ring_order(squares):
+    return list(range(0, squares, 2)) + list(range(1, squares, 2))[::-1]
+
+
+def swap(value, mask):
+    devices = lax.axis_size("ctx")
+    return lax.ppermute(value, "ctx", [(i, i ^ mask) for i in range(devices)])
+
+
+def ring(value, steps):
+    devices = lax.axis_size("ctx")
+    order = ring_order(devices // 8)
+    count = len(order)
+    to = {order[i]: order[(i + steps) % count] for i in range(count)}
+    return lax.ppermute(value, "ctx", [(i, i % 8 + 8 * to[i // 8]) for i in range(devices)])
+
+
+def place():
+    me = lax.axis_index("ctx")
+    return me % 2, (me // 2) % 2, (me // 4) % 2, me // 8
+
+
+def square_at(mine, steps, squares):
+    order = ring_order(squares)
+    at = jnp.int32(0)
+    for i, square in enumerate(order):
+        at = at + jnp.where(mine == square, order[(i + steps) % squares], 0).astype(jnp.int32)
+    return at
+
+
+def gather_pieces(piece):
+    squares = lax.axis_size("ctx") // 8
+    held = [piece]
+    for _ in range(squares - 1):
+        held.append(ring(held[-1], 1))
+    column = jnp.stack(held)
+    half = squares // 2
+    by_x, by_y = swap(column, 2), swap(column, 4)
+    far_first, far_second = swap(by_x[:half], 4), swap(by_y[half:], 2)
+    pieces = [column, by_x, by_y, far_first, far_second]
+    return pieces + [swap(p, 1) for p in pieces]
+
+
+def piece_slots(squares):
+    half = squares // 2
+    for core in range(2):
+        for k in range(squares):
+            yield 5 * core, k, k, 0, 0, core
+            yield 5 * core + 1, k, k, 0, 1, core
+            yield 5 * core + 2, k, k, 1, 0, core
+            if k < half:
+                yield 5 * core + 3, k, k, 1, 1, core
+            else:
+                yield 5 * core + 4, k - half, k, 1, 1, core
+
+
+VMEM = pl.BlockSpec(memory_space=pltpu.VMEM)
+PARAMS = pltpu.CompilerParams(vmem_limit_bytes=48 * 1024 * 1024)
+
+
+def assemble_rows(pieces, lead):
+    squares = lax.axis_size("ctx") // 8
+    rows, width = pieces[0].shape[-2:]
+    flat = [p.reshape(p.shape[0], lead, rows, width) for p in pieces]
+
+    def kernel(*refs):
+        out = refs[-1]
+        core, x, y, z = place()
+        for piece, slot, back, dy, dx, dc in piece_slots(squares):
+            source = square_at(z, -back, squares)
+            for t in range(lead):
+                out[t, source, y ^ dy, x ^ dx, core ^ dc] = refs[piece][slot, t]
+
+    out = pl.pallas_call(
+        kernel,
+        out_shape=jax.ShapeDtypeStruct((lead, squares, 2, 2, 2, rows, width), flat[0].dtype),
+        in_specs=[VMEM] * len(flat),
+        out_specs=VMEM,
+        compiler_params=PARAMS,
+    )(*flat)
+    return out.reshape(lead, squares * 8 * rows, width)
+
+
+def assemble_columns(pieces):
+    squares = lax.axis_size("ctx") // 8
+    rows, width = pieces[0].shape[-2:]
+
+    def kernel(*refs):
+        out = refs[-1]
+        core, x, y, z = place()
+        for piece, slot, back, dy, dx, dc in piece_slots(squares):
+            source = square_at(z, -back, squares)
+            columns = pl.ds(pl.multiple_of((core ^ dc) * width, 128), width)
+            out[source, y ^ dy, x ^ dx, :, columns] = refs[piece][slot]
+
+    out = pl.pallas_call(
+        kernel,
+        out_shape=jax.ShapeDtypeStruct((squares, 2, 2, rows, 2 * width), pieces[0].dtype),
+        in_specs=[VMEM] * len(pieces),
+        out_specs=VMEM,
+        compiler_params=PARAMS,
+    )(*pieces)
+    return out.reshape(squares * 4 * rows, 2 * width)
+
+
+def halves_by_core(value):
+    width = value.shape[-1] // 2
+    first = lax.axis_index("ctx") % 2 == 0
+    left, right = value[..., :width], value[..., width:]
+    return jnp.where(first, left, right), jnp.where(first, right, left)
+
+
+def in_core_order(own, other, axis):
+    first = lax.axis_index("ctx") % 2 == 0
+    return jnp.where(
+        first, jnp.concatenate([own, other], axis), jnp.concatenate([other, own], axis)
+    )
+
+
+def gather_weights(conv_weight, up_weight, down_weight):
+    conv_pieces = gather_pieces(conv_weight)
+    up_pieces = gather_pieces(up_weight)
+    own, other = halves_by_core(down_weight)
+    down_pieces = gather_pieces(in_core_order(own, swap(other, 1), 0))
+    taps = conv_weight.shape[0]
+    return (
+        assemble_rows(conv_pieces, taps),
+        assemble_rows(up_pieces, 1)[0],
+        assemble_columns(down_pieces),
+    )
+
+
+def relative_blocks(total):
+    squares = lax.axis_size("ctx") // 8
+    rows, width = total.shape[0] // (4 * squares), total.shape[1] // 2
+    blocks = total.reshape(squares, 2, 2, rows, 2 * width)
+
+    def kernel(blocks_ref, keep_ref, send_ref):
+        core, x, y, z = place()
+        keep = pl.ds(pl.multiple_of(core * width, 128), width)
+        send = pl.ds(pl.multiple_of((1 - core) * width, 128), width)
+        for k in range(squares):
+            at = square_at(z, k, squares)
+            for dy in range(2):
+                for dx in range(2):
+                    keep_ref[k, dy, dx] = blocks_ref[at, y ^ dy, x ^ dx, :, keep]
+                    send_ref[k, dy, dx] = blocks_ref[at, y ^ dy, x ^ dx, :, send].astype(
+                        jnp.bfloat16
+                    )
+
+    shape = (squares, 2, 2, rows, width)
+    return pl.pallas_call(
+        kernel,
+        out_shape=(
+            jax.ShapeDtypeStruct(shape, jnp.float32),
+            jax.ShapeDtypeStruct(shape, jnp.bfloat16),
+        ),
+        in_specs=[VMEM],
+        out_specs=(VMEM, VMEM),
+        compiler_params=PARAMS,
+    )(blocks)
+
+
+def scatter_sum(total):
+    squares = lax.axis_size("ctx") // 8
+    half = squares // 2
+    keep, send = relative_blocks(total)
+    chip = keep + swap(send, 1).astype(jnp.float32)
+    low = lambda v: v.astype(jnp.bfloat16)
+    wide = lambda v: v.astype(jnp.float32)
+    first = chip[:half, :, 0] + wide(swap(low(chip[:half, :, 1]), 2))
+    second = chip[half:, 0] + wide(swap(low(chip[half:, 1]), 4))
+    first = first[:, 0] + wide(swap(low(first[:, 1]), 4))
+    second = second[:, 0] + wide(swap(low(second[:, 1]), 2))
+    own = first[0]
+    for k in range(1, squares):
+        piece = first[k] if k < half else second[k - half]
+        own = own + wide(ring(low(piece), k))
+    rows = own.shape[0] // 2
+    is_first = lax.axis_index("ctx") % 2 == 0
+    mine = jnp.where(is_first, own[:rows], own[rows:])
+    theirs = jnp.where(is_first, own[rows:], own[:rows])
+    return in_core_order(mine, swap(theirs, 1), 1)
+
+
+def sum_all(value):
+    squares = lax.axis_size("ctx") // 8
+    for mask in (1, 2, 4):
+        value = value + swap(value, mask)
+    own = value
+    for k in range(1, squares):
+        value = value + ring(own, k)
+    return value
+
+
 def body(tokens, cotangent, norm_gain, conv_weight, up_weight, down_weight, contig_first_bins):
     seq_count, bin_count, feat_width = tokens.shape
     ctx_count = lax.axis_size("ctx")
     data_count = lax.axis_size("dp")
-    conv_full, up_full, down_full = (
-        lax.all_gather(conv_weight, "ctx", axis=1, tiled=True),
-        lax.all_gather(up_weight, "ctx", axis=0, tiled=True),
-        lax.all_gather(down_weight, "ctx", axis=0, tiled=True),
-    )
+    conv_full, up_full, down_full = gather_weights(conv_weight, up_weight, down_weight)
     bin_position = lax.axis_index("ctx") * bin_count + jnp.arange(bin_count, dtype=jnp.int32)
     left_valid_mask, right_valid_mask = tap_masks(
         bin_position, contig_first_bins, ctx_count * bin_count
@@ -87,6 +280,9 @@
         jnp.bfloat16
     )
     grad_flat = cotangent.reshape(-1, feat_width)
+    total = lax.dot_general(
+        hidden, grad_flat, (((0,), (0,)), ((), ())), preferred_element_type=jnp.float32
+    )
     hidden_grad = lax.dot_general(
         grad_flat, down_full, (((1,), (1,)), ((), ())), preferred_element_type=jnp.float32
     )
@@ -112,17 +308,12 @@
     ).astype(jnp.bfloat16)
     gain_term = jnp.sum(normed_grad * scaled_flat, axis=0)
     factor = float(ctx_count * data_count * bin_count * seq_count) ** (-0.5)
-    ff_count = hidden.shape[1]
-    ff_part = ff_count // ctx_count
     width_part = feat_width // data_count
-    blocks = jnp.einsum(
-        "rcf,rdw->cdfw",
-        hidden.reshape(-1, ctx_count, ff_part),
-        grad_flat.reshape(-1, data_count, width_part),
-        preferred_element_type=jnp.float32,
-    ).reshape(-1, width_part)
-    down_part = lax.psum_scatter(blocks, ("ctx", "dp"), scatter_dimension=0, tiled=True)
-    gain_all = lax.psum(gain_term, ("ctx", "dp"))
+    down_part = scatter_sum(total)
+    gain_all = sum_all(gain_term)
+    if data_count > 1:
+        down_part = lax.psum_scatter(down_part, "dp", scatter_dimension=1, tiled=True)
+        gain_all = lax.psum(gain_all, "dp")
     gain_part = lax.dynamic_slice_in_dim(gain_all, lax.axis_index("dp") * width_part, width_part)
     return (
         output.reshape(tokens.shape),

time: 356 us -> 131 us (0.37)
  waiting for transfers between devices: 169 us -> 32.5 us
  blocking collectives: 124 us -> 0 us
  starting transfers between devices: 14 us -> 63.5 us
  between operations: 14.1 us -> 1.29 us
  matrix products: 17.1 us -> 13 us
  Pallas kernels: 0 us -> 4.01 us
    all_gather x3 -> x0, waiting for transfers between devices: 163 us -> none  [the longest x1 59.5 us: body(): lax.all_gather(conv_weight, 'ctx', axis=1, tiled=True)]
    unnamed x1 -> x0, blocking collectives: 83 us -> none
    ppermute x0 -> x52, starting transfers between devices: none -> 56.6 us  [the longest x37 29.1 us: swap(): return lax.ppermute(value, 'ctx', [(i, i ^ mask) for i in range(devices)])]
    psum x1 -> x0, blocking collectives: 41.3 us -> none  [body(): gain_all = lax.psum(gain_term, ('ctx', 'dp'))]
    ppermute x0 -> x52, waiting for transfers between devices: none -> 32.5 us  [the longest x37 25.1 us: swap(): return lax.ppermute(value, 'ctx', [(i, i ^ mask) for i in range(devices)])]
    unnamed x4 -> x0, starting transfers between devices: 5.31 us -> none
    reshape x2 -> x0, local copies, waits for them, and re-layouts: 4.14 us -> none  [the longest x1 2.94 us: body(): blocks = jnp.einsum('rcf,rdw->cdfw', hidden.reshape(-1, ctx_count, ff_par...]
    pallas_call x0 -> x4, Pallas kernels: none -> 4.01 us  [the longest x2 3.59 us: assemble_rows(): pl.pallas_call(kernel, out_shape=jax.ShapeDtypeStruct((lead, squares, 2,...]
  transfers between devices with their start and end apart: 11 -> 56, of which waited for: 4 -> 14; matrix products, arithmetic and copies ran while one was open for 30% -> 10% of each run, Pallas kernels for 0% -> 0%
where the time goes in v1:
time: 131 us; the launch traced here: 130 us
  starting transfers between devices  63.5 us (48%)
  waiting for transfers between devices  32.5 us (25%)
  matrix products  13 us (10%)
  other arithmetic  9.25 us (7%)
  local copies, waits for them, and re-layouts  6.58 us (5%)
  Pallas kernels  4.01 us (3%)
    ppermute x37, starting transfers between devices, swap(): return lax.ppermute(value, 'ctx', [(i, i ^ mask) for i in range(devices)])  29.1 us
    ppermute x15, starting transfers between devices, ring(): lax.ppermute(value, 'ctx', [(i, i % 8 + 8 * to[i // 8]) for i in range(de...  27.5 us
    ppermute x37, waiting for transfers between devices, swap(): return lax.ppermute(value, 'ctx', [(i, i ^ mask) for i in range(devices)])  25.1 us
    ppermute x15, waiting for transfers between devices, ring(): lax.ppermute(value, 'ctx', [(i, i % 8 + 8 * to[i // 8]) for i in range(de...  7.37 us
    ppermute x2, starting transfers between devices, with_halo(): before = lax.ppermute(last, axis, up)  4.34 us
    dot_general x1, matrix products, body(): lax.dot_general(pre_grad, up_full, (((1,), (1,)), ((), ())), preferred_el...  3.73 us
    pallas_call x2, Pallas kernels, assemble_rows(): pl.pallas_call(kernel, out_shape=jax.ShapeDtypeStruct((lead, squares, 2,...  3.59 us
    unnamed x52, local copies, waits for them, and re-layouts  3.58 us
  transfers between devices with their start and end apart: 56, of which 14 were waited for; matrix products, arithmetic and copies ran while one was open for 10% of the time, Pallas kernels for 0%

profile of v1, /device:TPU:0, one launch (start us, length us, event | category | flops | bytes accessed | tf_op | source)
XLA Modules:
  0.0 130.1 jit_solution(17766316312565322840)
XLA Ops:
  2.0 3.6 %collective-permute-start.2 = (bf16[3,24,768]{2,1,0:T(8,128)(2,1)}, bf16[3,24,768]{2,1,0:T(8,128)(2,1)S(1)}, u32[]{:S(2)}, u32[]{:S(2)}) collective-permute-start(bf16[3,24,768]{2,1,0:T(8,128)(2,1)} %param.10), channel_id=1, source_target_pairs={{0,16},{1,17},{2,18},{3,19},{4,20},{5,21},{6,22},{7,23},{8,0},{9,1... | collective-permute-start | bytes 331784 | tf_op jit(solution)/shard_map/ppermute | solution.py:73
  5.7 1.6 %collective-permute-start.14 = (bf16[24,1152]{1,0:T(8,128)(2,1)}, bf16[24,1152]{1,0:T(8,128)(2,1)S(1)}, u32[]{:S(2)}, u32[]{:S(2)}) collective-permute-start(bf16[24,1152]{1,0:T(8,128)(2,1)} %param.11), channel_id=1, source_target_pairs={{0,16},{1,17},{2,18},{3,19},{4,20},{5,21},{6,22},{7,23},{8,0},{9,1... | collective-permute-start | bytes 165896 | tf_op jit(solution)/shard_map/ppermute | solution.py:73
  7.2 1.2 fusion.28
  8.8 1.7 %collective-permute-done.14 = bf16[24,1152]{1,0:T(8,128)(2,1)S(1)} collective-permute-done((bf16[24,1152]{1,0:T(8,128)(2,1)}, bf16[24,1152]{1,0:T(8,128)(2,1)S(1)}, u32[]{:S(2)}, u32[]{:S(2)}) %collective-permute-start.14) | collective-permute-done | bytes 55328 | tf_op jit(solution)/shard_map/ppermute | solution.py:73
  10.5 3.3 %collective-permute-start.15 = (bf16[24,1152]{1,0:T(8,128)(2,1)S(1)}, bf16[24,1152]{1,0:T(8,128)(2,1)S(1)}, u32[]{:S(2)}, u32[]{:S(2)}) collective-permute-start(bf16[24,1152]{1,0:T(8,128)(2,1)S(1)} %collective-permute-done.14), channel_id=1, source_target_pairs={{0,16},{1,17},{2,18},{3,19},{4,20},{5,21},{6,22},{7,23},{8,0},{9,1... | collective-permute-start | bytes 165896 | tf_op jit(solution)/shard_map/ppermute | solution.py:73
  13.8 1.2 fusion.27
  16.0 3.4 %collective-permute-start.16 = (bf16[24,1152]{1,0:T(8,128)(2,1)S(1)}, bf16[24,1152]{1,0:T(8,128)(2,1)S(1)}, u32[]{:S(2)}, u32[]{:S(2)}) collective-permute-start(bf16[24,1152]{1,0:T(8,128)(2,1)S(1)} %collective-permute-done.15), channel_id=1, source_target_pairs={{0,16},{1,17},{2,18},{3,19},{4,20},{5,21},{6,22},{7,23},{8,0},{9,1... | collective-permute-start | bytes 165896 | tf_op jit(solution)/shard_map/ppermute | solution.py:73
  19.4 1.3 collective-permute-start
  21.4 1.5 %collective-permute-start.29 = (bf16[72,384]{1,0:T(8,128)(2,1)S(1)}, bf16[72,384]{1,0:T(8,128)(2,1)S(1)}, u32[]{:S(2)}, u32[]{:S(2)}) collective-permute-start(bf16[72,384]{1,0:T(8,128)(2,1)S(1)} %collective-permute-done.28), channel_id=1, source_target_pairs={{0,16},{1,17},{2,18},{3,19},{4,20},{5,21},{6,22},{7,23},{8,0},{9,1... | collective-permute-start | bytes 165896 | tf_op jit(solution)/shard_map/ppermute | solution.py:73
  22.9 1.6 %collective-permute-start.17 = (bf16[4,24,1152]{2,1,0:T(8,128)(2,1)S(1)}, bf16[4,24,1152]{2,1,0:T(8,128)(2,1)S(1)}, u32[]{:S(2)}, u32[]{:S(2)}) collective-permute-start(bf16[4,24,1152]{2,1,0:T(8,128)(2,1)S(1)} %get-tuple-element.23), channel_id=1, source_target_pairs={{0,2},{1,3},{2,0},{3,1},{4,6},{5,7},{6,4},{7,5},{8,10},{9,11},{10,... | collective-permute-start | bytes 663560 | tf_op jit(solution)/shard_map/ppermute | solution.py:65
  24.5 1.5 %collective-permute-start.18 = (bf16[4,24,1152]{2,1,0:T(8,128)(2,1)S(1)}, bf16[4,24,1152]{2,1,0:T(8,128)(2,1)S(1)}, u32[]{:S(2)}, u32[]{:S(2)}) collective-permute-start(bf16[4,24,1152]{2,1,0:T(8,128)(2,1)S(1)} %get-tuple-element.23), channel_id=1, source_target_pairs={{0,4},{1,5},{2,6},{3,7},{4,0},{5,1},{6,2},{7,3},{8,12},{9,13},{10,... | collective-permute-start | bytes 663560 | tf_op jit(solution)/shard_map/ppermute | solution.py:65
  26.6 1.3 collective-permute-start.1
  27.9 4.3 %collective-permute-start.4 = (bf16[3,24,768]{2,1,0:T(8,128)(2,1)S(1)}, bf16[3,24,768]{2,1,0:T(8,128)(2,1)S(1)}, u32[]{:S(2)}, u32[]{:S(2)}) collective-permute-start(bf16[3,24,768]{2,1,0:T(8,128)(2,1)S(1)} %collective-permute-done.3), channel_id=1, source_target_pairs={{0,16},{1,17},{2,18},{3,19},{4,20},{5,21},{6,22},{7,23},{8,0},{9,1... | collective-permute-start | bytes 331784 | tf_op jit(solution)/shard_map/ppermute | solution.py:73
  32.9 1.5 %collective-permute-start.31 = (bf16[4,72,384]{2,1,0:T(8,128)(2,1)S(1)}, bf16[4,72,384]{2,1,0:T(8,128)(2,1)S(1)}, u32[]{:S(2)}, u32[]{:S(2)}) collective-permute-start(bf16[4,72,384]{2,1,0:T(8,128)(2,1)S(1)} %pad_maximum_fusion.6.refs_0_), channel_id=1, source_target_pairs={{0,4},{1,5},{2,6},{3,7},{4,0},{5,1},{6,2},{7,3},{8,12},{9,13},{10,... | collective-permute-start | bytes 663560 | tf_op jit(solution)/shard_map/ppermute | solution.py:65
  34.6 1.4 %collective-permute-done.4 = bf16[3,24,768]{2,1,0:T(8,128)(2,1)S(1)} collective-permute-done((bf16[3,24,768]{2,1,0:T(8,128)(2,1)S(1)}, bf16[3,24,768]{2,1,0:T(8,128)(2,1)S(1)}, u32[]{:S(2)}, u32[]{:S(2)}) %collective-permute-start.4) | collective-permute-done | bytes 110624 | tf_op jit(solution)/shard_map/ppermute | solution.py:73
  36.0 1.9 %collective-permute-start.19 = (bf16[2,24,1152]{2,1,0:T(8,128)(2,1)S(1)}, bf16[2,24,1152]{2,1,0:T(8,128)(2,1)S(1)}, u32[]{:S(2)}, u32[]{:S(2)}) collective-permute-start(bf16[2,24,1152]{2,1,0:T(8,128)(2,1)S(1)} %slice.137), channel_id=1, source_target_pairs={{0,4},{1,5},{2,6},{3,7},{4,0},{5,1},{6,2},{7,3},{8,12},{9,13},{10,... | collective-permute-start | bytes 331784 | tf_op jit(solution)/shard_map/ppermute | solution.py:65
  39.3 1.9 %collective-permute-start.5 = (bf16[4,3,24,768]{3,2,1,0:T(8,128)(2,1)}, bf16[4,3,24,768]{3,2,1,0:T(8,128)(2,1)}, u32[]{:S(2)}, u32[]{:S(2)}) collective-permute-start(bf16[4,3,24,768]{3,2,1,0:T(8,128)(2,1)} %pad_maximum_fusion.refs_0_), channel_id=1, source_target_pairs={{0,2},{1,3},{2,0},{3,1},{4,6},{5,7},{6,4},{7,5},{8,10},{9,11},{10,... | collective-permute-start | bytes 1327112 | tf_op jit(solution)/shard_map/ppermute | solution.py:65
  41.2 1.3 %collective-permute-start.6 = (bf16[4,3,24,768]{3,2,1,0:T(8,128)(2,1)}, bf16[4,3,24,768]{3,2,1,0:T(8,128)(2,1)}, u32[]{:S(2)}, u32[]{:S(2)}) collective-permute-start(bf16[4,3,24,768]{3,2,1,0:T(8,128)(2,1)} %pad_maximum_fusion.refs_0_), channel_id=1, source_target_pairs={{0,4},{1,5},{2,6},{3,7},{4,0},{5,1},{6,2},{7,3},{8,12},{9,13},{10,... | collective-permute-start | bytes 1327112 | tf_op jit(solution)/shard_map/ppermute | solution.py:65
  44.0 1.4 %collective-permute-start.33 = (bf16[2,72,384]{2,1,0:T(8,128)(2,1)S(1)}, bf16[2,72,384]{2,1,0:T(8,128)(2,1)S(1)}, u32[]{:S(2)}, u32[]{:S(2)}) collective-permute-start(bf16[2,72,384]{2,1,0:T(8,128)(2,1)S(1)} %slice.140), channel_id=1, source_target_pairs={{0,2},{1,3},{2,0},{3,1},{4,6},{5,7},{6,4},{7,5},{8,10},{9,11},{10,... | collective-permute-start | bytes 331784 | tf_op jit(solution)/shard_map/ppermute | solution.py:65
  45.4 9.8 %collective-permute-done.32.refs_3_ = bf16[2,72,384]{2,1,0:T(8,128)(2,1)S(1)} collective-permute-done((bf16[2,72,384]{2,1,0:T(8,128)(2,1)S(1)}, bf16[2,72,384]{2,1,0:T(8,128)(2,1)S(1)}, u32[]{:S(2)}, u32[]{:S(2)}) %collective-permute-start.32) | collective-permute-done | bytes 110624 | tf_op jit(solution)/shard_map/ppermute | solution.py:65
  57.8 1.0 slice.135
  58.8 1.0 slice.136
  62.2 5.5 %collective-permute-done.7.refs_3_ = bf16[2,3,24,768]{3,2,1,0:T(8,128)(2,1)S(1)} collective-permute-done((bf16[2,3,24,768]{3,2,1,0:T(8,128)(2,1)S(1)}, bf16[2,3,24,768]{3,2,1,0:T(8,128)(2,1)S(1)}, u32[]{:S(2)}, u32[]{:S(2)}) %collective-permute-start.7) | collective-permute-done | bytes 221216 | tf_op jit(solution)/shard_map/ppermute | solution.py:65
  69.7 0.9 copy-done.3
  71.8 3.4 %shard_map.102 = bf16[3,4,2,2,2,24,768]{6,5,4,3,2,1,0:T(8,128)(2,1)} custom-call(bf16[4,3,24,768]{3,2,1,0:T(8,128)(2,1)} %pad_maximum_fusion.refs_0_, bf16[4,3,24,768]{3,2,1,0:T(8,128)(2,1)} %collective-permute-done.5.refs_1_, bf16[4,3,24,768]{3,2,1,0:T(8,128)(2,1)} %collective-permute-done.6.refs_2_, ...), custom_call_target="tpu_custom_call" | custom-call | tf_op jit(solution)/shard_map/pallas_call | solution.py:132
  75.2 3.1 %convolution_add_fusion.2 = f32[256,768]{1,0:T(8,128)S(1)} fusion(bf16[2304,768]{1,0:T(8,128)(2,1)} %bitcast.178, bf16[1,256,768]{2,1,0:T(8,128)(2,1)S(1)} %get-tuple-element.20, bf16[1,256,768]{2,1,0:T(8,128)(2,1)S(1)} %copy-done.20, bf16[1,256,768]{2,1,0:T(8,128)(2,1)S(1)} %get-tuple-element.19, bf16[1,256,768]{2,1,0:T(8,128)(2,1)S(1)} %copy-done.14), kind=kOutput, calls=%fused_computation.8 | convolution fusion | flops 909901824 | bytes 5898240 | tf_op jit(solution)/shard_map/dot_general | solution.py:273
  78.3 1.9 %multiply_convert_fusion = (bf16[256,1152]{1,0:T(8,128)(2,1)}, f32[256,1152]{1,0:T(8,128)}) fusion(bf16[768,1152]{1,0:T(8,128)(2,1)S(1)} %bitcast.166, f32[256,768]{1,0:T(8,128)S(1)} %convolution_add_fusion.2), kind=kOutput, calls=%fused_computation.28 | convolution fusion | flops 454656000 | bytes 4325376 | tf_op jit(solution)/shard_map/dot_general | solution.py:277
  80.2 3.7 %convolution_add_fusion = f32[256,768]{1,0:T(8,128)} fusion(bf16[768,1152]{1,0:T(8,128)(2,1)S(1)} %bitcast.167, bf16[1152,768]{1,0:T(8,128)(2,1)S(1)} %bitcast.164, f32[256,1152]{1,0:T(8,128)} %get-tuple-element.34, bf16[1,256,768]{2,1,0:T(8,128)(2,1)} %param.8), kind=kOutput, calls=%fused_computation.6 | convolution fusion | flops 909312000 | bytes 5898240 | tf_op jit(solution)/shard_map/dot_general | solution.py:290
  84.0 2.0 %convert_bitcast_fusion.1 = (bf16[1,256,1,768]{3,1,2,0:T(8,128)(2,1)}, bf16[1,256,768]{2,1,0:T(8,128)(2,1)S(1)}) fusion(f32[256,768]{1,0:T(8,128)} %convolution_add_fusion), kind=kLoop, calls=%fused_computation.78 | loop fusion | flops 196608 | bytes 1572864 | tf_op jit(solution)/shard_map/stack;reshape | solution.py:297
  86.6 1.3 collective-permute-start.39
  87.9 3.0 %collective-permute-start.40 = (bf16[1,64,768]{2,1,0:T(8,128)(2,1)}, bf16[1,64,768]{2,1,0:T(8,128)(2,1)S(1)}, u32[]{:S(2)}, u32[]{:S(2)}) collective-permute-start(bf16[1,64,768]{2,1,0:T(8,128)(2,1)} %get-tuple-element.18), channel_id=1, source_target_pairs={{0,1},{1,2},{2,3},{3,4},{4,5},{5,6},{6,7},{7,8},{8,9},{9,10},{10,1... | collective-permute-start | bytes 294920 | tf_op jit(solution)/shard_map/ppermute | solution.py:22
  91.2 1.6 %fusion.41.blocks_ref = f32[4,2,2,72,768]{4,3,2,1,0:T(8,128)S(1)} fusion(bf16[4,2,2,72,256]{4,3,2,1,0:T(8,128)(2,1)S(1)} %bitcast.180, bf16[1,256,768]{2,1,0:T(8,128)(2,1)} %param.8), kind=kOutput, calls=%fused_computation.62 | convolution fusion | flops 452984832 | bytes 4521984 | tf_op jit(solution)/shard_map/dot_general | solution.py:283
  93.2 1.8 %collective-permute-start.41 = (bf16[4,2,2,72,384]{4,3,2,1,0:T(8,128)(2,1)S(1)}, bf16[4,2,2,72,384]{4,3,2,1,0:T(8,128)(2,1)S(1)}, u32[]{:S(2)}, u32[]{:S(2)}) collective-permute-start(bf16[4,2,2,72,384]{4,3,2,1,0:T(8,128)(2,1)S(1)} %get-tuple-element.7), channel_id=1, source_target_pairs={{0,1},{1,0},{2,3},{3,2},{4,5},{5,4},{6,7},{7,6},{8,9},{9,8},{10,11... | collective-permute-start | bytes 2654216 | tf_op jit(solution)/shard_map/ppermute | solution.py:65
  95.2 1.2 fusion.26
  96.5 1.6 %collective-permute-start.50 = (f32[768]{0:T(1024)S(1)}, f32[768]{0:T(1024)S(1)}, u32[]{:S(2)}, u32[]{:S(2)}) collective-permute-start(f32[768]{0:T(1024)S(1)} %get-tuple-element.8), channel_id=1, source_target_pairs={{0,1},{1,0},{2,3},{3,2},{4,5},{5,4},{6,7},{7,6},{8,9},{9,8},{10,11... | collective-permute-start | bytes 9224 | tf_op jit(solution)/shard_map/ppermute | solution.py:65
  98.1 1.4 %fusion.3 = bf16[1,256,768]{2,1,0:T(8,128)(2,1)} fusion(f32[256,768]{1,0:T(8,128)S(1)} %copy-done.18, bf16[256,1152]{1,0:T(8,128)(2,1)S(1)} %copy-done.12, bf16[1152,768]{1,0:T(8,128)(2,1)S(1)} %bitcast.165), kind=kOutput, calls=%fused_computation.10 | convolution fusion | flops 453378048 | bytes 3538944 | tf_op jit(solution)/shard_map/dot_general | solution.py:279
  99.5 1.5 %collective-permute-start.51 = (f32[768]{0:T(1024)S(1)}, f32[768]{0:T(1024)S(1)}, u32[]{:S(2)}, u32[]{:S(2)}) collective-permute-start(f32[768]{0:T(1024)S(1)} %add.146), channel_id=1, source_target_pairs={{0,2},{1,3},{2,0},{3,1},{4,6},{5,7},{6,4},{7,5},{8,10},{9,11},{10,... | collective-permute-start | bytes 9224 | tf_op jit(solution)/shard_map/ppermute | solution.py:65
  101.1 2.1 %collective-permute-done.51 = f32[768]{0:T(1024)S(1)} collective-permute-done((f32[768]{0:T(1024)S(1)}, f32[768]{0:T(1024)S(1)}, u32[]{:S(2)}, u32[]{:S(2)}) %collective-permute-start.51) | collective-permute-done | bytes 3104 | tf_op jit(solution)/shard_map/ppermute | solution.py:65
  103.1 1.5 %collective-permute-start.52 = (f32[768]{0:T(1024)S(1)}, f32[768]{0:T(1024)S(1)}, u32[]{:S(2)}, u32[]{:S(2)}) collective-permute-start(f32[768]{0:T(1024)S(1)} %add.147), channel_id=1, source_target_pairs={{0,4},{1,5},{2,6},{3,7},{4,0},{5,1},{6,2},{7,3},{8,12},{9,13},{10,... | collective-permute-start | bytes 9224 | tf_op jit(solution)/shard_map/ppermute | solution.py:65
  105.4 1.6 %collective-permute-start.42 = (bf16[2,2,72,384]{3,2,0,1:T(8,128)(2,1)S(1)}, bf16[2,2,72,384]{3,2,0,1:T(8,128)(2,1)S(1)}, u32[]{:S(2)}, u32[]{:S(2)}) collective-permute-start(bf16[2,2,72,384]{3,2,0,1:T(8,128)(2,1)S(1)} %slice_bitcast_fusion.5), channel_id=1, source_target_pairs={{0,2},{1,3},{2,0},{3,1},{4,6},{5,7},{6,4},{7,5},{8,10},{9,11},{10,... | collective-permute-start | bytes 663560 | tf_op jit(solution)/shard_map/ppermute | solution.py:65
  107.1 4.1 %collective-permute-done.45 = bf16[2,2,72,384]{3,2,0,1:T(8,128)(2,1)S(1)} collective-permute-done((bf16[2,2,72,384]{3,2,0,1:T(8,128)(2,1)S(1)}, bf16[2,2,72,384]{3,2,0,1:T(8,128)(2,1)S(1)}, u32[]{:S(2)}, u32[]{:S(2)}) %collective-permute-start.45) | collective-permute-done | bytes 221216 | tf_op jit(solution)/shard_map/ppermute | solution.py:65
  111.2 1.8 %collective-permute-start.46 = (bf16[2,72,384]{2,1,0:T(8,128)(2,1)S(1)}, bf16[2,72,384]{2,1,0:T(8,128)(2,1)S(1)}, u32[]{:S(2)}, u32[]{:S(2)}) collective-permute-start(bf16[2,72,384]{2,1,0:T(8,128)(2,1)S(1)} %fusion.52), channel_id=1, source_target_pairs={{0,2},{1,3},{2,0},{3,1},{4,6},{5,7},{6,4},{7,5},{8,10},{9,11},{10,... | collective-permute-start | bytes 331784 | tf_op jit(solution)/shard_map/ppermute | solution.py:65
  113.9 2.2 %collective-permute-done.46 = bf16[2,72,384]{2,1,0:T(8,128)(2,1)S(1)} collective-permute-done((bf16[2,72,384]{2,1,0:T(8,128)(2,1)S(1)}, bf16[2,72,384]{2,1,0:T(8,128)(2,1)S(1)}, u32[]{:S(2)}, u32[]{:S(2)}) %collective-permute-start.46) | collective-permute-done | bytes 110624 | tf_op jit(solution)/shard_map/ppermute | solution.py:65
  116.1 2.4 %collective-permute-start.47 = (bf16[72,384]{1,0:T(8,128)(2,1)S(1)}, bf16[72,384]{1,0:T(8,128)(2,1)S(1)}, u32[]{:S(2)}, u32[]{:S(2)}) collective-permute-start(bf16[72,384]{1,0:T(8,128)(2,1)S(1)} %get-tuple-element.27), channel_id=1, source_target_pairs={{0,24},{1,25},{2,26},{3,27},{4,28},{5,29},{6,30},{7,31},{8,16},{9,... | collective-permute-start | bytes 165896 | tf_op jit(solution)/shard_map/ppermute | solution.py:73
  118.9 2.7 %collective-permute-start.44 = (bf16[72,384]{1,0:T(8,128)(2,1)S(1)}, bf16[72,384]{1,0:T(8,128)(2,1)S(1)}, u32[]{:S(2)}, u32[]{:S(2)}) collective-permute-start(bf16[72,384]{1,0:T(8,128)(2,1)S(1)} %fusion.56), channel_id=1, source_target_pairs={{0,16},{1,17},{2,18},{3,19},{4,20},{5,21},{6,22},{7,23},{8,0},{9,1... | collective-permute-start | bytes 165896 | tf_op jit(solution)/shard_map/ppermute | solution.py:73
  121.6 1.0 fusion.34
  122.6 1.7 %collective-permute-start.54 = (f32[768]{0:T(1024)S(1)}, f32[768]{0:T(1024)S(1)}, u32[]{:S(2)}, u32[]{:S(2)}) collective-permute-start(f32[768]{0:T(1024)S(1)} %add.148), channel_id=1, source_target_pairs={{0,24},{1,25},{2,26},{3,27},{4,28},{5,29},{6,30},{7,31},{8,16},{9,... | collective-permute-start | bytes 9224 | tf_op jit(solution)/shard_map/ppermute | solution.py:73
  126.2 1.9 %collective-permute-done.54 = f32[768]{0:T(1024)S(1)} collective-permute-done((f32[768]{0:T(1024)S(1)}, f32[768]{0:T(1024)S(1)}, u32[]{:S(2)}, u32[]{:S(2)}) %collective-permute-start.54) | collective-permute-done | bytes 3104 | tf_op jit(solution)/shard_map/ppermute | solution.py:73
  (171 shorter events, 23.1 us)
Async XLA Ops:
  1.5 6.9 %collective-permute-start.26 = (bf16[36,384]{1,0:T(8,128)(2,1)S(1)}, bf16[36,384]{1,0:T(8,128)(2,1)S(1)}, u32[]{:S(2)}, u32[]{:S(2)}) collective-permute-start(bf16[36,384]{1,0:T(8,128)(2,1)S(1)} %get-tuple-element.30), channel_id=1, source_target_pairs={{0,1},{1,0},{2,3},{3,2},{4,5},{5,4},{6,7},{7,6},{8,9},{9,8},{10,11... | collective-permute-start | bytes 82952 | tf_op jit(solution)/shard_map/ppermute | solution.py:65
  2.0 18.7 %collective-permute-start.2 = (bf16[3,24,768]{2,1,0:T(8,128)(2,1)}, bf16[3,24,768]{2,1,0:T(8,128)(2,1)S(1)}, u32[]{:S(2)}, u32[]{:S(2)}) collective-permute-start(bf16[3,24,768]{2,1,0:T(8,128)(2,1)} %param.10), channel_id=1, source_target_pairs={{0,16},{1,17},{2,18},{3,19},{4,20},{5,21},{6,22},{7,23},{8,0},{9,1... | collective-permute-start | bytes 331784 | tf_op jit(solution)/shard_map/ppermute | solution.py:73
  5.7 4.9 %collective-permute-start.14 = (bf16[24,1152]{1,0:T(8,128)(2,1)}, bf16[24,1152]{1,0:T(8,128)(2,1)S(1)}, u32[]{:S(2)}, u32[]{:S(2)}) collective-permute-start(bf16[24,1152]{1,0:T(8,128)(2,1)} %param.11), channel_id=1, source_target_pairs={{0,16},{1,17},{2,18},{3,19},{4,20},{5,21},{6,22},{7,23},{8,0},{9,1... | collective-permute-start | bytes 165896 | tf_op jit(solution)/shard_map/ppermute | solution.py:73
  8.4 6.6 %collective-permute-start.27 = (bf16[72,384]{1,0:T(8,128)(2,1)S(1)}, bf16[72,384]{1,0:T(8,128)(2,1)S(1)}, u32[]{:S(2)}, u32[]{:S(2)}) collective-permute-start(bf16[72,384]{1,0:T(8,128)(2,1)S(1)} %maximum_select_fusion.2), channel_id=1, source_target_pairs={{0,16},{1,17},{2,18},{3,19},{4,20},{5,21},{6,22},{7,23},{8,0},{9,1... | collective-permute-start | bytes 165896 | tf_op jit(solution)/shard_map/ppermute | solution.py:73
  10.5 5.4 %collective-permute-start.15 = (bf16[24,1152]{1,0:T(8,128)(2,1)S(1)}, bf16[24,1152]{1,0:T(8,128)(2,1)S(1)}, u32[]{:S(2)}, u32[]{:S(2)}) collective-permute-start(bf16[24,1152]{1,0:T(8,128)(2,1)S(1)} %collective-permute-done.14), channel_id=1, source_target_pairs={{0,16},{1,17},{2,18},{3,19},{4,20},{5,21},{6,22},{7,23},{8,0},{9,1... | collective-permute-start | bytes 165896 | tf_op jit(solution)/shard_map/ppermute | solution.py:73
  15.0 6.4 %collective-permute-start.28 = (bf16[72,384]{1,0:T(8,128)(2,1)S(1)}, bf16[72,384]{1,0:T(8,128)(2,1)S(1)}, u32[]{:S(2)}, u32[]{:S(2)}) collective-permute-start(bf16[72,384]{1,0:T(8,128)(2,1)S(1)} %collective-permute-done.27), channel_id=1, source_target_pairs={{0,16},{1,17},{2,18},{3,19},{4,20},{5,21},{6,22},{7,23},{8,0},{9,1... | collective-permute-start | bytes 165896 | tf_op jit(solution)/shard_map/ppermute | solution.py:73
  16.0 6.9 %collective-permute-start.16 = (bf16[24,1152]{1,0:T(8,128)(2,1)S(1)}, bf16[24,1152]{1,0:T(8,128)(2,1)S(1)}, u32[]{:S(2)}, u32[]{:S(2)}) collective-permute-start(bf16[24,1152]{1,0:T(8,128)(2,1)S(1)} %collective-permute-done.15), channel_id=1, source_target_pairs={{0,16},{1,17},{2,18},{3,19},{4,20},{5,21},{6,22},{7,23},{8,0},{9,1... | collective-permute-start | bytes 165896 | tf_op jit(solution)/shard_map/ppermute | solution.py:73
  19.4 6.7 %collective-permute-start = (bf16[1,64,768]{2,1,0:T(8,128)(2,1)S(1)}, bf16[1,64,768]{2,1,0:T(8,128)(2,1)S(1)}, u32[]{:S(2)}, u32[]{:S(2)}) collective-permute-start(bf16[1,64,768]{2,1,0:T(8,128)(2,1)S(1)} %get-tuple-element.21), channel_id=1, source_target_pairs={{0,1},{1,2},{2,3},{3,4},{4,5},{5,6},{6,7},{7,8},{8,9},{9,10},{10,1... | collective-permute-start | bytes 294920 | tf_op jit(solution)/shard_map/ppermute | solution.py:22
  20.7 7.2 %collective-permute-start.3 = (bf16[3,24,768]{2,1,0:T(8,128)(2,1)S(1)}, bf16[3,24,768]{2,1,0:T(8,128)(2,1)S(1)}, u32[]{:S(2)}, u32[]{:S(2)}) collective-permute-start(bf16[3,24,768]{2,1,0:T(8,128)(2,1)S(1)} %collective-permute-done.2), channel_id=1, source_target_pairs={{0,16},{1,17},{2,18},{3,19},{4,20},{5,21},{6,22},{7,23},{8,0},{9,1... | collective-permute-start | bytes 331784 | tf_op jit(solution)/shard_map/ppermute | solution.py:73
  21.4 5.2 %collective-permute-start.29 = (bf16[72,384]{1,0:T(8,128)(2,1)S(1)}, bf16[72,384]{1,0:T(8,128)(2,1)S(1)}, u32[]{:S(2)}, u32[]{:S(2)}) collective-permute-start(bf16[72,384]{1,0:T(8,128)(2,1)S(1)} %collective-permute-done.28), channel_id=1, source_target_pairs={{0,16},{1,17},{2,18},{3,19},{4,20},{5,21},{6,22},{7,23},{8,0},{9,1... | collective-permute-start | bytes 165896 | tf_op jit(solution)/shard_map/ppermute | solution.py:73
  22.9 9.3 %collective-permute-start.17 = (bf16[4,24,1152]{2,1,0:T(8,128)(2,1)S(1)}, bf16[4,24,1152]{2,1,0:T(8,128)(2,1)S(1)}, u32[]{:S(2)}, u32[]{:S(2)}) collective-permute-start(bf16[4,24,1152]{2,1,0:T(8,128)(2,1)S(1)} %get-tuple-element.23), channel_id=1, source_target_pairs={{0,2},{1,3},{2,0},{3,1},{4,6},{5,7},{6,4},{7,5},{8,10},{9,11},{10,... | collective-permute-start | bytes 663560 | tf_op jit(solution)/shard_map/ppermute | solution.py:65
  24.5 8.4 %collective-permute-start.18 = (bf16[4,24,1152]{2,1,0:T(8,128)(2,1)S(1)}, bf16[4,24,1152]{2,1,0:T(8,128)(2,1)S(1)}, u32[]{:S(2)}, u32[]{:S(2)}) collective-permute-start(bf16[4,24,1152]{2,1,0:T(8,128)(2,1)S(1)} %get-tuple-element.23), channel_id=1, source_target_pairs={{0,4},{1,5},{2,6},{3,7},{4,0},{5,1},{6,2},{7,3},{8,12},{9,13},{10,... | collective-permute-start | bytes 663560 | tf_op jit(solution)/shard_map/ppermute | solution.py:65
  26.0 11.8 %collective-permute-start.21 = (bf16[4,24,1152]{2,1,0:T(8,128)(2,1)S(1)}, bf16[4,24,1152]{2,1,0:T(8,128)(2,1)S(1)}, u32[]{:S(2)}, u32[]{:S(2)}) collective-permute-start(bf16[4,24,1152]{2,1,0:T(8,128)(2,1)S(1)} %get-tuple-element.23), channel_id=1, source_target_pairs={{0,1},{1,0},{2,3},{3,2},{4,5},{5,4},{6,7},{7,6},{8,9},{9,8},{10,11... | collective-permute-start | bytes 663560 | tf_op jit(solution)/shard_map/ppermute | solution.py:65
  26.6 7.9 %collective-permute-start.1 = (bf16[1,64,768]{2,1,0:T(8,128)(2,1)S(1)}, bf16[1,64,768]{2,1,0:T(8,128)(2,1)S(1)}, u32[]{:S(2)}, u32[]{:S(2)}) collective-permute-start(bf16[1,64,768]{2,1,0:T(8,128)(2,1)S(1)} %get-tuple-element.22), channel_id=1, source_target_pairs={{1,0},{2,1},{3,2},{4,3},{5,4},{6,5},{7,6},{8,7},{9,8},{10,9},{11,1... | collective-permute-start | bytes 294920 | tf_op jit(solution)/shard_map/ppermute | solution.py:23
  27.9 8.1 %collective-permute-start.4 = (bf16[3,24,768]{2,1,0:T(8,128)(2,1)S(1)}, bf16[3,24,768]{2,1,0:T(8,128)(2,1)S(1)}, u32[]{:S(2)}, u32[]{:S(2)}) collective-permute-start(bf16[3,24,768]{2,1,0:T(8,128)(2,1)S(1)} %collective-permute-done.3), channel_id=1, source_target_pairs={{0,16},{1,17},{2,18},{3,19},{4,20},{5,21},{6,22},{7,23},{8,0},{9,1... | collective-permute-start | bytes 331784 | tf_op jit(solution)/shard_map/ppermute | solution.py:73
  32.2 7.1 %collective-permute-start.30 = (bf16[4,72,384]{2,1,0:T(8,128)(2,1)S(1)}, bf16[4,72,384]{2,1,0:T(8,128)(2,1)S(1)}, u32[]{:S(2)}, u32[]{:S(2)}) collective-permute-start(bf16[4,72,384]{2,1,0:T(8,128)(2,1)S(1)} %pad_maximum_fusion.6.refs_0_), channel_id=1, source_target_pairs={{0,2},{1,3},{2,0},{3,1},{4,6},{5,7},{6,4},{7,5},{8,10},{9,11},{10,... | collective-permute-start | bytes 663560 | tf_op jit(solution)/shard_map/ppermute | solution.py:65
  32.9 8.3 %collective-permute-start.31 = (bf16[4,72,384]{2,1,0:T(8,128)(2,1)S(1)}, bf16[4,72,384]{2,1,0:T(8,128)(2,1)S(1)}, u32[]{:S(2)}, u32[]{:S(2)}) collective-permute-start(bf16[4,72,384]{2,1,0:T(8,128)(2,1)S(1)} %pad_maximum_fusion.6.refs_0_), channel_id=1, source_target_pairs={{0,4},{1,5},{2,6},{3,7},{4,0},{5,1},{6,2},{7,3},{8,12},{9,13},{10,... | collective-permute-start | bytes 663560 | tf_op jit(solution)/shard_map/ppermute | solution.py:65
  34.5 8.1 %collective-permute-start.34 = (bf16[4,72,384]{2,1,0:T(8,128)(2,1)S(1)}, bf16[4,72,384]{2,1,0:T(8,128)(2,1)S(1)}, u32[]{:S(2)}, u32[]{:S(2)}) collective-permute-start(bf16[4,72,384]{2,1,0:T(8,128)(2,1)S(1)} %pad_maximum_fusion.6.refs_0_), channel_id=1, source_target_pairs={{0,1},{1,0},{2,3},{3,2},{4,5},{5,4},{6,7},{7,6},{8,9},{9,8},{10,11... | collective-permute-start | bytes 663560 | tf_op jit(solution)/shard_map/ppermute | solution.py:65
  36.0 8.0 %collective-permute-start.19 = (bf16[2,24,1152]{2,1,0:T(8,128)(2,1)S(1)}, bf16[2,24,1152]{2,1,0:T(8,128)(2,1)S(1)}, u32[]{:S(2)}, u32[]{:S(2)}) collective-permute-start(bf16[2,24,1152]{2,1,0:T(8,128)(2,1)S(1)} %slice.137), channel_id=1, source_target_pairs={{0,4},{1,5},{2,6},{3,7},{4,0},{5,1},{6,2},{7,3},{8,12},{9,13},{10,... | collective-permute-start | bytes 331784 | tf_op jit(solution)/shard_map/ppermute | solution.py:65
  37.9 7.5 %collective-permute-start.20 = (bf16[2,24,1152]{2,1,0:T(8,128)(2,1)S(1)}, bf16[2,24,1152]{2,1,0:T(8,128)(2,1)S(1)}, u32[]{:S(2)}, u32[]{:S(2)}) collective-permute-start(bf16[2,24,1152]{2,1,0:T(8,128)(2,1)S(1)} %slice.138), channel_id=1, source_target_pairs={{0,2},{1,3},{2,0},{3,1},{4,6},{5,7},{6,4},{7,5},{8,10},{9,11},{10,... | collective-permute-start | bytes 331784 | tf_op jit(solution)/shard_map/ppermute | solution.py:65
  39.3 17.9 %collective-permute-start.5 = (bf16[4,3,24,768]{3,2,1,0:T(8,128)(2,1)}, bf16[4,3,24,768]{3,2,1,0:T(8,128)(2,1)}, u32[]{:S(2)}, u32[]{:S(2)}) collective-permute-start(bf16[4,3,24,768]{3,2,1,0:T(8,128)(2,1)} %pad_maximum_fusion.refs_0_), channel_id=1, source_target_pairs={{0,2},{1,3},{2,0},{3,1},{4,6},{5,7},{6,4},{7,5},{8,10},{9,11},{10,... | collective-permute-start | bytes 1327112 | tf_op jit(solution)/shard_map/ppermute | solution.py:65
  41.2 16.4 %collective-permute-start.6 = (bf16[4,3,24,768]{3,2,1,0:T(8,128)(2,1)}, bf16[4,3,24,768]{3,2,1,0:T(8,128)(2,1)}, u32[]{:S(2)}, u32[]{:S(2)}) collective-permute-start(bf16[4,3,24,768]{3,2,1,0:T(8,128)(2,1)} %pad_maximum_fusion.refs_0_), channel_id=1, source_target_pairs={{0,4},{1,5},{2,6},{3,7},{4,0},{5,1},{6,2},{7,3},{8,12},{9,13},{10,... | collective-permute-start | bytes 1327112 | tf_op jit(solution)/shard_map/ppermute | solution.py:65
  43.3 11.9 %collective-permute-start.32 = (bf16[2,72,384]{2,1,0:T(8,128)(2,1)S(1)}, bf16[2,72,384]{2,1,0:T(8,128)(2,1)S(1)}, u32[]{:S(2)}, u32[]{:S(2)}) collective-permute-start(bf16[2,72,384]{2,1,0:T(8,128)(2,1)S(1)} %slice.139), channel_id=1, source_target_pairs={{0,4},{1,5},{2,6},{3,7},{4,0},{5,1},{6,2},{7,3},{8,12},{9,13},{10,... | collective-permute-start | bytes 331784 | tf_op jit(solution)/shard_map/ppermute | solution.py:65
  44.0 11.2 %collective-permute-start.33 = (bf16[2,72,384]{2,1,0:T(8,128)(2,1)S(1)}, bf16[2,72,384]{2,1,0:T(8,128)(2,1)S(1)}, u32[]{:S(2)}, u32[]{:S(2)}) collective-permute-start(bf16[2,72,384]{2,1,0:T(8,128)(2,1)S(1)} %slice.140), channel_id=1, source_target_pairs={{0,2},{1,3},{2,0},{3,1},{4,6},{5,7},{6,4},{7,5},{8,10},{9,11},{10,... | collective-permute-start | bytes 331784 | tf_op jit(solution)/shard_map/ppermute | solution.py:65
  45.4 11.7 %collective-permute-start.22 = (bf16[4,24,1152]{2,1,0:T(8,128)(2,1)S(1)}, bf16[4,24,1152]{2,1,0:T(8,128)(2,1)S(1)}, u32[]{:S(2)}, u32[]{:S(2)}) collective-permute-start(bf16[4,24,1152]{2,1,0:T(8,128)(2,1)S(1)} %collective-permute-done.17), channel_id=1, source_target_pairs={{0,1},{1,0},{2,3},{3,2},{4,5},{5,4},{6,7},{7,6},{8,9},{9,8},{10,11... | collective-permute-start | bytes 663560 | tf_op jit(solution)/shard_map/ppermute | solution.py:65
  56.7 4.9 %collective-permute-start.35 = (bf16[4,72,384]{2,1,0:T(8,128)(2,1)S(1)}, bf16[4,72,384]{2,1,0:T(8,128)(2,1)S(1)}, u32[]{:S(2)}, u32[]{:S(2)}) collective-permute-start(bf16[4,72,384]{2,1,0:T(8,128)(2,1)S(1)} %collective-permute-done.30.refs_1_), channel_id=1, source_target_pairs={{0,1},{1,0},{2,3},{3,2},{4,5},{5,4},{6,7},{7,6},{8,9},{9,8},{10,11... | collective-permute-start | bytes 663560 | tf_op jit(solution)/shard_map/ppermute | solution.py:65
  57.1 4.6 %collective-permute-start.36 = (bf16[4,72,384]{2,1,0:T(8,128)(2,1)S(1)}, bf16[4,72,384]{2,1,0:T(8,128)(2,1)S(1)}, u32[]{:S(2)}, u32[]{:S(2)}) collective-permute-start(bf16[4,72,384]{2,1,0:T(8,128)(2,1)S(1)} %collective-permute-done.31.refs_2_), channel_id=1, source_target_pairs={{0,1},{1,0},{2,3},{3,2},{4,5},{5,4},{6,7},{7,6},{8,9},{9,8},{10,11... | collective-permute-start | bytes 663560 | tf_op jit(solution)/shard_map/ppermute | solution.py:65
  59.8 12.0 %collective-permute-start.9 = (bf16[4,3,24,768]{3,2,1,0:T(8,128)(2,1)}, bf16[4,3,24,768]{3,2,1,0:T(8,128)(2,1)S(1)}, u32[]{:S(2)}, u32[]{:S(2)}) collective-permute-start(bf16[4,3,24,768]{3,2,1,0:T(8,128)(2,1)} %pad_maximum_fusion.refs_0_), channel_id=1, source_target_pairs={{0,1},{1,0},{2,3},{3,2},{4,5},{5,4},{6,7},{7,6},{8,9},{9,8},{10,11... | collective-permute-start | bytes 1327112 | tf_op jit(solution)/shard_map/ppermute | solution.py:65
  60.2 7.5 %collective-permute-start.7 = (bf16[2,3,24,768]{3,2,1,0:T(8,128)(2,1)S(1)}, bf16[2,3,24,768]{3,2,1,0:T(8,128)(2,1)S(1)}, u32[]{:S(2)}, u32[]{:S(2)}) collective-permute-start(bf16[2,3,24,768]{3,2,1,0:T(8,128)(2,1)S(1)} %slice.135), channel_id=1, source_target_pairs={{0,4},{1,5},{2,6},{3,7},{4,0},{5,1},{6,2},{7,3},{8,12},{9,13},{10,... | collective-permute-start | bytes 663560 | tf_op jit(solution)/shard_map/ppermute | solution.py:65
  61.0 7.2 %collective-permute-start.8 = (bf16[2,3,24,768]{3,2,1,0:T(8,128)(2,1)S(1)}, bf16[2,3,24,768]{3,2,1,0:T(8,128)(2,1)S(1)}, u32[]{:S(2)}, u32[]{:S(2)}) collective-permute-start(bf16[2,3,24,768]{3,2,1,0:T(8,128)(2,1)S(1)} %slice.136), channel_id=1, source_target_pairs={{0,2},{1,3},{2,0},{3,1},{4,6},{5,7},{6,4},{7,5},{8,10},{9,11},{10,... | collective-permute-start | bytes 663560 | tf_op jit(solution)/shard_map/ppermute | solution.py:65
  61.6 10.1 %collective-permute-start.10 = (bf16[4,3,24,768]{3,2,1,0:T(8,128)(2,1)}, bf16[4,3,24,768]{3,2,1,0:T(8,128)(2,1)S(1)}, u32[]{:S(2)}, u32[]{:S(2)}) collective-permute-start(bf16[4,3,24,768]{3,2,1,0:T(8,128)(2,1)} %collective-permute-done.5.refs_1_), channel_id=1, source_target_pairs={{0,1},{1,0},{2,3},{3,2},{4,5},{5,4},{6,7},{7,6},{8,9},{9,8},{10,11... | collective-permute-start | bytes 1327112 | tf_op jit(solution)/shard_map/ppermute | solution.py:65
  61.7 10.1 %collective-permute-start.11 = (bf16[4,3,24,768]{3,2,1,0:T(8,128)(2,1)}, bf16[4,3,24,768]{3,2,1,0:T(8,128)(2,1)S(1)}, u32[]{:S(2)}, u32[]{:S(2)}) collective-permute-start(bf16[4,3,24,768]{3,2,1,0:T(8,128)(2,1)} %collective-permute-done.6.refs_2_), channel_id=1, source_target_pairs={{0,1},{1,0},{2,3},{3,2},{4,5},{5,4},{6,7},{7,6},{8,9},{9,8},{10,11... | collective-permute-start | bytes 1327112 | tf_op jit(solution)/shard_map/ppermute | solution.py:65
  67.7 4.1 %collective-permute-start.12 = (bf16[2,3,24,768]{3,2,1,0:T(8,128)(2,1)S(1)}, bf16[2,3,24,768]{3,2,1,0:T(8,128)(2,1)S(1)}, u32[]{:S(2)}, u32[]{:S(2)}) collective-permute-start(bf16[2,3,24,768]{3,2,1,0:T(8,128)(2,1)S(1)} %collective-permute-done.7.refs_3_), channel_id=1, source_target_pairs={{0,1},{1,0},{2,3},{3,2},{4,5},{5,4},{6,7},{7,6},{8,9},{9,8},{10,11... | collective-permute-start | bytes 663560 | tf_op jit(solution)/shard_map/ppermute | solution.py:65
  86.6 8.3 %collective-permute-start.39 = (bf16[1,64,768]{2,1,0:T(8,128)(2,1)}, bf16[1,64,768]{2,1,0:T(8,128)(2,1)S(1)}, u32[]{:S(2)}, u32[]{:S(2)}) collective-permute-start(bf16[1,64,768]{2,1,0:T(8,128)(2,1)} %get-tuple-element.17), channel_id=1, source_target_pairs={{1,0},{2,1},{3,2},{4,3},{5,4},{6,5},{7,6},{8,7},{9,8},{10,9},{11,1... | collective-permute-start | bytes 294920 | tf_op jit(solution)/shard_map/ppermute | solution.py:23
  87.9 7.0 %collective-permute-start.40 = (bf16[1,64,768]{2,1,0:T(8,128)(2,1)}, bf16[1,64,768]{2,1,0:T(8,128)(2,1)S(1)}, u32[]{:S(2)}, u32[]{:S(2)}) collective-permute-start(bf16[1,64,768]{2,1,0:T(8,128)(2,1)} %get-tuple-element.18), channel_id=1, source_target_pairs={{0,1},{1,2},{2,3},{3,4},{4,5},{5,6},{6,7},{7,8},{8,9},{9,10},{10,1... | collective-permute-start | bytes 294920 | tf_op jit(solution)/shard_map/ppermute | solution.py:22
  93.2 11.5 %collective-permute-start.41 = (bf16[4,2,2,72,384]{4,3,2,1,0:T(8,128)(2,1)S(1)}, bf16[4,2,2,72,384]{4,3,2,1,0:T(8,128)(2,1)S(1)}, u32[]{:S(2)}, u32[]{:S(2)}) collective-permute-start(bf16[4,2,2,72,384]{4,3,2,1,0:T(8,128)(2,1)S(1)} %get-tuple-element.7), channel_id=1, source_target_pairs={{0,1},{1,0},{2,3},{3,2},{4,5},{5,4},{6,7},{7,6},{8,9},{9,8},{10,11... | collective-permute-start | bytes 2654216 | tf_op jit(solution)/shard_map/ppermute | solution.py:65
  99.5 3.6 %collective-permute-start.51 = (f32[768]{0:T(1024)S(1)}, f32[768]{0:T(1024)S(1)}, u32[]{:S(2)}, u32[]{:S(2)}) collective-permute-start(f32[768]{0:T(1024)S(1)} %add.146), channel_id=1, source_target_pairs={{0,2},{1,3},{2,0},{3,1},{4,6},{5,7},{6,4},{7,5},{8,10},{9,11},{10,... | collective-permute-start | bytes 9224 | tf_op jit(solution)/shard_map/ppermute | solution.py:65
  103.1 19.5 %collective-permute-start.52 = (f32[768]{0:T(1024)S(1)}, f32[768]{0:T(1024)S(1)}, u32[]{:S(2)}, u32[]{:S(2)}) collective-permute-start(f32[768]{0:T(1024)S(1)} %add.147), channel_id=1, source_target_pairs={{0,4},{1,5},{2,6},{3,7},{4,0},{5,1},{6,2},{7,3},{8,12},{9,13},{10,... | collective-permute-start | bytes 9224 | tf_op jit(solution)/shard_map/ppermute | solution.py:65
  104.9 6.3 %collective-permute-start.45 = (bf16[2,2,72,384]{3,2,0,1:T(8,128)(2,1)S(1)}, bf16[2,2,72,384]{3,2,0,1:T(8,128)(2,1)S(1)}, u32[]{:S(2)}, u32[]{:S(2)}) collective-permute-start(bf16[2,2,72,384]{3,2,0,1:T(8,128)(2,1)S(1)} %slice_bitcast_fusion.3), channel_id=1, source_target_pairs={{0,4},{1,5},{2,6},{3,7},{4,0},{5,1},{6,2},{7,3},{8,12},{9,13},{10,... | collective-permute-start | bytes 663560 | tf_op jit(solution)/shard_map/ppermute | solution.py:65
  105.4 7.6 %collective-permute-start.42 = (bf16[2,2,72,384]{3,2,0,1:T(8,128)(2,1)S(1)}, bf16[2,2,72,384]{3,2,0,1:T(8,128)(2,1)S(1)}, u32[]{:S(2)}, u32[]{:S(2)}) collective-permute-start(bf16[2,2,72,384]{3,2,0,1:T(8,128)(2,1)S(1)} %slice_bitcast_fusion.5), channel_id=1, source_target_pairs={{0,2},{1,3},{2,0},{3,1},{4,6},{5,7},{6,4},{7,5},{8,10},{9,11},{10,... | collective-permute-start | bytes 663560 | tf_op jit(solution)/shard_map/ppermute | solution.py:65
  111.2 4.8 %collective-permute-start.46 = (bf16[2,72,384]{2,1,0:T(8,128)(2,1)S(1)}, bf16[2,72,384]{2,1,0:T(8,128)(2,1)S(1)}, u32[]{:S(2)}, u32[]{:S(2)}) collective-permute-start(bf16[2,72,384]{2,1,0:T(8,128)(2,1)S(1)} %fusion.52), channel_id=1, source_target_pairs={{0,2},{1,3},{2,0},{3,1},{4,6},{5,7},{6,4},{7,5},{8,10},{9,11},{10,... | collective-permute-start | bytes 331784 | tf_op jit(solution)/shard_map/ppermute | solution.py:65
  113.1 5.7 %collective-permute-start.43 = (bf16[2,72,384]{2,1,0:T(8,128)(2,1)S(1)}, bf16[2,72,384]{2,1,0:T(8,128)(2,1)S(1)}, u32[]{:S(2)}, u32[]{:S(2)}) collective-permute-start(bf16[2,72,384]{2,1,0:T(8,128)(2,1)S(1)} %fusion.51), channel_id=1, source_target_pairs={{0,4},{1,5},{2,6},{3,7},{4,0},{5,1},{6,2},{7,3},{8,12},{9,13},{10,... | collective-permute-start | bytes 331784 | tf_op jit(solution)/shard_map/ppermute | solution.py:65
  116.1 8.2 %collective-permute-start.47 = (bf16[72,384]{1,0:T(8,128)(2,1)S(1)}, bf16[72,384]{1,0:T(8,128)(2,1)S(1)}, u32[]{:S(2)}, u32[]{:S(2)}) collective-permute-start(bf16[72,384]{1,0:T(8,128)(2,1)S(1)} %get-tuple-element.27), channel_id=1, source_target_pairs={{0,24},{1,25},{2,26},{3,27},{4,28},{5,29},{6,30},{7,31},{8,16},{9,... | collective-permute-start | bytes 165896 | tf_op jit(solution)/shard_map/ppermute | solution.py:73
  118.5 6.6 %collective-permute-start.48 = (bf16[72,384]{1,0:T(8,128)(2,1)S(1)}, bf16[72,384]{1,0:T(8,128)(2,1)S(1)}, u32[]{:S(2)}, u32[]{:S(2)}) collective-permute-start(bf16[72,384]{1,0:T(8,128)(2,1)S(1)} %get-tuple-element.28), channel_id=1, source_target_pairs={{0,8},{1,9},{2,10},{3,11},{4,12},{5,13},{6,14},{7,15},{8,24},{9,25... | collective-permute-start | bytes 165896 | tf_op jit(solution)/shard_map/ppermute | solution.py:73
  118.9 6.3 %collective-permute-start.44 = (bf16[72,384]{1,0:T(8,128)(2,1)S(1)}, bf16[72,384]{1,0:T(8,128)(2,1)S(1)}, u32[]{:S(2)}, u32[]{:S(2)}) collective-permute-start(bf16[72,384]{1,0:T(8,128)(2,1)S(1)} %fusion.56), channel_id=1, source_target_pairs={{0,16},{1,17},{2,18},{3,19},{4,20},{5,21},{6,22},{7,23},{8,0},{9,1... | collective-permute-start | bytes 165896 | tf_op jit(solution)/shard_map/ppermute | solution.py:73
  122.6 5.5 %collective-permute-start.54 = (f32[768]{0:T(1024)S(1)}, f32[768]{0:T(1024)S(1)}, u32[]{:S(2)}, u32[]{:S(2)}) collective-permute-start(f32[768]{0:T(1024)S(1)} %add.148), channel_id=1, source_target_pairs={{0,24},{1,25},{2,26},{3,27},{4,28},{5,29},{6,30},{7,31},{8,16},{9,... | collective-permute-start | bytes 9224 | tf_op jit(solution)/shard_map/ppermute | solution.py:73
  124.3 4.5 %collective-permute-start.55 = (f32[768]{0:T(1024)S(1)}, f32[768]{0:T(1024)S(1)}, u32[]{:S(2)}, u32[]{:S(2)}) collective-permute-start(f32[768]{0:T(1024)S(1)} %add.148), channel_id=1, source_target_pairs={{0,8},{1,9},{2,10},{3,11},{4,12},{5,13},{6,14},{7,15},{8,24},{9,25... | collective-permute-start | bytes 9224 | tf_op jit(solution)/shard_map/ppermute | solution.py:73
  125.2 4.2 %collective-permute-start.49 = (f32[36,384]{1,0:T(8,128)S(1)}, f32[36,384]{1,0:T(8,128)S(1)}, u32[]{:S(2)}, u32[]{:S(2)}) collective-permute-start(f32[36,384]{1,0:T(8,128)S(1)} %get-tuple-element.26), channel_id=1, source_target_pairs={{0,1},{1,0},{2,3},{3,2},{4,5},{5,4},{6,7},{7,6},{8,9},{9,8},{10,11... | collective-permute-start | bytes 165896 | tf_op jit(solution)/shard_map/ppermute | solution.py:65
  (34 other events, 314.6 us)

commit v2 on v0

v2 whole, which is shorter than its diff:
```python
import jax
import jax.numpy as jnp
from jax import lax
from jax.experimental import pallas as pl
from jax.experimental.pallas import tpu as pltpu
from jax.sharding import PartitionSpec as P

DILATION_BINS = 64


root_half = 0.7071067811865476
inv_root_two_pi = 0.3989422804014327


def swap(value, mask):
    devices = lax.axis_size("ctx")
    return lax.ppermute(value, "ctx", [(i, i ^ mask) for i in range(devices)])


def place():
    me = lax.axis_index("ctx")
    return me % 2, (me // 2) % 2, (me // 4) % 2, me // 8


def after(value, *others):
    return lax.optimization_barrier((value,) + others)[0]


VMEM = pl.BlockSpec(memory_space=pltpu.VMEM)
PARAMS = pltpu.CompilerParams(vmem_limit_bytes=20 * 1024 * 1024)

SMEM = pl.BlockSpec(memory_space=pltpu.SMEM)


def call(kernel, outs, *args, smem=(), scratch=(), cost=1):
    shapes = [jax.ShapeDtypeStruct(shape, dtype) for shape, dtype in outs]
    return pl.pallas_call(
        kernel,
        out_shape=shapes,
        in_specs=[SMEM if i in smem else VMEM for i in range(len(args))],
        out_specs=[VMEM] * len(shapes),
        scratch_shapes=list(scratch),
        compiler_params=PARAMS,
        cost_estimate=pl.CostEstimate(flops=1, bytes_accessed=cost, transcendentals=0),
    )(*args)


def segment_of(position, starts_ref):
    segment = jnp.zeros_like(position)
    for i in range(starts_ref.shape[0]):
        segment = segment + jnp.where(position >= starts_ref[i], 1, 0)
    return segment


def masks_at(first, rows, starts_ref, overall):
    position = first + lax.broadcasted_iota(jnp.int32, (rows, 1), 0)
    segment = segment_of(position, starts_ref)
    left = (position >= DILATION_BINS) & (segment_of(position - DILATION_BINS, starts_ref) == segment)
    right = (position + DILATION_BINS < overall) & (
        segment_of(position + DILATION_BINS, starts_ref) == segment
    )
    return left, right


def column_blocks(width):
    step = 384 if width % 384 == 0 else width
    return [slice(at, at + step) for at in range(0, width, step)]


def prepare(before, tokens, after_, gain, starts):
    seqs, bins, width = tokens.shape
    reach = DILATION_BINS
    overall = bins * lax.axis_size("ctx")

    def kernel(before_ref, tokens_ref, after_ref, gain_ref, starts_ref, taps_ref, scaled_ref, inverse_ref):
        first = lax.axis_index("ctx") * bins - reach
        left, right = masks_at(first, bins + 2 * reach, starts_ref, overall)
        for s in range(seqs):
            parts = []
            for ref in (before_ref, tokens_ref, after_ref):
                value = (tokens_ref[s] if ref is tokens_ref else ref[s, : 2 * reach]).astype(jnp.float32)
                inverse = lax.rsqrt(jnp.mean(value * value, axis=1, keepdims=True) + 1e-05)
                scaled = value * inverse
                if ref is tokens_ref:
                    scaled_ref[s] = scaled
                    inverse_ref[s] = inverse
                parts.append(scaled * gain_ref[...])
            normed = jnp.concatenate(parts, axis=0)
            rows = bins + 2 * reach
            taps_ref[s, :, :width] = jnp.where(left, normed[:rows], 0.0).astype(jnp.bfloat16)
            taps_ref[s, :, width : 2 * width] = normed[reach : reach + rows].astype(jnp.bfloat16)
            taps_ref[s, :, 2 * width :] = jnp.where(right, normed[2 * reach :], 0.0).astype(
                jnp.bfloat16
            )

    return call(
        kernel,
        [
            ((seqs, bins + 2 * reach, 3 * width), jnp.bfloat16),
            ((seqs, bins, width), jnp.float32),
            ((seqs, bins, 1), jnp.float32),
        ],
        before,
        tokens,
        after_,
        gain,
        starts,
        smem=(4,),
    )


def convolve(taps, before, tokens, after_, conv):
    seqs, bins, width = tokens.shape
    reach = DILATION_BINS
    rows = bins + 2 * reach

    def kernel(taps_ref, before_ref, tokens_ref, after_ref, conv_ref, mixed_ref):
        for s in range(seqs):
            for at in column_blocks(width):
                total = jnp.dot(
                    taps_ref[s], conv_ref[:, at], preferred_element_type=jnp.float32
                )
                mixed_ref[s, :reach, at] = total[:reach] + before_ref[s, reach : 2 * reach, at].astype(jnp.float32)
                mixed_ref[s, reach : reach + bins, at] = total[reach : reach + bins] + tokens_ref[
                    s, :, at
                ].astype(jnp.float32)
                mixed_ref[s, reach + bins :, at] = total[reach + bins :] + after_ref[
                    s, :reach, at
                ].astype(jnp.float32)

    return call(
        kernel,
        [((seqs, rows, width), jnp.float32)],
        taps,
        before,
        tokens,
        after_,
        conv.reshape(-1, width),
    )[0]


def expand(mixed, up, cotangent):
    seqs, bins, width = cotangent.shape
    hidden_width = up.shape[1]
    reach = DILATION_BINS

    def kernel(mixed_ref, up_ref, cotangent_ref, pre_ref, share_ref, hidden_ref, total_ref):
        for s in range(seqs):
            low = mixed_ref[s, reach : reach + bins].astype(jnp.bfloat16)
            for at in column_blocks(hidden_width):
                pre = jnp.dot(low, up_ref[:, at], preferred_element_type=jnp.float32)
                share = 0.5 * (1.0 + lax.erf(pre * root_half))
                hidden = (pre * share).astype(jnp.bfloat16)
                pre_ref[s, :, at] = pre
                share_ref[s, :, at] = share
                hidden_ref[s, :, at] = hidden
                term = lax.dot_general(
                    hidden,
                    cotangent_ref[s],
                    (((0,), (0,)), ((), ())),
                    preferred_element_type=jnp.float32,
                )
                if s == 0:
                    total_ref[at, :] = term
                else:
                    total_ref[at, :] += term

    return call(
        kernel,
        [
            ((seqs, bins, hidden_width), jnp.float32),
            ((seqs, bins, hidden_width), jnp.float32),
            ((seqs, bins, hidden_width), jnp.bfloat16),
            ((hidden_width, width), jnp.float32),
        ],
        mixed,
        up,
        cotangent,
    )


def slopes(mixed, up, pre, share):
    seqs, bins, hidden_width = pre.shape
    reach = DILATION_BINS
    rows = bins + 2 * reach

    def bell(value):
        return value * jnp.exp(-0.5 * value * value) * inv_root_two_pi

    def kernel(mixed_ref, up_ref, pre_ref, share_ref, slope_ref):
        for s in range(seqs):
            edges = jnp.concatenate(
                [mixed_ref[s, :reach], mixed_ref[s, reach + bins :]], axis=0
            ).astype(jnp.bfloat16)
            for at in column_blocks(hidden_width):
                edge = jnp.dot(edges, up_ref[:, at], preferred_element_type=jnp.float32)
                slope = 0.5 * (1.0 + lax.erf(edge * root_half)) + bell(edge)
                slope_ref[s, :reach, at] = slope[:reach]
                slope_ref[s, reach : reach + bins, at] = share_ref[s, :, at] + bell(pre_ref[s, :, at])
                slope_ref[s, reach + bins :, at] = slope[reach:]

    return call(
        kernel,
        [((seqs, rows, hidden_width), jnp.float32)],
        mixed,
        up,
        pre,
        share,
    )[0]


def backward(before, cotangent, after_, slope, down, up, conv, scaled, inverse, gain, starts):
    seqs, bins, width = cotangent.shape
    hidden_width = up.shape[1]
    reach = DILATION_BINS
    rows = bins + 2 * reach
    overall = bins * lax.axis_size("ctx")
    by_rows = (((1,), (1,)), ((), ()))

    def kernel(
        before_ref,
        cotangent_ref,
        after_ref,
        slope_ref,
        down_ref,
        up_ref,
        conv_ref,
        scaled_ref,
        inverse_ref,
        gain_ref,
        starts_ref,
        grad_ref,
        gain_term_ref,
        pre_grad,
        mixed_grad,
    ):
        first = lax.axis_index("ctx") * bins
        left, right = masks_at(first, bins, starts_ref, overall)
        for s in range(seqs):
            cot = jnp.concatenate(
                [before_ref[s, 2 * reach :], cotangent_ref[s], after_ref[s, 2 * reach :]], axis=0
            )
            for at in column_blocks(hidden_width):
                hidden_grad = lax.dot_general(
                    cot, down_ref[at, :], by_rows, preferred_element_type=jnp.float32
                )
                pre_grad[:, at] = (hidden_grad * slope_ref[s, :, at]).astype(jnp.bfloat16)
            for at in column_blocks(width):
                mixed_grad[:, at] = cot[:, at].astype(jnp.float32) + lax.dot_general(
                    pre_grad[...], up_ref[at, :], by_rows, preferred_element_type=jnp.float32
                )
            following = jnp.where(right, mixed_grad[2 * reach :, :], 0.0).astype(jnp.bfloat16)
            center = mixed_grad[reach : reach + bins, :].astype(jnp.bfloat16)
            preceding = jnp.where(left, mixed_grad[:bins, :], 0.0).astype(jnp.bfloat16)
            normed_grad = (
                lax.dot_general(following, conv_ref[0], by_rows, preferred_element_type=jnp.float32)
                + lax.dot_general(center, conv_ref[1], by_rows, preferred_element_type=jnp.float32)
                + lax.dot_general(preceding, conv_ref[2], by_rows, preferred_element_type=jnp.float32)
            )
            scaled = scaled_ref[s]
            term = jnp.sum(normed_grad * scaled, axis=0, keepdims=True)
            if s == 0:
                gain_term_ref[...] = term
            else:
                gain_term_ref[...] += term
            scaled_grad = normed_grad * gain_ref[...]
            inner = jnp.mean(scaled_grad * scaled, axis=1, keepdims=True)
            grad_ref[s] = (
                mixed_grad[reach : reach + bins, :]
                + inverse_ref[s] * (scaled_grad - scaled * inner)
            ).astype(jnp.bfloat16)

    return call(
        kernel,
        [((seqs, bins, width), jnp.bfloat16), ((1, width), jnp.float32)],
        before,
        cotangent,
        after_,
        slope,
        down,
        up,
        conv,
        scaled,
        inverse,
        gain,
        starts,
        smem=(10,),
        scratch=[
            pltpu.VMEM((rows, hidden_width), jnp.bfloat16),
            pltpu.VMEM((rows, width), jnp.float32),
        ],
    )


def project(mixed, hidden, down):
    seqs, bins, _ = hidden.shape
    width = down.shape[1]
    reach = DILATION_BINS

    def kernel(mixed_ref, hidden_ref, down_ref, out_ref):
        for s in range(seqs):
            for at in column_blocks(width):
                out_ref[s, :, at] = (
                    mixed_ref[s, reach : reach + bins, at]
                    + jnp.dot(hidden_ref[s], down_ref[:, at], preferred_element_type=jnp.float32)
                ).astype(jnp.bfloat16)

    return call(
        kernel,
        [((seqs, bins, width), jnp.bfloat16)],
        mixed,
        hidden,
        down,
    )[0]


def stack(pieces):
    def kernel(*refs):
        for i in range(len(pieces)):
            refs[-1][i] = refs[i][...]

    return call(kernel, [((len(pieces),) + pieces[0].shape, pieces[0].dtype)], *pieces)[0]


def join(*pieces):
    ends = [sum(piece.shape[0] for piece in pieces[: i + 1]) for i in range(len(pieces))]

    def kernel(*refs):
        for ref, end in zip(refs[:-1], ends):
            refs[-1][end - ref.shape[0] : end] = ref[...]

    return call(kernel, [((ends[-1],) + pieces[0].shape[1:], pieces[0].dtype)], *pieces)[0]


def join_rows(pieces, rows):
    ends = [sum(piece.shape[0] for piece in pieces[: i + 1]) for i in range(len(pieces))]
    held, width = pieces[0].shape[1:]

    def kernel(*refs):
        for ref, end in zip(refs[:-2], ends):
            refs[-2][end - ref.shape[0] : end] = ref[:, :rows]
            refs[-1][end - ref.shape[0] : end] = ref[:, rows:]

    shapes = [(ends[-1], rows, width), (ends[-1], held - rows, width)]
    return call(kernel, [(shape, pieces[0].dtype) for shape in shapes], *pieces)


def neighbours(tokens, cotangent):
    devices = lax.axis_size("ctx")
    pairs = [(i, i + 1) for i in range(1, devices - 1, 2)]
    pairs += [(j, i) for i, j in pairs]
    far, near = 2 * DILATION_BINS, DILATION_BINS
    seqs, bins, width = tokens.shape

    def cut(tokens_ref, cotangent_ref, last_ref, leading_ref):
        last_ref[:, :far] = tokens_ref[:, bins - far :]
        last_ref[:, far:] = cotangent_ref[:, bins - near :]
        leading_ref[:, :far] = tokens_ref[:, :far]
        leading_ref[:, far:] = cotangent_ref[:, :near]

    def kernel(tokens_ref, cotangent_ref, inner_ref, outer_ref):
        is_first = lax.axis_index("ctx") % 2 == 0

        @pl.when(is_first)
        def _():
            cut(tokens_ref, cotangent_ref, inner_ref, outer_ref)

        @pl.when(jnp.logical_not(is_first))
        def _():
            cut(tokens_ref, cotangent_ref, outer_ref, inner_ref)

    edge = ((seqs, far + near, width), tokens.dtype)
    inner, outer = call(kernel, [edge, edge], tokens, cotangent)
    return inner, lax.ppermute(outer, "ctx", pairs)


def in_order(inner, outer):
    def kernel(inner_ref, outer_ref, before_ref, after_ref):
        is_first = lax.axis_index("ctx") % 2 == 0

        @pl.when(is_first)
        def _():
            before_ref[...] = outer_ref[...]
            after_ref[...] = inner_ref[...]

        @pl.when(jnp.logical_not(is_first))
        def _():
            before_ref[...] = inner_ref[...]
            after_ref[...] = outer_ref[...]

    return call(kernel, [(inner.shape, inner.dtype)] * 2, inner, outer)


def line_slots(squares):
    def slots(z):
        slot, first, count = 0, 0, 2
        while first < squares:
            for corner in range(4):
                for k in range(count):
                    yield slot, square_of(z, first + k, squares), corner // 2, corner % 2
                    slot += 1
            first, count = first + count, first + count

    return slots


def assemble_conv(pieces, taps):
    squares = lax.axis_size("ctx") // 8
    width = pieces[0].shape[-1]
    rows = pieces[0].shape[-2] // taps

    def kernel(*refs):
        out = refs[-1]
        core, x, y, z = place()
        for dc in range(2):
            for slot, source, dy, dx in line_slots(squares)(z):
                for t in range(taps):
                    part = refs[dc][slot, t * rows : (t + 1) * rows]
                    out[t, source, y ^ dy, x ^ dx, core ^ dc] = part

    out = call(kernel, [((taps, squares, 2, 2, 2, rows, width), pieces[0].dtype)], *pieces)[0]
    return out.reshape(taps, squares * 8 * rows, width)


def assemble_down(pieces, rows):
    squares = lax.axis_size("ctx") // 8
    width = pieces[0].shape[-1]

    def kernel(own_ref, other_ref, out, wide):
        core, x, y, z = place()
        is_first = core == 0
        for slot, source, dy, dx in line_slots(squares)(z):
            mine = own_ref[slot, :rows].astype(jnp.float32)
            theirs = other_ref[slot, :rows].astype(jnp.float32)
            wide[:rows] = jnp.where(is_first, mine, theirs)
            wide[rows:] = jnp.where(is_first, theirs, mine)
            out[source, y ^ dy, x ^ dx] = wide[...].astype(jnp.bfloat16)

    out = call(
        kernel,
        [((squares, 2, 2, 2 * rows, width), pieces[0].dtype)],
        *pieces,
        scratch=[pltpu.VMEM((2 * rows, width), jnp.float32)],
    )[0]
    return out.reshape(squares * 8 * rows, width)


def assemble_up(pieces, rows, width):
    squares = lax.axis_size("ctx") // 8

    def kernel(*refs):
        out = refs[-1]
        core, x, y, z = place()
        for piece, index, source, dy, dx, dc in up_slots(squares)(z):
            out[source, y ^ dy, x ^ dx, core ^ dc] = refs[piece][index]

    out = call(kernel, [((squares, 2, 2, 2, rows, width), pieces[0].dtype)], *pieces)[0]
    return out.reshape(squares * 8 * rows, width)


def line_masks(squares):
    return [8 << i for i in reversed(range(squares.bit_length() - 1))]


def square_of(z, slot, squares):
    for i, mask in enumerate(line_masks(squares)):
        if slot >> i & 1:
            z = z ^ (mask // 8)
    return z


def up_slots(squares):
    def slots(z):
        for core in range(2):
            for k in range(squares):
                for corner in range(4):
                    source = square_of(z, k, squares)
                    yield core, (4 * k + corner,), source, corner // 2, corner % 2, core

    return slots


def all_after(values, others):
    count = len(values)
    return lax.optimization_barrier((*values, *others))[:count]


def load(*arrays):
    count = len(arrays)

    def kernel(*refs):
        ins, outs, sem = refs[:count], refs[count:-1], refs[-1]
        copies = [pltpu.make_async_copy(i, o, sem.at[at]) for at, (i, o) in enumerate(zip(ins, outs))]
        for copy in copies:
            copy.start()
        for copy in copies:
            copy.wait()

    return pl.pallas_call(
        kernel,
        out_shape=[jax.ShapeDtypeStruct(a.shape, a.dtype) for a in arrays],
        in_specs=[pl.BlockSpec(memory_space=pltpu.HBM)] * count,
        out_specs=[VMEM] * count,
        scratch_shapes=[pltpu.SemaphoreType.DMA((count,))],
        compiler_params=PARAMS,
        cost_estimate=pl.CostEstimate(flops=1, bytes_accessed=1, transcendentals=0),
    )(*arrays)


def gather(conv, up, down, tokens, cotangent, prepared):
    first, *rest = line_masks(lax.axis_size("ctx") // 8)
    width = conv.shape[-1]
    rows = conv.shape[0] * conv.shape[1]
    filler = jnp.zeros((-(rows + down.shape[0]) % 16, width), conv.dtype)
    both = jnp.concatenate([conv.reshape(rows, width), down, filler])
    inner, outer = neighbours(tokens, cotangent)
    new = swap(both, first)
    up_new = [swap(up, mask) for mask in (2, 4, 6)]
    (up,) = load(up)
    new, outer, both, *up_new = all_after((new, outer, both, *up_new), ())
    part = held = stack([both, new])
    up_held = stack([up] + up_new)
    parts = []
    for mask, next_mask in zip([first] + rest, rest + [None]):
        around = [swap(part, 2), swap(part, 4), swap(part, 6)]
        received = swap(up_held, mask)
        other = swap(inner, 1) if next_mask is None else swap(held, next_mask)
        part, held, up_held, received, other, *around = all_after(
            (part, held, up_held, received, other, *around), ()
        )
        up_held = join(up_held, received)
        parts += [part, *around]
        if next_mask is not None:
            held, part = join(held, other), other
    all_conv, all_down = join_rows(parts, rows)
    extra = prepared(tokens, cotangent, *in_order(other, outer))
    return [(piece, swap(piece, 1)) for piece in (all_conv, up_held, all_down)], extra


def core_rows(rows):
    start = (rows // 2 - 2) // 8 * 8
    return start, rows - start


def relative_blocks(total):
    squares = lax.axis_size("ctx") // 8
    rows, width = total.shape[0] // (4 * squares), total.shape[1]
    start, held = core_rows(rows)
    blocks = total.reshape(squares, 2, 2, rows, width)

    def kernel(blocks_ref, keep_ref, send_ref):
        core, x, y, z = place()
        keep = pl.ds(pl.multiple_of(core * start, 8), held)
        send = pl.ds(pl.multiple_of((1 - core) * start, 8), held)
        for k in range(squares):
            for dy in range(2):
                for dx in range(2):
                    keep_ref[k, dy, dx] = blocks_ref[z ^ k, y ^ dy, x ^ dx, keep, :]
                    send_ref[k, dy, dx] = blocks_ref[z ^ k, y ^ dy, x ^ dx, send, :].astype(jnp.bfloat16)

    shape = (squares, 2, 2, held, width)
    return call(kernel, [(shape, jnp.float32), (shape, jnp.bfloat16)], blocks)


def chip_sums(keep, received):
    squares, _, _, held, width = keep.shape

    def kernel(keep_ref, received_ref, own_ref, x_ref, y_ref, far_ref):
        for k in range(squares):
            for corner, ref in enumerate((own_ref, x_ref, y_ref, far_ref)):
                at = (k, corner // 2, corner % 2)
                ref[k] = (keep_ref[at] + received_ref[at].astype(jnp.float32)).astype(ref.dtype)

    shape = (squares, held, width)
    return call(
        kernel, [(shape, jnp.float32)] + [(shape, jnp.bfloat16)] * 3, keep, received
    )


def line_messages(own, received, gain, each):
    squares, held, width = own.shape

    def kernel(own_ref, x_ref, y_ref, far_ref, gain_ref, sum_ref, *message_refs):
        gain = gain_ref[...]
        high = gain.astype(jnp.bfloat16).astype(jnp.float32)
        row = lax.broadcasted_iota(jnp.int32, (held, width), 0)
        row = row - jnp.where(lax.axis_index("ctx") % 2 == 0, each, 0)
        for k in range(squares):
            total = own_ref[k]
            for ref in (x_ref, y_ref, far_ref):
                total = total + ref[k].astype(jnp.float32)
            if k == 0:
                sum_ref[...] = total
            else:
                total = jnp.where(row == 0, high, jnp.where(row == 1, gain - high, total))
                message_refs[k - 1][...] = total.astype(jnp.bfloat16)

    return call(
        kernel,
        [((held, width), jnp.float32)] + [((held, width), jnp.bfloat16)] * (squares - 1),
        own,
        *received,
        gain,
    )


def finish(own, gain, received, each, factor):
    held, width = own.shape

    def kernel(own_ref, gain_ref, *refs):
        received_refs, (down_ref, out_ref) = refs[:-2], refs[-2:]
        is_first = lax.axis_index("ctx") % 2 == 0
        total, gain = own_ref[...], gain_ref[...]
        for ref in received_refs:
            terms = ref[...].astype(jnp.float32)
            total = total + terms
            high = jnp.where(is_first, terms[each : each + 1], terms[:1])
            gain = gain + (high + jnp.where(is_first, terms[each + 1 : each + 2], terms[1:2]))
        down_ref[...] = jnp.where(is_first, total[:each], total[held - each :]) * factor
        out_ref[...] = (gain * factor).reshape(width)

    return call(
        kernel,
        [((each, width), jnp.float32), ((width,), jnp.float32)],
        own,
        gain,
        *received,
    )


def body(tokens, cotangent, norm_gain, conv_weight, up_weight, down_weight, contig_first_bins):
    seqs, bins, width = tokens.shape
    ctx_count = lax.axis_size("ctx")
    data_count = lax.axis_size("dp")
    squares = ctx_count // 8
    gain = norm_gain.reshape(1, width)


    def prepared(tokens, cotangent, before, after_):
        normed = prepare(before, tokens, after_, gain, contig_first_bins)
        return (tokens, cotangent, before, after_, *normed)

    (conv_pieces, up_pieces, down_pieces), extra = gather(
        conv_weight, up_weight, down_weight, tokens, cotangent, prepared
    )
    tokens, cotangent, before, after_, taps, scaled, inverse = extra
    conv = assemble_conv(conv_pieces, conv_weight.shape[0])
    mixed = convolve(taps, before, tokens, after_, conv)
    up = assemble_up(up_pieces, *up_weight.shape)
    pre, share, hidden, total = expand(mixed, up, cotangent)
    slope = slopes(mixed, up, pre, share)
    keep, send = relative_blocks(total)
    down = assemble_down(down_pieces, down_weight.shape[0])
    own_line, *others = chip_sums(keep, after(swap(send, 1), slope))
    received = [swap(v, mask) for v, mask in zip(others, (2, 4, 6))]
    input_grad, gain_term = backward(
        before,
        cotangent,
        after_,
        slope,
        down,
        up,
        conv,
        scaled,
        inverse,
        gain,
        contig_first_bins,
    )
    output = project(mixed, hidden, down)
    for mask in (1, 2, 4):
        if mask == 4:
            gain_term = after(gain_term, output)
        gain_term = gain_term + swap(gain_term, mask)
    factor = float(ctx_count * data_count * bins * seqs) ** (-0.5)
    each = total.shape[0] // ctx_count
    own_sum, *messages = line_messages(own_line, received, gain_term, each)
    arrived = [swap(message, 8 * (k + 1)) for k, message in enumerate(messages)]
    down_part, gain_all = finish(own_sum, gain_term, arrived, each, factor)
    gain_part = gain_all
    if data_count > 1:
        width_part = width // data_count
        down_part = lax.psum_scatter(down_part, "dp", scatter_dimension=1, tiled=True)
        gain_part = lax.psum(gain_part, "dp")
        at = lax.axis_index("dp") * width_part
        gain_part = lax.dynamic_slice_in_dim(gain_part, at, width_part)
    return output, input_grad, down_part, gain_part


def solution(mesh):
    placed = (
        P("dp", "ctx", None),
        P("dp", "ctx", None),
        P(),
        P(None, "ctx", None),
        P("ctx", None),
        P("ctx", None),
        P(),
    )
    return jax.shard_map(
        body,
        mesh=mesh,
        in_specs=placed,
        out_specs=(P("dp", "ctx", None), P("dp", "ctx", None), P("ctx", "dp"), P("dp")),
        check_vma=False,
    )
```

time: 356 us -> 98.5 us (0.28)
  blocking collectives: 124 us -> 0 us
  waiting for transfers between devices: 169 us -> 48.1 us
  matrix products: 17.1 us -> 0 us
  starting transfers between devices: 14 us -> 30.3 us
  Pallas kernels: 0 us -> 15.5 us
  between operations: 14.1 us -> 0.9 us
  local copies, waits for them, and re-layouts: 9.84 us -> 2.3 us
  other arithmetic: 7.71 us -> 1.04 us
    all_gather x3 -> x0, waiting for transfers between devices: 163 us -> none  [the longest x1 59.5 us: body(): lax.all_gather(conv_weight, 'ctx', axis=1, tiled=True)]
    unnamed x1 -> x0, blocking collectives: 83 us -> none
    ppermute x4 -> x28, waiting for transfers between devices: 3.85 us -> 48.1 us  [the longest x27 48.1 us: swap(): return lax.ppermute(value, 'ctx', [(i, i ^ mask) for i in range(devices)])]
    psum x1 -> x0, blocking collectives: 41.3 us -> none  [body(): gain_all = lax.psum(gain_term, ('ctx', 'dp'))]
    ppermute x4 -> x28, starting transfers between devices: 8.6 us -> 30.3 us  [the longest x27 29.6 us: swap(): return lax.ppermute(value, 'ctx', [(i, i ^ mask) for i in range(devices)])]
    dot_general x6 -> x0, matrix products: 17.1 us -> none  [the longest x1 3.42 us: body(): jnp.dot(hidden, down_full, preferred_element_type=jnp.float32)]
    pallas_call x0 -> x21, Pallas kernels: none -> 15.5 us  [the longest x20 15.5 us: call(): pl.pallas_call(kernel, out_shape=shapes, in_specs=[SMEM if i in smem else...]
    unnamed x4 -> x0, starting transfers between devices: 5.31 us -> none
  transfers between devices with their start and end apart: 11 -> 28, of which waited for: 4 -> 16; matrix products, arithmetic and copies ran while one was open for 30% -> 1% of each run, Pallas kernels for 0% -> 10%
where the time goes in v2:
time: 98.5 us; the launch traced here: 98.2 us
  waiting for transfers between devices  48.1 us (49%)
  starting transfers between devices  30.3 us (31%)
  Pallas kernels  15.5 us (16%)
  local copies, waits for them, and re-layouts  2.3 us (2%)
  other arithmetic  1.04 us (1%)
    ppermute x27, waiting for transfers between devices, swap(): return lax.ppermute(value, 'ctx', [(i, i ^ mask) for i in range(devices)])  48.1 us
    ppermute x27, starting transfers between devices, swap(): return lax.ppermute(value, 'ctx', [(i, i ^ mask) for i in range(devices)])  29.6 us
    pallas_call x20, Pallas kernels, call(): pl.pallas_call(kernel, out_shape=shapes, in_specs=[SMEM if i in smem else...  15.5 us
    unnamed x14, local copies, waits for them, and re-layouts  2.22 us
  transfers between devices with their start and end apart: 28, of which 16 were waited for; matrix products, arithmetic and copies ran while one was open for 1% of the time, Pallas kernels for 10%

profile of v2, /device:TPU:0, one launch (start us, length us, event | category | flops | bytes accessed | tf_op | source)
XLA Modules:
  0.0 98.2 jit_solution(7221029291406420348)
XLA Ops:
  0.6 1.0 %copy-done = bf16[1,256,768]{2,1,0:T(8,128)(2,1)S(1)} copy-done((bf16[1,256,768]{2,1,0:T(8,128)(2,1)S(1)}, bf16[1,256,768]{2,1,0:T(8,128)(2,1)}, u32[]{:S(2)}) %copy-start) | copy-done | bytes 393240
  1.6 1.0 %copy-done.2 = bf16[1,256,768]{2,1,0:T(8,128)(2,1)S(1)} copy-done((bf16[1,256,768]{2,1,0:T(8,128)(2,1)S(1)}, bf16[1,256,768]{2,1,0:T(8,128)(2,1)}, u32[]{:S(2)}) %copy-start.2) | copy-done | bytes 393240
  2.7 0.7 collective-permute-start.1
  3.4 1.0 %maximum_maximum_fusion.refs_0_ = bf16[112,768]{1,0:T(8,128)(2,1)S(1)} fusion(bf16[36,768]{1,0:T(8,128)(2,1)} %param.12, bf16[72,768]{1,0:T(8,128)(2,1)} %bitcast.14, bf16[112]{0:T(256)(128)(2,1)S(1)} %pad.2.clone), kind=kLoop, calls=%fused_computation | loop fusion | flops 516096 | bytes 338144 | tf_op jit(solution)/shard_map/concatenate | solution.py:515
  4.5 7.1 %collective-permute-start = (bf16[112,768]{1,0:T(8,128)(2,1)S(1)}, bf16[112,768]{1,0:T(8,128)(2,1)S(1)}, u32[]{:S(2)}, u32[]{:S(2)}) collective-permute-start(bf16[112,768]{1,0:T(8,128)(2,1)S(1)} %maximum_maximum_fusion.refs_0_), channel_id=1, source_target_pairs={{0,16},{1,17},{2,18},{3,19},{4,20},{5,21},{6,22},{7,23},{8,24},{9,... | collective-permute-start | bytes 516104 | tf_op jit(solution)/shard_map/ppermute | solution.py:17
  11.6 1.3 %collective-permute-start.3 = (bf16[24,1152]{1,0:T(8,128)(2,1)}, bf16[24,1152]{1,0:T(8,128)(2,1)S(1)}, u32[]{:S(2)}, u32[]{:S(2)}) collective-permute-start(bf16[24,1152]{1,0:T(8,128)(2,1)} %refs_0_.1), channel_id=1, source_target_pairs={{0,4},{1,5},{2,6},{3,7},{4,0},{5,1},{6,2},{7,3},{8,12},{9,13},{10,... | collective-permute-start | bytes 165896 | tf_op jit(solution)/shard_map/ppermute | solution.py:17
  12.8 2.2 %collective-permute-start.4 = (bf16[24,1152]{1,0:T(8,128)(2,1)}, bf16[24,1152]{1,0:T(8,128)(2,1)S(1)}, u32[]{:S(2)}, u32[]{:S(2)}) collective-permute-start(bf16[24,1152]{1,0:T(8,128)(2,1)} %refs_0_.1), channel_id=1, source_target_pairs={{0,6},{1,7},{2,4},{3,5},{4,2},{5,3},{6,0},{7,1},{8,14},{9,15},{10,... | collective-permute-start | bytes 165896 | tf_op jit(solution)/shard_map/ppermute | solution.py:17
  15.1 1.5 %collective-permute-done.2.refs_1_ = bf16[24,1152]{1,0:T(8,128)(2,1)S(1)} collective-permute-done((bf16[24,1152]{1,0:T(8,128)(2,1)}, bf16[24,1152]{1,0:T(8,128)(2,1)S(1)}, u32[]{:S(2)}, u32[]{:S(2)}) %collective-permute-start.2) | collective-permute-done | bytes 55328 | tf_op jit(solution)/shard_map/ppermute | solution.py:17
  16.6 1.9 %collective-permute-done.4.refs_3_ = bf16[24,1152]{1,0:T(8,128)(2,1)S(1)} collective-permute-done((bf16[24,1152]{1,0:T(8,128)(2,1)}, bf16[24,1152]{1,0:T(8,128)(2,1)S(1)}, u32[]{:S(2)}, u32[]{:S(2)}) %collective-permute-start.4) | collective-permute-done | bytes 55328 | tf_op jit(solution)/shard_map/ppermute | solution.py:17
  18.5 4.1 %collective-permute-done.refs_1_ = bf16[112,768]{1,0:T(8,128)(2,1)S(1)} collective-permute-done((bf16[112,768]{1,0:T(8,128)(2,1)S(1)}, bf16[112,768]{1,0:T(8,128)(2,1)S(1)}, u32[]{:S(2)}, u32[]{:S(2)}) %collective-permute-start) | collective-permute-done | bytes 172064 | tf_op jit(solution)/shard_map/ppermute | solution.py:17
  23.0 3.2 %collective-permute-start.9 = (bf16[2,112,768]{2,1,0:T(8,128)(2,1)S(1)}, bf16[2,112,768]{2,1,0:T(8,128)(2,1)S(1)}, u32[]{:S(2)}, u32[]{:S(2)}) collective-permute-start(bf16[2,112,768]{2,1,0:T(8,128)(2,1)S(1)} %shard_map.103.refs_0_), channel_id=1, source_target_pairs={{0,6},{1,7},{2,4},{3,5},{4,2},{5,3},{6,0},{7,1},{8,14},{9,15},{10,... | collective-permute-start | bytes 1032200 | tf_op jit(solution)/shard_map/ppermute | solution.py:17
  26.3 1.2 %collective-permute-start.5 = (bf16[4,24,1152]{2,1,0:T(8,128)(2,1)S(1)}, bf16[4,24,1152]{2,1,0:T(8,128)(2,1)S(1)}, u32[]{:S(2)}, u32[]{:S(2)}) collective-permute-start(bf16[4,24,1152]{2,1,0:T(8,128)(2,1)S(1)} %shard_map.105.refs_0_), channel_id=1, source_target_pairs={{0,16},{1,17},{2,18},{3,19},{4,20},{5,21},{6,22},{7,23},{8,24},{9,... | collective-permute-start | bytes 663560 | tf_op jit(solution)/shard_map/ppermute | solution.py:17
  27.5 10.3 %collective-permute-done.5.refs_1_ = bf16[4,24,1152]{2,1,0:T(8,128)(2,1)S(1)} collective-permute-done((bf16[4,24,1152]{2,1,0:T(8,128)(2,1)S(1)}, bf16[4,24,1152]{2,1,0:T(8,128)(2,1)S(1)}, u32[]{:S(2)}, u32[]{:S(2)}) %collective-permute-start.5) | collective-permute-done | bytes 221216 | tf_op jit(solution)/shard_map/ppermute | solution.py:17
  37.8 1.2 %collective-permute-done.8.refs_2_ = bf16[2,112,768]{2,1,0:T(8,128)(2,1)S(1)} collective-permute-done((bf16[2,112,768]{2,1,0:T(8,128)(2,1)S(1)}, bf16[2,112,768]{2,1,0:T(8,128)(2,1)S(1)}, u32[]{:S(2)}, u32[]{:S(2)}) %collective-permute-start.8) | collective-permute-done | bytes 344096 | tf_op jit(solution)/shard_map/ppermute | solution.py:17
  39.1 0.7 collective-permute-start.10
  39.8 1.6 %collective-permute-start.12 = (bf16[2,112,768]{2,1,0:T(8,128)(2,1)S(1)}, bf16[2,112,768]{2,1,0:T(8,128)(2,1)S(1)}, u32[]{:S(2)}, u32[]{:S(2)}) collective-permute-start(bf16[2,112,768]{2,1,0:T(8,128)(2,1)S(1)} %collective-permute-done.6.refs_4_), channel_id=1, source_target_pairs={{0,2},{1,3},{2,0},{3,1},{4,6},{5,7},{6,4},{7,5},{8,10},{9,11},{10,... | collective-permute-start | bytes 1032200 | tf_op jit(solution)/shard_map/ppermute | solution.py:17
  41.4 0.7 collective-permute-start.13
  42.1 1.2 %collective-permute-start.14 = (bf16[2,112,768]{2,1,0:T(8,128)(2,1)S(1)}, bf16[2,112,768]{2,1,0:T(8,128)(2,1)S(1)}, u32[]{:S(2)}, u32[]{:S(2)}) collective-permute-start(bf16[2,112,768]{2,1,0:T(8,128)(2,1)S(1)} %collective-permute-done.6.refs_4_), channel_id=1, source_target_pairs={{0,6},{1,7},{2,4},{3,5},{4,2},{5,3},{6,0},{7,1},{8,14},{9,15},{10,... | collective-permute-start | bytes 1032200 | tf_op jit(solution)/shard_map/ppermute | solution.py:17
  43.3 1.6 %collective-permute-done.11.inner_ref = bf16[1,192,768]{2,1,0:T(8,128)(2,1)S(1)} collective-permute-done((bf16[1,192,768]{2,1,0:T(8,128)(2,1)S(1)}, bf16[1,192,768]{2,1,0:T(8,128)(2,1)S(1)}, u32[]{:S(2)}, u32[]{:S(2)}) %collective-permute-start.11) | collective-permute-done | bytes 294944 | tf_op jit(solution)/shard_map/ppermute | solution.py:17
  44.9 5.9 %collective-permute-done.12.refs_5_ = bf16[2,112,768]{2,1,0:T(8,128)(2,1)S(1)} collective-permute-done((bf16[2,112,768]{2,1,0:T(8,128)(2,1)S(1)}, bf16[2,112,768]{2,1,0:T(8,128)(2,1)S(1)}, u32[]{:S(2)}, u32[]{:S(2)}) %collective-permute-start.12) | collective-permute-done | bytes 344096 | tf_op jit(solution)/shard_map/ppermute | solution.py:17
  50.8 6.8 %collective-permute-done.13.refs_6_ = bf16[2,112,768]{2,1,0:T(8,128)(2,1)S(1)} collective-permute-done((bf16[2,112,768]{2,1,0:T(8,128)(2,1)S(1)}, bf16[2,112,768]{2,1,0:T(8,128)(2,1)S(1)}, u32[]{:S(2)}, u32[]{:S(2)}) %collective-permute-start.13) | collective-permute-done | bytes 344096 | tf_op jit(solution)/shard_map/ppermute | solution.py:17
  58.0 0.6 collective-permute-start.16
  58.8 1.3 %shard_map.108 = (bf16[1,384,2304]{2,1,0:T(8,128)(2,1)S(1)}, f32[1,256,768]{2,1,0:T(8,128)S(1)}, f32[1,256,1]{2,1,0:T(8,128)S(1)}) custom-call(bf16[1,192,768]{2,1,0:T(8,128)(2,1)S(1)} %get-tuple-element.65.before_ref, bf16[1,256,768]{2,1,0:T(8,128)(2,1)S(1)} %copy-done.3, bf16[1,192,768]{2,1,0:T(8,128)(2,1)S(1)} %get-tuple-element.66.after_ref, ...), custom_call_target="tpu_custom_call" | custom-call | flops 1 | bytes 1 | tf_op jit(solution)/shard_map/pallas_call | solution.py:37
  60.1 2.8 %collective-permute-done.16.refs_1_ = bf16[16,24,1152]{2,1,0:T(8,128)(2,1)S(1)} collective-permute-done((bf16[16,24,1152]{2,1,0:T(8,128)(2,1)S(1)}, bf16[16,24,1152]{2,1,0:T(8,128)(2,1)S(1)}, u32[]{:S(2)}, u32[]{:S(2)}) %collective-permute-start.16) | collective-permute-done | bytes 884768 | tf_op jit(solution)/shard_map/ppermute | solution.py:17
  63.0 0.3 shard_map.110
  63.3 2.0 %shard_map.111.mixed_ref = f32[1,384,768]{2,1,0:T(8,128)S(1)} custom-call(bf16[1,384,2304]{2,1,0:T(8,128)(2,1)S(1)} %get-tuple-element.67.taps_ref, bf16[1,192,768]{2,1,0:T(8,128)(2,1)S(1)} %get-tuple-element.65.before_ref, bf16[1,256,768]{2,1,0:T(8,128)(2,1)S(1)} %copy-done.3, bf16[1,192,768]{2,1,0:T(8,128)(2,1)S(1)} %get-tuple-element.66.after_ref, ...), custom_call_target="tpu_custom_call" | custom-call | flops 1 | bytes 1 | tf_op jit(solution)/shard_map/pallas_call | solution.py:37
  65.3 1.8 %shard_map.114 = (f32[1,256,1152]{2,1,0:T(8,128)S(1)}, f32[1,256,1152]{2,1,0:T(8,128)S(1)}, bf16[1,256,1152]{2,1,0:T(8,128)(2,1)S(1)}, f32[1152,768]{1,0:T(8,128)S(1)}) custom-call(f32[1,384,768]{2,1,0:T(8,128)S(1)} %shard_map.111.mixed_ref, bf16[768,1152]{1,0:T(8,128)(2,1)S(1)} %bitcast.8, bf16[1,256,768]{2,1,0:T(8,128)(2,1)S(1)} %copy-done.1), custom_call_target="tpu_custom_call" | custom-call | flops 1 | bytes 1 | tf_op jit(solution)/shard_map/pallas_call | solution.py:37
  67.6 0.4 collective-permute-start.17
  68.0 0.9 shard_map.117.slope_ref
  68.9 1.1 %collective-permute-done.18.received_ref = bf16[4,2,2,40,768]{4,3,2,1,0:T(8,128)(2,1)S(1)} collective-permute-done((bf16[4,2,2,40,768]{4,3,2,1,0:T(8,128)(2,1)S(1)}, bf16[4,2,2,40,768]{4,3,2,1,0:T(8,128)(2,1)S(1)}, u32[]{:S(2)}, u32[]{:S(2)}) %collective-permute-start.18) | collective-permute-done | bytes 983072 | tf_op jit(solution)/shard_map/ppermute | solution.py:17
  70.2 0.4 collective-permute-start.19
  70.6 1.7 %collective-permute-start.20 = (bf16[4,40,768]{2,1,0:T(8,128)(2,1)S(1)}, bf16[4,40,768]{2,1,0:T(8,128)(2,1)S(1)}, u32[]{:S(2)}, u32[]{:S(2)}) collective-permute-start(bf16[4,40,768]{2,1,0:T(8,128)(2,1)S(1)} %get-tuple-element.92), channel_id=1, source_target_pairs={{0,4},{1,5},{2,6},{3,7},{4,0},{5,1},{6,2},{7,3},{8,12},{9,13},{10,... | collective-permute-start | bytes 737288 | tf_op jit(solution)/shard_map/ppermute | solution.py:17
  72.4 1.4 %collective-permute-start.21 = (bf16[4,40,768]{2,1,0:T(8,128)(2,1)S(1)}, bf16[4,40,768]{2,1,0:T(8,128)(2,1)S(1)}, u32[]{:S(2)}, u32[]{:S(2)}) collective-permute-start(bf16[4,40,768]{2,1,0:T(8,128)(2,1)S(1)} %get-tuple-element.93), channel_id=1, source_target_pairs={{0,6},{1,7},{2,4},{3,5},{4,2},{5,3},{6,0},{7,1},{8,14},{9,15},{10,... | collective-permute-start | bytes 737288 | tf_op jit(solution)/shard_map/ppermute | solution.py:17
  73.8 0.6 shard_map.115
  74.4 5.2 %shard_map.118 = (bf16[1,256,768]{2,1,0:T(8,128)(2,1)}, f32[1,768]{1,0:T(1,128)S(1)}) custom-call(bf16[1,192,768]{2,1,0:T(8,128)(2,1)S(1)} %get-tuple-element.65.before_ref, bf16[1,256,768]{2,1,0:T(8,128)(2,1)S(1)} %copy-done.1, bf16[1,192,768]{2,1,0:T(8,128)(2,1)S(1)} %get-tuple-element.66.after_ref, f32[1,384,1152]{2,1,0:T(8,128)S(1)} %shard_map.117.slope_ref, ...), custom_call_target="tpu_custom_call" | custom-call | flops 1 | bytes 1 | tf_op jit(solution)/shard_map/pallas_call | solution.py:37
  79.6 1.2 %collective-permute-done.22 = f32[1,768]{1,0:T(1,128)S(1)} collective-permute-done((f32[1,768]{1,0:T(1,128)S(1)}, f32[1,768]{1,0:T(1,128)S(1)}, u32[]{:S(2)}, u32[]{:S(2)}) %collective-permute-start.22) | collective-permute-done | bytes 3104 | tf_op jit(solution)/shard_map/ppermute | solution.py:17
  80.8 0.4 collective-permute-start.23
  81.1 1.6 %shard_map.116 = bf16[1,256,768]{2,1,0:T(8,128)(2,1)} custom-call(f32[1,384,768]{2,1,0:T(8,128)S(1)} %shard_map.111.mixed_ref, bf16[1,256,1152]{2,1,0:T(8,128)(2,1)S(1)} %get-tuple-element.79.hidden_ref, bf16[1152,768]{1,0:T(8,128)(2,1)S(1)} %bitcast.12), custom_call_target="tpu_custom_call" | custom-call | flops 1 | bytes 1 | tf_op jit(solution)/shard_map/pallas_call | solution.py:37
  82.7 1.7 %collective-permute-done.23 = f32[1,768]{1,0:T(1,128)S(1)} collective-permute-done((f32[1,768]{1,0:T(1,128)S(1)}, f32[1,768]{1,0:T(1,128)S(1)}, u32[]{:S(2)}, u32[]{:S(2)}) %collective-permute-start.23) | collective-permute-done | bytes 3104 | tf_op jit(solution)/shard_map/ppermute | solution.py:17
  84.4 0.4 collective-permute-start.24
  84.8 3.2 %collective-permute-done.24 = f32[1,768]{1,0:T(1,128)S(1)} collective-permute-done((f32[1,768]{1,0:T(1,128)S(1)}, f32[1,768]{1,0:T(1,128)S(1)}, u32[]{:S(2)}, u32[]{:S(2)}) %collective-permute-start.24) | collective-permute-done | bytes 3104 | tf_op jit(solution)/shard_map/ppermute | solution.py:17
  88.1 1.7 %collective-permute-start.25 = (bf16[40,768]{1,0:T(8,128)(2,1)S(1)}, bf16[40,768]{1,0:T(8,128)(2,1)S(1)}, u32[]{:S(2)}, u32[]{:S(2)}) collective-permute-start(bf16[40,768]{1,0:T(8,128)(2,1)S(1)} %get-tuple-element.97), channel_id=1, source_target_pairs={{0,8},{1,9},{2,10},{3,11},{4,12},{5,13},{6,14},{7,15},{8,0},{9,1},... | collective-permute-start | bytes 184328 | tf_op jit(solution)/shard_map/ppermute | solution.py:17
  89.9 1.6 %collective-permute-start.26 = (bf16[40,768]{1,0:T(8,128)(2,1)S(1)}, bf16[40,768]{1,0:T(8,128)(2,1)S(1)}, u32[]{:S(2)}, u32[]{:S(2)}) collective-permute-start(bf16[40,768]{1,0:T(8,128)(2,1)S(1)} %get-tuple-element.98), channel_id=1, source_target_pairs={{0,16},{1,17},{2,18},{3,19},{4,20},{5,21},{6,22},{7,23},{8,24},{9,... | collective-permute-start | bytes 184328 | tf_op jit(solution)/shard_map/ppermute | solution.py:17
  91.5 1.1 %collective-permute-start.27 = (bf16[40,768]{1,0:T(8,128)(2,1)S(1)}, bf16[40,768]{1,0:T(8,128)(2,1)S(1)}, u32[]{:S(2)}, u32[]{:S(2)}) collective-permute-start(bf16[40,768]{1,0:T(8,128)(2,1)S(1)} %get-tuple-element.99), channel_id=1, source_target_pairs={{0,24},{1,25},{2,26},{3,27},{4,28},{5,29},{6,30},{7,31},{8,16},{9,... | collective-permute-start | bytes 184328 | tf_op jit(solution)/shard_map/ppermute | solution.py:17
  92.6 0.4 collective-permute-done.25.refs_0_
  93.0 2.7 %collective-permute-done.26.refs_1_ = bf16[40,768]{1,0:T(8,128)(2,1)S(1)} collective-permute-done((bf16[40,768]{1,0:T(8,128)(2,1)S(1)}, bf16[40,768]{1,0:T(8,128)(2,1)S(1)}, u32[]{:S(2)}, u32[]{:S(2)}) %collective-permute-start.26) | collective-permute-done | bytes 61472 | tf_op jit(solution)/shard_map/ppermute | solution.py:17
  95.7 1.7 %collective-permute-done.27.refs_2_ = bf16[40,768]{1,0:T(8,128)(2,1)S(1)} collective-permute-done((bf16[40,768]{1,0:T(8,128)(2,1)S(1)}, bf16[40,768]{1,0:T(8,128)(2,1)S(1)}, u32[]{:S(2)}, u32[]{:S(2)}) %collective-permute-start.27) | collective-permute-done | bytes 61472 | tf_op jit(solution)/shard_map/ppermute | solution.py:17
  97.5 0.7 shard_map.122
  (50 shorter events, 2.2 us)
Async XLA Ops:
  0.6 1.0 %copy-start = (bf16[1,256,768]{2,1,0:T(8,128)(2,1)S(1)}, bf16[1,256,768]{2,1,0:T(8,128)(2,1)}, u32[]{:S(2)}) copy-start(bf16[1,256,768]{2,1,0:T(8,128)(2,1)} %cotangent_ref.5) | copy-start | bytes 1179652
  1.6 1.0 %copy-start.2 = (bf16[1,256,768]{2,1,0:T(8,128)(2,1)S(1)}, bf16[1,256,768]{2,1,0:T(8,128)(2,1)}, u32[]{:S(2)}) copy-start(bf16[1,256,768]{2,1,0:T(8,128)(2,1)} %tokens_ref.5) | copy-start | bytes 1179652
  2.6 23.6 %copy-start.4 = (bf16[24,1152]{1,0:T(8,128)(2,1)S(1)}, bf16[24,1152]{1,0:T(8,128)(2,1)}, u32[]{:S(2)}) copy-start(bf16[24,1152]{1,0:T(8,128)(2,1)} %refs_0_.1) | copy-start | bytes 165892
  2.7 19.9 %collective-permute-start.1 = (bf16[1,192,768]{2,1,0:T(8,128)(2,1)S(1)}, bf16[1,192,768]{2,1,0:T(8,128)(2,1)S(1)}, u32[]{:S(2)}, u32[]{:S(2)}) collective-permute-start(bf16[1,192,768]{2,1,0:T(8,128)(2,1)S(1)} %get-tuple-element.53), channel_id=1, source_target_pairs={{1,2},{3,4},{5,6},{7,8},{9,10},{11,12},{13,14},{15,16},{17,18},{19... | collective-permute-start | bytes 884744 | tf_op jit(solution)/shard_map/ppermute | solution.py:374
  4.5 18.1 %collective-permute-start = (bf16[112,768]{1,0:T(8,128)(2,1)S(1)}, bf16[112,768]{1,0:T(8,128)(2,1)S(1)}, u32[]{:S(2)}, u32[]{:S(2)}) collective-permute-start(bf16[112,768]{1,0:T(8,128)(2,1)S(1)} %maximum_maximum_fusion.refs_0_), channel_id=1, source_target_pairs={{0,16},{1,17},{2,18},{3,19},{4,20},{5,21},{6,22},{7,23},{8,24},{9,... | collective-permute-start | bytes 516104 | tf_op jit(solution)/shard_map/ppermute | solution.py:17
  11.6 5.0 %collective-permute-start.2 = (bf16[24,1152]{1,0:T(8,128)(2,1)}, bf16[24,1152]{1,0:T(8,128)(2,1)S(1)}, u32[]{:S(2)}, u32[]{:S(2)}) collective-permute-start(bf16[24,1152]{1,0:T(8,128)(2,1)} %refs_0_.1), channel_id=1, source_target_pairs={{0,2},{1,3},{2,0},{3,1},{4,6},{5,7},{6,4},{7,5},{8,10},{9,11},{10,... | collective-permute-start | bytes 165896 | tf_op jit(solution)/shard_map/ppermute | solution.py:17
  11.6 5.0 %collective-permute-start.3 = (bf16[24,1152]{1,0:T(8,128)(2,1)}, bf16[24,1152]{1,0:T(8,128)(2,1)S(1)}, u32[]{:S(2)}, u32[]{:S(2)}) collective-permute-start(bf16[24,1152]{1,0:T(8,128)(2,1)} %refs_0_.1), channel_id=1, source_target_pairs={{0,4},{1,5},{2,6},{3,7},{4,0},{5,1},{6,2},{7,3},{8,12},{9,13},{10,... | collective-permute-start | bytes 165896 | tf_op jit(solution)/shard_map/ppermute | solution.py:17
  12.8 5.6 %collective-permute-start.4 = (bf16[24,1152]{1,0:T(8,128)(2,1)}, bf16[24,1152]{1,0:T(8,128)(2,1)S(1)}, u32[]{:S(2)}, u32[]{:S(2)}) collective-permute-start(bf16[24,1152]{1,0:T(8,128)(2,1)} %refs_0_.1), channel_id=1, source_target_pairs={{0,6},{1,7},{2,4},{3,5},{4,2},{5,3},{6,0},{7,1},{8,14},{9,15},{10,... | collective-permute-start | bytes 165896 | tf_op jit(solution)/shard_map/ppermute | solution.py:17
  22.6 15.3 %collective-permute-start.6 = (bf16[2,112,768]{2,1,0:T(8,128)(2,1)S(1)}, bf16[2,112,768]{2,1,0:T(8,128)(2,1)S(1)}, u32[]{:S(2)}, u32[]{:S(2)}) collective-permute-start(bf16[2,112,768]{2,1,0:T(8,128)(2,1)S(1)} %shard_map.103.refs_0_), channel_id=1, source_target_pairs={{0,8},{1,9},{2,10},{3,11},{4,12},{5,13},{6,14},{7,15},{8,0},{9,1},... | collective-permute-start | bytes 1032200 | tf_op jit(solution)/shard_map/ppermute | solution.py:17
  22.7 15.2 %collective-permute-start.7 = (bf16[2,112,768]{2,1,0:T(8,128)(2,1)S(1)}, bf16[2,112,768]{2,1,0:T(8,128)(2,1)S(1)}, u32[]{:S(2)}, u32[]{:S(2)}) collective-permute-start(bf16[2,112,768]{2,1,0:T(8,128)(2,1)S(1)} %shard_map.103.refs_0_), channel_id=1, source_target_pairs={{0,2},{1,3},{2,0},{3,1},{4,6},{5,7},{6,4},{7,5},{8,10},{9,11},{10,... | collective-permute-start | bytes 1032200 | tf_op jit(solution)/shard_map/ppermute | solution.py:17
  22.7 16.3 %collective-permute-start.8 = (bf16[2,112,768]{2,1,0:T(8,128)(2,1)S(1)}, bf16[2,112,768]{2,1,0:T(8,128)(2,1)S(1)}, u32[]{:S(2)}, u32[]{:S(2)}) collective-permute-start(bf16[2,112,768]{2,1,0:T(8,128)(2,1)S(1)} %shard_map.103.refs_0_), channel_id=1, source_target_pairs={{0,4},{1,5},{2,6},{3,7},{4,0},{5,1},{6,2},{7,3},{8,12},{9,13},{10,... | collective-permute-start | bytes 1032200 | tf_op jit(solution)/shard_map/ppermute | solution.py:17
  23.0 16.0 %collective-permute-start.9 = (bf16[2,112,768]{2,1,0:T(8,128)(2,1)S(1)}, bf16[2,112,768]{2,1,0:T(8,128)(2,1)S(1)}, u32[]{:S(2)}, u32[]{:S(2)}) collective-permute-start(bf16[2,112,768]{2,1,0:T(8,128)(2,1)S(1)} %shard_map.103.refs_0_), channel_id=1, source_target_pairs={{0,6},{1,7},{2,4},{3,5},{4,2},{5,3},{6,0},{7,1},{8,14},{9,15},{10,... | collective-permute-start | bytes 1032200 | tf_op jit(solution)/shard_map/ppermute | solution.py:17
  26.3 11.5 %collective-permute-start.5 = (bf16[4,24,1152]{2,1,0:T(8,128)(2,1)S(1)}, bf16[4,24,1152]{2,1,0:T(8,128)(2,1)S(1)}, u32[]{:S(2)}, u32[]{:S(2)}) collective-permute-start(bf16[4,24,1152]{2,1,0:T(8,128)(2,1)S(1)} %shard_map.105.refs_0_), channel_id=1, source_target_pairs={{0,16},{1,17},{2,18},{3,19},{4,20},{5,21},{6,22},{7,23},{8,24},{9,... | collective-permute-start | bytes 663560 | tf_op jit(solution)/shard_map/ppermute | solution.py:17
  39.1 18.5 %collective-permute-start.10 = (bf16[8,24,1152]{2,1,0:T(8,128)(2,1)S(1)}, bf16[8,24,1152]{2,1,0:T(8,128)(2,1)S(1)}, u32[]{:S(2)}, u32[]{:S(2)}) collective-permute-start(bf16[8,24,1152]{2,1,0:T(8,128)(2,1)S(1)} %shard_map.106.refs_0_), channel_id=1, source_target_pairs={{0,8},{1,9},{2,10},{3,11},{4,12},{5,13},{6,14},{7,15},{8,0},{9,1},... | collective-permute-start | bytes 1327112 | tf_op jit(solution)/shard_map/ppermute | solution.py:17
  39.8 11.0 %collective-permute-start.12 = (bf16[2,112,768]{2,1,0:T(8,128)(2,1)S(1)}, bf16[2,112,768]{2,1,0:T(8,128)(2,1)S(1)}, u32[]{:S(2)}, u32[]{:S(2)}) collective-permute-start(bf16[2,112,768]{2,1,0:T(8,128)(2,1)S(1)} %collective-permute-done.6.refs_4_), channel_id=1, source_target_pairs={{0,2},{1,3},{2,0},{3,1},{4,6},{5,7},{6,4},{7,5},{8,10},{9,11},{10,... | collective-permute-start | bytes 1032200 | tf_op jit(solution)/shard_map/ppermute | solution.py:17
  41.4 16.2 %collective-permute-start.13 = (bf16[2,112,768]{2,1,0:T(8,128)(2,1)S(1)}, bf16[2,112,768]{2,1,0:T(8,128)(2,1)S(1)}, u32[]{:S(2)}, u32[]{:S(2)}) collective-permute-start(bf16[2,112,768]{2,1,0:T(8,128)(2,1)S(1)} %collective-permute-done.6.refs_4_), channel_id=1, source_target_pairs={{0,4},{1,5},{2,6},{3,7},{4,0},{5,1},{6,2},{7,3},{8,12},{9,13},{10,... | collective-permute-start | bytes 1032200 | tf_op jit(solution)/shard_map/ppermute | solution.py:17
  42.1 15.5 %collective-permute-start.14 = (bf16[2,112,768]{2,1,0:T(8,128)(2,1)S(1)}, bf16[2,112,768]{2,1,0:T(8,128)(2,1)S(1)}, u32[]{:S(2)}, u32[]{:S(2)}) collective-permute-start(bf16[2,112,768]{2,1,0:T(8,128)(2,1)S(1)} %collective-permute-done.6.refs_4_), channel_id=1, source_target_pairs={{0,6},{1,7},{2,4},{3,5},{4,2},{5,3},{6,0},{7,1},{8,14},{9,15},{10,... | collective-permute-start | bytes 1032200 | tf_op jit(solution)/shard_map/ppermute | solution.py:17
  43.3 15.2 %copy-start.6 = (f32[768]{0:T(1024)S(1)}, f32[768]{0:T(1024)}, u32[]{:S(2)}) copy-start(f32[768]{0:T(1024)} %param.9) | copy-start | bytes 9220
  43.3 1.6 %collective-permute-start.11 = (bf16[1,192,768]{2,1,0:T(8,128)(2,1)S(1)}, bf16[1,192,768]{2,1,0:T(8,128)(2,1)S(1)}, u32[]{:S(2)}, u32[]{:S(2)}) collective-permute-start(bf16[1,192,768]{2,1,0:T(8,128)(2,1)S(1)} %get-tuple-element.62), channel_id=1, source_target_pairs={{0,1},{1,0},{2,3},{3,2},{4,5},{5,4},{6,7},{7,6},{8,9},{9,8},{10,11... | collective-permute-start | bytes 884744 | tf_op jit(solution)/shard_map/ppermute | solution.py:17
  57.8 1.0 %copy-start.3 = (bf16[1,256,768]{2,1,0:T(8,128)(2,1)S(1)}, bf16[1,256,768]{2,1,0:T(8,128)(2,1)}, u32[]{:S(2)}) copy-start(bf16[1,256,768]{2,1,0:T(8,128)(2,1)} %tokens_ref.5) | copy-start | bytes 1179652
  57.8 1.0 %copy-start.5 = (s32[4]{0:T(128)S(1)}, s32[4]{0:T(128)}, u32[]{:S(2)}) copy-start(s32[4]{0:T(128)} %starts_ref.3) | copy-start | bytes 52
  57.8 5.2 %collective-permute-start.15 = (bf16[16,72,768]{2,1,0:T(8,128)(2,1)S(1)}, bf16[16,72,768]{2,1,0:T(8,128)(2,1)S(1)}, u32[]{:S(2)}, u32[]{:S(2)}) collective-permute-start(bf16[16,72,768]{2,1,0:T(8,128)(2,1)S(1)} %get-tuple-element.76.refs_0_), channel_id=1, source_target_pairs={{0,1},{1,0},{2,3},{3,2},{4,5},{5,4},{6,7},{7,6},{8,9},{9,8},{10,11... | collective-permute-start | bytes 5308424 | tf_op jit(solution)/shard_map/ppermute | solution.py:17
  58.0 4.9 %collective-permute-start.16 = (bf16[16,24,1152]{2,1,0:T(8,128)(2,1)S(1)}, bf16[16,24,1152]{2,1,0:T(8,128)(2,1)S(1)}, u32[]{:S(2)}, u32[]{:S(2)}) collective-permute-start(bf16[16,24,1152]{2,1,0:T(8,128)(2,1)S(1)} %shard_map.112.refs_0_), channel_id=1, source_target_pairs={{0,1},{1,0},{2,3},{3,2},{4,5},{5,4},{6,7},{7,6},{8,9},{9,8},{10,11... | collective-permute-start | bytes 2654216 | tf_op jit(solution)/shard_map/ppermute | solution.py:17
  63.3 2.0 %copy-start.1 = (bf16[1,256,768]{2,1,0:T(8,128)(2,1)S(1)}, bf16[1,256,768]{2,1,0:T(8,128)(2,1)}, u32[]{:S(2)}) copy-start(bf16[1,256,768]{2,1,0:T(8,128)(2,1)} %cotangent_ref.5) | copy-start | bytes 1179652
  67.4 2.6 %collective-permute-start.18 = (bf16[4,2,2,40,768]{4,3,2,1,0:T(8,128)(2,1)S(1)}, bf16[4,2,2,40,768]{4,3,2,1,0:T(8,128)(2,1)S(1)}, u32[]{:S(2)}, u32[]{:S(2)}) collective-permute-start(bf16[4,2,2,40,768]{4,3,2,1,0:T(8,128)(2,1)S(1)} %get-tuple-element.88), channel_id=1, source_target_pairs={{0,1},{1,0},{2,3},{3,2},{4,5},{5,4},{6,7},{7,6},{8,9},{9,8},{10,11... | collective-permute-start | bytes 2949128 | tf_op jit(solution)/shard_map/ppermute | solution.py:17
  67.6 6.2 %collective-permute-start.17 = (bf16[16,40,768]{2,1,0:T(8,128)(2,1)S(1)}, bf16[16,40,768]{2,1,0:T(8,128)(2,1)S(1)}, u32[]{:S(2)}, u32[]{:S(2)}) collective-permute-start(bf16[16,40,768]{2,1,0:T(8,128)(2,1)S(1)} %get-tuple-element.80.own_ref), channel_id=1, source_target_pairs={{0,1},{1,0},{2,3},{3,2},{4,5},{5,4},{6,7},{7,6},{8,9},{9,8},{10,11... | collective-permute-start | bytes 2949128 | tf_op jit(solution)/shard_map/ppermute | solution.py:17
  70.2 17.8 %collective-permute-start.19 = (bf16[4,40,768]{2,1,0:T(8,128)(2,1)S(1)}, bf16[4,40,768]{2,1,0:T(8,128)(2,1)S(1)}, u32[]{:S(2)}, u32[]{:S(2)}) collective-permute-start(bf16[4,40,768]{2,1,0:T(8,128)(2,1)S(1)} %get-tuple-element.91), channel_id=1, source_target_pairs={{0,2},{1,3},{2,0},{3,1},{4,6},{5,7},{6,4},{7,5},{8,10},{9,11},{10,... | collective-permute-start | bytes 737288 | tf_op jit(solution)/shard_map/ppermute | solution.py:17
  70.6 17.4 %collective-permute-start.20 = (bf16[4,40,768]{2,1,0:T(8,128)(2,1)S(1)}, bf16[4,40,768]{2,1,0:T(8,128)(2,1)S(1)}, u32[]{:S(2)}, u32[]{:S(2)}) collective-permute-start(bf16[4,40,768]{2,1,0:T(8,128)(2,1)S(1)} %get-tuple-element.92), channel_id=1, source_target_pairs={{0,4},{1,5},{2,6},{3,7},{4,0},{5,1},{6,2},{7,3},{8,12},{9,13},{10,... | collective-permute-start | bytes 737288 | tf_op jit(solution)/shard_map/ppermute | solution.py:17
  72.4 15.6 %collective-permute-start.21 = (bf16[4,40,768]{2,1,0:T(8,128)(2,1)S(1)}, bf16[4,40,768]{2,1,0:T(8,128)(2,1)S(1)}, u32[]{:S(2)}, u32[]{:S(2)}) collective-permute-start(bf16[4,40,768]{2,1,0:T(8,128)(2,1)S(1)} %get-tuple-element.93), channel_id=1, source_target_pairs={{0,6},{1,7},{2,4},{3,5},{4,2},{5,3},{6,0},{7,1},{8,14},{9,15},{10,... | collective-permute-start | bytes 737288 | tf_op jit(solution)/shard_map/ppermute | solution.py:17
  79.6 1.2 %collective-permute-start.22 = (f32[1,768]{1,0:T(1,128)S(1)}, f32[1,768]{1,0:T(1,128)S(1)}, u32[]{:S(2)}, u32[]{:S(2)}) collective-permute-start(f32[1,768]{1,0:T(1,128)S(1)} %get-tuple-element.94), channel_id=1, source_target_pairs={{0,1},{1,0},{2,3},{3,2},{4,5},{5,4},{6,7},{7,6},{8,9},{9,8},{10,11... | collective-permute-start | bytes 9224 | tf_op jit(solution)/shard_map/ppermute | solution.py:17
  80.8 3.6 %collective-permute-start.23 = (f32[1,768]{1,0:T(1,128)S(1)}, f32[1,768]{1,0:T(1,128)S(1)}, u32[]{:S(2)}, u32[]{:S(2)}) collective-permute-start(f32[1,768]{1,0:T(1,128)S(1)} %add.9), channel_id=1, source_target_pairs={{0,2},{1,3},{2,0},{3,1},{4,6},{5,7},{6,4},{7,5},{8,10},{9,11},{10,... | collective-permute-start | bytes 9224 | tf_op jit(solution)/shard_map/ppermute | solution.py:17
  84.4 3.6 %collective-permute-start.24 = (f32[1,768]{1,0:T(1,128)S(1)}, f32[1,768]{1,0:T(1,128)S(1)}, u32[]{:S(2)}, u32[]{:S(2)}) collective-permute-start(f32[1,768]{1,0:T(1,128)S(1)} %add.10), channel_id=1, source_target_pairs={{0,4},{1,5},{2,6},{3,7},{4,0},{5,1},{6,2},{7,3},{8,12},{9,13},{10,... | collective-permute-start | bytes 9224 | tf_op jit(solution)/shard_map/ppermute | solution.py:17
  88.1 4.9 %collective-permute-start.25 = (bf16[40,768]{1,0:T(8,128)(2,1)S(1)}, bf16[40,768]{1,0:T(8,128)(2,1)S(1)}, u32[]{:S(2)}, u32[]{:S(2)}) collective-permute-start(bf16[40,768]{1,0:T(8,128)(2,1)S(1)} %get-tuple-element.97), channel_id=1, source_target_pairs={{0,8},{1,9},{2,10},{3,11},{4,12},{5,13},{6,14},{7,15},{8,0},{9,1},... | collective-permute-start | bytes 184328 | tf_op jit(solution)/shard_map/ppermute | solution.py:17
  89.9 5.9 %collective-permute-start.26 = (bf16[40,768]{1,0:T(8,128)(2,1)S(1)}, bf16[40,768]{1,0:T(8,128)(2,1)S(1)}, u32[]{:S(2)}, u32[]{:S(2)}) collective-permute-start(bf16[40,768]{1,0:T(8,128)(2,1)S(1)} %get-tuple-element.98), channel_id=1, source_target_pairs={{0,16},{1,17},{2,18},{3,19},{4,20},{5,21},{6,22},{7,23},{8,24},{9,... | collective-permute-start | bytes 184328 | tf_op jit(solution)/shard_map/ppermute | solution.py:17
  91.5 6.0 %collective-permute-start.27 = (bf16[40,768]{1,0:T(8,128)(2,1)S(1)}, bf16[40,768]{1,0:T(8,128)(2,1)S(1)}, u32[]{:S(2)}, u32[]{:S(2)}) collective-permute-start(bf16[40,768]{1,0:T(8,128)(2,1)S(1)} %get-tuple-element.99), channel_id=1, source_target_pairs={{0,24},{1,25},{2,26},{3,27},{4,28},{5,29},{6,30},{7,31},{8,16},{9,... | collective-permute-start | bytes 184328 | tf_op jit(solution)/shard_map/ppermute | solution.py:17

commit v3 on v2

--- a/solution.py
+++ b/solution.py
@@ -27,6 +27,7 @@
 
 
 VMEM = pl.BlockSpec(memory_space=pltpu.VMEM)
+FIRST, SECOND, THIRD, LAST = 5000000000, 2000000000, 4500000000, 40000000000
 PARAMS = pltpu.CompilerParams(vmem_limit_bytes=20 * 1024 * 1024)
 
 SMEM = pl.BlockSpec(memory_space=pltpu.SMEM)
@@ -41,7 +42,7 @@
         out_specs=[VMEM] * len(shapes),
         scratch_shapes=list(scratch),
         compiler_params=PARAMS,
-        cost_estimate=pl.CostEstimate(flops=1, bytes_accessed=cost, transcendentals=0),
+        cost_estimate=pl.CostEstimate(flops=cost, bytes_accessed=1, transcendentals=0),
     )(*args)
 
 
@@ -109,44 +110,31 @@
     )
 
 
-def convolve(taps, before, tokens, after_, conv):
+def convolve(taps, tokens, conv):
     seqs, bins, width = tokens.shape
     reach = DILATION_BINS
-    rows = bins + 2 * reach
-
-    def kernel(taps_ref, before_ref, tokens_ref, after_ref, conv_ref, mixed_ref):
+
+    def kernel(taps_ref, tokens_ref, conv_ref, mixed_ref):
         for s in range(seqs):
             for at in column_blocks(width):
-                total = jnp.dot(
-                    taps_ref[s], conv_ref[:, at], preferred_element_type=jnp.float32
+                mixed_ref[s, :, at] = tokens_ref[s, :, at].astype(jnp.float32) + jnp.dot(
+                    taps_ref[s, reach : reach + bins],
+                    conv_ref[:, at],
+                    preferred_element_type=jnp.float32,
                 )
-                mixed_ref[s, :reach, at] = total[:reach] + before_ref[s, reach : 2 * reach, at].astype(jnp.float32)
-                mixed_ref[s, reach : reach + bins, at] = total[reach : reach + bins] + tokens_ref[
-                    s, :, at
-                ].astype(jnp.float32)
-                mixed_ref[s, reach + bins :, at] = total[reach + bins :] + after_ref[
-                    s, :reach, at
-                ].astype(jnp.float32)
-
-    return call(
-        kernel,
-        [((seqs, rows, width), jnp.float32)],
-        taps,
-        before,
-        tokens,
-        after_,
-        conv.reshape(-1, width),
+
+    return call(
+        kernel, [((seqs, bins, width), jnp.float32)], taps, tokens, conv.reshape(-1, width)
     )[0]
 
 
 def expand(mixed, up, cotangent):
     seqs, bins, width = cotangent.shape
     hidden_width = up.shape[1]
-    reach = DILATION_BINS
 
     def kernel(mixed_ref, up_ref, cotangent_ref, pre_ref, share_ref, hidden_ref, total_ref):
         for s in range(seqs):
-            low = mixed_ref[s, reach : reach + bins].astype(jnp.bfloat16)
+            low = mixed_ref[s].astype(jnp.bfloat16)
             for at in column_blocks(hidden_width):
                 pre = jnp.dot(low, up_ref[:, at], preferred_element_type=jnp.float32)
                 share = 0.5 * (1.0 + lax.erf(pre * root_half))
@@ -179,21 +167,26 @@
     )
 
 
-def slopes(mixed, up, pre, share):
+def slopes(taps, before, after_, conv, up, pre, share):
     seqs, bins, hidden_width = pre.shape
+    width = before.shape[2]
     reach = DILATION_BINS
     rows = bins + 2 * reach
 
     def bell(value):
         return value * jnp.exp(-0.5 * value * value) * inv_root_two_pi
 
-    def kernel(mixed_ref, up_ref, pre_ref, share_ref, slope_ref):
+    def kernel(taps_ref, before_ref, after_ref, conv_ref, up_ref, pre_ref, share_ref, slope_ref, mixed):
         for s in range(seqs):
-            edges = jnp.concatenate(
-                [mixed_ref[s, :reach], mixed_ref[s, reach + bins :]], axis=0
-            ).astype(jnp.bfloat16)
+            edges = jnp.concatenate([taps_ref[s, :reach], taps_ref[s, reach + bins :]], axis=0)
+            tokens = jnp.concatenate([before_ref[s, reach : 2 * reach], after_ref[s, :reach]], axis=0)
+            for at in column_blocks(width):
+                mixed[:, at] = (
+                    tokens[:, at].astype(jnp.float32)
+                    + jnp.dot(edges, conv_ref[:, at], preferred_element_type=jnp.float32)
+                ).astype(jnp.bfloat16)
             for at in column_blocks(hidden_width):
-                edge = jnp.dot(edges, up_ref[:, at], preferred_element_type=jnp.float32)
+                edge = jnp.dot(mixed[...], up_ref[:, at], preferred_element_type=jnp.float32)
                 slope = 0.5 * (1.0 + lax.erf(edge * root_half)) + bell(edge)
                 slope_ref[s, :reach, at] = slope[:reach]
                 slope_ref[s, reach : reach + bins, at] = share_ref[s, :, at] + bell(pre_ref[s, :, at])
@@ -202,14 +195,18 @@
     return call(
         kernel,
         [((seqs, rows, hidden_width), jnp.float32)],
-        mixed,
+        taps,
+        before,
+        after_,
+        conv.reshape(-1, width),
         up,
         pre,
         share,
+        scratch=[pltpu.VMEM((2 * reach, width), jnp.bfloat16)],
     )[0]
 
 
-def backward(before, cotangent, after_, slope, down, up, conv, scaled, inverse, gain, starts):
+def backward(before, cotangent, after_, slope, down, up, conv, scaled, starts):
     seqs, bins, width = cotangent.shape
     hidden_width = up.shape[1]
     reach = DILATION_BINS
@@ -226,10 +223,9 @@
         up_ref,
         conv_ref,
         scaled_ref,
-        inverse_ref,
-        gain_ref,
         starts_ref,
-        grad_ref,
+        mixed_grad_ref,
+        normed_grad_ref,
         gain_term_ref,
         pre_grad,
         mixed_grad,
@@ -252,27 +248,27 @@
             following = jnp.where(right, mixed_grad[2 * reach :, :], 0.0).astype(jnp.bfloat16)
             center = mixed_grad[reach : reach + bins, :].astype(jnp.bfloat16)
             preceding = jnp.where(left, mixed_grad[:bins, :], 0.0).astype(jnp.bfloat16)
-            normed_grad = (
-                lax.dot_general(following, conv_ref[0], by_rows, preferred_element_type=jnp.float32)
-                + lax.dot_general(center, conv_ref[1], by_rows, preferred_element_type=jnp.float32)
-                + lax.dot_general(preceding, conv_ref[2], by_rows, preferred_element_type=jnp.float32)
-            )
-            scaled = scaled_ref[s]
-            term = jnp.sum(normed_grad * scaled, axis=0, keepdims=True)
-            if s == 0:
-                gain_term_ref[...] = term
-            else:
-                gain_term_ref[...] += term
-            scaled_grad = normed_grad * gain_ref[...]
-            inner = jnp.mean(scaled_grad * scaled, axis=1, keepdims=True)
-            grad_ref[s] = (
-                mixed_grad[reach : reach + bins, :]
-                + inverse_ref[s] * (scaled_grad - scaled * inner)
-            ).astype(jnp.bfloat16)
-
-    return call(
-        kernel,
-        [((seqs, bins, width), jnp.bfloat16), ((1, width), jnp.float32)],
+            mixed_grad_ref[s] = mixed_grad[reach : reach + bins, :]
+            for at in column_blocks(width):
+                normed_grad = (
+                    lax.dot_general(following, conv_ref[0, at, :], by_rows, preferred_element_type=jnp.float32)
+                    + lax.dot_general(center, conv_ref[1, at, :], by_rows, preferred_element_type=jnp.float32)
+                    + lax.dot_general(preceding, conv_ref[2, at, :], by_rows, preferred_element_type=jnp.float32)
+                )
+                normed_grad_ref[s, :, at] = normed_grad
+                term = jnp.sum(normed_grad * scaled_ref[s, :, at], axis=0, keepdims=True)
+                if s == 0:
+                    gain_term_ref[:, at] = term
+                else:
+                    gain_term_ref[:, at] += term
+
+    return call(
+        kernel,
+        [
+            ((seqs, bins, width), jnp.float32),
+            ((seqs, bins, width), jnp.float32),
+            ((1, width), jnp.float32),
+        ],
         before,
         cotangent,
         after_,
@@ -281,10 +277,8 @@
         up,
         conv,
         scaled,
-        inverse,
-        gain,
         starts,
-        smem=(10,),
+        smem=(8,),
         scratch=[
             pltpu.VMEM((rows, hidden_width), jnp.bfloat16),
             pltpu.VMEM((rows, width), jnp.float32),
@@ -292,57 +286,93 @@
     )
 
 
-def project(mixed, hidden, down):
+def finish_rows(mixed, hidden, down, mixed_grad, normed_grad, scaled, inverse, gain):
     seqs, bins, _ = hidden.shape
     width = down.shape[1]
-    reach = DILATION_BINS
-
-    def kernel(mixed_ref, hidden_ref, down_ref, out_ref):
+
+    def kernel(
+        mixed_ref,
+        hidden_ref,
+        down_ref,
+        mixed_grad_ref,
+        normed_grad_ref,
+        scaled_ref,
+        inverse_ref,
+        gain_ref,
+        out_ref,
+        grad_ref,
+    ):
         for s in range(seqs):
+            scaled = scaled_ref[s]
+            scaled_grad = normed_grad_ref[s] * gain_ref[...]
+            inner = jnp.mean(scaled_grad * scaled, axis=1, keepdims=True)
+            grad_ref[s] = (
+                mixed_grad_ref[s] + inverse_ref[s] * (scaled_grad - scaled * inner)
+            ).astype(jnp.bfloat16)
             for at in column_blocks(width):
                 out_ref[s, :, at] = (
-                    mixed_ref[s, reach : reach + bins, at]
+                    mixed_ref[s, :, at]
                     + jnp.dot(hidden_ref[s], down_ref[:, at], preferred_element_type=jnp.float32)
                 ).astype(jnp.bfloat16)
 
     return call(
         kernel,
-        [((seqs, bins, width), jnp.bfloat16)],
+        [((seqs, bins, width), jnp.bfloat16)] * 2,
         mixed,
         hidden,
         down,
-    )[0]
-
-
-def stack(pieces):
+        mixed_grad,
+        normed_grad,
+        scaled,
+        inverse,
+        gain,
+    )
+
+
+def stack(pieces, cost=1):
     def kernel(*refs):
         for i in range(len(pieces)):
             refs[-1][i] = refs[i][...]
 
-    return call(kernel, [((len(pieces),) + pieces[0].shape, pieces[0].dtype)], *pieces)[0]
-
-
-def join(*pieces):
+    shape = (len(pieces),) + pieces[0].shape
+    return call(kernel, [(shape, pieces[0].dtype)], *pieces, cost=cost)[0]
+
+
+def join(*pieces, cost=1):
     ends = [sum(piece.shape[0] for piece in pieces[: i + 1]) for i in range(len(pieces))]
 
     def kernel(*refs):
         for ref, end in zip(refs[:-1], ends):
             refs[-1][end - ref.shape[0] : end] = ref[...]
 
-    return call(kernel, [((ends[-1],) + pieces[0].shape[1:], pieces[0].dtype)], *pieces)[0]
-
-
-def join_rows(pieces, rows):
-    ends = [sum(piece.shape[0] for piece in pieces[: i + 1]) for i in range(len(pieces))]
-    held, width = pieces[0].shape[1:]
+    shape = (ends[-1],) + pieces[0].shape[1:]
+    return call(kernel, [(shape, pieces[0].dtype)], *pieces, cost=cost)[0]
+
+
+def join_rows(pieces, rows, cost=1):
+    ends = [sum(stop - start for _, start, stop in pieces[: i + 1]) for i in range(len(pieces))]
+    held, width = pieces[0][0].shape[1:]
 
     def kernel(*refs):
-        for ref, end in zip(refs[:-2], ends):
-            refs[-2][end - ref.shape[0] : end] = ref[:, :rows]
-            refs[-1][end - ref.shape[0] : end] = ref[:, rows:]
+        for ref, (_, start, stop), end in zip(refs[:-2], pieces, ends):
+            at = slice(end - (stop - start), end)
+            refs[-2][at] = ref[start:stop, :rows]
+            refs[-1][at] = ref[start:stop, rows:]
 
     shapes = [(ends[-1], rows, width), (ends[-1], held - rows, width)]
-    return call(kernel, [(shape, pieces[0].dtype) for shape in shapes], *pieces)
+    arrays = [piece[0] for piece in pieces]
+    return call(kernel, [(shape, arrays[0].dtype) for shape in shapes], *arrays, cost=cost)
+
+
+def join_parts(*pieces):
+    ends = [sum(stop - start for _, start, stop in pieces[: i + 1]) for i in range(len(pieces))]
+
+    def kernel(*refs):
+        for ref, (_, start, stop), end in zip(refs[:-1], pieces, ends):
+            refs[-1][end - (stop - start) : end] = ref[start:stop]
+
+    shape = (ends[-1],) + pieces[0][0].shape[1:]
+    return call(kernel, [(shape, pieces[0][0].dtype)], *[p[0] for p in pieces])[0]
 
 
 def neighbours(tokens, cotangent):
@@ -396,8 +426,10 @@
         slot, first, count = 0, 0, 2
         while first < squares:
             for corner in range(4):
+                last = corner == 3 and first + count == squares
                 for k in range(count):
-                    yield slot, square_of(z, first + k, squares), corner // 2, corner % 2
+                    source = square_of(z, first + k, squares)
+                    yield int(last), k if last else slot, source, corner // 2, corner % 2
                     slot += 1
             first, count = first + count, first + count
 
@@ -413,9 +445,9 @@
         out = refs[-1]
         core, x, y, z = place()
         for dc in range(2):
-            for slot, source, dy, dx in line_slots(squares)(z):
+            for last, slot, source, dy, dx in line_slots(squares)(z):
                 for t in range(taps):
-                    part = refs[dc][slot, t * rows : (t + 1) * rows]
+                    part = refs[2 * last + dc][slot, t * rows : (t + 1) * rows]
                     out[t, source, y ^ dy, x ^ dx, core ^ dc] = part
 
     out = call(kernel, [((taps, squares, 2, 2, 2, rows, width), pieces[0].dtype)], *pieces)[0]
@@ -426,12 +458,13 @@
     squares = lax.axis_size("ctx") // 8
     width = pieces[0].shape[-1]
 
-    def kernel(own_ref, other_ref, out, wide):
+    def kernel(*refs):
+        out, wide = refs[-2:]
         core, x, y, z = place()
         is_first = core == 0
-        for slot, source, dy, dx in line_slots(squares)(z):
-            mine = own_ref[slot, :rows].astype(jnp.float32)
-            theirs = other_ref[slot, :rows].astype(jnp.float32)
+        for last, slot, source, dy, dx in line_slots(squares)(z):
+            mine = refs[2 * last][slot, :rows].astype(jnp.float32)
+            theirs = refs[2 * last + 1][slot, :rows].astype(jnp.float32)
             wide[:rows] = jnp.where(is_first, mine, theirs)
             wide[rows:] = jnp.where(is_first, theirs, mine)
             out[source, y ^ dy, x ^ dx] = wide[...].astype(jnp.bfloat16)
@@ -513,28 +546,45 @@
     rows = conv.shape[0] * conv.shape[1]
     filler = jnp.zeros((-(rows + down.shape[0]) % 16, width), conv.dtype)
     both = jnp.concatenate([conv.reshape(rows, width), down, filler])
-    inner, outer = neighbours(tokens, cotangent)
     new = swap(both, first)
     up_new = [swap(up, mask) for mask in (2, 4, 6)]
+    inner, outer = neighbours(*all_after((tokens, cotangent), (up_new[0],)))
     (up,) = load(up)
-    new, outer, both, *up_new = all_after((new, outer, both, *up_new), ())
-    part = held = stack([both, new])
-    up_held = stack([up] + up_new)
-    parts = []
+    new, both, *up_new = all_after((new, both, *up_new), ())
+    part = held = stack([both, new], cost=FIRST)
+    up_held = stack([up] + up_new, cost=SECOND)
+    pieces, late = [], None
     for mask, next_mask in zip([first] + rest, rest + [None]):
-        around = [swap(part, 2), swap(part, 4), swap(part, 6)]
-        received = swap(up_held, mask)
+        count = part.shape[0]
+        if late is None:
+            to_x, to_y = part, part
+        else:
+            old, old_x, old_y = late
+            to_x = join_parts((part, 0, count), (old_y, old // 2, old))
+            to_y = join_parts((part, 0, count), (old_x, 0, old // 2))
+        by_x, by_y, received = swap(to_x, 2), swap(to_y, 4), swap(up_held, mask)
         other = swap(inner, 1) if next_mask is None else swap(held, next_mask)
-        part, held, up_held, received, other, *around = all_after(
-            (part, held, up_held, received, other, *around), ()
-        )
         up_held = join(up_held, received)
-        parts += [part, *around]
+        if next_mask is None:
+            outer = stack([outer], cost=THIRD)
+        part, held, up_held, by_x, by_y, other, outer = all_after(
+            (part, held, up_held, by_x, by_y, other, outer), ()
+        ) if next_mask is None else (*all_after((part, held, up_held, by_x, by_y, other), ()), outer)
+        if late is not None:
+            pieces += [(by_y, count, count + old // 2), (by_x, count, count + old - old // 2)]
+        pieces += [(part, 0, count), (by_x, 0, count), (by_y, 0, count)]
+        late = (count, by_x, by_y)
         if next_mask is not None:
             held, part = join(held, other), other
-    all_conv, all_down = join_rows(parts, rows)
-    extra = prepared(tokens, cotangent, *in_order(other, outer))
-    return [(piece, swap(piece, 1)) for piece in (all_conv, up_held, all_down)], extra
+    half = count // 2
+    far_first = swap(join_parts((by_x, 0, half)), 4)
+    far_second = swap(join_parts((by_y, half, count)), 2)
+    extra = prepared(tokens, cotangent, *in_order(other, outer[0]))
+    far_first = after(far_first, extra[4])
+    most = join_rows(pieces, rows)
+    last = join_rows([(far_first, 0, half), (far_second, 0, count - half)], rows, cost=LAST)
+    pieces = [(most[0], last[0]), (up_held,), (most[1], last[1])]
+    return [[both for p in piece for both in (p, swap(p, 1))] for piece in pieces], extra
 
 
 def core_rows(rows):
@@ -645,28 +695,21 @@
     )
     tokens, cotangent, before, after_, taps, scaled, inverse = extra
     conv = assemble_conv(conv_pieces, conv_weight.shape[0])
-    mixed = convolve(taps, before, tokens, after_, conv)
+    mixed = convolve(taps, tokens, conv)
     up = assemble_up(up_pieces, *up_weight.shape)
+    mixed = after(mixed, *down_pieces)
     pre, share, hidden, total = expand(mixed, up, cotangent)
-    slope = slopes(mixed, up, pre, share)
+    slope = slopes(taps, before, after_, conv, up, pre, share)
     keep, send = relative_blocks(total)
     down = assemble_down(down_pieces, down_weight.shape[0])
-    own_line, *others = chip_sums(keep, after(swap(send, 1), slope))
+    own_line, *others = chip_sums(keep, after(swap(send, 1), slope, down))
     received = [swap(v, mask) for v, mask in zip(others, (2, 4, 6))]
-    input_grad, gain_term = backward(
-        before,
-        cotangent,
-        after_,
-        slope,
-        down,
-        up,
-        conv,
-        scaled,
-        inverse,
-        gain,
-        contig_first_bins,
-    )
-    output = project(mixed, hidden, down)
+    mixed_grad, normed_grad, gain_term = backward(
+        before, cotangent, after_, slope, down, up, conv, scaled, contig_first_bins
+    )
+    output, input_grad = finish_rows(
+        mixed, hidden, down, mixed_grad, normed_grad, scaled, inverse, gain
+    )
     for mask in (1, 2, 4):
         if mask == 4:
             gain_term = after(gain_term, output)

time: 98.5 us -> 87.6 us (0.89)
  waiting for transfers between devices: 48.1 us -> 35.8 us
  starting transfers between devices: 30.3 us -> 33.6 us
  local copies, waits for them, and re-layouts: 2.3 us -> 0.95 us
    ppermute x27 -> x29, waiting for transfers between devices: 48.1 us -> 35.8 us  [swap(): return lax.ppermute(value, 'ctx', [(i, i ^ mask) for i in range(devices)])]
    ppermute x27 -> x29, starting transfers between devices: 29.6 us -> 32.9 us  [swap(): return lax.ppermute(value, 'ctx', [(i, i ^ mask) for i in range(devices)])]
    unnamed x14 -> x10, local copies, waits for them, and re-layouts: 2.22 us -> 0.87 us
    pallas_call x20 -> x26, Pallas kernels: 15.5 us -> 15 us  [call(): pl.pallas_call(kernel, out_shape=shapes, in_specs=[SMEM if i in smem else...]
  transfers between devices with their start and end apart: 28 -> 30, of which waited for: 16 -> 14; matrix products, arithmetic and copies ran while one was open for 1% -> 0% of each run, Pallas kernels for 10% -> 14%
where the time goes in v3:
time: 87.6 us; the launch traced here: 87.4 us
  waiting for transfers between devices  35.8 us (41%)
  starting transfers between devices  33.6 us (38%)
  Pallas kernels  15 us (17%)
  other arithmetic  1.04 us (1%)
  between operations  0.97 us (1%)
  local copies, waits for them, and re-layouts  0.95 us (1%)
    ppermute x29, waiting for transfers between devices, swap(): return lax.ppermute(value, 'ctx', [(i, i ^ mask) for i in range(devices)])  35.8 us
    ppermute x29, starting transfers between devices, swap(): return lax.ppermute(value, 'ctx', [(i, i ^ mask) for i in range(devices)])  32.9 us
    pallas_call x26, Pallas kernels, call(): pl.pallas_call(kernel, out_shape=shapes, in_specs=[SMEM if i in smem else...  15 us
  transfers between devices with their start and end apart: 30, of which 14 were waited for; matrix products, arithmetic and copies ran while one was open for 0% of the time, Pallas kernels for 14%

profile of v3, /device:TPU:0, one launch (start us, length us, event | category | flops | bytes accessed | tf_op | source)
XLA Modules:
  0.0 87.4 jit_solution(17575196634411138377)
XLA Ops:
  0.7 1.0 %maximum_maximum_fusion.refs_0_ = bf16[112,768]{1,0:T(8,128)(2,1)S(1)} fusion(bf16[36,768]{1,0:T(8,128)(2,1)} %param.12, bf16[72,768]{1,0:T(8,128)(2,1)} %bitcast.17, bf16[112]{0:T(256)(128)(2,1)S(1)} %pad.2.clone), kind=kLoop, calls=%fused_computation | loop fusion | flops 516096 | bytes 338144 | tf_op jit(solution)/shard_map/concatenate | solution.py:548
  1.8 4.1 %collective-permute-start = (bf16[112,768]{1,0:T(8,128)(2,1)S(1)}, bf16[112,768]{1,0:T(8,128)(2,1)S(1)}, u32[]{:S(2)}, u32[]{:S(2)}) collective-permute-start(bf16[112,768]{1,0:T(8,128)(2,1)S(1)} %maximum_maximum_fusion.refs_0_), channel_id=1, source_target_pairs={{0,16},{1,17},{2,18},{3,19},{4,20},{5,21},{6,22},{7,23},{8,24},{9,... | collective-permute-start | bytes 516104 | tf_op jit(solution)/shard_map/ppermute | solution.py:17
  5.9 1.5 %collective-permute-start.2 = (bf16[24,1152]{1,0:T(8,128)(2,1)}, bf16[24,1152]{1,0:T(8,128)(2,1)S(1)}, u32[]{:S(2)}, u32[]{:S(2)}) collective-permute-start(bf16[24,1152]{1,0:T(8,128)(2,1)} %refs_0_.1), channel_id=1, source_target_pairs={{0,4},{1,5},{2,6},{3,7},{4,0},{5,1},{6,2},{7,3},{8,12},{9,13},{10,... | collective-permute-start | bytes 165896 | tf_op jit(solution)/shard_map/ppermute | solution.py:17
  7.4 1.5 %collective-permute-start.1 = (bf16[24,1152]{1,0:T(8,128)(2,1)}, bf16[24,1152]{1,0:T(8,128)(2,1)S(1)}, u32[]{:S(2)}, u32[]{:S(2)}) collective-permute-start(bf16[24,1152]{1,0:T(8,128)(2,1)} %refs_0_.1), channel_id=1, source_target_pairs={{0,2},{1,3},{2,0},{3,1},{4,6},{5,7},{6,4},{7,5},{8,10},{9,11},{10,... | collective-permute-start | bytes 165896 | tf_op jit(solution)/shard_map/ppermute | solution.py:17
  8.9 0.5 collective-permute-start.3
  9.3 0.8 copy-done.2
  10.3 1.5 %collective-permute-done.1.refs_1_ = bf16[24,1152]{1,0:T(8,128)(2,1)S(1)} collective-permute-done((bf16[24,1152]{1,0:T(8,128)(2,1)}, bf16[24,1152]{1,0:T(8,128)(2,1)S(1)}, u32[]{:S(2)}, u32[]{:S(2)}) %collective-permute-start.1) | collective-permute-done | bytes 55328 | tf_op jit(solution)/shard_map/ppermute | solution.py:17
  11.8 2.3 %collective-permute-done.3.refs_3_ = bf16[24,1152]{1,0:T(8,128)(2,1)S(1)} collective-permute-done((bf16[24,1152]{1,0:T(8,128)(2,1)}, bf16[24,1152]{1,0:T(8,128)(2,1)S(1)}, u32[]{:S(2)}, u32[]{:S(2)}) %collective-permute-start.3) | collective-permute-done | bytes 55328 | tf_op jit(solution)/shard_map/ppermute | solution.py:17
  14.2 1.6 %collective-permute-start.7 = (bf16[2,112,768]{2,1,0:T(8,128)(2,1)S(1)}, bf16[2,112,768]{2,1,0:T(8,128)(2,1)S(1)}, u32[]{:S(2)}, u32[]{:S(2)}) collective-permute-start(bf16[2,112,768]{2,1,0:T(8,128)(2,1)S(1)} %shard_map.102.refs_0_), channel_id=1, source_target_pairs={{0,8},{1,9},{2,10},{3,11},{4,12},{5,13},{6,14},{7,15},{8,0},{9,1},... | collective-permute-start | bytes 1032200 | tf_op jit(solution)/shard_map/ppermute | solution.py:17
  15.8 0.5 collective-permute-start.6
  16.3 1.4 %collective-permute-start.5 = (bf16[2,112,768]{2,1,0:T(8,128)(2,1)S(1)}, bf16[2,112,768]{2,1,0:T(8,128)(2,1)S(1)}, u32[]{:S(2)}, u32[]{:S(2)}) collective-permute-start(bf16[2,112,768]{2,1,0:T(8,128)(2,1)S(1)} %shard_map.102.refs_0_), channel_id=1, source_target_pairs={{0,2},{1,3},{2,0},{3,1},{4,6},{5,7},{6,4},{7,5},{8,10},{9,11},{10,... | collective-permute-start | bytes 1032200 | tf_op jit(solution)/shard_map/ppermute | solution.py:17
  17.8 3.4 %collective-permute-start.4 = (bf16[4,24,1152]{2,1,0:T(8,128)(2,1)S(1)}, bf16[4,24,1152]{2,1,0:T(8,128)(2,1)S(1)}, u32[]{:S(2)}, u32[]{:S(2)}) collective-permute-start(bf16[4,24,1152]{2,1,0:T(8,128)(2,1)S(1)} %shard_map.104.refs_0_), channel_id=1, source_target_pairs={{0,16},{1,17},{2,18},{3,19},{4,20},{5,21},{6,22},{7,23},{8,24},{9,... | collective-permute-start | bytes 663560 | tf_op jit(solution)/shard_map/ppermute | solution.py:17
  21.3 0.7 collective-permute-start.12
  22.0 8.9 %collective-permute-done.4.refs_1_ = bf16[4,24,1152]{2,1,0:T(8,128)(2,1)S(1)} collective-permute-done((bf16[4,24,1152]{2,1,0:T(8,128)(2,1)S(1)}, bf16[4,24,1152]{2,1,0:T(8,128)(2,1)S(1)}, u32[]{:S(2)}, u32[]{:S(2)}) %collective-permute-start.4) | collective-permute-done | bytes 221216 | tf_op jit(solution)/shard_map/ppermute | solution.py:17
  31.3 3.1 %collective-permute-start.8 = (bf16[8,24,1152]{2,1,0:T(8,128)(2,1)S(1)}, bf16[8,24,1152]{2,1,0:T(8,128)(2,1)S(1)}, u32[]{:S(2)}, u32[]{:S(2)}) collective-permute-start(bf16[8,24,1152]{2,1,0:T(8,128)(2,1)S(1)} %shard_map.105.refs_0_), channel_id=1, source_target_pairs={{0,8},{1,9},{2,10},{3,11},{4,12},{5,13},{6,14},{7,15},{8,0},{9,1},... | collective-permute-start | bytes 1327112 | tf_op jit(solution)/shard_map/ppermute | solution.py:17
  34.4 9.2 %collective-permute-done.8.refs_1_ = bf16[8,24,1152]{2,1,0:T(8,128)(2,1)S(1)} collective-permute-done((bf16[8,24,1152]{2,1,0:T(8,128)(2,1)S(1)}, bf16[8,24,1152]{2,1,0:T(8,128)(2,1)S(1)}, u32[]{:S(2)}, u32[]{:S(2)}) %collective-permute-start.8) | collective-permute-done | bytes 442400 | tf_op jit(solution)/shard_map/ppermute | solution.py:17
  43.8 0.6 collective-permute-start.14
  44.4 0.9 %collective-permute-start.15 = (bf16[1,112,768]{2,1,0:T(8,128)(2,1)S(1)}, bf16[1,112,768]{2,1,0:T(8,128)(2,1)S(1)}, u32[]{:S(2)}, u32[]{:S(2)}) collective-permute-start(bf16[1,112,768]{2,1,0:T(8,128)(2,1)S(1)} %shard_map.115), channel_id=1, source_target_pairs={{0,2},{1,3},{2,0},{3,1},{4,6},{5,7},{6,4},{7,5},{8,10},{9,11},{10,... | collective-permute-start | bytes 516104 | tf_op jit(solution)/shard_map/ppermute | solution.py:17
  45.6 0.5 collective-permute-start.19
  46.1 0.2 shard_map.111
  46.4 1.3 %shard_map.112 = (bf16[1,384,2304]{2,1,0:T(8,128)(2,1)S(1)}, f32[1,256,768]{2,1,0:T(8,128)S(1)}, f32[1,256,1]{2,1,0:T(8,128)S(1)}) custom-call(bf16[1,192,768]{2,1,0:T(8,128)(2,1)S(1)} %get-tuple-element.73.before_ref, bf16[1,256,768]{2,1,0:T(8,128)(2,1)S(1)} %copy-done, bf16[1,192,768]{2,1,0:T(8,128)(2,1)S(1)} %get-tuple-element.74.after_ref, ...), custom_call_target="tpu_custom_call" | custom-call | flops 1 | bytes 1 | tf_op jit(solution)/shard_map/pallas_call | solution.py:38
  47.6 1.6 %collective-permute-done.14.refs_0_ = bf16[1,112,768]{2,1,0:T(8,128)(2,1)S(1)} collective-permute-done((bf16[1,112,768]{2,1,0:T(8,128)(2,1)S(1)}, bf16[1,112,768]{2,1,0:T(8,128)(2,1)S(1)}, u32[]{:S(2)}, u32[]{:S(2)}) %collective-permute-start.14) | collective-permute-done | bytes 172064 | tf_op jit(solution)/shard_map/ppermute | solution.py:17
  49.3 0.6 collective-permute-done.15.refs_1_
  50.0 0.5 collective-permute-start.18
  50.6 1.1 %collective-permute-done.16.refs_3_ = bf16[2,72,768]{2,1,0:T(8,128)(2,1)S(1)} collective-permute-done((bf16[2,72,768]{2,1,0:T(8,128)(2,1)S(1)}, bf16[2,72,768]{2,1,0:T(8,128)(2,1)S(1)}, u32[]{:S(2)}, u32[]{:S(2)}) %collective-permute-start.16) | collective-permute-done | bytes 221216 | tf_op jit(solution)/shard_map/ppermute | solution.py:17
  51.7 0.3 shard_map.117
  52.0 1.4 %shard_map.118.mixed_ref = f32[1,256,768]{2,1,0:T(8,128)S(1)} custom-call(bf16[1,384,2304]{2,1,0:T(8,128)(2,1)S(1)} %get-tuple-element.75.taps_ref, bf16[1,256,768]{2,1,0:T(8,128)(2,1)S(1)} %copy-done, bf16[2304,768]{1,0:T(8,128)(2,1)S(1)} %bitcast.7), custom_call_target="tpu_custom_call" | custom-call | flops 1 | bytes 1 | tf_op jit(solution)/shard_map/pallas_call | solution.py:38
  53.4 1.8 %shard_map.120 = (f32[1,256,1152]{2,1,0:T(8,128)S(1)}, f32[1,256,1152]{2,1,0:T(8,128)S(1)}, bf16[1,256,1152]{2,1,0:T(8,128)(2,1)S(1)}, f32[1152,768]{1,0:T(8,128)S(1)}) custom-call(f32[1,256,768]{2,1,0:T(8,128)S(1)} %shard_map.118.mixed_ref, bf16[768,1152]{1,0:T(8,128)(2,1)S(1)} %bitcast.10, bf16[1,256,768]{2,1,0:T(8,128)(2,1)S(1)} %copy-done.1), custom_call_target="tpu_custom_call" | custom-call | flops 1 | bytes 1 | tf_op jit(solution)/shard_map/pallas_call | solution.py:38
  55.2 0.3 shard_map.125
  55.7 0.6 shard_map.121
  56.3 1.7 %shard_map.122.slope_ref = f32[1,384,1152]{2,1,0:T(8,128)S(1)} custom-call(bf16[1,384,2304]{2,1,0:T(8,128)(2,1)S(1)} %get-tuple-element.75.taps_ref, bf16[1,192,768]{2,1,0:T(8,128)(2,1)S(1)} %get-tuple-element.73.before_ref, bf16[1,192,768]{2,1,0:T(8,128)(2,1)S(1)} %get-tuple-element.74.after_ref, bf16[2304,768]{1,0:T(8,128)(2,1)S(1)} %bitcast.8, ...), custom_call_target="tpu_custom_call" | custom-call | flops 1 | bytes 1 | tf_op jit(solution)/shard_map/pallas_call | solution.py:38
  58.3 1.2 %collective-permute-start.21 = (bf16[4,40,768]{2,1,0:T(8,128)(2,1)S(1)}, bf16[4,40,768]{2,1,0:T(8,128)(2,1)S(1)}, u32[]{:S(2)}, u32[]{:S(2)}) collective-permute-start(bf16[4,40,768]{2,1,0:T(8,128)(2,1)S(1)} %get-tuple-element.101), channel_id=1, source_target_pairs={{0,2},{1,3},{2,0},{3,1},{4,6},{5,7},{6,4},{7,5},{8,10},{9,11},{10,... | collective-permute-start | bytes 737288 | tf_op jit(solution)/shard_map/ppermute | solution.py:17
  59.6 1.5 %collective-permute-start.22 = (bf16[4,40,768]{2,1,0:T(8,128)(2,1)S(1)}, bf16[4,40,768]{2,1,0:T(8,128)(2,1)S(1)}, u32[]{:S(2)}, u32[]{:S(2)}) collective-permute-start(bf16[4,40,768]{2,1,0:T(8,128)(2,1)S(1)} %get-tuple-element.102), channel_id=1, source_target_pairs={{0,4},{1,5},{2,6},{3,7},{4,0},{5,1},{6,2},{7,3},{8,12},{9,13},{10,... | collective-permute-start | bytes 737288 | tf_op jit(solution)/shard_map/ppermute | solution.py:17
  61.1 0.8 collective-permute-start.23
  61.9 3.9 %shard_map.123 = (f32[1,256,768]{2,1,0:T(8,128)S(1)}, f32[1,256,768]{2,1,0:T(8,128)S(1)}, f32[1,768]{1,0:T(1,128)S(1)}) custom-call(bf16[1,192,768]{2,1,0:T(8,128)(2,1)S(1)} %get-tuple-element.73.before_ref, bf16[1,256,768]{2,1,0:T(8,128)(2,1)S(1)} %copy-done.1, bf16[1,192,768]{2,1,0:T(8,128)(2,1)S(1)} %get-tuple-element.74.after_ref, ...), custom_call_target="tpu_custom_call" | custom-call | flops 1 | bytes 1 | tf_op jit(solution)/shard_map/pallas_call | solution.py:38
  65.9 1.1 %collective-permute-done.24 = f32[1,768]{1,0:T(1,128)S(1)} collective-permute-done((f32[1,768]{1,0:T(1,128)S(1)}, f32[1,768]{1,0:T(1,128)S(1)}, u32[]{:S(2)}, u32[]{:S(2)}) %collective-permute-start.24) | collective-permute-done | bytes 3104 | tf_op jit(solution)/shard_map/ppermute | solution.py:17
  67.1 1.2 %collective-permute-start.25 = (f32[1,768]{1,0:T(1,128)S(1)}, f32[1,768]{1,0:T(1,128)S(1)}, u32[]{:S(2)}, u32[]{:S(2)}) collective-permute-start(f32[1,768]{1,0:T(1,128)S(1)} %add.9), channel_id=1, source_target_pairs={{0,2},{1,3},{2,0},{3,1},{4,6},{5,7},{6,4},{7,5},{8,10},{9,11},{10,... | collective-permute-start | bytes 9224 | tf_op jit(solution)/shard_map/ppermute | solution.py:17
  68.2 1.8 %shard_map.124 = (bf16[1,256,768]{2,1,0:T(8,128)(2,1)}, bf16[1,256,768]{2,1,0:T(8,128)(2,1)}) custom-call(f32[1,256,768]{2,1,0:T(8,128)S(1)} %shard_map.118.mixed_ref, bf16[1,256,1152]{2,1,0:T(8,128)(2,1)S(1)} %get-tuple-element.87.hidden_ref, bf16[1152,768]{1,0:T(8,128)(2,1)S(1)} %bitcast.14, f32[1,256,768]{2,1,0:T(8,128)S(1)} %get-tuple-element.91.mixed_grad_ref, ...), custom_call_target="tpu_custom_call" | custom-call | flops 1 | bytes 1 | tf_op jit(solution)/shard_map/pallas_call | solution.py:38
  70.1 1.8 %collective-permute-done.25 = f32[1,768]{1,0:T(1,128)S(1)} collective-permute-done((f32[1,768]{1,0:T(1,128)S(1)}, f32[1,768]{1,0:T(1,128)S(1)}, u32[]{:S(2)}, u32[]{:S(2)}) %collective-permute-start.25) | collective-permute-done | bytes 3104 | tf_op jit(solution)/shard_map/ppermute | solution.py:17
  71.9 1.4 %collective-permute-start.26 = (f32[1,768]{1,0:T(1,128)S(1)}, f32[1,768]{1,0:T(1,128)S(1)}, u32[]{:S(2)}, u32[]{:S(2)}) collective-permute-start(f32[1,768]{1,0:T(1,128)S(1)} %add.10), channel_id=1, source_target_pairs={{0,4},{1,5},{2,6},{3,7},{4,0},{5,1},{6,2},{7,3},{8,12},{9,13},{10,... | collective-permute-start | bytes 9224 | tf_op jit(solution)/shard_map/ppermute | solution.py:17
  73.3 2.2 %collective-permute-done.26 = f32[1,768]{1,0:T(1,128)S(1)} collective-permute-done((f32[1,768]{1,0:T(1,128)S(1)}, f32[1,768]{1,0:T(1,128)S(1)}, u32[]{:S(2)}, u32[]{:S(2)}) %collective-permute-start.26) | collective-permute-done | bytes 3104 | tf_op jit(solution)/shard_map/ppermute | solution.py:17
  75.7 3.4 %collective-permute-start.27 = (bf16[40,768]{1,0:T(8,128)(2,1)S(1)}, bf16[40,768]{1,0:T(8,128)(2,1)S(1)}, u32[]{:S(2)}, u32[]{:S(2)}) collective-permute-start(bf16[40,768]{1,0:T(8,128)(2,1)S(1)} %get-tuple-element.107), channel_id=1, source_target_pairs={{0,8},{1,9},{2,10},{3,11},{4,12},{5,13},{6,14},{7,15},{8,0},{9,1},... | collective-permute-start | bytes 184328 | tf_op jit(solution)/shard_map/ppermute | solution.py:17
  79.1 1.6 %collective-permute-start.28 = (bf16[40,768]{1,0:T(8,128)(2,1)S(1)}, bf16[40,768]{1,0:T(8,128)(2,1)S(1)}, u32[]{:S(2)}, u32[]{:S(2)}) collective-permute-start(bf16[40,768]{1,0:T(8,128)(2,1)S(1)} %get-tuple-element.108), channel_id=1, source_target_pairs={{0,16},{1,17},{2,18},{3,19},{4,20},{5,21},{6,22},{7,23},{8,24},{9,... | collective-permute-start | bytes 184328 | tf_op jit(solution)/shard_map/ppermute | solution.py:17
  80.7 0.8 collective-permute-start.29
  81.5 0.4 collective-permute-done.27.refs_0_
  81.9 2.8 %collective-permute-done.28.refs_1_ = bf16[40,768]{1,0:T(8,128)(2,1)S(1)} collective-permute-done((bf16[40,768]{1,0:T(8,128)(2,1)S(1)}, bf16[40,768]{1,0:T(8,128)(2,1)S(1)}, u32[]{:S(2)}, u32[]{:S(2)}) %collective-permute-start.28) | collective-permute-done | bytes 61472 | tf_op jit(solution)/shard_map/ppermute | solution.py:17
  84.8 1.9 %collective-permute-done.29.refs_2_ = bf16[40,768]{1,0:T(8,128)(2,1)S(1)} collective-permute-done((bf16[40,768]{1,0:T(8,128)(2,1)S(1)}, bf16[40,768]{1,0:T(8,128)(2,1)S(1)}, u32[]{:S(2)}, u32[]{:S(2)}) %collective-permute-start.29) | collective-permute-done | bytes 61472 | tf_op jit(solution)/shard_map/ppermute | solution.py:17
  86.7 0.7 shard_map.128
  (56 shorter events, 2.1 us)
Async XLA Ops:
  1.8 12.4 %collective-permute-start = (bf16[112,768]{1,0:T(8,128)(2,1)S(1)}, bf16[112,768]{1,0:T(8,128)(2,1)S(1)}, u32[]{:S(2)}, u32[]{:S(2)}) collective-permute-start(bf16[112,768]{1,0:T(8,128)(2,1)S(1)} %maximum_maximum_fusion.refs_0_), channel_id=1, source_target_pairs={{0,16},{1,17},{2,18},{3,19},{4,20},{5,21},{6,22},{7,23},{8,24},{9,... | collective-permute-start | bytes 516104 | tf_op jit(solution)/shard_map/ppermute | solution.py:17
  5.9 4.4 %collective-permute-start.2 = (bf16[24,1152]{1,0:T(8,128)(2,1)}, bf16[24,1152]{1,0:T(8,128)(2,1)S(1)}, u32[]{:S(2)}, u32[]{:S(2)}) collective-permute-start(bf16[24,1152]{1,0:T(8,128)(2,1)} %refs_0_.1), channel_id=1, source_target_pairs={{0,4},{1,5},{2,6},{3,7},{4,0},{5,1},{6,2},{7,3},{8,12},{9,13},{10,... | collective-permute-start | bytes 165896 | tf_op jit(solution)/shard_map/ppermute | solution.py:17
  7.4 4.4 %collective-permute-start.1 = (bf16[24,1152]{1,0:T(8,128)(2,1)}, bf16[24,1152]{1,0:T(8,128)(2,1)S(1)}, u32[]{:S(2)}, u32[]{:S(2)}) collective-permute-start(bf16[24,1152]{1,0:T(8,128)(2,1)} %refs_0_.1), channel_id=1, source_target_pairs={{0,2},{1,3},{2,0},{3,1},{4,6},{5,7},{6,4},{7,5},{8,10},{9,11},{10,... | collective-permute-start | bytes 165896 | tf_op jit(solution)/shard_map/ppermute | solution.py:17
  8.9 5.3 %collective-permute-start.3 = (bf16[24,1152]{1,0:T(8,128)(2,1)}, bf16[24,1152]{1,0:T(8,128)(2,1)S(1)}, u32[]{:S(2)}, u32[]{:S(2)}) collective-permute-start(bf16[24,1152]{1,0:T(8,128)(2,1)} %refs_0_.1), channel_id=1, source_target_pairs={{0,6},{1,7},{2,4},{3,5},{4,2},{5,3},{6,0},{7,1},{8,14},{9,15},{10,... | collective-permute-start | bytes 165896 | tf_op jit(solution)/shard_map/ppermute | solution.py:17
  9.3 0.8 copy-start.2
  14.2 7.1 %copy-start = (bf16[1,256,768]{2,1,0:T(8,128)(2,1)S(1)}, bf16[1,256,768]{2,1,0:T(8,128)(2,1)}, u32[]{:S(2)}) copy-start(bf16[1,256,768]{2,1,0:T(8,128)(2,1)} %tokens_ref.4) | copy-start | bytes 1179652
  14.2 7.1 %copy-start.1 = (bf16[1,256,768]{2,1,0:T(8,128)(2,1)S(1)}, bf16[1,256,768]{2,1,0:T(8,128)(2,1)}, u32[]{:S(2)}) copy-start(bf16[1,256,768]{2,1,0:T(8,128)(2,1)} %cotangent_ref.4) | copy-start | bytes 1179652
  14.2 16.7 %collective-permute-start.7 = (bf16[2,112,768]{2,1,0:T(8,128)(2,1)S(1)}, bf16[2,112,768]{2,1,0:T(8,128)(2,1)S(1)}, u32[]{:S(2)}, u32[]{:S(2)}) collective-permute-start(bf16[2,112,768]{2,1,0:T(8,128)(2,1)S(1)} %shard_map.102.refs_0_), channel_id=1, source_target_pairs={{0,8},{1,9},{2,10},{3,11},{4,12},{5,13},{6,14},{7,15},{8,0},{9,1},... | collective-permute-start | bytes 1032200 | tf_op jit(solution)/shard_map/ppermute | solution.py:17
  15.8 15.1 %collective-permute-start.6 = (bf16[2,112,768]{2,1,0:T(8,128)(2,1)S(1)}, bf16[2,112,768]{2,1,0:T(8,128)(2,1)S(1)}, u32[]{:S(2)}, u32[]{:S(2)}) collective-permute-start(bf16[2,112,768]{2,1,0:T(8,128)(2,1)S(1)} %shard_map.102.refs_0_), channel_id=1, source_target_pairs={{0,4},{1,5},{2,6},{3,7},{4,0},{5,1},{6,2},{7,3},{8,12},{9,13},{10,... | collective-permute-start | bytes 1032200 | tf_op jit(solution)/shard_map/ppermute | solution.py:17
  16.3 14.6 %collective-permute-start.5 = (bf16[2,112,768]{2,1,0:T(8,128)(2,1)S(1)}, bf16[2,112,768]{2,1,0:T(8,128)(2,1)S(1)}, u32[]{:S(2)}, u32[]{:S(2)}) collective-permute-start(bf16[2,112,768]{2,1,0:T(8,128)(2,1)S(1)} %shard_map.102.refs_0_), channel_id=1, source_target_pairs={{0,2},{1,3},{2,0},{3,1},{4,6},{5,7},{6,4},{7,5},{8,10},{9,11},{10,... | collective-permute-start | bytes 1032200 | tf_op jit(solution)/shard_map/ppermute | solution.py:17
  17.8 13.1 %collective-permute-start.4 = (bf16[4,24,1152]{2,1,0:T(8,128)(2,1)S(1)}, bf16[4,24,1152]{2,1,0:T(8,128)(2,1)S(1)}, u32[]{:S(2)}, u32[]{:S(2)}) collective-permute-start(bf16[4,24,1152]{2,1,0:T(8,128)(2,1)S(1)} %shard_map.104.refs_0_), channel_id=1, source_target_pairs={{0,16},{1,17},{2,18},{3,19},{4,20},{5,21},{6,22},{7,23},{8,24},{9,... | collective-permute-start | bytes 663560 | tf_op jit(solution)/shard_map/ppermute | solution.py:17
  21.3 13.1 %collective-permute-start.12 = (bf16[1,192,768]{2,1,0:T(8,128)(2,1)S(1)}, bf16[1,192,768]{2,1,0:T(8,128)(2,1)S(1)}, u32[]{:S(2)}, u32[]{:S(2)}) collective-permute-start(bf16[1,192,768]{2,1,0:T(8,128)(2,1)S(1)} %get-tuple-element.70), channel_id=1, source_target_pairs={{1,2},{3,4},{5,6},{7,8},{9,10},{11,12},{13,14},{15,16},{17,18},{19... | collective-permute-start | bytes 884744 | tf_op jit(solution)/shard_map/ppermute | solution.py:404
  31.0 12.8 %collective-permute-start.10 = (bf16[3,112,768]{2,1,0:T(8,128)(2,1)S(1)}, bf16[3,112,768]{2,1,0:T(8,128)(2,1)S(1)}, u32[]{:S(2)}, u32[]{:S(2)}) collective-permute-start(bf16[3,112,768]{2,1,0:T(8,128)(2,1)S(1)} %shard_map.108), channel_id=1, source_target_pairs={{0,4},{1,5},{2,6},{3,7},{4,0},{5,1},{6,2},{7,3},{8,12},{9,13},{10,... | collective-permute-start | bytes 1548296 | tf_op jit(solution)/shard_map/ppermute | solution.py:17
  31.1 12.6 %collective-permute-start.9 = (bf16[3,112,768]{2,1,0:T(8,128)(2,1)S(1)}, bf16[3,112,768]{2,1,0:T(8,128)(2,1)S(1)}, u32[]{:S(2)}, u32[]{:S(2)}) collective-permute-start(bf16[3,112,768]{2,1,0:T(8,128)(2,1)S(1)} %shard_map.107), channel_id=1, source_target_pairs={{0,2},{1,3},{2,0},{3,1},{4,6},{5,7},{6,4},{7,5},{8,10},{9,11},{10,... | collective-permute-start | bytes 1548296 | tf_op jit(solution)/shard_map/ppermute | solution.py:17
  31.3 12.4 %collective-permute-start.8 = (bf16[8,24,1152]{2,1,0:T(8,128)(2,1)S(1)}, bf16[8,24,1152]{2,1,0:T(8,128)(2,1)S(1)}, u32[]{:S(2)}, u32[]{:S(2)}) collective-permute-start(bf16[8,24,1152]{2,1,0:T(8,128)(2,1)S(1)} %shard_map.105.refs_0_), channel_id=1, source_target_pairs={{0,8},{1,9},{2,10},{3,11},{4,12},{5,13},{6,14},{7,15},{8,0},{9,1},... | collective-permute-start | bytes 1327112 | tf_op jit(solution)/shard_map/ppermute | solution.py:17
  34.4 9.3 %collective-permute-start.11 = (bf16[1,192,768]{2,1,0:T(8,128)(2,1)S(1)}, bf16[1,192,768]{2,1,0:T(8,128)(2,1)S(1)}, u32[]{:S(2)}, u32[]{:S(2)}) collective-permute-start(bf16[1,192,768]{2,1,0:T(8,128)(2,1)S(1)} %get-tuple-element.69), channel_id=1, source_target_pairs={{0,1},{1,0},{2,3},{3,2},{4,5},{5,4},{6,7},{7,6},{8,9},{9,8},{10,11... | collective-permute-start | bytes 884744 | tf_op jit(solution)/shard_map/ppermute | solution.py:17
  34.4 10.9 %copy-start.4 = (f32[768]{0:T(1024)S(1)}, f32[768]{0:T(1024)}, u32[]{:S(2)}) copy-start(f32[768]{0:T(1024)} %param.9) | copy-start | bytes 9220
  43.8 5.5 %collective-permute-start.14 = (bf16[1,112,768]{2,1,0:T(8,128)(2,1)S(1)}, bf16[1,112,768]{2,1,0:T(8,128)(2,1)S(1)}, u32[]{:S(2)}, u32[]{:S(2)}) collective-permute-start(bf16[1,112,768]{2,1,0:T(8,128)(2,1)S(1)} %shard_map.114), channel_id=1, source_target_pairs={{0,4},{1,5},{2,6},{3,7},{4,0},{5,1},{6,2},{7,3},{8,12},{9,13},{10,... | collective-permute-start | bytes 516104 | tf_op jit(solution)/shard_map/ppermute | solution.py:17
  44.4 5.5 %collective-permute-start.15 = (bf16[1,112,768]{2,1,0:T(8,128)(2,1)S(1)}, bf16[1,112,768]{2,1,0:T(8,128)(2,1)S(1)}, u32[]{:S(2)}, u32[]{:S(2)}) collective-permute-start(bf16[1,112,768]{2,1,0:T(8,128)(2,1)S(1)} %shard_map.115), channel_id=1, source_target_pairs={{0,2},{1,3},{2,0},{3,1},{4,6},{5,7},{6,4},{7,5},{8,10},{9,11},{10,... | collective-permute-start | bytes 516104 | tf_op jit(solution)/shard_map/ppermute | solution.py:17
  45.3 1.1 %copy-start.3 = (s32[4]{0:T(128)S(1)}, s32[4]{0:T(128)}, u32[]{:S(2)}) copy-start(s32[4]{0:T(128)} %starts_ref.3) | copy-start | bytes 52
  45.5 7.9 %collective-permute-start.17 = (bf16[14,40,768]{2,1,0:T(8,128)(2,1)S(1)}, bf16[14,40,768]{2,1,0:T(8,128)(2,1)S(1)}, u32[]{:S(2)}, u32[]{:S(2)}) collective-permute-start(bf16[14,40,768]{2,1,0:T(8,128)(2,1)S(1)} %get-tuple-element.83.refs_0_), channel_id=1, source_target_pairs={{0,1},{1,0},{2,3},{3,2},{4,5},{5,4},{6,7},{7,6},{8,9},{9,8},{10,11... | collective-permute-start | bytes 2580488 | tf_op jit(solution)/shard_map/ppermute | solution.py:17
  45.6 4.9 %collective-permute-start.19 = (bf16[16,24,1152]{2,1,0:T(8,128)(2,1)S(1)}, bf16[16,24,1152]{2,1,0:T(8,128)(2,1)S(1)}, u32[]{:S(2)}, u32[]{:S(2)}) collective-permute-start(bf16[16,24,1152]{2,1,0:T(8,128)(2,1)S(1)} %shard_map.106.refs_0_), channel_id=1, source_target_pairs={{0,1},{1,0},{2,3},{3,2},{4,5},{5,4},{6,7},{7,6},{8,9},{9,8},{10,11... | collective-permute-start | bytes 2654216 | tf_op jit(solution)/shard_map/ppermute | solution.py:17
  46.1 5.7 %collective-permute-start.13 = (bf16[14,72,768]{2,1,0:T(8,128)(2,1)S(1)}, bf16[14,72,768]{2,1,0:T(8,128)(2,1)S(1)}, u32[]{:S(2)}, u32[]{:S(2)}) collective-permute-start(bf16[14,72,768]{2,1,0:T(8,128)(2,1)S(1)} %get-tuple-element.80.refs_0_), channel_id=1, source_target_pairs={{0,1},{1,0},{2,3},{3,2},{4,5},{5,4},{6,7},{7,6},{8,9},{9,8},{10,11... | collective-permute-start | bytes 4644872 | tf_op jit(solution)/shard_map/ppermute | solution.py:17
  49.9 1.9 %collective-permute-start.16 = (bf16[2,72,768]{2,1,0:T(8,128)(2,1)S(1)}, bf16[2,72,768]{2,1,0:T(8,128)(2,1)S(1)}, u32[]{:S(2)}, u32[]{:S(2)}) collective-permute-start(bf16[2,72,768]{2,1,0:T(8,128)(2,1)S(1)} %get-tuple-element.82.refs_2_), channel_id=1, source_target_pairs={{0,1},{1,0},{2,3},{3,2},{4,5},{5,4},{6,7},{7,6},{8,9},{9,8},{10,11... | collective-permute-start | bytes 663560 | tf_op jit(solution)/shard_map/ppermute | solution.py:17
  50.0 3.5 %collective-permute-start.18 = (bf16[2,40,768]{2,1,0:T(8,128)(2,1)S(1)}, bf16[2,40,768]{2,1,0:T(8,128)(2,1)S(1)}, u32[]{:S(2)}, u32[]{:S(2)}) collective-permute-start(bf16[2,40,768]{2,1,0:T(8,128)(2,1)S(1)} %get-tuple-element.84.refs_2_), channel_id=1, source_target_pairs={{0,1},{1,0},{2,3},{3,2},{4,5},{5,4},{6,7},{7,6},{8,9},{9,8},{10,11... | collective-permute-start | bytes 368648 | tf_op jit(solution)/shard_map/ppermute | solution.py:17
  55.5 2.6 %collective-permute-start.20 = (bf16[4,2,2,40,768]{4,3,2,1,0:T(8,128)(2,1)S(1)}, bf16[4,2,2,40,768]{4,3,2,1,0:T(8,128)(2,1)S(1)}, u32[]{:S(2)}, u32[]{:S(2)}) collective-permute-start(bf16[4,2,2,40,768]{4,3,2,1,0:T(8,128)(2,1)S(1)} %get-tuple-element.98), channel_id=1, source_target_pairs={{0,1},{1,0},{2,3},{3,2},{4,5},{5,4},{6,7},{7,6},{8,9},{9,8},{10,11... | collective-permute-start | bytes 2949128 | tf_op jit(solution)/shard_map/ppermute | solution.py:17
  58.3 17.2 %collective-permute-start.21 = (bf16[4,40,768]{2,1,0:T(8,128)(2,1)S(1)}, bf16[4,40,768]{2,1,0:T(8,128)(2,1)S(1)}, u32[]{:S(2)}, u32[]{:S(2)}) collective-permute-start(bf16[4,40,768]{2,1,0:T(8,128)(2,1)S(1)} %get-tuple-element.101), channel_id=1, source_target_pairs={{0,2},{1,3},{2,0},{3,1},{4,6},{5,7},{6,4},{7,5},{8,10},{9,11},{10,... | collective-permute-start | bytes 737288 | tf_op jit(solution)/shard_map/ppermute | solution.py:17
  59.6 15.9 %collective-permute-start.22 = (bf16[4,40,768]{2,1,0:T(8,128)(2,1)S(1)}, bf16[4,40,768]{2,1,0:T(8,128)(2,1)S(1)}, u32[]{:S(2)}, u32[]{:S(2)}) collective-permute-start(bf16[4,40,768]{2,1,0:T(8,128)(2,1)S(1)} %get-tuple-element.102), channel_id=1, source_target_pairs={{0,4},{1,5},{2,6},{3,7},{4,0},{5,1},{6,2},{7,3},{8,12},{9,13},{10,... | collective-permute-start | bytes 737288 | tf_op jit(solution)/shard_map/ppermute | solution.py:17
  61.1 14.4 %collective-permute-start.23 = (bf16[4,40,768]{2,1,0:T(8,128)(2,1)S(1)}, bf16[4,40,768]{2,1,0:T(8,128)(2,1)S(1)}, u32[]{:S(2)}, u32[]{:S(2)}) collective-permute-start(bf16[4,40,768]{2,1,0:T(8,128)(2,1)S(1)} %get-tuple-element.103), channel_id=1, source_target_pairs={{0,6},{1,7},{2,4},{3,5},{4,2},{5,3},{6,0},{7,1},{8,14},{9,15},{10,... | collective-permute-start | bytes 737288 | tf_op jit(solution)/shard_map/ppermute | solution.py:17
  65.8 1.2 %collective-permute-start.24 = (f32[1,768]{1,0:T(1,128)S(1)}, f32[1,768]{1,0:T(1,128)S(1)}, u32[]{:S(2)}, u32[]{:S(2)}) collective-permute-start(f32[1,768]{1,0:T(1,128)S(1)} %get-tuple-element.104), channel_id=1, source_target_pairs={{0,1},{1,0},{2,3},{3,2},{4,5},{5,4},{6,7},{7,6},{8,9},{9,8},{10,11... | collective-permute-start | bytes 9224 | tf_op jit(solution)/shard_map/ppermute | solution.py:17
  67.1 4.8 %collective-permute-start.25 = (f32[1,768]{1,0:T(1,128)S(1)}, f32[1,768]{1,0:T(1,128)S(1)}, u32[]{:S(2)}, u32[]{:S(2)}) collective-permute-start(f32[1,768]{1,0:T(1,128)S(1)} %add.9), channel_id=1, source_target_pairs={{0,2},{1,3},{2,0},{3,1},{4,6},{5,7},{6,4},{7,5},{8,10},{9,11},{10,... | collective-permute-start | bytes 9224 | tf_op jit(solution)/shard_map/ppermute | solution.py:17
  71.9 3.6 %collective-permute-start.26 = (f32[1,768]{1,0:T(1,128)S(1)}, f32[1,768]{1,0:T(1,128)S(1)}, u32[]{:S(2)}, u32[]{:S(2)}) collective-permute-start(f32[1,768]{1,0:T(1,128)S(1)} %add.10), channel_id=1, source_target_pairs={{0,4},{1,5},{2,6},{3,7},{4,0},{5,1},{6,2},{7,3},{8,12},{9,13},{10,... | collective-permute-start | bytes 9224 | tf_op jit(solution)/shard_map/ppermute | solution.py:17
  75.7 6.2 %collective-permute-start.27 = (bf16[40,768]{1,0:T(8,128)(2,1)S(1)}, bf16[40,768]{1,0:T(8,128)(2,1)S(1)}, u32[]{:S(2)}, u32[]{:S(2)}) collective-permute-start(bf16[40,768]{1,0:T(8,128)(2,1)S(1)} %get-tuple-element.107), channel_id=1, source_target_pairs={{0,8},{1,9},{2,10},{3,11},{4,12},{5,13},{6,14},{7,15},{8,0},{9,1},... | collective-permute-start | bytes 184328 | tf_op jit(solution)/shard_map/ppermute | solution.py:17
  79.1 5.7 %collective-permute-start.28 = (bf16[40,768]{1,0:T(8,128)(2,1)S(1)}, bf16[40,768]{1,0:T(8,128)(2,1)S(1)}, u32[]{:S(2)}, u32[]{:S(2)}) collective-permute-start(bf16[40,768]{1,0:T(8,128)(2,1)S(1)} %get-tuple-element.108), channel_id=1, source_target_pairs={{0,16},{1,17},{2,18},{3,19},{4,20},{5,21},{6,22},{7,23},{8,24},{9,... | collective-permute-start | bytes 184328 | tf_op jit(solution)/shard_map/ppermute | solution.py:17
  80.7 6.0 %collective-permute-start.29 = (bf16[40,768]{1,0:T(8,128)(2,1)S(1)}, bf16[40,768]{1,0:T(8,128)(2,1)S(1)}, u32[]{:S(2)}, u32[]{:S(2)}) collective-permute-start(bf16[40,768]{1,0:T(8,128)(2,1)S(1)} %get-tuple-element.109), channel_id=1, source_target_pairs={{0,24},{1,25},{2,26},{3,27},{4,28},{5,29},{6,30},{7,31},{8,16},{9,... | collective-permute-start | bytes 184328 | tf_op jit(solution)/shard_map/ppermute | solution.py:17

commit v4 on v3

--- a/solution.py
+++ b/solution.py
@@ -540,18 +540,32 @@
     )(*arrays)
 
 
+def pack(conv_parts, down_parts, cost):
+    taps, rows, width = conv_parts[0].shape
+    down_rows = down_parts[0].shape[0]
+    held = -(-(taps * rows + down_rows) // 16) * 16
+    count = len(conv_parts)
+
+    def kernel(*refs):
+        out = refs[-1]
+        for i in range(count):
+            for t in range(taps):
+                out[i, t * rows : (t + 1) * rows] = refs[i][t]
+            out[i, taps * rows : taps * rows + down_rows] = refs[count + i][...]
+
+    arrays = (*conv_parts, *down_parts)
+    return call(kernel, [((count, held, width), conv_parts[0].dtype)], *arrays, cost=cost)[0]
+
+
 def gather(conv, up, down, tokens, cotangent, prepared):
     first, *rest = line_masks(lax.axis_size("ctx") // 8)
-    width = conv.shape[-1]
     rows = conv.shape[0] * conv.shape[1]
-    filler = jnp.zeros((-(rows + down.shape[0]) % 16, width), conv.dtype)
-    both = jnp.concatenate([conv.reshape(rows, width), down, filler])
-    new = swap(both, first)
+    new, down_new = swap(conv, first), swap(down, first)
     up_new = [swap(up, mask) for mask in (2, 4, 6)]
     inner, outer = neighbours(*all_after((tokens, cotangent), (up_new[0],)))
-    (up,) = load(up)
-    new, both, *up_new = all_after((new, both, *up_new), ())
-    part = held = stack([both, new], cost=FIRST)
+    conv, up, down = load(conv, up, down)
+    new, down_new, *up_new = all_after((new, down_new, *up_new), ())
+    part = held = pack([conv, new], [down, down_new], cost=FIRST)
     up_held = stack([up] + up_new, cost=SECOND)
     pieces, late = [], None
     for mask, next_mask in zip([first] + rest, rest + [None]):
@@ -567,9 +581,11 @@
         up_held = join(up_held, received)
         if next_mask is None:
             outer = stack([outer], cost=THIRD)
-        part, held, up_held, by_x, by_y, other, outer = all_after(
-            (part, held, up_held, by_x, by_y, other, outer), ()
-        ) if next_mask is None else (*all_after((part, held, up_held, by_x, by_y, other), ()), outer)
+        phase = (part, held, up_held, by_x, by_y, other)
+        if next_mask is None:
+            part, held, up_held, by_x, by_y, other, outer = all_after((*phase, outer), ())
+        else:
+            part, held, up_held, by_x, by_y, other = all_after(phase, ())
         if late is not None:
             pieces += [(by_y, count, count + old // 2), (by_x, count, count + old - old // 2)]
         pieces += [(part, 0, count), (by_x, 0, count), (by_y, 0, count)]

time: 87.6 us -> 86.7 us (0.990)
  local copies, waits for them, and re-layouts: 0.95 us -> 2.56 us
  waiting for transfers between devices: 35.8 us -> 34.3 us
  other arithmetic: 1.04 us -> 0.01 us
    unnamed x10 -> x14, local copies, waits for them, and re-layouts: 0.87 us -> 2.56 us
    ppermute x29 -> x30, waiting for transfers between devices: 35.8 us -> 34.3 us  [swap(): return lax.ppermute(value, 'ctx', [(i, i ^ mask) for i in range(devices)])]
    concatenate x1 -> x0, other arithmetic: 1.03 us -> none  [gather(): both = jnp.concatenate([conv.reshape(rows, width), down, filler])]
    ppermute x29 -> x30, starting transfers between devices: 32.9 us -> 32.7 us  [swap(): return lax.ppermute(value, 'ctx', [(i, i ^ mask) for i in range(devices)])]
  transfers between devices with their start and end apart: 30 -> 31, of which waited for: 14 -> 15; matrix products, arithmetic and copies ran while one was open for 0% -> 0% of each run, Pallas kernels for 14% -> 14%
where the time goes in v4:
time: 86.7 us; the launch traced here: 86.5 us
  waiting for transfers between devices  34.3 us (40%)
  starting transfers between devices  33.4 us (39%)
  Pallas kernels  15.2 us (18%)
  local copies, waits for them, and re-layouts  2.56 us (3%)
  between operations  0.95 us (1%)
    ppermute x30, waiting for transfers between devices, swap(): return lax.ppermute(value, 'ctx', [(i, i ^ mask) for i in range(devices)])  34.3 us
    ppermute x30, starting transfers between devices, swap(): return lax.ppermute(value, 'ctx', [(i, i ^ mask) for i in range(devices)])  32.7 us
    pallas_call x26, Pallas kernels, call(): pl.pallas_call(kernel, out_shape=shapes, in_specs=[SMEM if i in smem else...  15 us
    unnamed x14, local copies, waits for them, and re-layouts  2.56 us
  transfers between devices with their start and end apart: 31, of which 15 were waited for; matrix products, arithmetic and copies ran while one was open for 0% of the time, Pallas kernels for 14%

profile of v4, /device:TPU:0, one launch (start us, length us, event | category | flops | bytes accessed | tf_op | source)
XLA Modules:
  0.0 86.5 jit_solution(5582193468073256469)
XLA Ops:
  0.6 4.1 %collective-permute-start = (bf16[3,24,768]{2,1,0:T(8,128)(2,1)}, bf16[3,24,768]{2,1,0:T(8,128)(2,1)S(1)}, u32[]{:S(2)}, u32[]{:S(2)}) collective-permute-start(bf16[3,24,768]{2,1,0:T(8,128)(2,1)} %refs_0_.1), channel_id=1, source_target_pairs={{0,16},{1,17},{2,18},{3,19},{4,20},{5,21},{6,22},{7,23},{8,24},{9,... | collective-permute-start | bytes 331784 | tf_op jit(solution)/shard_map/ppermute | solution.py:17
  4.7 1.5 %collective-permute-start.2 = (bf16[24,1152]{1,0:T(8,128)(2,1)}, bf16[24,1152]{1,0:T(8,128)(2,1)S(1)}, u32[]{:S(2)}, u32[]{:S(2)}) collective-permute-start(bf16[24,1152]{1,0:T(8,128)(2,1)} %refs_1_.1), channel_id=1, source_target_pairs={{0,2},{1,3},{2,0},{3,1},{4,6},{5,7},{6,4},{7,5},{8,10},{9,11},{10,... | collective-permute-start | bytes 165896 | tf_op jit(solution)/shard_map/ppermute | solution.py:17
  6.2 1.5 %collective-permute-start.4 = (bf16[24,1152]{1,0:T(8,128)(2,1)}, bf16[24,1152]{1,0:T(8,128)(2,1)S(1)}, u32[]{:S(2)}, u32[]{:S(2)}) collective-permute-start(bf16[24,1152]{1,0:T(8,128)(2,1)} %refs_1_.1), channel_id=1, source_target_pairs={{0,6},{1,7},{2,4},{3,5},{4,2},{5,3},{6,0},{7,1},{8,14},{9,15},{10,... | collective-permute-start | bytes 165896 | tf_op jit(solution)/shard_map/ppermute | solution.py:17
  7.7 0.5 collective-permute-start.3
  8.3 0.9 %copy-done.2 = bf16[3,24,768]{2,1,0:T(8,128)(2,1)S(1)} copy-done((bf16[3,24,768]{2,1,0:T(8,128)(2,1)S(1)}, bf16[3,24,768]{2,1,0:T(8,128)(2,1)}, u32[]{:S(2)}) %copy-start.2) | copy-done | bytes 110616
  9.2 0.8 copy-done.3
  10.0 0.8 copy-done.4
  11.1 0.3 collective-permute-done.4.refs_3_
  11.5 0.6 collective-permute-done.3.refs_2_
  12.1 1.5 %collective-permute-done.1.refs_3_ = bf16[36,768]{1,0:T(8,128)(2,1)S(1)} collective-permute-done((bf16[36,768]{1,0:T(8,128)(2,1)}, bf16[36,768]{1,0:T(8,128)(2,1)S(1)}, u32[]{:S(2)}, u32[]{:S(2)}) %collective-permute-start.1) | collective-permute-done | bytes 55328 | tf_op jit(solution)/shard_map/ppermute | solution.py:17
  13.6 1.6 %collective-permute-start.8 = (bf16[2,112,768]{2,1,0:T(8,128)(2,1)S(1)}, bf16[2,112,768]{2,1,0:T(8,128)(2,1)S(1)}, u32[]{:S(2)}, u32[]{:S(2)}) collective-permute-start(bf16[2,112,768]{2,1,0:T(8,128)(2,1)S(1)} %shard_map.103.refs_0_), channel_id=1, source_target_pairs={{0,8},{1,9},{2,10},{3,11},{4,12},{5,13},{6,14},{7,15},{8,0},{9,1},... | collective-permute-start | bytes 1032200 | tf_op jit(solution)/shard_map/ppermute | solution.py:17
  15.2 1.5 %collective-permute-start.7 = (bf16[2,112,768]{2,1,0:T(8,128)(2,1)S(1)}, bf16[2,112,768]{2,1,0:T(8,128)(2,1)S(1)}, u32[]{:S(2)}, u32[]{:S(2)}) collective-permute-start(bf16[2,112,768]{2,1,0:T(8,128)(2,1)S(1)} %shard_map.103.refs_0_), channel_id=1, source_target_pairs={{0,4},{1,5},{2,6},{3,7},{4,0},{5,1},{6,2},{7,3},{8,12},{9,13},{10,... | collective-permute-start | bytes 1032200 | tf_op jit(solution)/shard_map/ppermute | solution.py:17
  16.7 1.5 %collective-permute-start.6 = (bf16[2,112,768]{2,1,0:T(8,128)(2,1)S(1)}, bf16[2,112,768]{2,1,0:T(8,128)(2,1)S(1)}, u32[]{:S(2)}, u32[]{:S(2)}) collective-permute-start(bf16[2,112,768]{2,1,0:T(8,128)(2,1)S(1)} %shard_map.103.refs_0_), channel_id=1, source_target_pairs={{0,2},{1,3},{2,0},{3,1},{4,6},{5,7},{6,4},{7,5},{8,10},{9,11},{10,... | collective-permute-start | bytes 1032200 | tf_op jit(solution)/shard_map/ppermute | solution.py:17
  18.3 2.0 %collective-permute-start.5 = (bf16[4,24,1152]{2,1,0:T(8,128)(2,1)S(1)}, bf16[4,24,1152]{2,1,0:T(8,128)(2,1)S(1)}, u32[]{:S(2)}, u32[]{:S(2)}) collective-permute-start(bf16[4,24,1152]{2,1,0:T(8,128)(2,1)S(1)} %shard_map.104.refs_0_), channel_id=1, source_target_pairs={{0,16},{1,17},{2,18},{3,19},{4,20},{5,21},{6,22},{7,23},{8,24},{9,... | collective-permute-start | bytes 663560 | tf_op jit(solution)/shard_map/ppermute | solution.py:17
  20.4 0.7 collective-permute-start.13
  21.0 9.0 %collective-permute-done.5.refs_1_ = bf16[4,24,1152]{2,1,0:T(8,128)(2,1)S(1)} collective-permute-done((bf16[4,24,1152]{2,1,0:T(8,128)(2,1)S(1)}, bf16[4,24,1152]{2,1,0:T(8,128)(2,1)S(1)}, u32[]{:S(2)}, u32[]{:S(2)}) %collective-permute-start.5) | collective-permute-done | bytes 221216 | tf_op jit(solution)/shard_map/ppermute | solution.py:17
  30.2 1.5 %collective-permute-start.10 = (bf16[3,112,768]{2,1,0:T(8,128)(2,1)S(1)}, bf16[3,112,768]{2,1,0:T(8,128)(2,1)S(1)}, u32[]{:S(2)}, u32[]{:S(2)}) collective-permute-start(bf16[3,112,768]{2,1,0:T(8,128)(2,1)S(1)} %shard_map.107), channel_id=1, source_target_pairs={{0,2},{1,3},{2,0},{3,1},{4,6},{5,7},{6,4},{7,5},{8,10},{9,11},{10,... | collective-permute-start | bytes 1548296 | tf_op jit(solution)/shard_map/ppermute | solution.py:17
  31.8 1.7 %collective-permute-start.9 = (bf16[8,24,1152]{2,1,0:T(8,128)(2,1)S(1)}, bf16[8,24,1152]{2,1,0:T(8,128)(2,1)S(1)}, u32[]{:S(2)}, u32[]{:S(2)}) collective-permute-start(bf16[8,24,1152]{2,1,0:T(8,128)(2,1)S(1)} %shard_map.105.refs_0_), channel_id=1, source_target_pairs={{0,8},{1,9},{2,10},{3,11},{4,12},{5,13},{6,14},{7,15},{8,0},{9,1},... | collective-permute-start | bytes 1327112 | tf_op jit(solution)/shard_map/ppermute | solution.py:17
  33.5 9.2 %collective-permute-done.9.refs_1_ = bf16[8,24,1152]{2,1,0:T(8,128)(2,1)S(1)} collective-permute-done((bf16[8,24,1152]{2,1,0:T(8,128)(2,1)S(1)}, bf16[8,24,1152]{2,1,0:T(8,128)(2,1)S(1)}, u32[]{:S(2)}, u32[]{:S(2)}) %collective-permute-start.9) | collective-permute-done | bytes 442400 | tf_op jit(solution)/shard_map/ppermute | solution.py:17
  42.9 0.6 collective-permute-start.15
  43.4 1.0 %collective-permute-start.16 = (bf16[1,112,768]{2,1,0:T(8,128)(2,1)S(1)}, bf16[1,112,768]{2,1,0:T(8,128)(2,1)S(1)}, u32[]{:S(2)}, u32[]{:S(2)}) collective-permute-start(bf16[1,112,768]{2,1,0:T(8,128)(2,1)S(1)} %shard_map.115), channel_id=1, source_target_pairs={{0,2},{1,3},{2,0},{3,1},{4,6},{5,7},{6,4},{7,5},{8,10},{9,11},{10,... | collective-permute-start | bytes 516104 | tf_op jit(solution)/shard_map/ppermute | solution.py:17
  44.7 0.5 collective-permute-start.20
  45.5 1.3 %shard_map.112 = (bf16[1,384,2304]{2,1,0:T(8,128)(2,1)S(1)}, f32[1,256,768]{2,1,0:T(8,128)S(1)}, f32[1,256,1]{2,1,0:T(8,128)S(1)}) custom-call(bf16[1,192,768]{2,1,0:T(8,128)(2,1)S(1)} %get-tuple-element.79.before_ref, bf16[1,256,768]{2,1,0:T(8,128)(2,1)S(1)} %copy-done, bf16[1,192,768]{2,1,0:T(8,128)(2,1)S(1)} %get-tuple-element.80.after_ref, ...), custom_call_target="tpu_custom_call" | custom-call | flops 1 | bytes 1 | tf_op jit(solution)/shard_map/pallas_call | solution.py:38
  46.8 1.6 %collective-permute-done.15.refs_0_ = bf16[1,112,768]{2,1,0:T(8,128)(2,1)S(1)} collective-permute-done((bf16[1,112,768]{2,1,0:T(8,128)(2,1)S(1)}, bf16[1,112,768]{2,1,0:T(8,128)(2,1)S(1)}, u32[]{:S(2)}, u32[]{:S(2)}) %collective-permute-start.15) | collective-permute-done | bytes 172064 | tf_op jit(solution)/shard_map/ppermute | solution.py:17
  48.3 0.6 collective-permute-done.16.refs_1_
  49.0 0.5 collective-permute-start.19
  49.7 1.1 %collective-permute-done.17.refs_3_ = bf16[2,72,768]{2,1,0:T(8,128)(2,1)S(1)} collective-permute-done((bf16[2,72,768]{2,1,0:T(8,128)(2,1)S(1)}, bf16[2,72,768]{2,1,0:T(8,128)(2,1)S(1)}, u32[]{:S(2)}, u32[]{:S(2)}) %collective-permute-start.17) | collective-permute-done | bytes 221216 | tf_op jit(solution)/shard_map/ppermute | solution.py:17
  51.1 1.4 %shard_map.118.mixed_ref = f32[1,256,768]{2,1,0:T(8,128)S(1)} custom-call(bf16[1,384,2304]{2,1,0:T(8,128)(2,1)S(1)} %get-tuple-element.81.taps_ref, bf16[1,256,768]{2,1,0:T(8,128)(2,1)S(1)} %copy-done, bf16[2304,768]{1,0:T(8,128)(2,1)S(1)} %bitcast.6), custom_call_target="tpu_custom_call" | custom-call | flops 1 | bytes 1 | tf_op jit(solution)/shard_map/pallas_call | solution.py:38
  52.5 1.8 %shard_map.120 = (f32[1,256,1152]{2,1,0:T(8,128)S(1)}, f32[1,256,1152]{2,1,0:T(8,128)S(1)}, bf16[1,256,1152]{2,1,0:T(8,128)(2,1)S(1)}, f32[1152,768]{1,0:T(8,128)S(1)}) custom-call(f32[1,256,768]{2,1,0:T(8,128)S(1)} %shard_map.118.mixed_ref, bf16[768,1152]{1,0:T(8,128)(2,1)S(1)} %bitcast.9, bf16[1,256,768]{2,1,0:T(8,128)(2,1)S(1)} %copy-done.1), custom_call_target="tpu_custom_call" | custom-call | flops 1 | bytes 1 | tf_op jit(solution)/shard_map/pallas_call | solution.py:38
  54.8 0.6 shard_map.121
  55.5 1.7 %shard_map.122.slope_ref = f32[1,384,1152]{2,1,0:T(8,128)S(1)} custom-call(bf16[1,384,2304]{2,1,0:T(8,128)(2,1)S(1)} %get-tuple-element.81.taps_ref, bf16[1,192,768]{2,1,0:T(8,128)(2,1)S(1)} %get-tuple-element.79.before_ref, bf16[1,192,768]{2,1,0:T(8,128)(2,1)S(1)} %get-tuple-element.80.after_ref, bf16[2304,768]{1,0:T(8,128)(2,1)S(1)} %bitcast.7, ...), custom_call_target="tpu_custom_call" | custom-call | flops 1 | bytes 1 | tf_op jit(solution)/shard_map/pallas_call | solution.py:38
  57.5 1.2 %collective-permute-start.22 = (bf16[4,40,768]{2,1,0:T(8,128)(2,1)S(1)}, bf16[4,40,768]{2,1,0:T(8,128)(2,1)S(1)}, u32[]{:S(2)}, u32[]{:S(2)}) collective-permute-start(bf16[4,40,768]{2,1,0:T(8,128)(2,1)S(1)} %get-tuple-element.107), channel_id=1, source_target_pairs={{0,2},{1,3},{2,0},{3,1},{4,6},{5,7},{6,4},{7,5},{8,10},{9,11},{10,... | collective-permute-start | bytes 737288 | tf_op jit(solution)/shard_map/ppermute | solution.py:17
  58.7 1.5 %collective-permute-start.23 = (bf16[4,40,768]{2,1,0:T(8,128)(2,1)S(1)}, bf16[4,40,768]{2,1,0:T(8,128)(2,1)S(1)}, u32[]{:S(2)}, u32[]{:S(2)}) collective-permute-start(bf16[4,40,768]{2,1,0:T(8,128)(2,1)S(1)} %get-tuple-element.108), channel_id=1, source_target_pairs={{0,4},{1,5},{2,6},{3,7},{4,0},{5,1},{6,2},{7,3},{8,12},{9,13},{10,... | collective-permute-start | bytes 737288 | tf_op jit(solution)/shard_map/ppermute | solution.py:17
  60.2 0.8 collective-permute-start.24
  61.0 3.9 %shard_map.123 = (f32[1,256,768]{2,1,0:T(8,128)S(1)}, f32[1,256,768]{2,1,0:T(8,128)S(1)}, f32[1,768]{1,0:T(1,128)S(1)}) custom-call(bf16[1,192,768]{2,1,0:T(8,128)(2,1)S(1)} %get-tuple-element.79.before_ref, bf16[1,256,768]{2,1,0:T(8,128)(2,1)S(1)} %copy-done.1, bf16[1,192,768]{2,1,0:T(8,128)(2,1)S(1)} %get-tuple-element.80.after_ref, ...), custom_call_target="tpu_custom_call" | custom-call | flops 1 | bytes 1 | tf_op jit(solution)/shard_map/pallas_call | solution.py:38
  65.0 1.1 %collective-permute-done.25 = f32[1,768]{1,0:T(1,128)S(1)} collective-permute-done((f32[1,768]{1,0:T(1,128)S(1)}, f32[1,768]{1,0:T(1,128)S(1)}, u32[]{:S(2)}, u32[]{:S(2)}) %collective-permute-start.25) | collective-permute-done | bytes 3104 | tf_op jit(solution)/shard_map/ppermute | solution.py:17
  66.2 1.1 %collective-permute-start.26 = (f32[1,768]{1,0:T(1,128)S(1)}, f32[1,768]{1,0:T(1,128)S(1)}, u32[]{:S(2)}, u32[]{:S(2)}) collective-permute-start(f32[1,768]{1,0:T(1,128)S(1)} %add.9), channel_id=1, source_target_pairs={{0,2},{1,3},{2,0},{3,1},{4,6},{5,7},{6,4},{7,5},{8,10},{9,11},{10,... | collective-permute-start | bytes 9224 | tf_op jit(solution)/shard_map/ppermute | solution.py:17
  67.3 1.8 %shard_map.124 = (bf16[1,256,768]{2,1,0:T(8,128)(2,1)}, bf16[1,256,768]{2,1,0:T(8,128)(2,1)}) custom-call(f32[1,256,768]{2,1,0:T(8,128)S(1)} %shard_map.118.mixed_ref, bf16[1,256,1152]{2,1,0:T(8,128)(2,1)S(1)} %get-tuple-element.93.hidden_ref, bf16[1152,768]{1,0:T(8,128)(2,1)S(1)} %bitcast.13, f32[1,256,768]{2,1,0:T(8,128)S(1)} %get-tuple-element.97.mixed_grad_ref, ...), custom_call_target="tpu_custom_call" | custom-call | flops 1 | bytes 1 | tf_op jit(solution)/shard_map/pallas_call | solution.py:38
  69.1 1.9 %collective-permute-done.26 = f32[1,768]{1,0:T(1,128)S(1)} collective-permute-done((f32[1,768]{1,0:T(1,128)S(1)}, f32[1,768]{1,0:T(1,128)S(1)}, u32[]{:S(2)}, u32[]{:S(2)}) %collective-permute-start.26) | collective-permute-done | bytes 3104 | tf_op jit(solution)/shard_map/ppermute | solution.py:17
  71.0 1.5 %collective-permute-start.27 = (f32[1,768]{1,0:T(1,128)S(1)}, f32[1,768]{1,0:T(1,128)S(1)}, u32[]{:S(2)}, u32[]{:S(2)}) collective-permute-start(f32[1,768]{1,0:T(1,128)S(1)} %add.10), channel_id=1, source_target_pairs={{0,4},{1,5},{2,6},{3,7},{4,0},{5,1},{6,2},{7,3},{8,12},{9,13},{10,... | collective-permute-start | bytes 9224 | tf_op jit(solution)/shard_map/ppermute | solution.py:17
  72.5 2.1 %collective-permute-done.27 = f32[1,768]{1,0:T(1,128)S(1)} collective-permute-done((f32[1,768]{1,0:T(1,128)S(1)}, f32[1,768]{1,0:T(1,128)S(1)}, u32[]{:S(2)}, u32[]{:S(2)}) %collective-permute-start.27) | collective-permute-done | bytes 3104 | tf_op jit(solution)/shard_map/ppermute | solution.py:17
  74.8 3.4 %collective-permute-start.28 = (bf16[40,768]{1,0:T(8,128)(2,1)S(1)}, bf16[40,768]{1,0:T(8,128)(2,1)S(1)}, u32[]{:S(2)}, u32[]{:S(2)}) collective-permute-start(bf16[40,768]{1,0:T(8,128)(2,1)S(1)} %get-tuple-element.113), channel_id=1, source_target_pairs={{0,8},{1,9},{2,10},{3,11},{4,12},{5,13},{6,14},{7,15},{8,0},{9,1},... | collective-permute-start | bytes 184328 | tf_op jit(solution)/shard_map/ppermute | solution.py:17
  78.2 1.6 %collective-permute-start.29 = (bf16[40,768]{1,0:T(8,128)(2,1)S(1)}, bf16[40,768]{1,0:T(8,128)(2,1)S(1)}, u32[]{:S(2)}, u32[]{:S(2)}) collective-permute-start(bf16[40,768]{1,0:T(8,128)(2,1)S(1)} %get-tuple-element.114), channel_id=1, source_target_pairs={{0,16},{1,17},{2,18},{3,19},{4,20},{5,21},{6,22},{7,23},{8,24},{9,... | collective-permute-start | bytes 184328 | tf_op jit(solution)/shard_map/ppermute | solution.py:17
  79.8 0.9 %collective-permute-start.30 = (bf16[40,768]{1,0:T(8,128)(2,1)S(1)}, bf16[40,768]{1,0:T(8,128)(2,1)S(1)}, u32[]{:S(2)}, u32[]{:S(2)}) collective-permute-start(bf16[40,768]{1,0:T(8,128)(2,1)S(1)} %get-tuple-element.115), channel_id=1, source_target_pairs={{0,24},{1,25},{2,26},{3,27},{4,28},{5,29},{6,30},{7,31},{8,16},{9,... | collective-permute-start | bytes 184328 | tf_op jit(solution)/shard_map/ppermute | solution.py:17
  80.6 0.4 collective-permute-done.28.refs_0_
  81.1 2.8 %collective-permute-done.29.refs_1_ = bf16[40,768]{1,0:T(8,128)(2,1)S(1)} collective-permute-done((bf16[40,768]{1,0:T(8,128)(2,1)S(1)}, bf16[40,768]{1,0:T(8,128)(2,1)S(1)}, u32[]{:S(2)}, u32[]{:S(2)}) %collective-permute-start.29) | collective-permute-done | bytes 61472 | tf_op jit(solution)/shard_map/ppermute | solution.py:17
  83.9 1.9 %collective-permute-done.30.refs_2_ = bf16[40,768]{1,0:T(8,128)(2,1)S(1)} collective-permute-done((bf16[40,768]{1,0:T(8,128)(2,1)S(1)}, bf16[40,768]{1,0:T(8,128)(2,1)S(1)}, u32[]{:S(2)}, u32[]{:S(2)}) %collective-permute-start.30) | collective-permute-done | bytes 61472 | tf_op jit(solution)/shard_map/ppermute | solution.py:17
  85.8 0.7 shard_map.128
  (59 shorter events, 2.9 us)
Async XLA Ops:
  0.6 12.9 %collective-permute-start = (bf16[3,24,768]{2,1,0:T(8,128)(2,1)}, bf16[3,24,768]{2,1,0:T(8,128)(2,1)S(1)}, u32[]{:S(2)}, u32[]{:S(2)}) collective-permute-start(bf16[3,24,768]{2,1,0:T(8,128)(2,1)} %refs_0_.1), channel_id=1, source_target_pairs={{0,16},{1,17},{2,18},{3,19},{4,20},{5,21},{6,22},{7,23},{8,24},{9,... | collective-permute-start | bytes 331784 | tf_op jit(solution)/shard_map/ppermute | solution.py:17
  4.7 6.4 %collective-permute-start.2 = (bf16[24,1152]{1,0:T(8,128)(2,1)}, bf16[24,1152]{1,0:T(8,128)(2,1)S(1)}, u32[]{:S(2)}, u32[]{:S(2)}) collective-permute-start(bf16[24,1152]{1,0:T(8,128)(2,1)} %refs_1_.1), channel_id=1, source_target_pairs={{0,2},{1,3},{2,0},{3,1},{4,6},{5,7},{6,4},{7,5},{8,10},{9,11},{10,... | collective-permute-start | bytes 165896 | tf_op jit(solution)/shard_map/ppermute | solution.py:17
  6.2 5.3 %collective-permute-start.4 = (bf16[24,1152]{1,0:T(8,128)(2,1)}, bf16[24,1152]{1,0:T(8,128)(2,1)S(1)}, u32[]{:S(2)}, u32[]{:S(2)}) collective-permute-start(bf16[24,1152]{1,0:T(8,128)(2,1)} %refs_1_.1), channel_id=1, source_target_pairs={{0,6},{1,7},{2,4},{3,5},{4,2},{5,3},{6,0},{7,1},{8,14},{9,15},{10,... | collective-permute-start | bytes 165896 | tf_op jit(solution)/shard_map/ppermute | solution.py:17
  7.7 4.4 %collective-permute-start.3 = (bf16[24,1152]{1,0:T(8,128)(2,1)}, bf16[24,1152]{1,0:T(8,128)(2,1)S(1)}, u32[]{:S(2)}, u32[]{:S(2)}) collective-permute-start(bf16[24,1152]{1,0:T(8,128)(2,1)} %refs_1_.1), channel_id=1, source_target_pairs={{0,4},{1,5},{2,6},{3,7},{4,0},{5,1},{6,2},{7,3},{8,12},{9,13},{10,... | collective-permute-start | bytes 165896 | tf_op jit(solution)/shard_map/ppermute | solution.py:17
  8.2 5.3 %collective-permute-start.1 = (bf16[36,768]{1,0:T(8,128)(2,1)}, bf16[36,768]{1,0:T(8,128)(2,1)S(1)}, u32[]{:S(2)}, u32[]{:S(2)}) collective-permute-start(bf16[36,768]{1,0:T(8,128)(2,1)} %refs_2_.1), channel_id=1, source_target_pairs={{0,16},{1,17},{2,18},{3,19},{4,20},{5,21},{6,22},{7,23},{8,24},{9,... | collective-permute-start | bytes 165896 | tf_op jit(solution)/shard_map/ppermute | solution.py:17
  8.3 0.9 %copy-start.2 = (bf16[3,24,768]{2,1,0:T(8,128)(2,1)S(1)}, bf16[3,24,768]{2,1,0:T(8,128)(2,1)}, u32[]{:S(2)}) copy-start(bf16[3,24,768]{2,1,0:T(8,128)(2,1)} %refs_0_.1) | copy-start | bytes 331780
  9.2 0.8 copy-start.3
  10.0 0.8 copy-start.4
  13.6 16.5 %collective-permute-start.8 = (bf16[2,112,768]{2,1,0:T(8,128)(2,1)S(1)}, bf16[2,112,768]{2,1,0:T(8,128)(2,1)S(1)}, u32[]{:S(2)}, u32[]{:S(2)}) collective-permute-start(bf16[2,112,768]{2,1,0:T(8,128)(2,1)S(1)} %shard_map.103.refs_0_), channel_id=1, source_target_pairs={{0,8},{1,9},{2,10},{3,11},{4,12},{5,13},{6,14},{7,15},{8,0},{9,1},... | collective-permute-start | bytes 1032200 | tf_op jit(solution)/shard_map/ppermute | solution.py:17
  15.2 14.8 %collective-permute-start.7 = (bf16[2,112,768]{2,1,0:T(8,128)(2,1)S(1)}, bf16[2,112,768]{2,1,0:T(8,128)(2,1)S(1)}, u32[]{:S(2)}, u32[]{:S(2)}) collective-permute-start(bf16[2,112,768]{2,1,0:T(8,128)(2,1)S(1)} %shard_map.103.refs_0_), channel_id=1, source_target_pairs={{0,4},{1,5},{2,6},{3,7},{4,0},{5,1},{6,2},{7,3},{8,12},{9,13},{10,... | collective-permute-start | bytes 1032200 | tf_op jit(solution)/shard_map/ppermute | solution.py:17
  16.7 13.3 %collective-permute-start.6 = (bf16[2,112,768]{2,1,0:T(8,128)(2,1)S(1)}, bf16[2,112,768]{2,1,0:T(8,128)(2,1)S(1)}, u32[]{:S(2)}, u32[]{:S(2)}) collective-permute-start(bf16[2,112,768]{2,1,0:T(8,128)(2,1)S(1)} %shard_map.103.refs_0_), channel_id=1, source_target_pairs={{0,2},{1,3},{2,0},{3,1},{4,6},{5,7},{6,4},{7,5},{8,10},{9,11},{10,... | collective-permute-start | bytes 1032200 | tf_op jit(solution)/shard_map/ppermute | solution.py:17
  18.2 2.1 %copy-start = (bf16[1,256,768]{2,1,0:T(8,128)(2,1)S(1)}, bf16[1,256,768]{2,1,0:T(8,128)(2,1)}, u32[]{:S(2)}) copy-start(bf16[1,256,768]{2,1,0:T(8,128)(2,1)} %tokens_ref.4) | copy-start | bytes 1179652
  18.2 2.1 %copy-start.1 = (bf16[1,256,768]{2,1,0:T(8,128)(2,1)S(1)}, bf16[1,256,768]{2,1,0:T(8,128)(2,1)}, u32[]{:S(2)}) copy-start(bf16[1,256,768]{2,1,0:T(8,128)(2,1)} %cotangent_ref.4) | copy-start | bytes 1179652
  18.3 11.7 %collective-permute-start.5 = (bf16[4,24,1152]{2,1,0:T(8,128)(2,1)S(1)}, bf16[4,24,1152]{2,1,0:T(8,128)(2,1)S(1)}, u32[]{:S(2)}, u32[]{:S(2)}) collective-permute-start(bf16[4,24,1152]{2,1,0:T(8,128)(2,1)S(1)} %shard_map.104.refs_0_), channel_id=1, source_target_pairs={{0,16},{1,17},{2,18},{3,19},{4,20},{5,21},{6,22},{7,23},{8,24},{9,... | collective-permute-start | bytes 663560 | tf_op jit(solution)/shard_map/ppermute | solution.py:17
  20.4 13.1 %collective-permute-start.13 = (bf16[1,192,768]{2,1,0:T(8,128)(2,1)S(1)}, bf16[1,192,768]{2,1,0:T(8,128)(2,1)S(1)}, u32[]{:S(2)}, u32[]{:S(2)}) collective-permute-start(bf16[1,192,768]{2,1,0:T(8,128)(2,1)S(1)} %get-tuple-element.76), channel_id=1, source_target_pairs={{1,2},{3,4},{5,6},{7,8},{9,10},{11,12},{13,14},{15,16},{17,18},{19... | collective-permute-start | bytes 884744 | tf_op jit(solution)/shard_map/ppermute | solution.py:404
  30.1 12.7 %collective-permute-start.11 = (bf16[3,112,768]{2,1,0:T(8,128)(2,1)S(1)}, bf16[3,112,768]{2,1,0:T(8,128)(2,1)S(1)}, u32[]{:S(2)}, u32[]{:S(2)}) collective-permute-start(bf16[3,112,768]{2,1,0:T(8,128)(2,1)S(1)} %shard_map.108), channel_id=1, source_target_pairs={{0,4},{1,5},{2,6},{3,7},{4,0},{5,1},{6,2},{7,3},{8,12},{9,13},{10,... | collective-permute-start | bytes 1548296 | tf_op jit(solution)/shard_map/ppermute | solution.py:17
  30.2 12.6 %collective-permute-start.10 = (bf16[3,112,768]{2,1,0:T(8,128)(2,1)S(1)}, bf16[3,112,768]{2,1,0:T(8,128)(2,1)S(1)}, u32[]{:S(2)}, u32[]{:S(2)}) collective-permute-start(bf16[3,112,768]{2,1,0:T(8,128)(2,1)S(1)} %shard_map.107), channel_id=1, source_target_pairs={{0,2},{1,3},{2,0},{3,1},{4,6},{5,7},{6,4},{7,5},{8,10},{9,11},{10,... | collective-permute-start | bytes 1548296 | tf_op jit(solution)/shard_map/ppermute | solution.py:17
  31.8 11.0 %collective-permute-start.9 = (bf16[8,24,1152]{2,1,0:T(8,128)(2,1)S(1)}, bf16[8,24,1152]{2,1,0:T(8,128)(2,1)S(1)}, u32[]{:S(2)}, u32[]{:S(2)}) collective-permute-start(bf16[8,24,1152]{2,1,0:T(8,128)(2,1)S(1)} %shard_map.105.refs_0_), channel_id=1, source_target_pairs={{0,8},{1,9},{2,10},{3,11},{4,12},{5,13},{6,14},{7,15},{8,0},{9,1},... | collective-permute-start | bytes 1327112 | tf_op jit(solution)/shard_map/ppermute | solution.py:17
  33.5 9.3 %collective-permute-start.12 = (bf16[1,192,768]{2,1,0:T(8,128)(2,1)S(1)}, bf16[1,192,768]{2,1,0:T(8,128)(2,1)S(1)}, u32[]{:S(2)}, u32[]{:S(2)}) collective-permute-start(bf16[1,192,768]{2,1,0:T(8,128)(2,1)S(1)} %get-tuple-element.75), channel_id=1, source_target_pairs={{0,1},{1,0},{2,3},{3,2},{4,5},{5,4},{6,7},{7,6},{8,9},{9,8},{10,11... | collective-permute-start | bytes 884744 | tf_op jit(solution)/shard_map/ppermute | solution.py:17
  33.5 10.9 %copy-start.6 = (f32[768]{0:T(1024)S(1)}, f32[768]{0:T(1024)}, u32[]{:S(2)}) copy-start(f32[768]{0:T(1024)} %param.9) | copy-start | bytes 9220
  42.9 5.5 %collective-permute-start.15 = (bf16[1,112,768]{2,1,0:T(8,128)(2,1)S(1)}, bf16[1,112,768]{2,1,0:T(8,128)(2,1)S(1)}, u32[]{:S(2)}, u32[]{:S(2)}) collective-permute-start(bf16[1,112,768]{2,1,0:T(8,128)(2,1)S(1)} %shard_map.114), channel_id=1, source_target_pairs={{0,4},{1,5},{2,6},{3,7},{4,0},{5,1},{6,2},{7,3},{8,12},{9,13},{10,... | collective-permute-start | bytes 516104 | tf_op jit(solution)/shard_map/ppermute | solution.py:17
  43.4 5.5 %collective-permute-start.16 = (bf16[1,112,768]{2,1,0:T(8,128)(2,1)S(1)}, bf16[1,112,768]{2,1,0:T(8,128)(2,1)S(1)}, u32[]{:S(2)}, u32[]{:S(2)}) collective-permute-start(bf16[1,112,768]{2,1,0:T(8,128)(2,1)S(1)} %shard_map.115), channel_id=1, source_target_pairs={{0,2},{1,3},{2,0},{3,1},{4,6},{5,7},{6,4},{7,5},{8,10},{9,11},{10,... | collective-permute-start | bytes 516104 | tf_op jit(solution)/shard_map/ppermute | solution.py:17
  44.4 1.1 %copy-start.5 = (s32[4]{0:T(128)S(1)}, s32[4]{0:T(128)}, u32[]{:S(2)}) copy-start(s32[4]{0:T(128)} %starts_ref.3) | copy-start | bytes 52
  44.6 7.9 %collective-permute-start.18 = (bf16[14,40,768]{2,1,0:T(8,128)(2,1)S(1)}, bf16[14,40,768]{2,1,0:T(8,128)(2,1)S(1)}, u32[]{:S(2)}, u32[]{:S(2)}) collective-permute-start(bf16[14,40,768]{2,1,0:T(8,128)(2,1)S(1)} %get-tuple-element.89.refs_0_), channel_id=1, source_target_pairs={{0,1},{1,0},{2,3},{3,2},{4,5},{5,4},{6,7},{7,6},{8,9},{9,8},{10,11... | collective-permute-start | bytes 2580488 | tf_op jit(solution)/shard_map/ppermute | solution.py:17
  44.7 4.9 %collective-permute-start.20 = (bf16[16,24,1152]{2,1,0:T(8,128)(2,1)S(1)}, bf16[16,24,1152]{2,1,0:T(8,128)(2,1)S(1)}, u32[]{:S(2)}, u32[]{:S(2)}) collective-permute-start(bf16[16,24,1152]{2,1,0:T(8,128)(2,1)S(1)} %shard_map.106.refs_0_), channel_id=1, source_target_pairs={{0,1},{1,0},{2,3},{3,2},{4,5},{5,4},{6,7},{7,6},{8,9},{9,8},{10,11... | collective-permute-start | bytes 2654216 | tf_op jit(solution)/shard_map/ppermute | solution.py:17
  45.2 5.7 %collective-permute-start.14 = (bf16[14,72,768]{2,1,0:T(8,128)(2,1)S(1)}, bf16[14,72,768]{2,1,0:T(8,128)(2,1)S(1)}, u32[]{:S(2)}, u32[]{:S(2)}) collective-permute-start(bf16[14,72,768]{2,1,0:T(8,128)(2,1)S(1)} %get-tuple-element.86.refs_0_), channel_id=1, source_target_pairs={{0,1},{1,0},{2,3},{3,2},{4,5},{5,4},{6,7},{7,6},{8,9},{9,8},{10,11... | collective-permute-start | bytes 4644872 | tf_op jit(solution)/shard_map/ppermute | solution.py:17
  48.9 1.9 %collective-permute-start.17 = (bf16[2,72,768]{2,1,0:T(8,128)(2,1)S(1)}, bf16[2,72,768]{2,1,0:T(8,128)(2,1)S(1)}, u32[]{:S(2)}, u32[]{:S(2)}) collective-permute-start(bf16[2,72,768]{2,1,0:T(8,128)(2,1)S(1)} %get-tuple-element.88.refs_2_), channel_id=1, source_target_pairs={{0,1},{1,0},{2,3},{3,2},{4,5},{5,4},{6,7},{7,6},{8,9},{9,8},{10,11... | collective-permute-start | bytes 663560 | tf_op jit(solution)/shard_map/ppermute | solution.py:17
  49.0 3.5 %collective-permute-start.19 = (bf16[2,40,768]{2,1,0:T(8,128)(2,1)S(1)}, bf16[2,40,768]{2,1,0:T(8,128)(2,1)S(1)}, u32[]{:S(2)}, u32[]{:S(2)}) collective-permute-start(bf16[2,40,768]{2,1,0:T(8,128)(2,1)S(1)} %get-tuple-element.90.refs_2_), channel_id=1, source_target_pairs={{0,1},{1,0},{2,3},{3,2},{4,5},{5,4},{6,7},{7,6},{8,9},{9,8},{10,11... | collective-permute-start | bytes 368648 | tf_op jit(solution)/shard_map/ppermute | solution.py:17
  54.6 2.6 %collective-permute-start.21 = (bf16[4,2,2,40,768]{4,3,2,1,0:T(8,128)(2,1)S(1)}, bf16[4,2,2,40,768]{4,3,2,1,0:T(8,128)(2,1)S(1)}, u32[]{:S(2)}, u32[]{:S(2)}) collective-permute-start(bf16[4,2,2,40,768]{4,3,2,1,0:T(8,128)(2,1)S(1)} %get-tuple-element.104), channel_id=1, source_target_pairs={{0,1},{1,0},{2,3},{3,2},{4,5},{5,4},{6,7},{7,6},{8,9},{9,8},{10,11... | collective-permute-start | bytes 2949128 | tf_op jit(solution)/shard_map/ppermute | solution.py:17
  57.5 17.2 %collective-permute-start.22 = (bf16[4,40,768]{2,1,0:T(8,128)(2,1)S(1)}, bf16[4,40,768]{2,1,0:T(8,128)(2,1)S(1)}, u32[]{:S(2)}, u32[]{:S(2)}) collective-permute-start(bf16[4,40,768]{2,1,0:T(8,128)(2,1)S(1)} %get-tuple-element.107), channel_id=1, source_target_pairs={{0,2},{1,3},{2,0},{3,1},{4,6},{5,7},{6,4},{7,5},{8,10},{9,11},{10,... | collective-permute-start | bytes 737288 | tf_op jit(solution)/shard_map/ppermute | solution.py:17
  58.7 16.0 %collective-permute-start.23 = (bf16[4,40,768]{2,1,0:T(8,128)(2,1)S(1)}, bf16[4,40,768]{2,1,0:T(8,128)(2,1)S(1)}, u32[]{:S(2)}, u32[]{:S(2)}) collective-permute-start(bf16[4,40,768]{2,1,0:T(8,128)(2,1)S(1)} %get-tuple-element.108), channel_id=1, source_target_pairs={{0,4},{1,5},{2,6},{3,7},{4,0},{5,1},{6,2},{7,3},{8,12},{9,13},{10,... | collective-permute-start | bytes 737288 | tf_op jit(solution)/shard_map/ppermute | solution.py:17
  60.2 14.5 %collective-permute-start.24 = (bf16[4,40,768]{2,1,0:T(8,128)(2,1)S(1)}, bf16[4,40,768]{2,1,0:T(8,128)(2,1)S(1)}, u32[]{:S(2)}, u32[]{:S(2)}) collective-permute-start(bf16[4,40,768]{2,1,0:T(8,128)(2,1)S(1)} %get-tuple-element.109), channel_id=1, source_target_pairs={{0,6},{1,7},{2,4},{3,5},{4,2},{5,3},{6,0},{7,1},{8,14},{9,15},{10,... | collective-permute-start | bytes 737288 | tf_op jit(solution)/shard_map/ppermute | solution.py:17
  64.9 1.2 %collective-permute-start.25 = (f32[1,768]{1,0:T(1,128)S(1)}, f32[1,768]{1,0:T(1,128)S(1)}, u32[]{:S(2)}, u32[]{:S(2)}) collective-permute-start(f32[1,768]{1,0:T(1,128)S(1)} %get-tuple-element.110), channel_id=1, source_target_pairs={{0,1},{1,0},{2,3},{3,2},{4,5},{5,4},{6,7},{7,6},{8,9},{9,8},{10,11... | collective-permute-start | bytes 9224 | tf_op jit(solution)/shard_map/ppermute | solution.py:17
  66.2 4.8 %collective-permute-start.26 = (f32[1,768]{1,0:T(1,128)S(1)}, f32[1,768]{1,0:T(1,128)S(1)}, u32[]{:S(2)}, u32[]{:S(2)}) collective-permute-start(f32[1,768]{1,0:T(1,128)S(1)} %add.9), channel_id=1, source_target_pairs={{0,2},{1,3},{2,0},{3,1},{4,6},{5,7},{6,4},{7,5},{8,10},{9,11},{10,... | collective-permute-start | bytes 9224 | tf_op jit(solution)/shard_map/ppermute | solution.py:17
  71.0 3.6 %collective-permute-start.27 = (f32[1,768]{1,0:T(1,128)S(1)}, f32[1,768]{1,0:T(1,128)S(1)}, u32[]{:S(2)}, u32[]{:S(2)}) collective-permute-start(f32[1,768]{1,0:T(1,128)S(1)} %add.10), channel_id=1, source_target_pairs={{0,4},{1,5},{2,6},{3,7},{4,0},{5,1},{6,2},{7,3},{8,12},{9,13},{10,... | collective-permute-start | bytes 9224 | tf_op jit(solution)/shard_map/ppermute | solution.py:17
  74.8 6.3 %collective-permute-start.28 = (bf16[40,768]{1,0:T(8,128)(2,1)S(1)}, bf16[40,768]{1,0:T(8,128)(2,1)S(1)}, u32[]{:S(2)}, u32[]{:S(2)}) collective-permute-start(bf16[40,768]{1,0:T(8,128)(2,1)S(1)} %get-tuple-element.113), channel_id=1, source_target_pairs={{0,8},{1,9},{2,10},{3,11},{4,12},{5,13},{6,14},{7,15},{8,0},{9,1},... | collective-permute-start | bytes 184328 | tf_op jit(solution)/shard_map/ppermute | solution.py:17
  78.2 5.7 %collective-permute-start.29 = (bf16[40,768]{1,0:T(8,128)(2,1)S(1)}, bf16[40,768]{1,0:T(8,128)(2,1)S(1)}, u32[]{:S(2)}, u32[]{:S(2)}) collective-permute-start(bf16[40,768]{1,0:T(8,128)(2,1)S(1)} %get-tuple-element.114), channel_id=1, source_target_pairs={{0,16},{1,17},{2,18},{3,19},{4,20},{5,21},{6,22},{7,23},{8,24},{9,... | collective-permute-start | bytes 184328 | tf_op jit(solution)/shard_map/ppermute | solution.py:17
  79.8 6.0 %collective-permute-start.30 = (bf16[40,768]{1,0:T(8,128)(2,1)S(1)}, bf16[40,768]{1,0:T(8,128)(2,1)S(1)}, u32[]{:S(2)}, u32[]{:S(2)}) collective-permute-start(bf16[40,768]{1,0:T(8,128)(2,1)S(1)} %get-tuple-element.115), channel_id=1, source_target_pairs={{0,24},{1,25},{2,26},{3,27},{4,28},{5,29},{6,30},{7,31},{8,16},{9,... | collective-permute-start | bytes 184328 | tf_op jit(solution)/shard_map/ppermute | solution.py:17

commit v5 on v4

--- a/solution.py
+++ b/solution.py
@@ -64,8 +64,7 @@
 
 
 def column_blocks(width):
-    step = 384 if width % 384 == 0 else width
-    return [slice(at, at + step) for at in range(0, width, step)]
+    return [slice(0, width)]
 
 
 def prepare(before, tokens, after_, gain, starts):

time: 86.7 us -> 86 us (level)
  Pallas kernels: 15.2 us -> 14.3 us
    pallas_call x26, Pallas kernels: 15 us -> 14 us  [call(): pl.pallas_call(kernel, out_shape=shapes, in_specs=[SMEM if i in smem else...]
where the time goes in v5:
time: 86 us; the launch traced here: 85.7 us
  waiting for transfers between devices  34.6 us (40%)
  starting transfers between devices  33.4 us (39%)
  Pallas kernels  14.3 us (17%)
  local copies, waits for them, and re-layouts  2.56 us (3%)
  between operations  0.96 us (1%)
    ppermute x30, waiting for transfers between devices, swap(): return lax.ppermute(value, 'ctx', [(i, i ^ mask) for i in range(devices)])  34.6 us
    ppermute x30, starting transfers between devices, swap(): return lax.ppermute(value, 'ctx', [(i, i ^ mask) for i in range(devices)])  32.7 us
    pallas_call x26, Pallas kernels, call(): pl.pallas_call(kernel, out_shape=shapes, in_specs=[SMEM if i in smem else...  14 us
    unnamed x14, local copies, waits for them, and re-layouts  2.56 us
  transfers between devices with their start and end apart: 31, of which 15 were waited for; matrix products, arithmetic and copies ran while one was open for 0% of the time, Pallas kernels for 14%

profile of v5, /device:TPU:0, one launch (start us, length us, event | category | flops | bytes accessed | tf_op | source)
XLA Modules:
  0.0 85.7 jit_solution(8354126182235144448)
XLA Ops:
  0.6 4.1 %collective-permute-start = (bf16[3,24,768]{2,1,0:T(8,128)(2,1)}, bf16[3,24,768]{2,1,0:T(8,128)(2,1)S(1)}, u32[]{:S(2)}, u32[]{:S(2)}) collective-permute-start(bf16[3,24,768]{2,1,0:T(8,128)(2,1)} %refs_0_.1), channel_id=1, source_target_pairs={{0,16},{1,17},{2,18},{3,19},{4,20},{5,21},{6,22},{7,23},{8,24},{9,... | collective-permute-start | bytes 331784 | tf_op jit(solution)/shard_map/ppermute | solution.py:17
  4.7 1.5 %collective-permute-start.2 = (bf16[24,1152]{1,0:T(8,128)(2,1)}, bf16[24,1152]{1,0:T(8,128)(2,1)S(1)}, u32[]{:S(2)}, u32[]{:S(2)}) collective-permute-start(bf16[24,1152]{1,0:T(8,128)(2,1)} %refs_1_.1), channel_id=1, source_target_pairs={{0,2},{1,3},{2,0},{3,1},{4,6},{5,7},{6,4},{7,5},{8,10},{9,11},{10,... | collective-permute-start | bytes 165896 | tf_op jit(solution)/shard_map/ppermute | solution.py:17
  6.2 1.5 %collective-permute-start.4 = (bf16[24,1152]{1,0:T(8,128)(2,1)}, bf16[24,1152]{1,0:T(8,128)(2,1)S(1)}, u32[]{:S(2)}, u32[]{:S(2)}) collective-permute-start(bf16[24,1152]{1,0:T(8,128)(2,1)} %refs_1_.1), channel_id=1, source_target_pairs={{0,6},{1,7},{2,4},{3,5},{4,2},{5,3},{6,0},{7,1},{8,14},{9,15},{10,... | collective-permute-start | bytes 165896 | tf_op jit(solution)/shard_map/ppermute | solution.py:17
  7.7 0.5 collective-permute-start.3
  8.3 0.9 %copy-done.2 = bf16[3,24,768]{2,1,0:T(8,128)(2,1)S(1)} copy-done((bf16[3,24,768]{2,1,0:T(8,128)(2,1)S(1)}, bf16[3,24,768]{2,1,0:T(8,128)(2,1)}, u32[]{:S(2)}) %copy-start.2) | copy-done | bytes 110616
  9.2 0.8 copy-done.3
  10.0 0.8 copy-done.4
  11.1 0.3 collective-permute-done.4.refs_3_
  11.5 0.6 collective-permute-done.3.refs_2_
  12.1 1.5 %collective-permute-done.1.refs_3_ = bf16[36,768]{1,0:T(8,128)(2,1)S(1)} collective-permute-done((bf16[36,768]{1,0:T(8,128)(2,1)}, bf16[36,768]{1,0:T(8,128)(2,1)S(1)}, u32[]{:S(2)}, u32[]{:S(2)}) %collective-permute-start.1) | collective-permute-done | bytes 55328 | tf_op jit(solution)/shard_map/ppermute | solution.py:17
  13.6 1.6 %collective-permute-start.8 = (bf16[2,112,768]{2,1,0:T(8,128)(2,1)S(1)}, bf16[2,112,768]{2,1,0:T(8,128)(2,1)S(1)}, u32[]{:S(2)}, u32[]{:S(2)}) collective-permute-start(bf16[2,112,768]{2,1,0:T(8,128)(2,1)S(1)} %shard_map.103.refs_0_), channel_id=1, source_target_pairs={{0,8},{1,9},{2,10},{3,11},{4,12},{5,13},{6,14},{7,15},{8,0},{9,1},... | collective-permute-start | bytes 1032200 | tf_op jit(solution)/shard_map/ppermute | solution.py:17
  15.2 1.5 %collective-permute-start.7 = (bf16[2,112,768]{2,1,0:T(8,128)(2,1)S(1)}, bf16[2,112,768]{2,1,0:T(8,128)(2,1)S(1)}, u32[]{:S(2)}, u32[]{:S(2)}) collective-permute-start(bf16[2,112,768]{2,1,0:T(8,128)(2,1)S(1)} %shard_map.103.refs_0_), channel_id=1, source_target_pairs={{0,4},{1,5},{2,6},{3,7},{4,0},{5,1},{6,2},{7,3},{8,12},{9,13},{10,... | collective-permute-start | bytes 1032200 | tf_op jit(solution)/shard_map/ppermute | solution.py:17
  16.7 1.5 %collective-permute-start.6 = (bf16[2,112,768]{2,1,0:T(8,128)(2,1)S(1)}, bf16[2,112,768]{2,1,0:T(8,128)(2,1)S(1)}, u32[]{:S(2)}, u32[]{:S(2)}) collective-permute-start(bf16[2,112,768]{2,1,0:T(8,128)(2,1)S(1)} %shard_map.103.refs_0_), channel_id=1, source_target_pairs={{0,2},{1,3},{2,0},{3,1},{4,6},{5,7},{6,4},{7,5},{8,10},{9,11},{10,... | collective-permute-start | bytes 1032200 | tf_op jit(solution)/shard_map/ppermute | solution.py:17
  18.3 2.0 %collective-permute-start.5 = (bf16[4,24,1152]{2,1,0:T(8,128)(2,1)S(1)}, bf16[4,24,1152]{2,1,0:T(8,128)(2,1)S(1)}, u32[]{:S(2)}, u32[]{:S(2)}) collective-permute-start(bf16[4,24,1152]{2,1,0:T(8,128)(2,1)S(1)} %shard_map.104.refs_0_), channel_id=1, source_target_pairs={{0,16},{1,17},{2,18},{3,19},{4,20},{5,21},{6,22},{7,23},{8,24},{9,... | collective-permute-start | bytes 663560 | tf_op jit(solution)/shard_map/ppermute | solution.py:17
  20.4 0.7 collective-permute-start.13
  21.0 9.0 %collective-permute-done.5.refs_1_ = bf16[4,24,1152]{2,1,0:T(8,128)(2,1)S(1)} collective-permute-done((bf16[4,24,1152]{2,1,0:T(8,128)(2,1)S(1)}, bf16[4,24,1152]{2,1,0:T(8,128)(2,1)S(1)}, u32[]{:S(2)}, u32[]{:S(2)}) %collective-permute-start.5) | collective-permute-done | bytes 221216 | tf_op jit(solution)/shard_map/ppermute | solution.py:17
  30.2 1.5 %collective-permute-start.10 = (bf16[3,112,768]{2,1,0:T(8,128)(2,1)S(1)}, bf16[3,112,768]{2,1,0:T(8,128)(2,1)S(1)}, u32[]{:S(2)}, u32[]{:S(2)}) collective-permute-start(bf16[3,112,768]{2,1,0:T(8,128)(2,1)S(1)} %shard_map.107), channel_id=1, source_target_pairs={{0,2},{1,3},{2,0},{3,1},{4,6},{5,7},{6,4},{7,5},{8,10},{9,11},{10,... | collective-permute-start | bytes 1548296 | tf_op jit(solution)/shard_map/ppermute | solution.py:17
  31.8 1.7 %collective-permute-start.9 = (bf16[8,24,1152]{2,1,0:T(8,128)(2,1)S(1)}, bf16[8,24,1152]{2,1,0:T(8,128)(2,1)S(1)}, u32[]{:S(2)}, u32[]{:S(2)}) collective-permute-start(bf16[8,24,1152]{2,1,0:T(8,128)(2,1)S(1)} %shard_map.105.refs_0_), channel_id=1, source_target_pairs={{0,8},{1,9},{2,10},{3,11},{4,12},{5,13},{6,14},{7,15},{8,0},{9,1},... | collective-permute-start | bytes 1327112 | tf_op jit(solution)/shard_map/ppermute | solution.py:17
  33.5 9.2 %collective-permute-done.9.refs_1_ = bf16[8,24,1152]{2,1,0:T(8,128)(2,1)S(1)} collective-permute-done((bf16[8,24,1152]{2,1,0:T(8,128)(2,1)S(1)}, bf16[8,24,1152]{2,1,0:T(8,128)(2,1)S(1)}, u32[]{:S(2)}, u32[]{:S(2)}) %collective-permute-start.9) | collective-permute-done | bytes 442400 | tf_op jit(solution)/shard_map/ppermute | solution.py:17
  42.9 0.6 collective-permute-start.15
  43.4 1.0 %collective-permute-start.16 = (bf16[1,112,768]{2,1,0:T(8,128)(2,1)S(1)}, bf16[1,112,768]{2,1,0:T(8,128)(2,1)S(1)}, u32[]{:S(2)}, u32[]{:S(2)}) collective-permute-start(bf16[1,112,768]{2,1,0:T(8,128)(2,1)S(1)} %shard_map.115), channel_id=1, source_target_pairs={{0,2},{1,3},{2,0},{3,1},{4,6},{5,7},{6,4},{7,5},{8,10},{9,11},{10,... | collective-permute-start | bytes 516104 | tf_op jit(solution)/shard_map/ppermute | solution.py:17
  44.7 0.5 collective-permute-start.20
  45.5 1.3 %shard_map.112 = (bf16[1,384,2304]{2,1,0:T(8,128)(2,1)S(1)}, f32[1,256,768]{2,1,0:T(8,128)S(1)}, f32[1,256,1]{2,1,0:T(8,128)S(1)}) custom-call(bf16[1,192,768]{2,1,0:T(8,128)(2,1)S(1)} %get-tuple-element.79.before_ref, bf16[1,256,768]{2,1,0:T(8,128)(2,1)S(1)} %copy-done, bf16[1,192,768]{2,1,0:T(8,128)(2,1)S(1)} %get-tuple-element.80.after_ref, ...), custom_call_target="tpu_custom_call" | custom-call | flops 1 | bytes 1 | tf_op jit(solution)/shard_map/pallas_call | solution.py:38
  46.8 1.6 %collective-permute-done.15.refs_0_ = bf16[1,112,768]{2,1,0:T(8,128)(2,1)S(1)} collective-permute-done((bf16[1,112,768]{2,1,0:T(8,128)(2,1)S(1)}, bf16[1,112,768]{2,1,0:T(8,128)(2,1)S(1)}, u32[]{:S(2)}, u32[]{:S(2)}) %collective-permute-start.15) | collective-permute-done | bytes 172064 | tf_op jit(solution)/shard_map/ppermute | solution.py:17
  48.3 0.6 collective-permute-done.16.refs_1_
  49.0 0.5 collective-permute-start.19
  49.7 1.1 %collective-permute-done.17.refs_3_ = bf16[2,72,768]{2,1,0:T(8,128)(2,1)S(1)} collective-permute-done((bf16[2,72,768]{2,1,0:T(8,128)(2,1)S(1)}, bf16[2,72,768]{2,1,0:T(8,128)(2,1)S(1)}, u32[]{:S(2)}, u32[]{:S(2)}) %collective-permute-start.17) | collective-permute-done | bytes 221216 | tf_op jit(solution)/shard_map/ppermute | solution.py:17
  51.1 1.1 %shard_map.118.mixed_ref = f32[1,256,768]{2,1,0:T(8,128)S(1)} custom-call(bf16[1,384,2304]{2,1,0:T(8,128)(2,1)S(1)} %get-tuple-element.81.taps_ref, bf16[1,256,768]{2,1,0:T(8,128)(2,1)S(1)} %copy-done, bf16[2304,768]{1,0:T(8,128)(2,1)S(1)} %bitcast.6), custom_call_target="tpu_custom_call" | custom-call | flops 1 | bytes 1 | tf_op jit(solution)/shard_map/pallas_call | solution.py:38
  52.2 1.3 %shard_map.120 = (f32[1,256,1152]{2,1,0:T(8,128)S(1)}, f32[1,256,1152]{2,1,0:T(8,128)S(1)}, bf16[1,256,1152]{2,1,0:T(8,128)(2,1)S(1)}, f32[1152,768]{1,0:T(8,128)S(1)}) custom-call(f32[1,256,768]{2,1,0:T(8,128)S(1)} %shard_map.118.mixed_ref, bf16[768,1152]{1,0:T(8,128)(2,1)S(1)} %bitcast.9, bf16[1,256,768]{2,1,0:T(8,128)(2,1)S(1)} %copy-done.1), custom_call_target="tpu_custom_call" | custom-call | flops 1 | bytes 1 | tf_op jit(solution)/shard_map/pallas_call | solution.py:38
  54.0 0.6 shard_map.121
  54.6 1.7 %shard_map.122.slope_ref = f32[1,384,1152]{2,1,0:T(8,128)S(1)} custom-call(bf16[1,384,2304]{2,1,0:T(8,128)(2,1)S(1)} %get-tuple-element.81.taps_ref, bf16[1,192,768]{2,1,0:T(8,128)(2,1)S(1)} %get-tuple-element.79.before_ref, bf16[1,192,768]{2,1,0:T(8,128)(2,1)S(1)} %get-tuple-element.80.after_ref, bf16[2304,768]{1,0:T(8,128)(2,1)S(1)} %bitcast.7, ...), custom_call_target="tpu_custom_call" | custom-call | flops 1 | bytes 1 | tf_op jit(solution)/shard_map/pallas_call | solution.py:38
  56.6 1.2 %collective-permute-start.22 = (bf16[4,40,768]{2,1,0:T(8,128)(2,1)S(1)}, bf16[4,40,768]{2,1,0:T(8,128)(2,1)S(1)}, u32[]{:S(2)}, u32[]{:S(2)}) collective-permute-start(bf16[4,40,768]{2,1,0:T(8,128)(2,1)S(1)} %get-tuple-element.107), channel_id=1, source_target_pairs={{0,2},{1,3},{2,0},{3,1},{4,6},{5,7},{6,4},{7,5},{8,10},{9,11},{10,... | collective-permute-start | bytes 737288 | tf_op jit(solution)/shard_map/ppermute | solution.py:17
  57.8 1.5 %collective-permute-start.23 = (bf16[4,40,768]{2,1,0:T(8,128)(2,1)S(1)}, bf16[4,40,768]{2,1,0:T(8,128)(2,1)S(1)}, u32[]{:S(2)}, u32[]{:S(2)}) collective-permute-start(bf16[4,40,768]{2,1,0:T(8,128)(2,1)S(1)} %get-tuple-element.108), channel_id=1, source_target_pairs={{0,4},{1,5},{2,6},{3,7},{4,0},{5,1},{6,2},{7,3},{8,12},{9,13},{10,... | collective-permute-start | bytes 737288 | tf_op jit(solution)/shard_map/ppermute | solution.py:17
  59.3 0.8 collective-permute-start.24
  60.2 3.8 %shard_map.123 = (f32[1,256,768]{2,1,0:T(8,128)S(1)}, f32[1,256,768]{2,1,0:T(8,128)S(1)}, f32[1,768]{1,0:T(1,128)S(1)}) custom-call(bf16[1,192,768]{2,1,0:T(8,128)(2,1)S(1)} %get-tuple-element.79.before_ref, bf16[1,256,768]{2,1,0:T(8,128)(2,1)S(1)} %copy-done.1, bf16[1,192,768]{2,1,0:T(8,128)(2,1)S(1)} %get-tuple-element.80.after_ref, ...), custom_call_target="tpu_custom_call" | custom-call | flops 1 | bytes 1 | tf_op jit(solution)/shard_map/pallas_call | solution.py:38
  64.1 1.1 %collective-permute-done.25 = f32[1,768]{1,0:T(1,128)S(1)} collective-permute-done((f32[1,768]{1,0:T(1,128)S(1)}, f32[1,768]{1,0:T(1,128)S(1)}, u32[]{:S(2)}, u32[]{:S(2)}) %collective-permute-start.25) | collective-permute-done | bytes 3104 | tf_op jit(solution)/shard_map/ppermute | solution.py:17
  65.3 1.1 %collective-permute-start.26 = (f32[1,768]{1,0:T(1,128)S(1)}, f32[1,768]{1,0:T(1,128)S(1)}, u32[]{:S(2)}, u32[]{:S(2)}) collective-permute-start(f32[1,768]{1,0:T(1,128)S(1)} %add.9), channel_id=1, source_target_pairs={{0,2},{1,3},{2,0},{3,1},{4,6},{5,7},{6,4},{7,5},{8,10},{9,11},{10,... | collective-permute-start | bytes 9224 | tf_op jit(solution)/shard_map/ppermute | solution.py:17
  66.4 1.7 %shard_map.124 = (bf16[1,256,768]{2,1,0:T(8,128)(2,1)}, bf16[1,256,768]{2,1,0:T(8,128)(2,1)}) custom-call(f32[1,256,768]{2,1,0:T(8,128)S(1)} %shard_map.118.mixed_ref, bf16[1,256,1152]{2,1,0:T(8,128)(2,1)S(1)} %get-tuple-element.93.hidden_ref, bf16[1152,768]{1,0:T(8,128)(2,1)S(1)} %bitcast.13, f32[1,256,768]{2,1,0:T(8,128)S(1)} %get-tuple-element.97.mixed_grad_ref, ...), custom_call_target="tpu_custom_call" | custom-call | flops 1 | bytes 1 | tf_op jit(solution)/shard_map/pallas_call | solution.py:38
  68.1 2.2 %collective-permute-done.26 = f32[1,768]{1,0:T(1,128)S(1)} collective-permute-done((f32[1,768]{1,0:T(1,128)S(1)}, f32[1,768]{1,0:T(1,128)S(1)}, u32[]{:S(2)}, u32[]{:S(2)}) %collective-permute-start.26) | collective-permute-done | bytes 3104 | tf_op jit(solution)/shard_map/ppermute | solution.py:17
  70.3 1.5 %collective-permute-start.27 = (f32[1,768]{1,0:T(1,128)S(1)}, f32[1,768]{1,0:T(1,128)S(1)}, u32[]{:S(2)}, u32[]{:S(2)}) collective-permute-start(f32[1,768]{1,0:T(1,128)S(1)} %add.10), channel_id=1, source_target_pairs={{0,4},{1,5},{2,6},{3,7},{4,0},{5,1},{6,2},{7,3},{8,12},{9,13},{10,... | collective-permute-start | bytes 9224 | tf_op jit(solution)/shard_map/ppermute | solution.py:17
  71.8 2.1 %collective-permute-done.27 = f32[1,768]{1,0:T(1,128)S(1)} collective-permute-done((f32[1,768]{1,0:T(1,128)S(1)}, f32[1,768]{1,0:T(1,128)S(1)}, u32[]{:S(2)}, u32[]{:S(2)}) %collective-permute-start.27) | collective-permute-done | bytes 3104 | tf_op jit(solution)/shard_map/ppermute | solution.py:17
  74.1 3.4 %collective-permute-start.28 = (bf16[40,768]{1,0:T(8,128)(2,1)S(1)}, bf16[40,768]{1,0:T(8,128)(2,1)S(1)}, u32[]{:S(2)}, u32[]{:S(2)}) collective-permute-start(bf16[40,768]{1,0:T(8,128)(2,1)S(1)} %get-tuple-element.113), channel_id=1, source_target_pairs={{0,8},{1,9},{2,10},{3,11},{4,12},{5,13},{6,14},{7,15},{8,0},{9,1},... | collective-permute-start | bytes 184328 | tf_op jit(solution)/shard_map/ppermute | solution.py:17
  77.4 1.6 %collective-permute-start.29 = (bf16[40,768]{1,0:T(8,128)(2,1)S(1)}, bf16[40,768]{1,0:T(8,128)(2,1)S(1)}, u32[]{:S(2)}, u32[]{:S(2)}) collective-permute-start(bf16[40,768]{1,0:T(8,128)(2,1)S(1)} %get-tuple-element.114), channel_id=1, source_target_pairs={{0,16},{1,17},{2,18},{3,19},{4,20},{5,21},{6,22},{7,23},{8,24},{9,... | collective-permute-start | bytes 184328 | tf_op jit(solution)/shard_map/ppermute | solution.py:17
  79.0 0.9 %collective-permute-start.30 = (bf16[40,768]{1,0:T(8,128)(2,1)S(1)}, bf16[40,768]{1,0:T(8,128)(2,1)S(1)}, u32[]{:S(2)}, u32[]{:S(2)}) collective-permute-start(bf16[40,768]{1,0:T(8,128)(2,1)S(1)} %get-tuple-element.115), channel_id=1, source_target_pairs={{0,24},{1,25},{2,26},{3,27},{4,28},{5,29},{6,30},{7,31},{8,16},{9,... | collective-permute-start | bytes 184328 | tf_op jit(solution)/shard_map/ppermute | solution.py:17
  79.9 0.4 collective-permute-done.28.refs_0_
  80.3 2.9 %collective-permute-done.29.refs_1_ = bf16[40,768]{1,0:T(8,128)(2,1)S(1)} collective-permute-done((bf16[40,768]{1,0:T(8,128)(2,1)S(1)}, bf16[40,768]{1,0:T(8,128)(2,1)S(1)}, u32[]{:S(2)}, u32[]{:S(2)}) %collective-permute-start.29) | collective-permute-done | bytes 61472 | tf_op jit(solution)/shard_map/ppermute | solution.py:17
  83.2 1.8 %collective-permute-done.30.refs_2_ = bf16[40,768]{1,0:T(8,128)(2,1)S(1)} collective-permute-done((bf16[40,768]{1,0:T(8,128)(2,1)S(1)}, bf16[40,768]{1,0:T(8,128)(2,1)S(1)}, u32[]{:S(2)}, u32[]{:S(2)}) %collective-permute-start.30) | collective-permute-done | bytes 61472 | tf_op jit(solution)/shard_map/ppermute | solution.py:17
  85.0 0.7 shard_map.128
  (59 shorter events, 2.8 us)
Async XLA Ops:
  0.6 12.9 %collective-permute-start = (bf16[3,24,768]{2,1,0:T(8,128)(2,1)}, bf16[3,24,768]{2,1,0:T(8,128)(2,1)S(1)}, u32[]{:S(2)}, u32[]{:S(2)}) collective-permute-start(bf16[3,24,768]{2,1,0:T(8,128)(2,1)} %refs_0_.1), channel_id=1, source_target_pairs={{0,16},{1,17},{2,18},{3,19},{4,20},{5,21},{6,22},{7,23},{8,24},{9,... | collective-permute-start | bytes 331784 | tf_op jit(solution)/shard_map/ppermute | solution.py:17
  4.7 6.4 %collective-permute-start.2 = (bf16[24,1152]{1,0:T(8,128)(2,1)}, bf16[24,1152]{1,0:T(8,128)(2,1)S(1)}, u32[]{:S(2)}, u32[]{:S(2)}) collective-permute-start(bf16[24,1152]{1,0:T(8,128)(2,1)} %refs_1_.1), channel_id=1, source_target_pairs={{0,2},{1,3},{2,0},{3,1},{4,6},{5,7},{6,4},{7,5},{8,10},{9,11},{10,... | collective-permute-start | bytes 165896 | tf_op jit(solution)/shard_map/ppermute | solution.py:17
  6.2 5.3 %collective-permute-start.4 = (bf16[24,1152]{1,0:T(8,128)(2,1)}, bf16[24,1152]{1,0:T(8,128)(2,1)S(1)}, u32[]{:S(2)}, u32[]{:S(2)}) collective-permute-start(bf16[24,1152]{1,0:T(8,128)(2,1)} %refs_1_.1), channel_id=1, source_target_pairs={{0,6},{1,7},{2,4},{3,5},{4,2},{5,3},{6,0},{7,1},{8,14},{9,15},{10,... | collective-permute-start | bytes 165896 | tf_op jit(solution)/shard_map/ppermute | solution.py:17
  7.7 4.4 %collective-permute-start.3 = (bf16[24,1152]{1,0:T(8,128)(2,1)}, bf16[24,1152]{1,0:T(8,128)(2,1)S(1)}, u32[]{:S(2)}, u32[]{:S(2)}) collective-permute-start(bf16[24,1152]{1,0:T(8,128)(2,1)} %refs_1_.1), channel_id=1, source_target_pairs={{0,4},{1,5},{2,6},{3,7},{4,0},{5,1},{6,2},{7,3},{8,12},{9,13},{10,... | collective-permute-start | bytes 165896 | tf_op jit(solution)/shard_map/ppermute | solution.py:17
  8.2 5.3 %collective-permute-start.1 = (bf16[36,768]{1,0:T(8,128)(2,1)}, bf16[36,768]{1,0:T(8,128)(2,1)S(1)}, u32[]{:S(2)}, u32[]{:S(2)}) collective-permute-start(bf16[36,768]{1,0:T(8,128)(2,1)} %refs_2_.1), channel_id=1, source_target_pairs={{0,16},{1,17},{2,18},{3,19},{4,20},{5,21},{6,22},{7,23},{8,24},{9,... | collective-permute-start | bytes 165896 | tf_op jit(solution)/shard_map/ppermute | solution.py:17
  8.3 0.9 %copy-start.2 = (bf16[3,24,768]{2,1,0:T(8,128)(2,1)S(1)}, bf16[3,24,768]{2,1,0:T(8,128)(2,1)}, u32[]{:S(2)}) copy-start(bf16[3,24,768]{2,1,0:T(8,128)(2,1)} %refs_0_.1) | copy-start | bytes 331780
  9.2 0.8 copy-start.3
  10.0 0.8 copy-start.4
  13.6 16.5 %collective-permute-start.8 = (bf16[2,112,768]{2,1,0:T(8,128)(2,1)S(1)}, bf16[2,112,768]{2,1,0:T(8,128)(2,1)S(1)}, u32[]{:S(2)}, u32[]{:S(2)}) collective-permute-start(bf16[2,112,768]{2,1,0:T(8,128)(2,1)S(1)} %shard_map.103.refs_0_), channel_id=1, source_target_pairs={{0,8},{1,9},{2,10},{3,11},{4,12},{5,13},{6,14},{7,15},{8,0},{9,1},... | collective-permute-start | bytes 1032200 | tf_op jit(solution)/shard_map/ppermute | solution.py:17
  15.2 14.8 %collective-permute-start.7 = (bf16[2,112,768]{2,1,0:T(8,128)(2,1)S(1)}, bf16[2,112,768]{2,1,0:T(8,128)(2,1)S(1)}, u32[]{:S(2)}, u32[]{:S(2)}) collective-permute-start(bf16[2,112,768]{2,1,0:T(8,128)(2,1)S(1)} %shard_map.103.refs_0_), channel_id=1, source_target_pairs={{0,4},{1,5},{2,6},{3,7},{4,0},{5,1},{6,2},{7,3},{8,12},{9,13},{10,... | collective-permute-start | bytes 1032200 | tf_op jit(solution)/shard_map/ppermute | solution.py:17
  16.7 13.3 %collective-permute-start.6 = (bf16[2,112,768]{2,1,0:T(8,128)(2,1)S(1)}, bf16[2,112,768]{2,1,0:T(8,128)(2,1)S(1)}, u32[]{:S(2)}, u32[]{:S(2)}) collective-permute-start(bf16[2,112,768]{2,1,0:T(8,128)(2,1)S(1)} %shard_map.103.refs_0_), channel_id=1, source_target_pairs={{0,2},{1,3},{2,0},{3,1},{4,6},{5,7},{6,4},{7,5},{8,10},{9,11},{10,... | collective-permute-start | bytes 1032200 | tf_op jit(solution)/shard_map/ppermute | solution.py:17
  18.2 2.1 %copy-start = (bf16[1,256,768]{2,1,0:T(8,128)(2,1)S(1)}, bf16[1,256,768]{2,1,0:T(8,128)(2,1)}, u32[]{:S(2)}) copy-start(bf16[1,256,768]{2,1,0:T(8,128)(2,1)} %tokens_ref.4) | copy-start | bytes 1179652
  18.2 2.1 %copy-start.1 = (bf16[1,256,768]{2,1,0:T(8,128)(2,1)S(1)}, bf16[1,256,768]{2,1,0:T(8,128)(2,1)}, u32[]{:S(2)}) copy-start(bf16[1,256,768]{2,1,0:T(8,128)(2,1)} %cotangent_ref.4) | copy-start | bytes 1179652
  18.3 11.7 %collective-permute-start.5 = (bf16[4,24,1152]{2,1,0:T(8,128)(2,1)S(1)}, bf16[4,24,1152]{2,1,0:T(8,128)(2,1)S(1)}, u32[]{:S(2)}, u32[]{:S(2)}) collective-permute-start(bf16[4,24,1152]{2,1,0:T(8,128)(2,1)S(1)} %shard_map.104.refs_0_), channel_id=1, source_target_pairs={{0,16},{1,17},{2,18},{3,19},{4,20},{5,21},{6,22},{7,23},{8,24},{9,... | collective-permute-start | bytes 663560 | tf_op jit(solution)/shard_map/ppermute | solution.py:17
  20.4 13.1 %collective-permute-start.13 = (bf16[1,192,768]{2,1,0:T(8,128)(2,1)S(1)}, bf16[1,192,768]{2,1,0:T(8,128)(2,1)S(1)}, u32[]{:S(2)}, u32[]{:S(2)}) collective-permute-start(bf16[1,192,768]{2,1,0:T(8,128)(2,1)S(1)} %get-tuple-element.76), channel_id=1, source_target_pairs={{1,2},{3,4},{5,6},{7,8},{9,10},{11,12},{13,14},{15,16},{17,18},{19... | collective-permute-start | bytes 884744 | tf_op jit(solution)/shard_map/ppermute | solution.py:403
  30.1 12.7 %collective-permute-start.11 = (bf16[3,112,768]{2,1,0:T(8,128)(2,1)S(1)}, bf16[3,112,768]{2,1,0:T(8,128)(2,1)S(1)}, u32[]{:S(2)}, u32[]{:S(2)}) collective-permute-start(bf16[3,112,768]{2,1,0:T(8,128)(2,1)S(1)} %shard_map.108), channel_id=1, source_target_pairs={{0,4},{1,5},{2,6},{3,7},{4,0},{5,1},{6,2},{7,3},{8,12},{9,13},{10,... | collective-permute-start | bytes 1548296 | tf_op jit(solution)/shard_map/ppermute | solution.py:17
  30.2 12.6 %collective-permute-start.10 = (bf16[3,112,768]{2,1,0:T(8,128)(2,1)S(1)}, bf16[3,112,768]{2,1,0:T(8,128)(2,1)S(1)}, u32[]{:S(2)}, u32[]{:S(2)}) collective-permute-start(bf16[3,112,768]{2,1,0:T(8,128)(2,1)S(1)} %shard_map.107), channel_id=1, source_target_pairs={{0,2},{1,3},{2,0},{3,1},{4,6},{5,7},{6,4},{7,5},{8,10},{9,11},{10,... | collective-permute-start | bytes 1548296 | tf_op jit(solution)/shard_map/ppermute | solution.py:17
  31.8 11.0 %collective-permute-start.9 = (bf16[8,24,1152]{2,1,0:T(8,128)(2,1)S(1)}, bf16[8,24,1152]{2,1,0:T(8,128)(2,1)S(1)}, u32[]{:S(2)}, u32[]{:S(2)}) collective-permute-start(bf16[8,24,1152]{2,1,0:T(8,128)(2,1)S(1)} %shard_map.105.refs_0_), channel_id=1, source_target_pairs={{0,8},{1,9},{2,10},{3,11},{4,12},{5,13},{6,14},{7,15},{8,0},{9,1},... | collective-permute-start | bytes 1327112 | tf_op jit(solution)/shard_map/ppermute | solution.py:17
  33.5 9.3 %collective-permute-start.12 = (bf16[1,192,768]{2,1,0:T(8,128)(2,1)S(1)}, bf16[1,192,768]{2,1,0:T(8,128)(2,1)S(1)}, u32[]{:S(2)}, u32[]{:S(2)}) collective-permute-start(bf16[1,192,768]{2,1,0:T(8,128)(2,1)S(1)} %get-tuple-element.75), channel_id=1, source_target_pairs={{0,1},{1,0},{2,3},{3,2},{4,5},{5,4},{6,7},{7,6},{8,9},{9,8},{10,11... | collective-permute-start | bytes 884744 | tf_op jit(solution)/shard_map/ppermute | solution.py:17
  33.5 10.9 %copy-start.6 = (f32[768]{0:T(1024)S(1)}, f32[768]{0:T(1024)}, u32[]{:S(2)}) copy-start(f32[768]{0:T(1024)} %param.9) | copy-start | bytes 9220
  42.9 5.5 %collective-permute-start.15 = (bf16[1,112,768]{2,1,0:T(8,128)(2,1)S(1)}, bf16[1,112,768]{2,1,0:T(8,128)(2,1)S(1)}, u32[]{:S(2)}, u32[]{:S(2)}) collective-permute-start(bf16[1,112,768]{2,1,0:T(8,128)(2,1)S(1)} %shard_map.114), channel_id=1, source_target_pairs={{0,4},{1,5},{2,6},{3,7},{4,0},{5,1},{6,2},{7,3},{8,12},{9,13},{10,... | collective-permute-start | bytes 516104 | tf_op jit(solution)/shard_map/ppermute | solution.py:17
  43.4 5.5 %collective-permute-start.16 = (bf16[1,112,768]{2,1,0:T(8,128)(2,1)S(1)}, bf16[1,112,768]{2,1,0:T(8,128)(2,1)S(1)}, u32[]{:S(2)}, u32[]{:S(2)}) collective-permute-start(bf16[1,112,768]{2,1,0:T(8,128)(2,1)S(1)} %shard_map.115), channel_id=1, source_target_pairs={{0,2},{1,3},{2,0},{3,1},{4,6},{5,7},{6,4},{7,5},{8,10},{9,11},{10,... | collective-permute-start | bytes 516104 | tf_op jit(solution)/shard_map/ppermute | solution.py:17
  44.4 1.1 %copy-start.5 = (s32[4]{0:T(128)S(1)}, s32[4]{0:T(128)}, u32[]{:S(2)}) copy-start(s32[4]{0:T(128)} %starts_ref.3) | copy-start | bytes 52
  44.6 7.6 %collective-permute-start.18 = (bf16[14,40,768]{2,1,0:T(8,128)(2,1)S(1)}, bf16[14,40,768]{2,1,0:T(8,128)(2,1)S(1)}, u32[]{:S(2)}, u32[]{:S(2)}) collective-permute-start(bf16[14,40,768]{2,1,0:T(8,128)(2,1)S(1)} %get-tuple-element.89.refs_0_), channel_id=1, source_target_pairs={{0,1},{1,0},{2,3},{3,2},{4,5},{5,4},{6,7},{7,6},{8,9},{9,8},{10,11... | collective-permute-start | bytes 2580488 | tf_op jit(solution)/shard_map/ppermute | solution.py:17
  44.7 4.9 %collective-permute-start.20 = (bf16[16,24,1152]{2,1,0:T(8,128)(2,1)S(1)}, bf16[16,24,1152]{2,1,0:T(8,128)(2,1)S(1)}, u32[]{:S(2)}, u32[]{:S(2)}) collective-permute-start(bf16[16,24,1152]{2,1,0:T(8,128)(2,1)S(1)} %shard_map.106.refs_0_), channel_id=1, source_target_pairs={{0,1},{1,0},{2,3},{3,2},{4,5},{5,4},{6,7},{7,6},{8,9},{9,8},{10,11... | collective-permute-start | bytes 2654216 | tf_op jit(solution)/shard_map/ppermute | solution.py:17
  45.2 5.7 %collective-permute-start.14 = (bf16[14,72,768]{2,1,0:T(8,128)(2,1)S(1)}, bf16[14,72,768]{2,1,0:T(8,128)(2,1)S(1)}, u32[]{:S(2)}, u32[]{:S(2)}) collective-permute-start(bf16[14,72,768]{2,1,0:T(8,128)(2,1)S(1)} %get-tuple-element.86.refs_0_), channel_id=1, source_target_pairs={{0,1},{1,0},{2,3},{3,2},{4,5},{5,4},{6,7},{7,6},{8,9},{9,8},{10,11... | collective-permute-start | bytes 4644872 | tf_op jit(solution)/shard_map/ppermute | solution.py:17
  48.9 1.9 %collective-permute-start.17 = (bf16[2,72,768]{2,1,0:T(8,128)(2,1)S(1)}, bf16[2,72,768]{2,1,0:T(8,128)(2,1)S(1)}, u32[]{:S(2)}, u32[]{:S(2)}) collective-permute-start(bf16[2,72,768]{2,1,0:T(8,128)(2,1)S(1)} %get-tuple-element.88.refs_2_), channel_id=1, source_target_pairs={{0,1},{1,0},{2,3},{3,2},{4,5},{5,4},{6,7},{7,6},{8,9},{9,8},{10,11... | collective-permute-start | bytes 663560 | tf_op jit(solution)/shard_map/ppermute | solution.py:17
  49.0 3.2 %collective-permute-start.19 = (bf16[2,40,768]{2,1,0:T(8,128)(2,1)S(1)}, bf16[2,40,768]{2,1,0:T(8,128)(2,1)S(1)}, u32[]{:S(2)}, u32[]{:S(2)}) collective-permute-start(bf16[2,40,768]{2,1,0:T(8,128)(2,1)S(1)} %get-tuple-element.90.refs_2_), channel_id=1, source_target_pairs={{0,1},{1,0},{2,3},{3,2},{4,5},{5,4},{6,7},{7,6},{8,9},{9,8},{10,11... | collective-permute-start | bytes 368648 | tf_op jit(solution)/shard_map/ppermute | solution.py:17
  53.8 2.6 %collective-permute-start.21 = (bf16[4,2,2,40,768]{4,3,2,1,0:T(8,128)(2,1)S(1)}, bf16[4,2,2,40,768]{4,3,2,1,0:T(8,128)(2,1)S(1)}, u32[]{:S(2)}, u32[]{:S(2)}) collective-permute-start(bf16[4,2,2,40,768]{4,3,2,1,0:T(8,128)(2,1)S(1)} %get-tuple-element.104), channel_id=1, source_target_pairs={{0,1},{1,0},{2,3},{3,2},{4,5},{5,4},{6,7},{7,6},{8,9},{9,8},{10,11... | collective-permute-start | bytes 2949128 | tf_op jit(solution)/shard_map/ppermute | solution.py:17
  56.6 17.2 %collective-permute-start.22 = (bf16[4,40,768]{2,1,0:T(8,128)(2,1)S(1)}, bf16[4,40,768]{2,1,0:T(8,128)(2,1)S(1)}, u32[]{:S(2)}, u32[]{:S(2)}) collective-permute-start(bf16[4,40,768]{2,1,0:T(8,128)(2,1)S(1)} %get-tuple-element.107), channel_id=1, source_target_pairs={{0,2},{1,3},{2,0},{3,1},{4,6},{5,7},{6,4},{7,5},{8,10},{9,11},{10,... | collective-permute-start | bytes 737288 | tf_op jit(solution)/shard_map/ppermute | solution.py:17
  57.8 16.1 %collective-permute-start.23 = (bf16[4,40,768]{2,1,0:T(8,128)(2,1)S(1)}, bf16[4,40,768]{2,1,0:T(8,128)(2,1)S(1)}, u32[]{:S(2)}, u32[]{:S(2)}) collective-permute-start(bf16[4,40,768]{2,1,0:T(8,128)(2,1)S(1)} %get-tuple-element.108), channel_id=1, source_target_pairs={{0,4},{1,5},{2,6},{3,7},{4,0},{5,1},{6,2},{7,3},{8,12},{9,13},{10,... | collective-permute-start | bytes 737288 | tf_op jit(solution)/shard_map/ppermute | solution.py:17
  59.3 14.5 %collective-permute-start.24 = (bf16[4,40,768]{2,1,0:T(8,128)(2,1)S(1)}, bf16[4,40,768]{2,1,0:T(8,128)(2,1)S(1)}, u32[]{:S(2)}, u32[]{:S(2)}) collective-permute-start(bf16[4,40,768]{2,1,0:T(8,128)(2,1)S(1)} %get-tuple-element.109), channel_id=1, source_target_pairs={{0,6},{1,7},{2,4},{3,5},{4,2},{5,3},{6,0},{7,1},{8,14},{9,15},{10,... | collective-permute-start | bytes 737288 | tf_op jit(solution)/shard_map/ppermute | solution.py:17
  64.0 1.2 %collective-permute-start.25 = (f32[1,768]{1,0:T(1,128)S(1)}, f32[1,768]{1,0:T(1,128)S(1)}, u32[]{:S(2)}, u32[]{:S(2)}) collective-permute-start(f32[1,768]{1,0:T(1,128)S(1)} %get-tuple-element.110), channel_id=1, source_target_pairs={{0,1},{1,0},{2,3},{3,2},{4,5},{5,4},{6,7},{7,6},{8,9},{9,8},{10,11... | collective-permute-start | bytes 9224 | tf_op jit(solution)/shard_map/ppermute | solution.py:17
  65.3 5.0 %collective-permute-start.26 = (f32[1,768]{1,0:T(1,128)S(1)}, f32[1,768]{1,0:T(1,128)S(1)}, u32[]{:S(2)}, u32[]{:S(2)}) collective-permute-start(f32[1,768]{1,0:T(1,128)S(1)} %add.9), channel_id=1, source_target_pairs={{0,2},{1,3},{2,0},{3,1},{4,6},{5,7},{6,4},{7,5},{8,10},{9,11},{10,... | collective-permute-start | bytes 9224 | tf_op jit(solution)/shard_map/ppermute | solution.py:17
  70.3 3.6 %collective-permute-start.27 = (f32[1,768]{1,0:T(1,128)S(1)}, f32[1,768]{1,0:T(1,128)S(1)}, u32[]{:S(2)}, u32[]{:S(2)}) collective-permute-start(f32[1,768]{1,0:T(1,128)S(1)} %add.10), channel_id=1, source_target_pairs={{0,4},{1,5},{2,6},{3,7},{4,0},{5,1},{6,2},{7,3},{8,12},{9,13},{10,... | collective-permute-start | bytes 9224 | tf_op jit(solution)/shard_map/ppermute | solution.py:17
  74.1 6.2 %collective-permute-start.28 = (bf16[40,768]{1,0:T(8,128)(2,1)S(1)}, bf16[40,768]{1,0:T(8,128)(2,1)S(1)}, u32[]{:S(2)}, u32[]{:S(2)}) collective-permute-start(bf16[40,768]{1,0:T(8,128)(2,1)S(1)} %get-tuple-element.113), channel_id=1, source_target_pairs={{0,8},{1,9},{2,10},{3,11},{4,12},{5,13},{6,14},{7,15},{8,0},{9,1},... | collective-permute-start | bytes 184328 | tf_op jit(solution)/shard_map/ppermute | solution.py:17
  77.4 5.8 %collective-permute-start.29 = (bf16[40,768]{1,0:T(8,128)(2,1)S(1)}, bf16[40,768]{1,0:T(8,128)(2,1)S(1)}, u32[]{:S(2)}, u32[]{:S(2)}) collective-permute-start(bf16[40,768]{1,0:T(8,128)(2,1)S(1)} %get-tuple-element.114), channel_id=1, source_target_pairs={{0,16},{1,17},{2,18},{3,19},{4,20},{5,21},{6,22},{7,23},{8,24},{9,... | collective-permute-start | bytes 184328 | tf_op jit(solution)/shard_map/ppermute | solution.py:17
  79.0 6.0 %collective-permute-start.30 = (bf16[40,768]{1,0:T(8,128)(2,1)S(1)}, bf16[40,768]{1,0:T(8,128)(2,1)S(1)}, u32[]{:S(2)}, u32[]{:S(2)}) collective-permute-start(bf16[40,768]{1,0:T(8,128)(2,1)S(1)} %get-tuple-element.115), channel_id=1, source_target_pairs={{0,24},{1,25},{2,26},{3,27},{4,28},{5,29},{6,30},{7,31},{8,16},{9,... | collective-permute-start | bytes 184328 | tf_op jit(solution)/shard_map/ppermute | solution.py:17

commit v6 on v5

--- a/solution.py
+++ b/solution.py
@@ -577,7 +577,7 @@
             to_y = join_parts((part, 0, count), (old_x, 0, old // 2))
         by_x, by_y, received = swap(to_x, 2), swap(to_y, 4), swap(up_held, mask)
         other = swap(inner, 1) if next_mask is None else swap(held, next_mask)
-        up_held = join(up_held, received)
+        up_held = join(up_held, received, cost=1 if next_mask is None else 1_500_000_000)
         if next_mask is None:
             outer = stack([outer], cost=THIRD)
         phase = (part, held, up_held, by_x, by_y, other)
@@ -717,7 +717,7 @@
     slope = slopes(taps, before, after_, conv, up, pre, share)
     keep, send = relative_blocks(total)
     down = assemble_down(down_pieces, down_weight.shape[0])
-    own_line, *others = chip_sums(keep, after(swap(send, 1), slope, down))
+    own_line, *others = chip_sums(keep, after(swap(send, 1), down))
     received = [swap(v, mask) for v, mask in zip(others, (2, 4, 6))]
     mixed_grad, normed_grad, gain_term = backward(
         before, cotangent, after_, slope, down, up, conv, scaled, contig_first_bins

time: 86 us -> 85.9 us (level)
  starting transfers between devices: 33.4 us -> 31.4 us
  waiting for transfers between devices: 34.6 us -> 36.4 us
    ppermute x30, starting transfers between devices: 32.7 us -> 30.7 us  [swap(): return lax.ppermute(value, 'ctx', [(i, i ^ mask) for i in range(devices)])]
    ppermute x30, waiting for transfers between devices: 34.6 us -> 36.4 us  [swap(): return lax.ppermute(value, 'ctx', [(i, i ^ mask) for i in range(devices)])]
  transfers between devices with their start and end apart: 31 -> 31, of which waited for: 15 -> 18; matrix products, arithmetic and copies ran while one was open for 0% -> 0% of each run, Pallas kernels for 14% -> 14%
where the time goes in v6:
time: 85.9 us; the launch traced here: 85.6 us
  waiting for transfers between devices  36.4 us (42%)
  starting transfers between devices  31.4 us (37%)
  Pallas kernels  14.3 us (17%)
  local copies, waits for them, and re-layouts  2.56 us (3%)
  between operations  0.93 us (1%)
    ppermute x30, waiting for transfers between devices, swap(): return lax.ppermute(value, 'ctx', [(i, i ^ mask) for i in range(devices)])  36.4 us
    ppermute x30, starting transfers between devices, swap(): return lax.ppermute(value, 'ctx', [(i, i ^ mask) for i in range(devices)])  30.7 us
    pallas_call x26, Pallas kernels, call(): pl.pallas_call(kernel, out_shape=shapes, in_specs=[SMEM if i in smem else...  14 us
    unnamed x14, local copies, waits for them, and re-layouts  2.56 us
  transfers between devices with their start and end apart: 31, of which 18 were waited for; matrix products, arithmetic and copies ran while one was open for 0% of the time, Pallas kernels for 14%

profile of v6, /device:TPU:0, one launch (start us, length us, event | category | flops | bytes accessed | tf_op | source)
XLA Modules:
  0.0 85.6 jit_solution(5443525232676212827)
XLA Ops:
  0.6 4.1 %collective-permute-start = (bf16[3,24,768]{2,1,0:T(8,128)(2,1)}, bf16[3,24,768]{2,1,0:T(8,128)(2,1)S(1)}, u32[]{:S(2)}, u32[]{:S(2)}) collective-permute-start(bf16[3,24,768]{2,1,0:T(8,128)(2,1)} %refs_0_.1), channel_id=1, source_target_pairs={{0,16},{1,17},{2,18},{3,19},{4,20},{5,21},{6,22},{7,23},{8,24},{9,... | collective-permute-start | bytes 331784 | tf_op jit(solution)/shard_map/ppermute | solution.py:17
  4.7 1.5 %collective-permute-start.2 = (bf16[24,1152]{1,0:T(8,128)(2,1)}, bf16[24,1152]{1,0:T(8,128)(2,1)S(1)}, u32[]{:S(2)}, u32[]{:S(2)}) collective-permute-start(bf16[24,1152]{1,0:T(8,128)(2,1)} %refs_1_.1), channel_id=1, source_target_pairs={{0,2},{1,3},{2,0},{3,1},{4,6},{5,7},{6,4},{7,5},{8,10},{9,11},{10,... | collective-permute-start | bytes 165896 | tf_op jit(solution)/shard_map/ppermute | solution.py:17
  6.2 1.5 %collective-permute-start.4 = (bf16[24,1152]{1,0:T(8,128)(2,1)}, bf16[24,1152]{1,0:T(8,128)(2,1)S(1)}, u32[]{:S(2)}, u32[]{:S(2)}) collective-permute-start(bf16[24,1152]{1,0:T(8,128)(2,1)} %refs_1_.1), channel_id=1, source_target_pairs={{0,6},{1,7},{2,4},{3,5},{4,2},{5,3},{6,0},{7,1},{8,14},{9,15},{10,... | collective-permute-start | bytes 165896 | tf_op jit(solution)/shard_map/ppermute | solution.py:17
  7.7 0.5 collective-permute-start.3
  8.3 0.9 %copy-done.2 = bf16[3,24,768]{2,1,0:T(8,128)(2,1)S(1)} copy-done((bf16[3,24,768]{2,1,0:T(8,128)(2,1)S(1)}, bf16[3,24,768]{2,1,0:T(8,128)(2,1)}, u32[]{:S(2)}) %copy-start.2) | copy-done | bytes 110616
  9.2 0.8 copy-done.3
  10.0 0.8 copy-done.4
  11.1 0.3 collective-permute-done.4.refs_3_
  11.5 0.6 collective-permute-done.3.refs_2_
  12.1 1.5 %collective-permute-done.1.refs_3_ = bf16[36,768]{1,0:T(8,128)(2,1)S(1)} collective-permute-done((bf16[36,768]{1,0:T(8,128)(2,1)}, bf16[36,768]{1,0:T(8,128)(2,1)S(1)}, u32[]{:S(2)}, u32[]{:S(2)}) %collective-permute-start.1) | collective-permute-done | bytes 55328 | tf_op jit(solution)/shard_map/ppermute | solution.py:17
  13.6 0.5 collective-permute-start.5
  14.2 3.1 %collective-permute-start.8 = (bf16[2,112,768]{2,1,0:T(8,128)(2,1)S(1)}, bf16[2,112,768]{2,1,0:T(8,128)(2,1)S(1)}, u32[]{:S(2)}, u32[]{:S(2)}) collective-permute-start(bf16[2,112,768]{2,1,0:T(8,128)(2,1)S(1)} %shard_map.103.refs_0_), channel_id=1, source_target_pairs={{0,8},{1,9},{2,10},{3,11},{4,12},{5,13},{6,14},{7,15},{8,0},{9,1},... | collective-permute-start | bytes 1032200 | tf_op jit(solution)/shard_map/ppermute | solution.py:17
  17.3 1.5 %collective-permute-start.7 = (bf16[2,112,768]{2,1,0:T(8,128)(2,1)S(1)}, bf16[2,112,768]{2,1,0:T(8,128)(2,1)S(1)}, u32[]{:S(2)}, u32[]{:S(2)}) collective-permute-start(bf16[2,112,768]{2,1,0:T(8,128)(2,1)S(1)} %shard_map.103.refs_0_), channel_id=1, source_target_pairs={{0,4},{1,5},{2,6},{3,7},{4,0},{5,1},{6,2},{7,3},{8,12},{9,13},{10,... | collective-permute-start | bytes 1032200 | tf_op jit(solution)/shard_map/ppermute | solution.py:17
  18.8 1.5 %collective-permute-start.6 = (bf16[2,112,768]{2,1,0:T(8,128)(2,1)S(1)}, bf16[2,112,768]{2,1,0:T(8,128)(2,1)S(1)}, u32[]{:S(2)}, u32[]{:S(2)}) collective-permute-start(bf16[2,112,768]{2,1,0:T(8,128)(2,1)S(1)} %shard_map.103.refs_0_), channel_id=1, source_target_pairs={{0,2},{1,3},{2,0},{3,1},{4,6},{5,7},{6,4},{7,5},{8,10},{9,11},{10,... | collective-permute-start | bytes 1032200 | tf_op jit(solution)/shard_map/ppermute | solution.py:17
  20.4 0.7 collective-permute-start.13
  21.0 3.7 %collective-permute-done.5.refs_1_ = bf16[4,24,1152]{2,1,0:T(8,128)(2,1)S(1)} collective-permute-done((bf16[4,24,1152]{2,1,0:T(8,128)(2,1)S(1)}, bf16[4,24,1152]{2,1,0:T(8,128)(2,1)S(1)}, u32[]{:S(2)}, u32[]{:S(2)}) %collective-permute-start.5) | collective-permute-done | bytes 221216 | tf_op jit(solution)/shard_map/ppermute | solution.py:17
  24.8 2.9 %collective-permute-done.8.refs_0_.refs_5_ = bf16[2,112,768]{2,1,0:T(8,128)(2,1)S(1)} collective-permute-done((bf16[2,112,768]{2,1,0:T(8,128)(2,1)S(1)}, bf16[2,112,768]{2,1,0:T(8,128)(2,1)S(1)}, u32[]{:S(2)}, u32[]{:S(2)}) %collective-permute-start.8) | collective-permute-done | bytes 344096 | tf_op jit(solution)/shard_map/ppermute | solution.py:17
  27.6 4.4 %collective-permute-done.6.refs_1_ = bf16[2,112,768]{2,1,0:T(8,128)(2,1)S(1)} collective-permute-done((bf16[2,112,768]{2,1,0:T(8,128)(2,1)S(1)}, bf16[2,112,768]{2,1,0:T(8,128)(2,1)S(1)}, u32[]{:S(2)}, u32[]{:S(2)}) %collective-permute-start.6) | collective-permute-done | bytes 344096 | tf_op jit(solution)/shard_map/ppermute | solution.py:17
  32.1 2.5 %collective-permute-start.10 = (bf16[3,112,768]{2,1,0:T(8,128)(2,1)S(1)}, bf16[3,112,768]{2,1,0:T(8,128)(2,1)S(1)}, u32[]{:S(2)}, u32[]{:S(2)}) collective-permute-start(bf16[3,112,768]{2,1,0:T(8,128)(2,1)S(1)} %shard_map.107), channel_id=1, source_target_pairs={{0,2},{1,3},{2,0},{3,1},{4,6},{5,7},{6,4},{7,5},{8,10},{9,11},{10,... | collective-permute-start | bytes 1548296 | tf_op jit(solution)/shard_map/ppermute | solution.py:17
  34.8 8.2 %collective-permute-done.9.refs_1_ = bf16[8,24,1152]{2,1,0:T(8,128)(2,1)S(1)} collective-permute-done((bf16[8,24,1152]{2,1,0:T(8,128)(2,1)S(1)}, bf16[8,24,1152]{2,1,0:T(8,128)(2,1)S(1)}, u32[]{:S(2)}, u32[]{:S(2)}) %collective-permute-start.9) | collective-permute-done | bytes 442400 | tf_op jit(solution)/shard_map/ppermute | solution.py:17
  43.1 2.3 %collective-permute-done.10.refs_4_.refs_6_.refs_0_ = bf16[3,112,768]{2,1,0:T(8,128)(2,1)S(1)} collective-permute-done((bf16[3,112,768]{2,1,0:T(8,128)(2,1)S(1)}, bf16[3,112,768]{2,1,0:T(8,128)(2,1)S(1)}, u32[]{:S(2)}, u32[]{:S(2)}) %collective-permute-start.10) | collective-permute-done | bytes 516128 | tf_op jit(solution)/shard_map/ppermute | solution.py:17
  45.5 2.0 %collective-permute-start.16 = (bf16[1,112,768]{2,1,0:T(8,128)(2,1)S(1)}, bf16[1,112,768]{2,1,0:T(8,128)(2,1)S(1)}, u32[]{:S(2)}, u32[]{:S(2)}) collective-permute-start(bf16[1,112,768]{2,1,0:T(8,128)(2,1)S(1)} %shard_map.115), channel_id=1, source_target_pairs={{0,2},{1,3},{2,0},{3,1},{4,6},{5,7},{6,4},{7,5},{8,10},{9,11},{10,... | collective-permute-start | bytes 516104 | tf_op jit(solution)/shard_map/ppermute | solution.py:17
  47.8 0.5 collective-permute-start.20
  48.6 1.3 %shard_map.112 = (bf16[1,384,2304]{2,1,0:T(8,128)(2,1)S(1)}, f32[1,256,768]{2,1,0:T(8,128)S(1)}, f32[1,256,1]{2,1,0:T(8,128)S(1)}) custom-call(bf16[1,192,768]{2,1,0:T(8,128)(2,1)S(1)} %get-tuple-element.79.before_ref, bf16[1,256,768]{2,1,0:T(8,128)(2,1)S(1)} %copy-done, bf16[1,192,768]{2,1,0:T(8,128)(2,1)S(1)} %get-tuple-element.80.after_ref, ...), custom_call_target="tpu_custom_call" | custom-call | flops 1 | bytes 1 | tf_op jit(solution)/shard_map/pallas_call | solution.py:38
  49.8 1.0 %collective-permute-done.15.refs_0_ = bf16[1,112,768]{2,1,0:T(8,128)(2,1)S(1)} collective-permute-done((bf16[1,112,768]{2,1,0:T(8,128)(2,1)S(1)}, bf16[1,112,768]{2,1,0:T(8,128)(2,1)S(1)}, u32[]{:S(2)}, u32[]{:S(2)}) %collective-permute-start.15) | collective-permute-done | bytes 172064 | tf_op jit(solution)/shard_map/ppermute | solution.py:17
  51.0 0.5 collective-permute-start.19
  51.7 2.2 %collective-permute-done.17.refs_3_ = bf16[2,72,768]{2,1,0:T(8,128)(2,1)S(1)} collective-permute-done((bf16[2,72,768]{2,1,0:T(8,128)(2,1)S(1)}, bf16[2,72,768]{2,1,0:T(8,128)(2,1)S(1)}, u32[]{:S(2)}, u32[]{:S(2)}) %collective-permute-start.17) | collective-permute-done | bytes 221216 | tf_op jit(solution)/shard_map/ppermute | solution.py:17
  54.2 1.1 %shard_map.118.mixed_ref = f32[1,256,768]{2,1,0:T(8,128)S(1)} custom-call(bf16[1,384,2304]{2,1,0:T(8,128)(2,1)S(1)} %get-tuple-element.81.taps_ref, bf16[1,256,768]{2,1,0:T(8,128)(2,1)S(1)} %copy-done, bf16[2304,768]{1,0:T(8,128)(2,1)S(1)} %bitcast.6), custom_call_target="tpu_custom_call" | custom-call | flops 1 | bytes 1 | tf_op jit(solution)/shard_map/pallas_call | solution.py:38
  55.3 1.3 %shard_map.120 = (f32[1,256,1152]{2,1,0:T(8,128)S(1)}, f32[1,256,1152]{2,1,0:T(8,128)S(1)}, bf16[1,256,1152]{2,1,0:T(8,128)(2,1)S(1)}, f32[1152,768]{1,0:T(8,128)S(1)}) custom-call(f32[1,256,768]{2,1,0:T(8,128)S(1)} %shard_map.118.mixed_ref, bf16[768,1152]{1,0:T(8,128)(2,1)S(1)} %bitcast.9, bf16[1,256,768]{2,1,0:T(8,128)(2,1)S(1)} %copy-done.1), custom_call_target="tpu_custom_call" | custom-call | flops 1 | bytes 1 | tf_op jit(solution)/shard_map/pallas_call | solution.py:38
  57.1 0.6 shard_map.121
  57.7 1.8 %collective-permute-done.21.received_ref = bf16[4,2,2,40,768]{4,3,2,1,0:T(8,128)(2,1)S(1)} collective-permute-done((bf16[4,2,2,40,768]{4,3,2,1,0:T(8,128)(2,1)S(1)}, bf16[4,2,2,40,768]{4,3,2,1,0:T(8,128)(2,1)S(1)}, u32[]{:S(2)}, u32[]{:S(2)}) %collective-permute-start.21) | collective-permute-done | bytes 983072 | tf_op jit(solution)/shard_map/ppermute | solution.py:17
  59.7 0.6 collective-permute-start.22
  60.3 1.5 %collective-permute-start.23 = (bf16[4,40,768]{2,1,0:T(8,128)(2,1)S(1)}, bf16[4,40,768]{2,1,0:T(8,128)(2,1)S(1)}, u32[]{:S(2)}, u32[]{:S(2)}) collective-permute-start(bf16[4,40,768]{2,1,0:T(8,128)(2,1)S(1)} %get-tuple-element.108), channel_id=1, source_target_pairs={{0,4},{1,5},{2,6},{3,7},{4,0},{5,1},{6,2},{7,3},{8,12},{9,13},{10,... | collective-permute-start | bytes 737288 | tf_op jit(solution)/shard_map/ppermute | solution.py:17
  61.9 1.4 %collective-permute-start.24 = (bf16[4,40,768]{2,1,0:T(8,128)(2,1)S(1)}, bf16[4,40,768]{2,1,0:T(8,128)(2,1)S(1)}, u32[]{:S(2)}, u32[]{:S(2)}) collective-permute-start(bf16[4,40,768]{2,1,0:T(8,128)(2,1)S(1)} %get-tuple-element.109), channel_id=1, source_target_pairs={{0,6},{1,7},{2,4},{3,5},{4,2},{5,3},{6,0},{7,1},{8,14},{9,15},{10,... | collective-permute-start | bytes 737288 | tf_op jit(solution)/shard_map/ppermute | solution.py:17
  63.3 1.8 %shard_map.122.slope_ref = f32[1,384,1152]{2,1,0:T(8,128)S(1)} custom-call(bf16[1,384,2304]{2,1,0:T(8,128)(2,1)S(1)} %get-tuple-element.81.taps_ref, bf16[1,192,768]{2,1,0:T(8,128)(2,1)S(1)} %get-tuple-element.79.before_ref, bf16[1,192,768]{2,1,0:T(8,128)(2,1)S(1)} %get-tuple-element.80.after_ref, bf16[2304,768]{1,0:T(8,128)(2,1)S(1)} %bitcast.7, ...), custom_call_target="tpu_custom_call" | custom-call | flops 1 | bytes 1 | tf_op jit(solution)/shard_map/pallas_call | solution.py:38
  65.0 3.8 %shard_map.123 = (f32[1,256,768]{2,1,0:T(8,128)S(1)}, f32[1,256,768]{2,1,0:T(8,128)S(1)}, f32[1,768]{1,0:T(1,128)S(1)}) custom-call(bf16[1,192,768]{2,1,0:T(8,128)(2,1)S(1)} %get-tuple-element.79.before_ref, bf16[1,256,768]{2,1,0:T(8,128)(2,1)S(1)} %copy-done.1, bf16[1,192,768]{2,1,0:T(8,128)(2,1)S(1)} %get-tuple-element.80.after_ref, ...), custom_call_target="tpu_custom_call" | custom-call | flops 1 | bytes 1 | tf_op jit(solution)/shard_map/pallas_call | solution.py:38
  69.0 1.1 %collective-permute-done.25 = f32[1,768]{1,0:T(1,128)S(1)} collective-permute-done((f32[1,768]{1,0:T(1,128)S(1)}, f32[1,768]{1,0:T(1,128)S(1)}, u32[]{:S(2)}, u32[]{:S(2)}) %collective-permute-start.25) | collective-permute-done | bytes 3104 | tf_op jit(solution)/shard_map/ppermute | solution.py:17
  70.1 0.5 collective-permute-start.26
  70.7 1.7 %shard_map.124 = (bf16[1,256,768]{2,1,0:T(8,128)(2,1)}, bf16[1,256,768]{2,1,0:T(8,128)(2,1)}) custom-call(f32[1,256,768]{2,1,0:T(8,128)S(1)} %shard_map.118.mixed_ref, bf16[1,256,1152]{2,1,0:T(8,128)(2,1)S(1)} %get-tuple-element.93.hidden_ref, bf16[1152,768]{1,0:T(8,128)(2,1)S(1)} %bitcast.13, f32[1,256,768]{2,1,0:T(8,128)S(1)} %get-tuple-element.97.mixed_grad_ref, ...), custom_call_target="tpu_custom_call" | custom-call | flops 1 | bytes 1 | tf_op jit(solution)/shard_map/pallas_call | solution.py:38
  72.4 1.4 %collective-permute-done.26 = f32[1,768]{1,0:T(1,128)S(1)} collective-permute-done((f32[1,768]{1,0:T(1,128)S(1)}, f32[1,768]{1,0:T(1,128)S(1)}, u32[]{:S(2)}, u32[]{:S(2)}) %collective-permute-start.26) | collective-permute-done | bytes 3104 | tf_op jit(solution)/shard_map/ppermute | solution.py:17
  73.7 1.5 %collective-permute-start.27 = (f32[1,768]{1,0:T(1,128)S(1)}, f32[1,768]{1,0:T(1,128)S(1)}, u32[]{:S(2)}, u32[]{:S(2)}) collective-permute-start(f32[1,768]{1,0:T(1,128)S(1)} %add.10), channel_id=1, source_target_pairs={{0,4},{1,5},{2,6},{3,7},{4,0},{5,1},{6,2},{7,3},{8,12},{9,13},{10,... | collective-permute-start | bytes 9224 | tf_op jit(solution)/shard_map/ppermute | solution.py:17
  75.3 2.1 %collective-permute-done.27 = f32[1,768]{1,0:T(1,128)S(1)} collective-permute-done((f32[1,768]{1,0:T(1,128)S(1)}, f32[1,768]{1,0:T(1,128)S(1)}, u32[]{:S(2)}, u32[]{:S(2)}) %collective-permute-start.27) | collective-permute-done | bytes 3104 | tf_op jit(solution)/shard_map/ppermute | solution.py:17
  77.5 0.5 collective-permute-start.28
  78.0 0.8 collective-permute-start.29
  78.8 3.2 %collective-permute-start.30 = (bf16[40,768]{1,0:T(8,128)(2,1)S(1)}, bf16[40,768]{1,0:T(8,128)(2,1)S(1)}, u32[]{:S(2)}, u32[]{:S(2)}) collective-permute-start(bf16[40,768]{1,0:T(8,128)(2,1)S(1)} %get-tuple-element.115), channel_id=1, source_target_pairs={{0,24},{1,25},{2,26},{3,27},{4,28},{5,29},{6,30},{7,31},{8,16},{9,... | collective-permute-start | bytes 184328 | tf_op jit(solution)/shard_map/ppermute | solution.py:17
  82.1 1.1 %collective-permute-done.29.refs_1_ = bf16[40,768]{1,0:T(8,128)(2,1)S(1)} collective-permute-done((bf16[40,768]{1,0:T(8,128)(2,1)S(1)}, bf16[40,768]{1,0:T(8,128)(2,1)S(1)}, u32[]{:S(2)}, u32[]{:S(2)}) %collective-permute-start.29) | collective-permute-done | bytes 61472 | tf_op jit(solution)/shard_map/ppermute | solution.py:17
  83.2 1.8 %collective-permute-done.30.refs_2_ = bf16[40,768]{1,0:T(8,128)(2,1)S(1)} collective-permute-done((bf16[40,768]{1,0:T(8,128)(2,1)S(1)}, bf16[40,768]{1,0:T(8,128)(2,1)S(1)}, u32[]{:S(2)}, u32[]{:S(2)}) %collective-permute-start.30) | collective-permute-done | bytes 61472 | tf_op jit(solution)/shard_map/ppermute | solution.py:17
  84.9 0.7 shard_map.128
  (59 shorter events, 3.1 us)
Async XLA Ops:
  0.6 12.9 %collective-permute-start = (bf16[3,24,768]{2,1,0:T(8,128)(2,1)}, bf16[3,24,768]{2,1,0:T(8,128)(2,1)S(1)}, u32[]{:S(2)}, u32[]{:S(2)}) collective-permute-start(bf16[3,24,768]{2,1,0:T(8,128)(2,1)} %refs_0_.1), channel_id=1, source_target_pairs={{0,16},{1,17},{2,18},{3,19},{4,20},{5,21},{6,22},{7,23},{8,24},{9,... | collective-permute-start | bytes 331784 | tf_op jit(solution)/shard_map/ppermute | solution.py:17
  4.7 6.4 %collective-permute-start.2 = (bf16[24,1152]{1,0:T(8,128)(2,1)}, bf16[24,1152]{1,0:T(8,128)(2,1)S(1)}, u32[]{:S(2)}, u32[]{:S(2)}) collective-permute-start(bf16[24,1152]{1,0:T(8,128)(2,1)} %refs_1_.1), channel_id=1, source_target_pairs={{0,2},{1,3},{2,0},{3,1},{4,6},{5,7},{6,4},{7,5},{8,10},{9,11},{10,... | collective-permute-start | bytes 165896 | tf_op jit(solution)/shard_map/ppermute | solution.py:17
  6.2 5.3 %collective-permute-start.4 = (bf16[24,1152]{1,0:T(8,128)(2,1)}, bf16[24,1152]{1,0:T(8,128)(2,1)S(1)}, u32[]{:S(2)}, u32[]{:S(2)}) collective-permute-start(bf16[24,1152]{1,0:T(8,128)(2,1)} %refs_1_.1), channel_id=1, source_target_pairs={{0,6},{1,7},{2,4},{3,5},{4,2},{5,3},{6,0},{7,1},{8,14},{9,15},{10,... | collective-permute-start | bytes 165896 | tf_op jit(solution)/shard_map/ppermute | solution.py:17
  7.7 4.4 %collective-permute-start.3 = (bf16[24,1152]{1,0:T(8,128)(2,1)}, bf16[24,1152]{1,0:T(8,128)(2,1)S(1)}, u32[]{:S(2)}, u32[]{:S(2)}) collective-permute-start(bf16[24,1152]{1,0:T(8,128)(2,1)} %refs_1_.1), channel_id=1, source_target_pairs={{0,4},{1,5},{2,6},{3,7},{4,0},{5,1},{6,2},{7,3},{8,12},{9,13},{10,... | collective-permute-start | bytes 165896 | tf_op jit(solution)/shard_map/ppermute | solution.py:17
  8.2 5.3 %collective-permute-start.1 = (bf16[36,768]{1,0:T(8,128)(2,1)}, bf16[36,768]{1,0:T(8,128)(2,1)S(1)}, u32[]{:S(2)}, u32[]{:S(2)}) collective-permute-start(bf16[36,768]{1,0:T(8,128)(2,1)} %refs_2_.1), channel_id=1, source_target_pairs={{0,16},{1,17},{2,18},{3,19},{4,20},{5,21},{6,22},{7,23},{8,24},{9,... | collective-permute-start | bytes 165896 | tf_op jit(solution)/shard_map/ppermute | solution.py:17
  8.3 0.9 %copy-start.2 = (bf16[3,24,768]{2,1,0:T(8,128)(2,1)S(1)}, bf16[3,24,768]{2,1,0:T(8,128)(2,1)}, u32[]{:S(2)}) copy-start(bf16[3,24,768]{2,1,0:T(8,128)(2,1)} %refs_0_.1) | copy-start | bytes 331780
  9.2 0.8 copy-start.3
  10.0 0.8 copy-start.4
  13.6 11.1 %collective-permute-start.5 = (bf16[4,24,1152]{2,1,0:T(8,128)(2,1)S(1)}, bf16[4,24,1152]{2,1,0:T(8,128)(2,1)S(1)}, u32[]{:S(2)}, u32[]{:S(2)}) collective-permute-start(bf16[4,24,1152]{2,1,0:T(8,128)(2,1)S(1)} %shard_map.104.refs_0_), channel_id=1, source_target_pairs={{0,16},{1,17},{2,18},{3,19},{4,20},{5,21},{6,22},{7,23},{8,24},{9,... | collective-permute-start | bytes 663560 | tf_op jit(solution)/shard_map/ppermute | solution.py:17
  14.1 6.2 %copy-start = (bf16[1,256,768]{2,1,0:T(8,128)(2,1)S(1)}, bf16[1,256,768]{2,1,0:T(8,128)(2,1)}, u32[]{:S(2)}) copy-start(bf16[1,256,768]{2,1,0:T(8,128)(2,1)} %tokens_ref.4) | copy-start | bytes 1179652
  14.1 6.2 %copy-start.1 = (bf16[1,256,768]{2,1,0:T(8,128)(2,1)S(1)}, bf16[1,256,768]{2,1,0:T(8,128)(2,1)}, u32[]{:S(2)}) copy-start(bf16[1,256,768]{2,1,0:T(8,128)(2,1)} %cotangent_ref.4) | copy-start | bytes 1179652
  14.2 13.5 %collective-permute-start.8 = (bf16[2,112,768]{2,1,0:T(8,128)(2,1)S(1)}, bf16[2,112,768]{2,1,0:T(8,128)(2,1)S(1)}, u32[]{:S(2)}, u32[]{:S(2)}) collective-permute-start(bf16[2,112,768]{2,1,0:T(8,128)(2,1)S(1)} %shard_map.103.refs_0_), channel_id=1, source_target_pairs={{0,8},{1,9},{2,10},{3,11},{4,12},{5,13},{6,14},{7,15},{8,0},{9,1},... | collective-permute-start | bytes 1032200 | tf_op jit(solution)/shard_map/ppermute | solution.py:17
  17.3 10.3 %collective-permute-start.7 = (bf16[2,112,768]{2,1,0:T(8,128)(2,1)S(1)}, bf16[2,112,768]{2,1,0:T(8,128)(2,1)S(1)}, u32[]{:S(2)}, u32[]{:S(2)}) collective-permute-start(bf16[2,112,768]{2,1,0:T(8,128)(2,1)S(1)} %shard_map.103.refs_0_), channel_id=1, source_target_pairs={{0,4},{1,5},{2,6},{3,7},{4,0},{5,1},{6,2},{7,3},{8,12},{9,13},{10,... | collective-permute-start | bytes 1032200 | tf_op jit(solution)/shard_map/ppermute | solution.py:17
  18.8 13.2 %collective-permute-start.6 = (bf16[2,112,768]{2,1,0:T(8,128)(2,1)S(1)}, bf16[2,112,768]{2,1,0:T(8,128)(2,1)S(1)}, u32[]{:S(2)}, u32[]{:S(2)}) collective-permute-start(bf16[2,112,768]{2,1,0:T(8,128)(2,1)S(1)} %shard_map.103.refs_0_), channel_id=1, source_target_pairs={{0,2},{1,3},{2,0},{3,1},{4,6},{5,7},{6,4},{7,5},{8,10},{9,11},{10,... | collective-permute-start | bytes 1032200 | tf_op jit(solution)/shard_map/ppermute | solution.py:17
  20.4 14.4 %collective-permute-start.13 = (bf16[1,192,768]{2,1,0:T(8,128)(2,1)S(1)}, bf16[1,192,768]{2,1,0:T(8,128)(2,1)S(1)}, u32[]{:S(2)}, u32[]{:S(2)}) collective-permute-start(bf16[1,192,768]{2,1,0:T(8,128)(2,1)S(1)} %get-tuple-element.76), channel_id=1, source_target_pairs={{1,2},{3,4},{5,6},{7,8},{9,10},{11,12},{13,14},{15,16},{17,18},{19... | collective-permute-start | bytes 884744 | tf_op jit(solution)/shard_map/ppermute | solution.py:403
  32.0 11.1 %collective-permute-start.11 = (bf16[3,112,768]{2,1,0:T(8,128)(2,1)S(1)}, bf16[3,112,768]{2,1,0:T(8,128)(2,1)S(1)}, u32[]{:S(2)}, u32[]{:S(2)}) collective-permute-start(bf16[3,112,768]{2,1,0:T(8,128)(2,1)S(1)} %shard_map.108), channel_id=1, source_target_pairs={{0,4},{1,5},{2,6},{3,7},{4,0},{5,1},{6,2},{7,3},{8,12},{9,13},{10,... | collective-permute-start | bytes 1548296 | tf_op jit(solution)/shard_map/ppermute | solution.py:17
  32.1 13.2 %collective-permute-start.10 = (bf16[3,112,768]{2,1,0:T(8,128)(2,1)S(1)}, bf16[3,112,768]{2,1,0:T(8,128)(2,1)S(1)}, u32[]{:S(2)}, u32[]{:S(2)}) collective-permute-start(bf16[3,112,768]{2,1,0:T(8,128)(2,1)S(1)} %shard_map.107), channel_id=1, source_target_pairs={{0,2},{1,3},{2,0},{3,1},{4,6},{5,7},{6,4},{7,5},{8,10},{9,11},{10,... | collective-permute-start | bytes 1548296 | tf_op jit(solution)/shard_map/ppermute | solution.py:17
  34.7 8.3 %collective-permute-start.9 = (bf16[8,24,1152]{2,1,0:T(8,128)(2,1)S(1)}, bf16[8,24,1152]{2,1,0:T(8,128)(2,1)S(1)}, u32[]{:S(2)}, u32[]{:S(2)}) collective-permute-start(bf16[8,24,1152]{2,1,0:T(8,128)(2,1)S(1)} %shard_map.105.refs_0_), channel_id=1, source_target_pairs={{0,8},{1,9},{2,10},{3,11},{4,12},{5,13},{6,14},{7,15},{8,0},{9,1},... | collective-permute-start | bytes 1327112 | tf_op jit(solution)/shard_map/ppermute | solution.py:17
  34.8 8.3 %collective-permute-start.12 = (bf16[1,192,768]{2,1,0:T(8,128)(2,1)S(1)}, bf16[1,192,768]{2,1,0:T(8,128)(2,1)S(1)}, u32[]{:S(2)}, u32[]{:S(2)}) collective-permute-start(bf16[1,192,768]{2,1,0:T(8,128)(2,1)S(1)} %get-tuple-element.75), channel_id=1, source_target_pairs={{0,1},{1,0},{2,3},{3,2},{4,5},{5,4},{6,7},{7,6},{8,9},{9,8},{10,11... | collective-permute-start | bytes 884744 | tf_op jit(solution)/shard_map/ppermute | solution.py:17
  34.8 12.7 %copy-start.6 = (f32[768]{0:T(1024)S(1)}, f32[768]{0:T(1024)}, u32[]{:S(2)}) copy-start(f32[768]{0:T(1024)} %param.9) | copy-start | bytes 9220
  45.4 5.5 %collective-permute-start.15 = (bf16[1,112,768]{2,1,0:T(8,128)(2,1)S(1)}, bf16[1,112,768]{2,1,0:T(8,128)(2,1)S(1)}, u32[]{:S(2)}, u32[]{:S(2)}) collective-permute-start(bf16[1,112,768]{2,1,0:T(8,128)(2,1)S(1)} %shard_map.114), channel_id=1, source_target_pairs={{0,4},{1,5},{2,6},{3,7},{4,0},{5,1},{6,2},{7,3},{8,12},{9,13},{10,... | collective-permute-start | bytes 516104 | tf_op jit(solution)/shard_map/ppermute | solution.py:17
  45.5 5.5 %collective-permute-start.16 = (bf16[1,112,768]{2,1,0:T(8,128)(2,1)S(1)}, bf16[1,112,768]{2,1,0:T(8,128)(2,1)S(1)}, u32[]{:S(2)}, u32[]{:S(2)}) collective-permute-start(bf16[1,112,768]{2,1,0:T(8,128)(2,1)S(1)} %shard_map.115), channel_id=1, source_target_pairs={{0,2},{1,3},{2,0},{3,1},{4,6},{5,7},{6,4},{7,5},{8,10},{9,11},{10,... | collective-permute-start | bytes 516104 | tf_op jit(solution)/shard_map/ppermute | solution.py:17
  47.5 1.1 %copy-start.5 = (s32[4]{0:T(128)S(1)}, s32[4]{0:T(128)}, u32[]{:S(2)}) copy-start(s32[4]{0:T(128)} %starts_ref.3) | copy-start | bytes 52
  47.7 7.6 %collective-permute-start.18 = (bf16[14,40,768]{2,1,0:T(8,128)(2,1)S(1)}, bf16[14,40,768]{2,1,0:T(8,128)(2,1)S(1)}, u32[]{:S(2)}, u32[]{:S(2)}) collective-permute-start(bf16[14,40,768]{2,1,0:T(8,128)(2,1)S(1)} %get-tuple-element.89.refs_0_), channel_id=1, source_target_pairs={{0,1},{1,0},{2,3},{3,2},{4,5},{5,4},{6,7},{7,6},{8,9},{9,8},{10,11... | collective-permute-start | bytes 2580488 | tf_op jit(solution)/shard_map/ppermute | solution.py:17
  47.8 3.8 %collective-permute-start.20 = (bf16[16,24,1152]{2,1,0:T(8,128)(2,1)S(1)}, bf16[16,24,1152]{2,1,0:T(8,128)(2,1)S(1)}, u32[]{:S(2)}, u32[]{:S(2)}) collective-permute-start(bf16[16,24,1152]{2,1,0:T(8,128)(2,1)S(1)} %shard_map.106.refs_0_), channel_id=1, source_target_pairs={{0,1},{1,0},{2,3},{3,2},{4,5},{5,4},{6,7},{7,6},{8,9},{9,8},{10,11... | collective-permute-start | bytes 2654216 | tf_op jit(solution)/shard_map/ppermute | solution.py:17
  48.3 5.7 %collective-permute-start.14 = (bf16[14,72,768]{2,1,0:T(8,128)(2,1)S(1)}, bf16[14,72,768]{2,1,0:T(8,128)(2,1)S(1)}, u32[]{:S(2)}, u32[]{:S(2)}) collective-permute-start(bf16[14,72,768]{2,1,0:T(8,128)(2,1)S(1)} %get-tuple-element.86.refs_0_), channel_id=1, source_target_pairs={{0,1},{1,0},{2,3},{3,2},{4,5},{5,4},{6,7},{7,6},{8,9},{9,8},{10,11... | collective-permute-start | bytes 4644872 | tf_op jit(solution)/shard_map/ppermute | solution.py:17
  51.0 3.0 %collective-permute-start.17 = (bf16[2,72,768]{2,1,0:T(8,128)(2,1)S(1)}, bf16[2,72,768]{2,1,0:T(8,128)(2,1)S(1)}, u32[]{:S(2)}, u32[]{:S(2)}) collective-permute-start(bf16[2,72,768]{2,1,0:T(8,128)(2,1)S(1)} %get-tuple-element.88.refs_2_), channel_id=1, source_target_pairs={{0,1},{1,0},{2,3},{3,2},{4,5},{5,4},{6,7},{7,6},{8,9},{9,8},{10,11... | collective-permute-start | bytes 663560 | tf_op jit(solution)/shard_map/ppermute | solution.py:17
  51.0 4.3 %collective-permute-start.19 = (bf16[2,40,768]{2,1,0:T(8,128)(2,1)S(1)}, bf16[2,40,768]{2,1,0:T(8,128)(2,1)S(1)}, u32[]{:S(2)}, u32[]{:S(2)}) collective-permute-start(bf16[2,40,768]{2,1,0:T(8,128)(2,1)S(1)} %get-tuple-element.90.refs_2_), channel_id=1, source_target_pairs={{0,1},{1,0},{2,3},{3,2},{4,5},{5,4},{6,7},{7,6},{8,9},{9,8},{10,11... | collective-permute-start | bytes 368648 | tf_op jit(solution)/shard_map/ppermute | solution.py:17
  56.9 2.6 %collective-permute-start.21 = (bf16[4,2,2,40,768]{4,3,2,1,0:T(8,128)(2,1)S(1)}, bf16[4,2,2,40,768]{4,3,2,1,0:T(8,128)(2,1)S(1)}, u32[]{:S(2)}, u32[]{:S(2)}) collective-permute-start(bf16[4,2,2,40,768]{4,3,2,1,0:T(8,128)(2,1)S(1)} %get-tuple-element.104), channel_id=1, source_target_pairs={{0,1},{1,0},{2,3},{3,2},{4,5},{5,4},{6,7},{7,6},{8,9},{9,8},{10,11... | collective-permute-start | bytes 2949128 | tf_op jit(solution)/shard_map/ppermute | solution.py:17
  59.7 17.6 %collective-permute-start.22 = (bf16[4,40,768]{2,1,0:T(8,128)(2,1)S(1)}, bf16[4,40,768]{2,1,0:T(8,128)(2,1)S(1)}, u32[]{:S(2)}, u32[]{:S(2)}) collective-permute-start(bf16[4,40,768]{2,1,0:T(8,128)(2,1)S(1)} %get-tuple-element.107), channel_id=1, source_target_pairs={{0,2},{1,3},{2,0},{3,1},{4,6},{5,7},{6,4},{7,5},{8,10},{9,11},{10,... | collective-permute-start | bytes 737288 | tf_op jit(solution)/shard_map/ppermute | solution.py:17
  60.3 17.0 %collective-permute-start.23 = (bf16[4,40,768]{2,1,0:T(8,128)(2,1)S(1)}, bf16[4,40,768]{2,1,0:T(8,128)(2,1)S(1)}, u32[]{:S(2)}, u32[]{:S(2)}) collective-permute-start(bf16[4,40,768]{2,1,0:T(8,128)(2,1)S(1)} %get-tuple-element.108), channel_id=1, source_target_pairs={{0,4},{1,5},{2,6},{3,7},{4,0},{5,1},{6,2},{7,3},{8,12},{9,13},{10,... | collective-permute-start | bytes 737288 | tf_op jit(solution)/shard_map/ppermute | solution.py:17
  61.9 15.5 %collective-permute-start.24 = (bf16[4,40,768]{2,1,0:T(8,128)(2,1)S(1)}, bf16[4,40,768]{2,1,0:T(8,128)(2,1)S(1)}, u32[]{:S(2)}, u32[]{:S(2)}) collective-permute-start(bf16[4,40,768]{2,1,0:T(8,128)(2,1)S(1)} %get-tuple-element.109), channel_id=1, source_target_pairs={{0,6},{1,7},{2,4},{3,5},{4,2},{5,3},{6,0},{7,1},{8,14},{9,15},{10,... | collective-permute-start | bytes 737288 | tf_op jit(solution)/shard_map/ppermute | solution.py:17
  68.9 1.2 %collective-permute-start.25 = (f32[1,768]{1,0:T(1,128)S(1)}, f32[1,768]{1,0:T(1,128)S(1)}, u32[]{:S(2)}, u32[]{:S(2)}) collective-permute-start(f32[1,768]{1,0:T(1,128)S(1)} %get-tuple-element.110), channel_id=1, source_target_pairs={{0,1},{1,0},{2,3},{3,2},{4,5},{5,4},{6,7},{7,6},{8,9},{9,8},{10,11... | collective-permute-start | bytes 9224 | tf_op jit(solution)/shard_map/ppermute | solution.py:17
  70.1 3.6 %collective-permute-start.26 = (f32[1,768]{1,0:T(1,128)S(1)}, f32[1,768]{1,0:T(1,128)S(1)}, u32[]{:S(2)}, u32[]{:S(2)}) collective-permute-start(f32[1,768]{1,0:T(1,128)S(1)} %add.9), channel_id=1, source_target_pairs={{0,2},{1,3},{2,0},{3,1},{4,6},{5,7},{6,4},{7,5},{8,10},{9,11},{10,... | collective-permute-start | bytes 9224 | tf_op jit(solution)/shard_map/ppermute | solution.py:17
  73.7 3.6 %collective-permute-start.27 = (f32[1,768]{1,0:T(1,128)S(1)}, f32[1,768]{1,0:T(1,128)S(1)}, u32[]{:S(2)}, u32[]{:S(2)}) collective-permute-start(f32[1,768]{1,0:T(1,128)S(1)} %add.10), channel_id=1, source_target_pairs={{0,4},{1,5},{2,6},{3,7},{4,0},{5,1},{6,2},{7,3},{8,12},{9,13},{10,... | collective-permute-start | bytes 9224 | tf_op jit(solution)/shard_map/ppermute | solution.py:17
  77.5 4.5 %collective-permute-start.28 = (bf16[40,768]{1,0:T(8,128)(2,1)S(1)}, bf16[40,768]{1,0:T(8,128)(2,1)S(1)}, u32[]{:S(2)}, u32[]{:S(2)}) collective-permute-start(bf16[40,768]{1,0:T(8,128)(2,1)S(1)} %get-tuple-element.113), channel_id=1, source_target_pairs={{0,8},{1,9},{2,10},{3,11},{4,12},{5,13},{6,14},{7,15},{8,0},{9,1},... | collective-permute-start | bytes 184328 | tf_op jit(solution)/shard_map/ppermute | solution.py:17
  78.0 5.2 %collective-permute-start.29 = (bf16[40,768]{1,0:T(8,128)(2,1)S(1)}, bf16[40,768]{1,0:T(8,128)(2,1)S(1)}, u32[]{:S(2)}, u32[]{:S(2)}) collective-permute-start(bf16[40,768]{1,0:T(8,128)(2,1)S(1)} %get-tuple-element.114), channel_id=1, source_target_pairs={{0,16},{1,17},{2,18},{3,19},{4,20},{5,21},{6,22},{7,23},{8,24},{9,... | collective-permute-start | bytes 184328 | tf_op jit(solution)/shard_map/ppermute | solution.py:17
  78.8 6.1 %collective-permute-start.30 = (bf16[40,768]{1,0:T(8,128)(2,1)S(1)}, bf16[40,768]{1,0:T(8,128)(2,1)S(1)}, u32[]{:S(2)}, u32[]{:S(2)}) collective-permute-start(bf16[40,768]{1,0:T(8,128)(2,1)S(1)} %get-tuple-element.115), channel_id=1, source_target_pairs={{0,24},{1,25},{2,26},{3,27},{4,28},{5,29},{6,30},{7,31},{8,16},{9,... | collective-permute-start | bytes 184328 | tf_op jit(solution)/shard_map/ppermute | solution.py:17

commit v7 on v5

--- a/solution.py
+++ b/solution.py
@@ -726,8 +726,6 @@
         mixed, hidden, down, mixed_grad, normed_grad, scaled, inverse, gain
     )
     for mask in (1, 2, 4):
-        if mask == 4:
-            gain_term = after(gain_term, output)
         gain_term = gain_term + swap(gain_term, mask)
     factor = float(ctx_count * data_count * bins * seqs) ** (-0.5)
     each = total.shape[0] // ctx_count

time: 86 us -> 86 us (level)
  transfers between devices with their start and end apart: 31 -> 31, of which waited for: 15 -> 14; matrix products, arithmetic and copies ran while one was open for 0% -> 0% of each run, Pallas kernels for 14% -> 14%
where the time goes in v7:
time: 86 us; the launch traced here: 85.7 us
  waiting for transfers between devices  34.6 us (40%)
  starting transfers between devices  33.4 us (39%)
  Pallas kernels  14.2 us (17%)
  local copies, waits for them, and re-layouts  2.56 us (3%)
  between operations  0.96 us (1%)
    ppermute x30, waiting for transfers between devices, swap(): return lax.ppermute(value, 'ctx', [(i, i ^ mask) for i in range(devices)])  34.6 us
    ppermute x30, starting transfers between devices, swap(): return lax.ppermute(value, 'ctx', [(i, i ^ mask) for i in range(devices)])  32.7 us
    pallas_call x26, Pallas kernels, call(): pl.pallas_call(kernel, out_shape=shapes, in_specs=[SMEM if i in smem else...  13.9 us
    unnamed x14, local copies, waits for them, and re-layouts  2.56 us
  transfers between devices with their start and end apart: 31, of which 14 were waited for; matrix products, arithmetic and copies ran while one was open for 0% of the time, Pallas kernels for 14%

profile of v7, /device:TPU:0, one launch (start us, length us, event | category | flops | bytes accessed | tf_op | source)
XLA Modules:
  0.0 85.7 jit_solution(7571177774483116159)
XLA Ops:
  0.6 4.1 %collective-permute-start = (bf16[3,24,768]{2,1,0:T(8,128)(2,1)}, bf16[3,24,768]{2,1,0:T(8,128)(2,1)S(1)}, u32[]{:S(2)}, u32[]{:S(2)}) collective-permute-start(bf16[3,24,768]{2,1,0:T(8,128)(2,1)} %refs_0_.1), channel_id=1, source_target_pairs={{0,16},{1,17},{2,18},{3,19},{4,20},{5,21},{6,22},{7,23},{8,24},{9,... | collective-permute-start | bytes 331784 | tf_op jit(solution)/shard_map/ppermute | solution.py:17
  4.7 1.5 %collective-permute-start.2 = (bf16[24,1152]{1,0:T(8,128)(2,1)}, bf16[24,1152]{1,0:T(8,128)(2,1)S(1)}, u32[]{:S(2)}, u32[]{:S(2)}) collective-permute-start(bf16[24,1152]{1,0:T(8,128)(2,1)} %refs_1_.1), channel_id=1, source_target_pairs={{0,2},{1,3},{2,0},{3,1},{4,6},{5,7},{6,4},{7,5},{8,10},{9,11},{10,... | collective-permute-start | bytes 165896 | tf_op jit(solution)/shard_map/ppermute | solution.py:17
  6.2 1.5 %collective-permute-start.4 = (bf16[24,1152]{1,0:T(8,128)(2,1)}, bf16[24,1152]{1,0:T(8,128)(2,1)S(1)}, u32[]{:S(2)}, u32[]{:S(2)}) collective-permute-start(bf16[24,1152]{1,0:T(8,128)(2,1)} %refs_1_.1), channel_id=1, source_target_pairs={{0,6},{1,7},{2,4},{3,5},{4,2},{5,3},{6,0},{7,1},{8,14},{9,15},{10,... | collective-permute-start | bytes 165896 | tf_op jit(solution)/shard_map/ppermute | solution.py:17
  7.7 0.5 collective-permute-start.3
  8.3 0.9 %copy-done.2 = bf16[3,24,768]{2,1,0:T(8,128)(2,1)S(1)} copy-done((bf16[3,24,768]{2,1,0:T(8,128)(2,1)S(1)}, bf16[3,24,768]{2,1,0:T(8,128)(2,1)}, u32[]{:S(2)}) %copy-start.2) | copy-done | bytes 110616
  9.2 0.8 copy-done.3
  10.0 0.8 copy-done.4
  10.8 0.3 shard_map.102
  11.1 0.3 collective-permute-done.4.refs_3_
  11.5 0.6 collective-permute-done.3.refs_2_
  12.1 1.5 %collective-permute-done.1.refs_3_ = bf16[36,768]{1,0:T(8,128)(2,1)S(1)} collective-permute-done((bf16[36,768]{1,0:T(8,128)(2,1)}, bf16[36,768]{1,0:T(8,128)(2,1)S(1)}, u32[]{:S(2)}, u32[]{:S(2)}) %collective-permute-start.1) | collective-permute-done | bytes 55328 | tf_op jit(solution)/shard_map/ppermute | solution.py:17
  13.6 1.6 %collective-permute-start.8 = (bf16[2,112,768]{2,1,0:T(8,128)(2,1)S(1)}, bf16[2,112,768]{2,1,0:T(8,128)(2,1)S(1)}, u32[]{:S(2)}, u32[]{:S(2)}) collective-permute-start(bf16[2,112,768]{2,1,0:T(8,128)(2,1)S(1)} %shard_map.103.refs_0_), channel_id=1, source_target_pairs={{0,8},{1,9},{2,10},{3,11},{4,12},{5,13},{6,14},{7,15},{8,0},{9,1},... | collective-permute-start | bytes 1032200 | tf_op jit(solution)/shard_map/ppermute | solution.py:17
  15.2 1.5 %collective-permute-start.7 = (bf16[2,112,768]{2,1,0:T(8,128)(2,1)S(1)}, bf16[2,112,768]{2,1,0:T(8,128)(2,1)S(1)}, u32[]{:S(2)}, u32[]{:S(2)}) collective-permute-start(bf16[2,112,768]{2,1,0:T(8,128)(2,1)S(1)} %shard_map.103.refs_0_), channel_id=1, source_target_pairs={{0,4},{1,5},{2,6},{3,7},{4,0},{5,1},{6,2},{7,3},{8,12},{9,13},{10,... | collective-permute-start | bytes 1032200 | tf_op jit(solution)/shard_map/ppermute | solution.py:17
  16.7 1.5 %collective-permute-start.6 = (bf16[2,112,768]{2,1,0:T(8,128)(2,1)S(1)}, bf16[2,112,768]{2,1,0:T(8,128)(2,1)S(1)}, u32[]{:S(2)}, u32[]{:S(2)}) collective-permute-start(bf16[2,112,768]{2,1,0:T(8,128)(2,1)S(1)} %shard_map.103.refs_0_), channel_id=1, source_target_pairs={{0,2},{1,3},{2,0},{3,1},{4,6},{5,7},{6,4},{7,5},{8,10},{9,11},{10,... | collective-permute-start | bytes 1032200 | tf_op jit(solution)/shard_map/ppermute | solution.py:17
  18.3 2.0 %collective-permute-start.5 = (bf16[4,24,1152]{2,1,0:T(8,128)(2,1)S(1)}, bf16[4,24,1152]{2,1,0:T(8,128)(2,1)S(1)}, u32[]{:S(2)}, u32[]{:S(2)}) collective-permute-start(bf16[4,24,1152]{2,1,0:T(8,128)(2,1)S(1)} %shard_map.104.refs_0_), channel_id=1, source_target_pairs={{0,16},{1,17},{2,18},{3,19},{4,20},{5,21},{6,22},{7,23},{8,24},{9,... | collective-permute-start | bytes 663560 | tf_op jit(solution)/shard_map/ppermute | solution.py:17
  20.4 0.7 collective-permute-start.13
  21.0 9.0 %collective-permute-done.5.refs_1_ = bf16[4,24,1152]{2,1,0:T(8,128)(2,1)S(1)} collective-permute-done((bf16[4,24,1152]{2,1,0:T(8,128)(2,1)S(1)}, bf16[4,24,1152]{2,1,0:T(8,128)(2,1)S(1)}, u32[]{:S(2)}, u32[]{:S(2)}) %collective-permute-start.5) | collective-permute-done | bytes 221216 | tf_op jit(solution)/shard_map/ppermute | solution.py:17
  30.2 1.5 %collective-permute-start.10 = (bf16[3,112,768]{2,1,0:T(8,128)(2,1)S(1)}, bf16[3,112,768]{2,1,0:T(8,128)(2,1)S(1)}, u32[]{:S(2)}, u32[]{:S(2)}) collective-permute-start(bf16[3,112,768]{2,1,0:T(8,128)(2,1)S(1)} %shard_map.107), channel_id=1, source_target_pairs={{0,2},{1,3},{2,0},{3,1},{4,6},{5,7},{6,4},{7,5},{8,10},{9,11},{10,... | collective-permute-start | bytes 1548296 | tf_op jit(solution)/shard_map/ppermute | solution.py:17
  31.8 1.7 %collective-permute-start.9 = (bf16[8,24,1152]{2,1,0:T(8,128)(2,1)S(1)}, bf16[8,24,1152]{2,1,0:T(8,128)(2,1)S(1)}, u32[]{:S(2)}, u32[]{:S(2)}) collective-permute-start(bf16[8,24,1152]{2,1,0:T(8,128)(2,1)S(1)} %shard_map.105.refs_0_), channel_id=1, source_target_pairs={{0,8},{1,9},{2,10},{3,11},{4,12},{5,13},{6,14},{7,15},{8,0},{9,1},... | collective-permute-start | bytes 1327112 | tf_op jit(solution)/shard_map/ppermute | solution.py:17
  33.5 9.2 %collective-permute-done.9.refs_1_ = bf16[8,24,1152]{2,1,0:T(8,128)(2,1)S(1)} collective-permute-done((bf16[8,24,1152]{2,1,0:T(8,128)(2,1)S(1)}, bf16[8,24,1152]{2,1,0:T(8,128)(2,1)S(1)}, u32[]{:S(2)}, u32[]{:S(2)}) %collective-permute-start.9) | collective-permute-done | bytes 442400 | tf_op jit(solution)/shard_map/ppermute | solution.py:17
  42.9 0.6 collective-permute-start.15
  43.4 1.0 %collective-permute-start.16 = (bf16[1,112,768]{2,1,0:T(8,128)(2,1)S(1)}, bf16[1,112,768]{2,1,0:T(8,128)(2,1)S(1)}, u32[]{:S(2)}, u32[]{:S(2)}) collective-permute-start(bf16[1,112,768]{2,1,0:T(8,128)(2,1)S(1)} %shard_map.115), channel_id=1, source_target_pairs={{0,2},{1,3},{2,0},{3,1},{4,6},{5,7},{6,4},{7,5},{8,10},{9,11},{10,... | collective-permute-start | bytes 516104 | tf_op jit(solution)/shard_map/ppermute | solution.py:17
  44.7 0.5 collective-permute-start.20
  45.5 1.3 %shard_map.112 = (bf16[1,384,2304]{2,1,0:T(8,128)(2,1)S(1)}, f32[1,256,768]{2,1,0:T(8,128)S(1)}, f32[1,256,1]{2,1,0:T(8,128)S(1)}) custom-call(bf16[1,192,768]{2,1,0:T(8,128)(2,1)S(1)} %get-tuple-element.78.before_ref, bf16[1,256,768]{2,1,0:T(8,128)(2,1)S(1)} %copy-done, bf16[1,192,768]{2,1,0:T(8,128)(2,1)S(1)} %get-tuple-element.79.after_ref, ...), custom_call_target="tpu_custom_call" | custom-call | flops 1 | bytes 1 | tf_op jit(solution)/shard_map/pallas_call | solution.py:38
  46.8 1.6 %collective-permute-done.15.refs_0_ = bf16[1,112,768]{2,1,0:T(8,128)(2,1)S(1)} collective-permute-done((bf16[1,112,768]{2,1,0:T(8,128)(2,1)S(1)}, bf16[1,112,768]{2,1,0:T(8,128)(2,1)S(1)}, u32[]{:S(2)}, u32[]{:S(2)}) %collective-permute-start.15) | collective-permute-done | bytes 172064 | tf_op jit(solution)/shard_map/ppermute | solution.py:17
  48.3 0.6 collective-permute-done.16.refs_1_
  49.0 0.5 collective-permute-start.19
  49.7 1.1 %collective-permute-done.17.refs_3_ = bf16[2,72,768]{2,1,0:T(8,128)(2,1)S(1)} collective-permute-done((bf16[2,72,768]{2,1,0:T(8,128)(2,1)S(1)}, bf16[2,72,768]{2,1,0:T(8,128)(2,1)S(1)}, u32[]{:S(2)}, u32[]{:S(2)}) %collective-permute-start.17) | collective-permute-done | bytes 221216 | tf_op jit(solution)/shard_map/ppermute | solution.py:17
  51.1 1.1 %shard_map.118.mixed_ref = f32[1,256,768]{2,1,0:T(8,128)S(1)} custom-call(bf16[1,384,2304]{2,1,0:T(8,128)(2,1)S(1)} %get-tuple-element.80.taps_ref, bf16[1,256,768]{2,1,0:T(8,128)(2,1)S(1)} %copy-done, bf16[2304,768]{1,0:T(8,128)(2,1)S(1)} %bitcast.6), custom_call_target="tpu_custom_call" | custom-call | flops 1 | bytes 1 | tf_op jit(solution)/shard_map/pallas_call | solution.py:38
  52.2 1.3 %shard_map.120 = (f32[1,256,1152]{2,1,0:T(8,128)S(1)}, f32[1,256,1152]{2,1,0:T(8,128)S(1)}, bf16[1,256,1152]{2,1,0:T(8,128)(2,1)S(1)}, f32[1152,768]{1,0:T(8,128)S(1)}) custom-call(f32[1,256,768]{2,1,0:T(8,128)S(1)} %shard_map.118.mixed_ref, bf16[768,1152]{1,0:T(8,128)(2,1)S(1)} %bitcast.9, bf16[1,256,768]{2,1,0:T(8,128)(2,1)S(1)} %copy-done.1), custom_call_target="tpu_custom_call" | custom-call | flops 1 | bytes 1 | tf_op jit(solution)/shard_map/pallas_call | solution.py:38
  54.0 0.6 shard_map.121
  54.6 1.7 %shard_map.122.slope_ref = f32[1,384,1152]{2,1,0:T(8,128)S(1)} custom-call(bf16[1,384,2304]{2,1,0:T(8,128)(2,1)S(1)} %get-tuple-element.80.taps_ref, bf16[1,192,768]{2,1,0:T(8,128)(2,1)S(1)} %get-tuple-element.78.before_ref, bf16[1,192,768]{2,1,0:T(8,128)(2,1)S(1)} %get-tuple-element.79.after_ref, bf16[2304,768]{1,0:T(8,128)(2,1)S(1)} %bitcast.7, ...), custom_call_target="tpu_custom_call" | custom-call | flops 1 | bytes 1 | tf_op jit(solution)/shard_map/pallas_call | solution.py:38
  56.6 1.2 %collective-permute-start.22 = (bf16[4,40,768]{2,1,0:T(8,128)(2,1)S(1)}, bf16[4,40,768]{2,1,0:T(8,128)(2,1)S(1)}, u32[]{:S(2)}, u32[]{:S(2)}) collective-permute-start(bf16[4,40,768]{2,1,0:T(8,128)(2,1)S(1)} %get-tuple-element.106), channel_id=1, source_target_pairs={{0,2},{1,3},{2,0},{3,1},{4,6},{5,7},{6,4},{7,5},{8,10},{9,11},{10,... | collective-permute-start | bytes 737288 | tf_op jit(solution)/shard_map/ppermute | solution.py:17
  57.8 1.5 %collective-permute-start.23 = (bf16[4,40,768]{2,1,0:T(8,128)(2,1)S(1)}, bf16[4,40,768]{2,1,0:T(8,128)(2,1)S(1)}, u32[]{:S(2)}, u32[]{:S(2)}) collective-permute-start(bf16[4,40,768]{2,1,0:T(8,128)(2,1)S(1)} %get-tuple-element.107), channel_id=1, source_target_pairs={{0,4},{1,5},{2,6},{3,7},{4,0},{5,1},{6,2},{7,3},{8,12},{9,13},{10,... | collective-permute-start | bytes 737288 | tf_op jit(solution)/shard_map/ppermute | solution.py:17
  59.3 0.8 collective-permute-start.24
  60.2 3.8 %shard_map.123 = (f32[1,256,768]{2,1,0:T(8,128)S(1)}, f32[1,256,768]{2,1,0:T(8,128)S(1)}, f32[1,768]{1,0:T(1,128)S(1)}) custom-call(bf16[1,192,768]{2,1,0:T(8,128)(2,1)S(1)} %get-tuple-element.78.before_ref, bf16[1,256,768]{2,1,0:T(8,128)(2,1)S(1)} %copy-done.1, bf16[1,192,768]{2,1,0:T(8,128)(2,1)S(1)} %get-tuple-element.79.after_ref, ...), custom_call_target="tpu_custom_call" | custom-call | flops 1 | bytes 1 | tf_op jit(solution)/shard_map/pallas_call | solution.py:38
  64.1 1.1 %collective-permute-done.25 = f32[1,768]{1,0:T(1,128)S(1)} collective-permute-done((f32[1,768]{1,0:T(1,128)S(1)}, f32[1,768]{1,0:T(1,128)S(1)}, u32[]{:S(2)}, u32[]{:S(2)}) %collective-permute-start.25) | collective-permute-done | bytes 3104 | tf_op jit(solution)/shard_map/ppermute | solution.py:17
  65.3 1.1 %collective-permute-start.26 = (f32[1,768]{1,0:T(1,128)S(1)}, f32[1,768]{1,0:T(1,128)S(1)}, u32[]{:S(2)}, u32[]{:S(2)}) collective-permute-start(f32[1,768]{1,0:T(1,128)S(1)} %add.9), channel_id=1, source_target_pairs={{0,2},{1,3},{2,0},{3,1},{4,6},{5,7},{6,4},{7,5},{8,10},{9,11},{10,... | collective-permute-start | bytes 9224 | tf_op jit(solution)/shard_map/ppermute | solution.py:17
  66.4 3.9 %collective-permute-done.26 = f32[1,768]{1,0:T(1,128)S(1)} collective-permute-done((f32[1,768]{1,0:T(1,128)S(1)}, f32[1,768]{1,0:T(1,128)S(1)}, u32[]{:S(2)}, u32[]{:S(2)}) %collective-permute-start.26) | collective-permute-done | bytes 3104 | tf_op jit(solution)/shard_map/ppermute | solution.py:17
  70.3 1.5 %collective-permute-start.27 = (f32[1,768]{1,0:T(1,128)S(1)}, f32[1,768]{1,0:T(1,128)S(1)}, u32[]{:S(2)}, u32[]{:S(2)}) collective-permute-start(f32[1,768]{1,0:T(1,128)S(1)} %add.10), channel_id=1, source_target_pairs={{0,4},{1,5},{2,6},{3,7},{4,0},{5,1},{6,2},{7,3},{8,12},{9,13},{10,... | collective-permute-start | bytes 9224 | tf_op jit(solution)/shard_map/ppermute | solution.py:17
  71.8 2.1 %collective-permute-done.27 = f32[1,768]{1,0:T(1,128)S(1)} collective-permute-done((f32[1,768]{1,0:T(1,128)S(1)}, f32[1,768]{1,0:T(1,128)S(1)}, u32[]{:S(2)}, u32[]{:S(2)}) %collective-permute-start.27) | collective-permute-done | bytes 3104 | tf_op jit(solution)/shard_map/ppermute | solution.py:17
  74.1 3.4 %collective-permute-start.28 = (bf16[40,768]{1,0:T(8,128)(2,1)S(1)}, bf16[40,768]{1,0:T(8,128)(2,1)S(1)}, u32[]{:S(2)}, u32[]{:S(2)}) collective-permute-start(bf16[40,768]{1,0:T(8,128)(2,1)S(1)} %get-tuple-element.111), channel_id=1, source_target_pairs={{0,8},{1,9},{2,10},{3,11},{4,12},{5,13},{6,14},{7,15},{8,0},{9,1},... | collective-permute-start | bytes 184328 | tf_op jit(solution)/shard_map/ppermute | solution.py:17
  77.4 1.6 %collective-permute-start.29 = (bf16[40,768]{1,0:T(8,128)(2,1)S(1)}, bf16[40,768]{1,0:T(8,128)(2,1)S(1)}, u32[]{:S(2)}, u32[]{:S(2)}) collective-permute-start(bf16[40,768]{1,0:T(8,128)(2,1)S(1)} %get-tuple-element.112), channel_id=1, source_target_pairs={{0,16},{1,17},{2,18},{3,19},{4,20},{5,21},{6,22},{7,23},{8,24},{9,... | collective-permute-start | bytes 184328 | tf_op jit(solution)/shard_map/ppermute | solution.py:17
  79.0 0.9 %collective-permute-start.30 = (bf16[40,768]{1,0:T(8,128)(2,1)S(1)}, bf16[40,768]{1,0:T(8,128)(2,1)S(1)}, u32[]{:S(2)}, u32[]{:S(2)}) collective-permute-start(bf16[40,768]{1,0:T(8,128)(2,1)S(1)} %get-tuple-element.113), channel_id=1, source_target_pairs={{0,24},{1,25},{2,26},{3,27},{4,28},{5,29},{6,30},{7,31},{8,16},{9,... | collective-permute-start | bytes 184328 | tf_op jit(solution)/shard_map/ppermute | solution.py:17
  79.9 1.7 %shard_map.124 = (bf16[1,256,768]{2,1,0:T(8,128)(2,1)}, bf16[1,256,768]{2,1,0:T(8,128)(2,1)}) custom-call(f32[1,256,768]{2,1,0:T(8,128)S(1)} %shard_map.118.mixed_ref, bf16[1,256,1152]{2,1,0:T(8,128)(2,1)S(1)} %get-tuple-element.92.hidden_ref, bf16[1152,768]{1,0:T(8,128)(2,1)S(1)} %bitcast.13, f32[1,256,768]{2,1,0:T(8,128)S(1)} %get-tuple-element.96.mixed_grad_ref, ...), custom_call_target="tpu_custom_call" | custom-call | flops 1 | bytes 1 | tf_op jit(solution)/shard_map/pallas_call | solution.py:38
  81.5 1.6 %collective-permute-done.29.refs_1_ = bf16[40,768]{1,0:T(8,128)(2,1)S(1)} collective-permute-done((bf16[40,768]{1,0:T(8,128)(2,1)S(1)}, bf16[40,768]{1,0:T(8,128)(2,1)S(1)}, u32[]{:S(2)}, u32[]{:S(2)}) %collective-permute-start.29) | collective-permute-done | bytes 61472 | tf_op jit(solution)/shard_map/ppermute | solution.py:17
  83.2 1.8 %collective-permute-done.30.refs_2_ = bf16[40,768]{1,0:T(8,128)(2,1)S(1)} collective-permute-done((bf16[40,768]{1,0:T(8,128)(2,1)S(1)}, bf16[40,768]{1,0:T(8,128)(2,1)S(1)}, u32[]{:S(2)}, u32[]{:S(2)}) %collective-permute-start.30) | collective-permute-done | bytes 61472 | tf_op jit(solution)/shard_map/ppermute | solution.py:17
  85.0 0.7 shard_map.128
  (59 shorter events, 2.5 us)
Async XLA Ops:
  0.6 12.9 %collective-permute-start = (bf16[3,24,768]{2,1,0:T(8,128)(2,1)}, bf16[3,24,768]{2,1,0:T(8,128)(2,1)S(1)}, u32[]{:S(2)}, u32[]{:S(2)}) collective-permute-start(bf16[3,24,768]{2,1,0:T(8,128)(2,1)} %refs_0_.1), channel_id=1, source_target_pairs={{0,16},{1,17},{2,18},{3,19},{4,20},{5,21},{6,22},{7,23},{8,24},{9,... | collective-permute-start | bytes 331784 | tf_op jit(solution)/shard_map/ppermute | solution.py:17
  4.7 6.4 %collective-permute-start.2 = (bf16[24,1152]{1,0:T(8,128)(2,1)}, bf16[24,1152]{1,0:T(8,128)(2,1)S(1)}, u32[]{:S(2)}, u32[]{:S(2)}) collective-permute-start(bf16[24,1152]{1,0:T(8,128)(2,1)} %refs_1_.1), channel_id=1, source_target_pairs={{0,2},{1,3},{2,0},{3,1},{4,6},{5,7},{6,4},{7,5},{8,10},{9,11},{10,... | collective-permute-start | bytes 165896 | tf_op jit(solution)/shard_map/ppermute | solution.py:17
  6.2 5.3 %collective-permute-start.4 = (bf16[24,1152]{1,0:T(8,128)(2,1)}, bf16[24,1152]{1,0:T(8,128)(2,1)S(1)}, u32[]{:S(2)}, u32[]{:S(2)}) collective-permute-start(bf16[24,1152]{1,0:T(8,128)(2,1)} %refs_1_.1), channel_id=1, source_target_pairs={{0,6},{1,7},{2,4},{3,5},{4,2},{5,3},{6,0},{7,1},{8,14},{9,15},{10,... | collective-permute-start | bytes 165896 | tf_op jit(solution)/shard_map/ppermute | solution.py:17
  7.7 4.4 %collective-permute-start.3 = (bf16[24,1152]{1,0:T(8,128)(2,1)}, bf16[24,1152]{1,0:T(8,128)(2,1)S(1)}, u32[]{:S(2)}, u32[]{:S(2)}) collective-permute-start(bf16[24,1152]{1,0:T(8,128)(2,1)} %refs_1_.1), channel_id=1, source_target_pairs={{0,4},{1,5},{2,6},{3,7},{4,0},{5,1},{6,2},{7,3},{8,12},{9,13},{10,... | collective-permute-start | bytes 165896 | tf_op jit(solution)/shard_map/ppermute | solution.py:17
  8.2 5.3 %collective-permute-start.1 = (bf16[36,768]{1,0:T(8,128)(2,1)}, bf16[36,768]{1,0:T(8,128)(2,1)S(1)}, u32[]{:S(2)}, u32[]{:S(2)}) collective-permute-start(bf16[36,768]{1,0:T(8,128)(2,1)} %refs_2_.1), channel_id=1, source_target_pairs={{0,16},{1,17},{2,18},{3,19},{4,20},{5,21},{6,22},{7,23},{8,24},{9,... | collective-permute-start | bytes 165896 | tf_op jit(solution)/shard_map/ppermute | solution.py:17
  8.3 0.9 %copy-start.2 = (bf16[3,24,768]{2,1,0:T(8,128)(2,1)S(1)}, bf16[3,24,768]{2,1,0:T(8,128)(2,1)}, u32[]{:S(2)}) copy-start(bf16[3,24,768]{2,1,0:T(8,128)(2,1)} %refs_0_.1) | copy-start | bytes 331780
  9.2 0.8 copy-start.3
  10.0 0.8 copy-start.4
  13.6 16.5 %collective-permute-start.8 = (bf16[2,112,768]{2,1,0:T(8,128)(2,1)S(1)}, bf16[2,112,768]{2,1,0:T(8,128)(2,1)S(1)}, u32[]{:S(2)}, u32[]{:S(2)}) collective-permute-start(bf16[2,112,768]{2,1,0:T(8,128)(2,1)S(1)} %shard_map.103.refs_0_), channel_id=1, source_target_pairs={{0,8},{1,9},{2,10},{3,11},{4,12},{5,13},{6,14},{7,15},{8,0},{9,1},... | collective-permute-start | bytes 1032200 | tf_op jit(solution)/shard_map/ppermute | solution.py:17
  15.2 14.8 %collective-permute-start.7 = (bf16[2,112,768]{2,1,0:T(8,128)(2,1)S(1)}, bf16[2,112,768]{2,1,0:T(8,128)(2,1)S(1)}, u32[]{:S(2)}, u32[]{:S(2)}) collective-permute-start(bf16[2,112,768]{2,1,0:T(8,128)(2,1)S(1)} %shard_map.103.refs_0_), channel_id=1, source_target_pairs={{0,4},{1,5},{2,6},{3,7},{4,0},{5,1},{6,2},{7,3},{8,12},{9,13},{10,... | collective-permute-start | bytes 1032200 | tf_op jit(solution)/shard_map/ppermute | solution.py:17
  16.7 13.3 %collective-permute-start.6 = (bf16[2,112,768]{2,1,0:T(8,128)(2,1)S(1)}, bf16[2,112,768]{2,1,0:T(8,128)(2,1)S(1)}, u32[]{:S(2)}, u32[]{:S(2)}) collective-permute-start(bf16[2,112,768]{2,1,0:T(8,128)(2,1)S(1)} %shard_map.103.refs_0_), channel_id=1, source_target_pairs={{0,2},{1,3},{2,0},{3,1},{4,6},{5,7},{6,4},{7,5},{8,10},{9,11},{10,... | collective-permute-start | bytes 1032200 | tf_op jit(solution)/shard_map/ppermute | solution.py:17
  18.2 2.1 %copy-start = (bf16[1,256,768]{2,1,0:T(8,128)(2,1)S(1)}, bf16[1,256,768]{2,1,0:T(8,128)(2,1)}, u32[]{:S(2)}) copy-start(bf16[1,256,768]{2,1,0:T(8,128)(2,1)} %tokens_ref.4) | copy-start | bytes 1179652
  18.2 2.1 %copy-start.1 = (bf16[1,256,768]{2,1,0:T(8,128)(2,1)S(1)}, bf16[1,256,768]{2,1,0:T(8,128)(2,1)}, u32[]{:S(2)}) copy-start(bf16[1,256,768]{2,1,0:T(8,128)(2,1)} %cotangent_ref.4) | copy-start | bytes 1179652
  18.3 11.7 %collective-permute-start.5 = (bf16[4,24,1152]{2,1,0:T(8,128)(2,1)S(1)}, bf16[4,24,1152]{2,1,0:T(8,128)(2,1)S(1)}, u32[]{:S(2)}, u32[]{:S(2)}) collective-permute-start(bf16[4,24,1152]{2,1,0:T(8,128)(2,1)S(1)} %shard_map.104.refs_0_), channel_id=1, source_target_pairs={{0,16},{1,17},{2,18},{3,19},{4,20},{5,21},{6,22},{7,23},{8,24},{9,... | collective-permute-start | bytes 663560 | tf_op jit(solution)/shard_map/ppermute | solution.py:17
  20.4 13.1 %collective-permute-start.13 = (bf16[1,192,768]{2,1,0:T(8,128)(2,1)S(1)}, bf16[1,192,768]{2,1,0:T(8,128)(2,1)S(1)}, u32[]{:S(2)}, u32[]{:S(2)}) collective-permute-start(bf16[1,192,768]{2,1,0:T(8,128)(2,1)S(1)} %get-tuple-element.75), channel_id=1, source_target_pairs={{1,2},{3,4},{5,6},{7,8},{9,10},{11,12},{13,14},{15,16},{17,18},{19... | collective-permute-start | bytes 884744 | tf_op jit(solution)/shard_map/ppermute | solution.py:403
  30.1 12.7 %collective-permute-start.11 = (bf16[3,112,768]{2,1,0:T(8,128)(2,1)S(1)}, bf16[3,112,768]{2,1,0:T(8,128)(2,1)S(1)}, u32[]{:S(2)}, u32[]{:S(2)}) collective-permute-start(bf16[3,112,768]{2,1,0:T(8,128)(2,1)S(1)} %shard_map.108), channel_id=1, source_target_pairs={{0,4},{1,5},{2,6},{3,7},{4,0},{5,1},{6,2},{7,3},{8,12},{9,13},{10,... | collective-permute-start | bytes 1548296 | tf_op jit(solution)/shard_map/ppermute | solution.py:17
  30.2 12.6 %collective-permute-start.10 = (bf16[3,112,768]{2,1,0:T(8,128)(2,1)S(1)}, bf16[3,112,768]{2,1,0:T(8,128)(2,1)S(1)}, u32[]{:S(2)}, u32[]{:S(2)}) collective-permute-start(bf16[3,112,768]{2,1,0:T(8,128)(2,1)S(1)} %shard_map.107), channel_id=1, source_target_pairs={{0,2},{1,3},{2,0},{3,1},{4,6},{5,7},{6,4},{7,5},{8,10},{9,11},{10,... | collective-permute-start | bytes 1548296 | tf_op jit(solution)/shard_map/ppermute | solution.py:17
  31.8 11.0 %collective-permute-start.9 = (bf16[8,24,1152]{2,1,0:T(8,128)(2,1)S(1)}, bf16[8,24,1152]{2,1,0:T(8,128)(2,1)S(1)}, u32[]{:S(2)}, u32[]{:S(2)}) collective-permute-start(bf16[8,24,1152]{2,1,0:T(8,128)(2,1)S(1)} %shard_map.105.refs_0_), channel_id=1, source_target_pairs={{0,8},{1,9},{2,10},{3,11},{4,12},{5,13},{6,14},{7,15},{8,0},{9,1},... | collective-permute-start | bytes 1327112 | tf_op jit(solution)/shard_map/ppermute | solution.py:17
  33.5 9.3 %collective-permute-start.12 = (bf16[1,192,768]{2,1,0:T(8,128)(2,1)S(1)}, bf16[1,192,768]{2,1,0:T(8,128)(2,1)S(1)}, u32[]{:S(2)}, u32[]{:S(2)}) collective-permute-start(bf16[1,192,768]{2,1,0:T(8,128)(2,1)S(1)} %get-tuple-element.74), channel_id=1, source_target_pairs={{0,1},{1,0},{2,3},{3,2},{4,5},{5,4},{6,7},{7,6},{8,9},{9,8},{10,11... | collective-permute-start | bytes 884744 | tf_op jit(solution)/shard_map/ppermute | solution.py:17
  33.5 10.9 %copy-start.6 = (f32[768]{0:T(1024)S(1)}, f32[768]{0:T(1024)}, u32[]{:S(2)}) copy-start(f32[768]{0:T(1024)} %param.9) | copy-start | bytes 9220
  42.9 5.5 %collective-permute-start.15 = (bf16[1,112,768]{2,1,0:T(8,128)(2,1)S(1)}, bf16[1,112,768]{2,1,0:T(8,128)(2,1)S(1)}, u32[]{:S(2)}, u32[]{:S(2)}) collective-permute-start(bf16[1,112,768]{2,1,0:T(8,128)(2,1)S(1)} %shard_map.114), channel_id=1, source_target_pairs={{0,4},{1,5},{2,6},{3,7},{4,0},{5,1},{6,2},{7,3},{8,12},{9,13},{10,... | collective-permute-start | bytes 516104 | tf_op jit(solution)/shard_map/ppermute | solution.py:17
  43.4 5.5 %collective-permute-start.16 = (bf16[1,112,768]{2,1,0:T(8,128)(2,1)S(1)}, bf16[1,112,768]{2,1,0:T(8,128)(2,1)S(1)}, u32[]{:S(2)}, u32[]{:S(2)}) collective-permute-start(bf16[1,112,768]{2,1,0:T(8,128)(2,1)S(1)} %shard_map.115), channel_id=1, source_target_pairs={{0,2},{1,3},{2,0},{3,1},{4,6},{5,7},{6,4},{7,5},{8,10},{9,11},{10,... | collective-permute-start | bytes 516104 | tf_op jit(solution)/shard_map/ppermute | solution.py:17
  44.4 1.1 %copy-start.5 = (s32[4]{0:T(128)S(1)}, s32[4]{0:T(128)}, u32[]{:S(2)}) copy-start(s32[4]{0:T(128)} %starts_ref.3) | copy-start | bytes 52
  44.6 7.6 %collective-permute-start.18 = (bf16[14,40,768]{2,1,0:T(8,128)(2,1)S(1)}, bf16[14,40,768]{2,1,0:T(8,128)(2,1)S(1)}, u32[]{:S(2)}, u32[]{:S(2)}) collective-permute-start(bf16[14,40,768]{2,1,0:T(8,128)(2,1)S(1)} %get-tuple-element.88.refs_0_), channel_id=1, source_target_pairs={{0,1},{1,0},{2,3},{3,2},{4,5},{5,4},{6,7},{7,6},{8,9},{9,8},{10,11... | collective-permute-start | bytes 2580488 | tf_op jit(solution)/shard_map/ppermute | solution.py:17
  44.7 4.9 %collective-permute-start.20 = (bf16[16,24,1152]{2,1,0:T(8,128)(2,1)S(1)}, bf16[16,24,1152]{2,1,0:T(8,128)(2,1)S(1)}, u32[]{:S(2)}, u32[]{:S(2)}) collective-permute-start(bf16[16,24,1152]{2,1,0:T(8,128)(2,1)S(1)} %shard_map.106.refs_0_), channel_id=1, source_target_pairs={{0,1},{1,0},{2,3},{3,2},{4,5},{5,4},{6,7},{7,6},{8,9},{9,8},{10,11... | collective-permute-start | bytes 2654216 | tf_op jit(solution)/shard_map/ppermute | solution.py:17
  45.2 5.7 %collective-permute-start.14 = (bf16[14,72,768]{2,1,0:T(8,128)(2,1)S(1)}, bf16[14,72,768]{2,1,0:T(8,128)(2,1)S(1)}, u32[]{:S(2)}, u32[]{:S(2)}) collective-permute-start(bf16[14,72,768]{2,1,0:T(8,128)(2,1)S(1)} %get-tuple-element.85.refs_0_), channel_id=1, source_target_pairs={{0,1},{1,0},{2,3},{3,2},{4,5},{5,4},{6,7},{7,6},{8,9},{9,8},{10,11... | collective-permute-start | bytes 4644872 | tf_op jit(solution)/shard_map/ppermute | solution.py:17
  48.9 1.9 %collective-permute-start.17 = (bf16[2,72,768]{2,1,0:T(8,128)(2,1)S(1)}, bf16[2,72,768]{2,1,0:T(8,128)(2,1)S(1)}, u32[]{:S(2)}, u32[]{:S(2)}) collective-permute-start(bf16[2,72,768]{2,1,0:T(8,128)(2,1)S(1)} %get-tuple-element.87.refs_2_), channel_id=1, source_target_pairs={{0,1},{1,0},{2,3},{3,2},{4,5},{5,4},{6,7},{7,6},{8,9},{9,8},{10,11... | collective-permute-start | bytes 663560 | tf_op jit(solution)/shard_map/ppermute | solution.py:17
  49.0 3.2 %collective-permute-start.19 = (bf16[2,40,768]{2,1,0:T(8,128)(2,1)S(1)}, bf16[2,40,768]{2,1,0:T(8,128)(2,1)S(1)}, u32[]{:S(2)}, u32[]{:S(2)}) collective-permute-start(bf16[2,40,768]{2,1,0:T(8,128)(2,1)S(1)} %get-tuple-element.89.refs_2_), channel_id=1, source_target_pairs={{0,1},{1,0},{2,3},{3,2},{4,5},{5,4},{6,7},{7,6},{8,9},{9,8},{10,11... | collective-permute-start | bytes 368648 | tf_op jit(solution)/shard_map/ppermute | solution.py:17
  53.8 2.6 %collective-permute-start.21 = (bf16[4,2,2,40,768]{4,3,2,1,0:T(8,128)(2,1)S(1)}, bf16[4,2,2,40,768]{4,3,2,1,0:T(8,128)(2,1)S(1)}, u32[]{:S(2)}, u32[]{:S(2)}) collective-permute-start(bf16[4,2,2,40,768]{4,3,2,1,0:T(8,128)(2,1)S(1)} %get-tuple-element.103), channel_id=1, source_target_pairs={{0,1},{1,0},{2,3},{3,2},{4,5},{5,4},{6,7},{7,6},{8,9},{9,8},{10,11... | collective-permute-start | bytes 2949128 | tf_op jit(solution)/shard_map/ppermute | solution.py:17
  56.6 17.2 %collective-permute-start.22 = (bf16[4,40,768]{2,1,0:T(8,128)(2,1)S(1)}, bf16[4,40,768]{2,1,0:T(8,128)(2,1)S(1)}, u32[]{:S(2)}, u32[]{:S(2)}) collective-permute-start(bf16[4,40,768]{2,1,0:T(8,128)(2,1)S(1)} %get-tuple-element.106), channel_id=1, source_target_pairs={{0,2},{1,3},{2,0},{3,1},{4,6},{5,7},{6,4},{7,5},{8,10},{9,11},{10,... | collective-permute-start | bytes 737288 | tf_op jit(solution)/shard_map/ppermute | solution.py:17
  57.8 16.1 %collective-permute-start.23 = (bf16[4,40,768]{2,1,0:T(8,128)(2,1)S(1)}, bf16[4,40,768]{2,1,0:T(8,128)(2,1)S(1)}, u32[]{:S(2)}, u32[]{:S(2)}) collective-permute-start(bf16[4,40,768]{2,1,0:T(8,128)(2,1)S(1)} %get-tuple-element.107), channel_id=1, source_target_pairs={{0,4},{1,5},{2,6},{3,7},{4,0},{5,1},{6,2},{7,3},{8,12},{9,13},{10,... | collective-permute-start | bytes 737288 | tf_op jit(solution)/shard_map/ppermute | solution.py:17
  59.3 14.5 %collective-permute-start.24 = (bf16[4,40,768]{2,1,0:T(8,128)(2,1)S(1)}, bf16[4,40,768]{2,1,0:T(8,128)(2,1)S(1)}, u32[]{:S(2)}, u32[]{:S(2)}) collective-permute-start(bf16[4,40,768]{2,1,0:T(8,128)(2,1)S(1)} %get-tuple-element.108), channel_id=1, source_target_pairs={{0,6},{1,7},{2,4},{3,5},{4,2},{5,3},{6,0},{7,1},{8,14},{9,15},{10,... | collective-permute-start | bytes 737288 | tf_op jit(solution)/shard_map/ppermute | solution.py:17
  64.0 1.2 %collective-permute-start.25 = (f32[1,768]{1,0:T(1,128)S(1)}, f32[1,768]{1,0:T(1,128)S(1)}, u32[]{:S(2)}, u32[]{:S(2)}) collective-permute-start(f32[1,768]{1,0:T(1,128)S(1)} %get-tuple-element.109), channel_id=1, source_target_pairs={{0,1},{1,0},{2,3},{3,2},{4,5},{5,4},{6,7},{7,6},{8,9},{9,8},{10,11... | collective-permute-start | bytes 9224 | tf_op jit(solution)/shard_map/ppermute | solution.py:17
  65.3 5.0 %collective-permute-start.26 = (f32[1,768]{1,0:T(1,128)S(1)}, f32[1,768]{1,0:T(1,128)S(1)}, u32[]{:S(2)}, u32[]{:S(2)}) collective-permute-start(f32[1,768]{1,0:T(1,128)S(1)} %add.9), channel_id=1, source_target_pairs={{0,2},{1,3},{2,0},{3,1},{4,6},{5,7},{6,4},{7,5},{8,10},{9,11},{10,... | collective-permute-start | bytes 9224 | tf_op jit(solution)/shard_map/ppermute | solution.py:17
  70.3 3.6 %collective-permute-start.27 = (f32[1,768]{1,0:T(1,128)S(1)}, f32[1,768]{1,0:T(1,128)S(1)}, u32[]{:S(2)}, u32[]{:S(2)}) collective-permute-start(f32[1,768]{1,0:T(1,128)S(1)} %add.10), channel_id=1, source_target_pairs={{0,4},{1,5},{2,6},{3,7},{4,0},{5,1},{6,2},{7,3},{8,12},{9,13},{10,... | collective-permute-start | bytes 9224 | tf_op jit(solution)/shard_map/ppermute | solution.py:17
  74.1 7.5 %collective-permute-start.28 = (bf16[40,768]{1,0:T(8,128)(2,1)S(1)}, bf16[40,768]{1,0:T(8,128)(2,1)S(1)}, u32[]{:S(2)}, u32[]{:S(2)}) collective-permute-start(bf16[40,768]{1,0:T(8,128)(2,1)S(1)} %get-tuple-element.111), channel_id=1, source_target_pairs={{0,8},{1,9},{2,10},{3,11},{4,12},{5,13},{6,14},{7,15},{8,0},{9,1},... | collective-permute-start | bytes 184328 | tf_op jit(solution)/shard_map/ppermute | solution.py:17
  77.4 5.7 %collective-permute-start.29 = (bf16[40,768]{1,0:T(8,128)(2,1)S(1)}, bf16[40,768]{1,0:T(8,128)(2,1)S(1)}, u32[]{:S(2)}, u32[]{:S(2)}) collective-permute-start(bf16[40,768]{1,0:T(8,128)(2,1)S(1)} %get-tuple-element.112), channel_id=1, source_target_pairs={{0,16},{1,17},{2,18},{3,19},{4,20},{5,21},{6,22},{7,23},{8,24},{9,... | collective-permute-start | bytes 184328 | tf_op jit(solution)/shard_map/ppermute | solution.py:17
  79.0 6.0 %collective-permute-start.30 = (bf16[40,768]{1,0:T(8,128)(2,1)S(1)}, bf16[40,768]{1,0:T(8,128)(2,1)S(1)}, u32[]{:S(2)}, u32[]{:S(2)}) collective-permute-start(bf16[40,768]{1,0:T(8,128)(2,1)S(1)} %get-tuple-element.113), channel_id=1, source_target_pairs={{0,24},{1,25},{2,26},{3,27},{4,28},{5,29},{6,30},{7,31},{8,16},{9,... | collective-permute-start | bytes 184328 | tf_op jit(solution)/shard_map/ppermute | solution.py:17
